TPU v7x, 32 devices: a whole 2x2x4 slice. The times are simulated.
32 devices in a mesh: groups: 1, expert: 32 (over z, y, x, core).
Axes of the slice: x: 2, y: 2, z: 4, core: 2. Of those that a mesh axis runs over, the one named last changes fastest.
Arguments:
- tokens: bfloat16 [512, 3584], P(('groups', 'expert')), may hold values from -6 to 6
- expert_ids: int32 [512, 8], P(('groups', 'expert')), may hold values from 0 to 15, all different within a row; in each aligned block of 16 rows (0 to 15, 16 to 31, ...) at most 10 rows name the same one
- gate_values: float32 [512, 8], P(('groups', 'expert')), may hold values from 0.1 to 1
- cotangent: bfloat16 [512, 3584], P(('groups', 'expert')), may hold values from -6 to 6
- gate_weight: bfloat16 [32, 3584, 512], P('expert'), may hold values from -0.09375 to 0.09375
- up_weight: bfloat16 [32, 3584, 512], P('expert'), may hold values from -0.09375 to 0.09375
- down_weight: bfloat16 [32, 512, 3584], P('expert'), may hold values from -0.1875 to 0.1875
Outputs:
- layer_out: bfloat16 [512, 3584], P(('groups', 'expert'))
- token_grad: bfloat16 [512, 3584], P(('groups', 'expert'))
Inputs may be any that keep to these rules, and one draw needn't show every extreme that they name: `expert_ids`: each row names 8 different experts; among the rows of one device no expert is named by more than 10 rows, a bound that some block reaches of them.
All inputs are finite; a program needn't handle non-finite values.
Results may differ from a plain program's by a relative error of at most 0.012.
Values may be sent and summed in bfloat16 or wider, within the bound.
No kernel may reach another device: no remote copies, remote signals or barrier semaphores. Data moves between devices by JAX's collectives and lax.ppermute only.
A program may use at most 128 MiB of HBM per device.

v0:
```python
import jax
import jax.numpy as jnp
from jax import lax
from jax.sharding import PartitionSpec as P


def silu_parts(values):
    sigma = jax.nn.sigmoid(values)
    return (values * sigma, sigma * (1.0 + values * (1.0 - sigma)))


def send_home(partial_value, devices, capacity, model_width):
    experts = devices // 2
    arrived = lax.all_to_all(
        partial_value.reshape(devices, capacity, model_width),
        "expert",
        split_axis=0,
        concat_axis=0,
        tiled=True,
    )
    paired = arrived.reshape(experts, 2, capacity, model_width).astype(jnp.float32)
    summed = (paired[:, 0] + paired[:, 1]).astype(jnp.bfloat16)
    return summed.reshape(experts * capacity, model_width)


def on_device(tokens, expert_ids, gate_values, cotangent, gate_weight, up_weight, down_weight):
    tok_dev, top_count = expert_ids.shape
    model_width = tokens.shape[1]
    devices = lax.axis_size("expert")
    experts = devices // 2
    capacity = min(tok_dev, tok_dev * top_count * 5 // (4 * experts))
    blocks = model_width // 128
    route_rows = tok_dev * top_count
    received_rows = devices * capacity
    flat_ids = expert_ids.reshape(route_rows)
    onehot = (flat_ids[:, None] == jnp.arange(experts, dtype=jnp.int32)[None, :]).astype(
        jnp.float32
    )
    route_order = jnp.arange(route_rows, dtype=jnp.int32)
    earlier_mask = (route_order[:, None] > route_order[None, :]).astype(jnp.float32)
    earlier_count = jnp.dot(earlier_mask, onehot, precision=lax.Precision.HIGHEST)
    slot_index = jnp.sum(onehot * earlier_count, axis=1).astype(jnp.int32)
    positions = flat_ids * capacity + slot_index
    placement = (
        positions[:, None] == jnp.arange(experts * capacity, dtype=jnp.int32)[None, :]
    ).astype(jnp.bfloat16)
    selector = jnp.sum(placement.reshape(tok_dev, top_count, experts * capacity), axis=1)
    blocked = tokens.astype(jnp.float32).reshape(tok_dev, blocks, 128)
    block_scale = (jnp.max(jnp.abs(blocked), axis=2) + 1e-06).astype(jnp.bfloat16)
    quantized = (blocked / block_scale.astype(jnp.float32)[:, :, None]).astype(jnp.bfloat16)
    quantized = quantized.reshape(tok_dev, model_width)
    contract_rows = (((0,), (0,)), ((), ()))
    send_rows = lax.dot_general(
        selector, quantized, contract_rows, preferred_element_type=jnp.float32
    ).astype(jnp.bfloat16)
    send_scales = lax.dot_general(
        selector, block_scale, contract_rows, preferred_element_type=jnp.float32
    ).astype(jnp.bfloat16)
    rows_out = jnp.repeat(send_rows.reshape(experts, capacity, model_width), 2, axis=0)
    scales_out = jnp.repeat(send_scales.reshape(experts, capacity, blocks), 2, axis=0)
    got_rows, got_scales = (
        lax.all_to_all(rows_out, "expert", split_axis=0, concat_axis=0, tiled=True),
        lax.all_to_all(scales_out, "expert", split_axis=0, concat_axis=0, tiled=True),
    )
    got_rows = got_rows.reshape(received_rows, blocks, 128)
    got_scales = got_scales.reshape(received_rows, blocks, 1)
    dequant = (got_rows.astype(jnp.float32) * got_scales.astype(jnp.float32)).astype(jnp.bfloat16)
    dequant = dequant.reshape(received_rows, model_width)
    gate_slab = gate_weight[0]
    up_slab = up_weight[0]
    down_slab = down_weight[0]
    pre_gate = jnp.dot(dequant, gate_slab, preferred_element_type=jnp.float32)
    pre_up = jnp.dot(dequant, up_slab, preferred_element_type=jnp.float32)
    activated, silu_slope = silu_parts(pre_gate)
    hidden = (activated * pre_up).astype(jnp.bfloat16)
    partial_value = jnp.dot(hidden, down_slab, preferred_element_type=jnp.float32).astype(
        jnp.bfloat16
    )
    expert_out = send_home(partial_value, devices, capacity, model_width)
    gathered = expert_out[positions].reshape(tok_dev, top_count, model_width)
    layer_out = jnp.sum(gathered.astype(jnp.float32) * gate_values[:, :, None], axis=1).astype(
        jnp.bfloat16
    )
    route_grad = (gate_values[:, :, None] * cotangent.astype(jnp.float32)[:, None, :]).astype(
        jnp.bfloat16
    )
    route_grad = route_grad.reshape(route_rows, model_width)
    send_grads = lax.dot_general(
        placement, route_grad, contract_rows, preferred_element_type=jnp.float32
    ).astype(jnp.bfloat16)
    grads_out = jnp.repeat(send_grads.reshape(experts, capacity, model_width), 2, axis=0)
    got_grads = lax.all_to_all(grads_out, "expert", split_axis=0, concat_axis=0, tiled=True)
    got_grads = got_grads.reshape(received_rows, model_width)
    contract_cols = (((1,), (1,)), ((), ()))
    hidden_grad = lax.dot_general(
        got_grads, down_slab, contract_cols, preferred_element_type=jnp.float32
    )
    gate_grad = (hidden_grad * pre_up * silu_slope).astype(jnp.bfloat16)
    up_grad = (hidden_grad * activated).astype(jnp.bfloat16)
    back_part = lax.dot_general(
        gate_grad, gate_slab, contract_cols, preferred_element_type=jnp.float32
    )
    back_part = back_part + lax.dot_general(
        up_grad, up_slab, contract_cols, preferred_element_type=jnp.float32
    )
    back_part = back_part.astype(jnp.bfloat16)
    row_grad = send_home(back_part, devices, capacity, model_width)
    routed_grad = row_grad[positions].reshape(tok_dev, top_count, model_width)
    token_grad = jnp.sum(routed_grad.astype(jnp.float32), axis=1).astype(jnp.bfloat16)
    return (layer_out, token_grad)


def solution(mesh):
    placed = (
        P(("groups", "expert"), None),
        P(("groups", "expert"), None),
        P(("groups", "expert"), None),
        P(("groups", "expert"), None),
        P("expert", None, None),
        P("expert", None, None),
        P("expert", None, None),
    )
    return jax.shard_map(
        on_device,
        mesh=mesh,
        in_specs=placed,
        out_specs=(P(("groups", "expert"), None), P(("groups", "expert"), None)),
        check_vma=False,
    )
```

profile of v0, /device:TPU:0, one launch (start us, length us, event | category | flops | bytes accessed | tf_op | source)
XLA Modules:
  0.0 375.9 jit_solution(12459477417248694236)
XLA Ops:
  0.6 0.8 copy.27
  1.5 0.2 fusion.21
  1.8 0.1 fusion.32
  1.9 0.9 convert_abs_fusion
  2.9 0.1 reduce_max.9
  3.0 0.2 convolution_convert_fusion.3
  3.4 0.8 reshape.186
  4.1 7.3 %all-to-all-start.1 = ((bf16[32,2,140]{2,1,0:T(2,128)(2,1)}), bf16[32,2,140]{2,1,0:T(2,128)(2,1)S(1)}, u32[]{:S(2)}, u32[]{:S(2)}) async-start(bf16[32,2,140]{2,1,0:T(2,128)(2,1)} %reshape.186), calls=%async_computation.1 | async-start | bytes 65536 | tf_op jit(solution)/shard_map/all_to_all | solution.py:63
  11.6 1.4 convolution_convert_fusion.2
  13.0 0.4 reshape.155
  13.4 5.3 %all-to-all-done.1 = bf16[32,2,140]{2,1,0:T(2,128)(2,1)S(1)} async-done(((bf16[32,2,140]{2,1,0:T(2,128)(2,1)}), bf16[32,2,140]{2,1,0:T(2,128)(2,1)S(1)}, u32[]{:S(2)}, u32[]{:S(2)}) %all-to-all-start.1) | async-done | bytes 17952 | tf_op jit(solution)/shard_map/all_to_all | solution.py:63
  18.7 2.2 broadcast_in_dim.6
  20.9 3.7 all-to-all-start
  24.8 0.6 convolution_convert_fusion.1
  25.4 0.4 reshape.160
  25.8 81.5 %all-to-all-done = bf16[32,10,3584]{2,1,0:T(8,128)(2,1)} async-done(((bf16[32,10,3584]{2,1,0:T(8,128)(2,1)}), bf16[32,10,3584]{2,1,0:T(8,128)(2,1)}, u32[]{:S(2)}, u32[]{:S(2)}) %all-to-all-start) | async-done | bytes 2293792 | tf_op jit(solution)/shard_map/all_to_all | solution.py:62
  107.3 2.2 broadcast_in_dim.8
  109.6 3.9 %all-to-all-start.3 = ((bf16[32,10,3584]{2,1,0:T(8,128)(2,1)}), bf16[32,10,3584]{2,1,0:T(8,128)(2,1)}, u32[]{:S(2)}, u32[]{:S(2)}) async-start(bf16[32,10,3584]{2,1,0:T(8,128)(2,1)} %bitcast.75), calls=%async_computation.3 | async-start | bytes 7340032 | tf_op jit(solution)/shard_map/all_to_all | solution.py:92
  113.5 0.1 reshape.187
  113.7 6.4 %reshape.165 = f32[320,28,128]{2,1,0:T(8,128)} reshape(bf16[32,10,3584]{2,1,0:T(8,128)(2,1)} %all-to-all-done) | data formatting | bytes 6881280 | tf_op jit(solution)/shard_map/convert_element_type | solution.py:67
  120.1 4.4 %multiply_convert_fusion = bf16[320,28,128]{2,1,0:T(8,128)(2,1)S(1)} fusion(f32[320,28,128]{2,1,0:T(8,128)} %reshape.165, f32[320,28]{1,0:T(8,128)S(1)} %reshape.166), kind=kLoop, calls=%fused_computation.5 | loop fusion | flops 2293760 | bytes 6917120 | tf_op jit(solution)/shard_map/convert_element_type | solution.py:67
  124.5 1.4 fusion.9
  125.9 0.6 copy-done
  126.6 1.4 fusion.13
  128.0 0.9 copy-done.8
  128.8 1.4 convolution_convert_fusion
  130.2 2.6 reshape.159
  132.9 63.3 %all-to-all-done.3 = bf16[32,10,3584]{2,1,0:T(8,128)(2,1)} async-done(((bf16[32,10,3584]{2,1,0:T(8,128)(2,1)}), bf16[32,10,3584]{2,1,0:T(8,128)(2,1)}, u32[]{:S(2)}, u32[]{:S(2)}) %all-to-all-start.3) | async-done | bytes 2293792 | tf_op jit(solution)/shard_map/all_to_all | solution.py:92
  196.2 4.3 %all-to-all-start.2 = ((bf16[32,10,3584]{2,1,0:T(8,128)(2,1)}), bf16[32,10,3584]{2,1,0:T(8,128)(2,1)}, u32[]{:S(2)}, u32[]{:S(2)}) async-start(bf16[32,10,3584]{2,1,0:T(8,128)(2,1)} %reshape.159), calls=%async_computation.2 | async-start | bytes 7340032 | tf_op jit(solution)/shard_map/all_to_all | solution.py:14
  200.4 3.1 reshape.162
  203.6 3.6 fusion.5
  207.2 1.5 fusion.11
  208.7 0.6 copy-done.3
  209.2 1.4 fusion
  210.7 2.6 reshape.163
  213.3 69.7 %all-to-all-done.2 = bf16[32,10,3584]{2,1,0:T(8,128)(2,1)} async-done(((bf16[32,10,3584]{2,1,0:T(8,128)(2,1)}), bf16[32,10,3584]{2,1,0:T(8,128)(2,1)}, u32[]{:S(2)}, u32[]{:S(2)}) %all-to-all-start.2) | async-done | bytes 2293792 | tf_op jit(solution)/shard_map/all_to_all | solution.py:14
  283.0 4.0 %all-to-all-start.4 = ((bf16[32,10,3584]{2,1,0:T(8,128)(2,1)}), bf16[32,10,3584]{2,1,0:T(8,128)(2,1)}, u32[]{:S(2)}, u32[]{:S(2)}) async-start(bf16[32,10,3584]{2,1,0:T(8,128)(2,1)} %reshape.163), calls=%async_computation.4 | async-start | bytes 7340032 | tf_op jit(solution)/shard_map/all_to_all | solution.py:14
  287.1 3.0 convert.7
  290.1 0.4 fusion.4
  290.6 0.4 convert_element_type.183
  291.0 1.1 gather_fusion
  292.1 1.3 fusion.19
  293.5 76.1 %all-to-all-done.4 = bf16[32,10,3584]{2,1,0:T(8,128)(2,1)} async-done(((bf16[32,10,3584]{2,1,0:T(8,128)(2,1)}), bf16[32,10,3584]{2,1,0:T(8,128)(2,1)}, u32[]{:S(2)}, u32[]{:S(2)}) %all-to-all-start.4) | async-done | bytes 2293792 | tf_op jit(solution)/shard_map/all_to_all | solution.py:14
  369.6 3.0 convert.8
  372.6 0.4 fusion.2
  373.1 0.4 convert_element_type.197
  373.5 1.1 gather_fusion.1
  374.7 1.2 bitcast_reduce_fusion
  (33 shorter events, 0.9 us)
Async XLA Ops:
  4.1 14.6 %all-to-all-start.1 = ((bf16[32,2,140]{2,1,0:T(2,128)(2,1)}), bf16[32,2,140]{2,1,0:T(2,128)(2,1)S(1)}, u32[]{:S(2)}, u32[]{:S(2)}) async-start(bf16[32,2,140]{2,1,0:T(2,128)(2,1)} %reshape.186), calls=%async_computation.1 | async-start | bytes 65536 | tf_op jit(solution)/shard_map/all_to_all | solution.py:63
  20.9 3.7 copy-start.7
  20.9 3.8 %copy-start.6 = (bf16[16,3584]{1,0:T(8,128)(2,1)S(1)}, bf16[16,3584]{1,0:T(8,128)(2,1)}, u32[]{:S(2)}) copy-start(bf16[16,3584]{1,0:T(8,128)(2,1)} %param.10) | copy-start | bytes 344068
  20.9 86.4 %all-to-all-start = ((bf16[32,10,3584]{2,1,0:T(8,128)(2,1)}), bf16[32,10,3584]{2,1,0:T(8,128)(2,1)}, u32[]{:S(2)}, u32[]{:S(2)}) async-start(bf16[32,10,3584]{2,1,0:T(8,128)(2,1)} %bitcast.76), calls=%async_computation | async-start | bytes 7340032 | tf_op jit(solution)/shard_map/all_to_all | solution.py:62
  109.6 86.6 %all-to-all-start.3 = ((bf16[32,10,3584]{2,1,0:T(8,128)(2,1)}), bf16[32,10,3584]{2,1,0:T(8,128)(2,1)}, u32[]{:S(2)}, u32[]{:S(2)}) async-start(bf16[32,10,3584]{2,1,0:T(8,128)(2,1)} %bitcast.75), calls=%async_computation.3 | async-start | bytes 7340032 | tf_op jit(solution)/shard_map/all_to_all | solution.py:92
  120.1 4.5 %copy-start.2 = (bf16[1,3584,512]{2,1,0:T(8,128)(2,1)S(1)}, bf16[1,3584,512]{2,1,0:T(8,128)(2,1)}, u32[]{:S(2)}) copy-start(bf16[1,3584,512]{2,1,0:T(8,128)(2,1)} %param.12) | copy-start | bytes 11010052
  124.5 2.0 copy-start
  126.6 1.4 copy-start.4
  126.6 2.3 copy-start.8
  196.2 86.9 %all-to-all-start.2 = ((bf16[32,10,3584]{2,1,0:T(8,128)(2,1)}), bf16[32,10,3584]{2,1,0:T(8,128)(2,1)}, u32[]{:S(2)}, u32[]{:S(2)}) async-start(bf16[32,10,3584]{2,1,0:T(8,128)(2,1)} %reshape.159), calls=%async_computation.2 | async-start | bytes 7340032 | tf_op jit(solution)/shard_map/all_to_all | solution.py:14
  203.6 3.6 copy-start.1
  203.6 3.6 copy-start.5
  207.2 2.0 copy-start.3
  283.0 86.6 %all-to-all-start.4 = ((bf16[32,10,3584]{2,1,0:T(8,128)(2,1)}), bf16[32,10,3584]{2,1,0:T(8,128)(2,1)}, u32[]{:S(2)}, u32[]{:S(2)}) async-start(bf16[32,10,3584]{2,1,0:T(8,128)(2,1)} %reshape.163), calls=%async_computation.4 | async-start | bytes 7340032 | tf_op jit(solution)/shard_map/all_to_all | solution.py:14
where the time goes:
time: 377 us; the launch traced here: 376 us
  waiting for transfers between devices  296 us (79%)
  local copies, waits for them, and re-layouts  27.7 us (7%)
  starting transfers between devices  23.2 us (6%)
  other arithmetic  15.2 us (4%)
  matrix products  12.9 us (3%)
    all_to_all x2, waiting for transfers between devices, send_home(): lax.all_to_all(partial_value.reshape(devices, capacity, model_width), 'ex...  146 us
    all_to_all x1, waiting for transfers between devices, on_device(): lax.all_to_all(rows_out, 'expert', split_axis=0, concat_axis=0, tiled=True)  81.5 us
    all_to_all x1, waiting for transfers between devices, on_device(): lax.all_to_all(grads_out, 'expert', split_axis=0, concat_axis=0, tiled=True)  63.3 us
    all_to_all x2, starting transfers between devices, send_home(): lax.all_to_all(partial_value.reshape(devices, capacity, model_width), 'ex...  8.27 us
  transfers between devices with their start and end apart: 5, of which 5 were waited for; matrix products, arithmetic and copies ran while one was open for 10% of the time, Pallas kernels for 0%

commit v1 on v0

v1 whole, which is shorter than its diff:
```python
import jax
import jax.numpy as jnp
from jax import lax
from jax.sharding import PartitionSpec as P


def code_rows(tokens, blocks):
    blocked = tokens.astype(jnp.float32).reshape(tokens.shape[0], blocks, 128)
    scale = lax.reduce_precision(jnp.max(jnp.abs(blocked), axis=2) + 1e-06, 8, 7)[:, :, None]
    quantized = lax.reduce_precision(blocked / scale, 8, 7)
    dequant = (quantized * scale).astype(jnp.bfloat16)
    return dequant.reshape(tokens.shape)


def gate_columns(expert_ids, gate_values, experts):
    named = expert_ids[:, :, None] == jnp.arange(experts, dtype=jnp.int32)[None, None, :]
    rest = jnp.sum(jnp.where(named, gate_values[:, :, None], 0.0), axis=1)
    pieces = []
    for _ in range(3):
        piece = lax.reduce_precision(rest, 8, 7)
        pieces.append(piece.astype(jnp.bfloat16))
        rest = rest - piece
    return jnp.concatenate(pieces, axis=1)


def on_device(tokens, expert_ids, gate_values, cotangent, gate_weight, up_weight, down_weight):
    width = tokens.shape[1]
    devices = lax.axis_size("expert")
    experts = devices // 2
    expert = lax.axis_index("expert") // 2
    dequant = code_rows(tokens, width // 128)
    columns = gate_columns(expert_ids, gate_values, experts)
    padding = -columns.shape[1] % 128
    columns = jnp.pad(columns, ((0, 0), (0, padding)))
    rows = lax.all_gather(jnp.concatenate([dequant, columns], axis=1), "expert", tiled=True)
    cots = lax.all_gather(cotangent, "expert", tiled=True)
    x = rows[:, :width]
    pieces = rows[:, width : width + 3 * experts].astype(jnp.float32)
    pieces = pieces.reshape(-1, 3, experts)
    mine = (jnp.arange(experts, dtype=jnp.int32) == expert).astype(jnp.float32)
    gate = jnp.sum(jnp.sum(pieces, axis=1) * mine, axis=1, keepdims=True)

    gate_slab, up_slab, down_slab = gate_weight[0], up_weight[0], down_weight[0]
    f32 = jnp.float32
    pre_gate = jnp.dot(x, gate_slab, preferred_element_type=f32)
    pre_up = jnp.dot(x, up_slab, preferred_element_type=f32)
    sigma = jax.nn.sigmoid(pre_gate)
    activated = pre_gate * sigma
    slope = sigma * (1.0 + pre_gate * (1.0 - sigma))
    hidden = (activated * pre_up).astype(jnp.bfloat16)
    partial = jnp.dot(hidden, down_slab, preferred_element_type=f32)
    layer_out = lax.psum_scatter(
        (partial * gate).astype(jnp.bfloat16), "expert", scatter_dimension=0, tiled=True
    )
    contract_cols = (((1,), (1,)), ((), ()))
    hidden_grad = gate * lax.dot_general(cots, down_slab, contract_cols, preferred_element_type=f32)
    gate_grad = (hidden_grad * pre_up * slope).astype(jnp.bfloat16)
    up_grad = (hidden_grad * activated).astype(jnp.bfloat16)
    back = lax.dot_general(gate_grad, gate_slab, contract_cols, preferred_element_type=f32)
    back = back + lax.dot_general(up_grad, up_slab, contract_cols, preferred_element_type=f32)
    token_grad = lax.psum_scatter(
        back.astype(jnp.bfloat16), "expert", scatter_dimension=0, tiled=True
    )
    return layer_out, token_grad


def solution(mesh):
    rows = P(("groups", "expert"), None)
    slabs = P("expert", None, None)
    return jax.shard_map(
        on_device,
        mesh=mesh,
        in_specs=(rows, rows, rows, rows, slabs, slabs, slabs),
        out_specs=(rows, rows),
        check_vma=False,
    )
```

time: 377 us -> 424 us (1.12)
  waiting for transfers between devices: 296 us -> 381 us
  local copies, waits for them, and re-layouts: 27.7 us -> 2.71 us
  starting transfers between devices: 23.2 us -> 0.16 us
  between operations: 1 us -> 13.9 us
  other arithmetic: 15.2 us -> 3.06 us
  matrix products: 12.9 us -> 23.1 us
    all_to_all x5 -> x0, waiting for transfers between devices: 296 us -> none  [the longest x2 146 us: send_home(): lax.all_to_all(partial_value.reshape(devices, capacity, model_width), 'ex...]
    reduce_scatter x0 -> x2, waiting for transfers between devices: none -> 268 us  [the longest x1 138 us: on_device(): lax.psum_scatter(back.astype(jnp.bfloat16), 'expert', scatter_dimension=0...]
    all_gather x0 -> x2, waiting for transfers between devices: none -> 112 us  [the longest x1 62.9 us: on_device(): lax.all_gather(jnp.concatenate([dequant, columns], axis=1), 'expert', til...]
    all_to_all x5 -> x0, starting transfers between devices: 23.2 us -> none  [the longest x2 8.27 us: send_home(): lax.all_to_all(partial_value.reshape(devices, capacity, model_width), 'ex...]
    convert_element_type x8 -> x3, other arithmetic: 11.3 us -> 1.06 us  [the longest x1 1.05 us: code_rows(): dequant = (quantized * scale).astype(jnp.bfloat16)]
    dot_general x9 -> x5, matrix products: 11.4 us -> 20.8 us  [the longest x1 5.37 us: on_device(): lax.dot_general(cots, down_slab, contract_cols, preferred_element_type=f32)]
    reshape x6 -> x0, local copies, waits for them, and re-layouts: 9.24 us -> none  [the longest x2 5.24 us: send_home(): partial_value.reshape(devices, capacity, model_width)]
    convert_element_type x6 -> x0, local copies, waits for them, and re-layouts: 7.5 us -> none  [the longest x1 6.36 us: on_device(): got_rows.astype(jnp.float32) * got_scales.astype(jnp.float32)]
  transfers between devices with their start and end apart: 5 -> 4, of which waited for: 5 -> 4; matrix products, arithmetic and copies ran while one was open for 10% -> 6% of each run, Pallas kernels for 0% -> 0%
where the time goes in v1:
time: 424 us
  waiting for transfers between devices  381 us (90%)
  matrix products  23.1 us (5%)
  between operations  13.9 us (3%)
    reduce_scatter x1, waiting for transfers between devices, on_device(): lax.psum_scatter(back.astype(jnp.bfloat16), 'expert', scatter_dimension=0...  138 us
    reduce_scatter x1, waiting for transfers between devices, on_device(): lax.psum_scatter((partial * gate).astype(jnp.bfloat16), 'expert', scatter...  130 us
    all_gather x1, waiting for transfers between devices, on_device(): lax.all_gather(jnp.concatenate([dequant, columns], axis=1), 'expert', til...  62.9 us
    all_gather x1, waiting for transfers between devices, on_device(): cots = lax.all_gather(cotangent, 'expert', tiled=True)  49.4 us
  transfers between devices with their start and end apart: 4, of which 4 were waited for; matrix products, arithmetic and copies ran while one was open for 6% of the time, Pallas kernels for 0%

profile of v1, /device:TPU:0, one launch (start us, length us, event | category | flops | bytes accessed | tf_op | source)
XLA Modules:
  0.0 424.1 jit_solution(6969196539938673122)
XLA Ops:
  7.2 0.0 all-gather.3.cloned.1.call-start
  7.2 0.8 copy.28
  8.0 0.8 copy.29
  8.7 0.1 select_reduce_fusion
  8.8 0.9 convert_abs_fusion
  9.8 0.1 reduce_max.9
  10.0 0.1 div.22
  10.1 1.1 fusion.19
  11.2 0.1 fusion.28
  11.2 0.7 pad_maximum_fusion
  11.9 0.0 all-gather.3.cloned.1.call-update
  11.9 0.0 all-gather.5.cloned.1.call-start
  12.0 0.7 all-gather.5.cloned.1.call-update
  12.7 0.0 reduce-scatter.3.cloned.1.call-start
  12.7 62.9 %all-gather.3.cloned.1.call-done = bf16[512,3712]{1,0:T(8,128)(2,1)} async-done(((bf16[16,3712]{1,0:T(8,128)(2,1)}), bf16[512,3712]{1,0:T(8,128)(2,1)}) %all-gather.3.cloned.1.call-update) | async-done | bytes 3801104 | tf_op jit(solution)/shard_map/all_gather | solution.py:35
  75.7 0.9 slice.9
  76.6 0.1 copy.31
  76.7 0.1 multiply_reduce_fusion
  76.8 0.0 copy-start.1
  76.8 0.0 copy-start.3
  76.8 5.3 %fusion.8 = f32[512,512]{1,0:T(8,128)S(1)} fusion(bf16[1,3584,512]{2,1,0:T(8,128)(2,1)} %param.11, bf16[512,3712]{1,0:T(8,128)(2,1)} %all-gather.3.cloned.1.call-done), kind=kOutput, calls=%fused_computation.10 | convolution fusion | flops 1879048192 | bytes 8388608 | tf_op jit(solution)/shard_map/dot_general | solution.py:45
  82.1 0.0 copy-done.1
  82.2 0.0 copy-done.3
  82.2 0.0 copy-start.4
  82.2 2.1 fusion.4
  84.2 0.0 copy-done.4
  84.2 4.0 multiply_convert_fusion
  88.2 0.0 reduce-scatter.3.cloned.1.call-update
  88.3 0.0 reduce-scatter.5.cloned.1.call-start
  88.3 49.4 %all-gather.5.cloned.1.call-done = bf16[512,3584]{1,0:T(8,128)(2,1)} async-done(((bf16[16,3584]{1,0:T(8,128)(2,1)}), bf16[512,3584]{1,0:T(8,128)(2,1)}) %all-gather.5.cloned.1.call-update) | async-done | bytes 3670032 | tf_op jit(solution)/shard_map/all_gather | solution.py:36
  137.7 0.0 copy-start
  137.7 5.4 %fusion.12 = f32[512,512]{1,0:T(8,128)S(1)} fusion(bf16[512,3584]{1,0:T(8,128)(2,1)} %all-gather.5.cloned.1.call-done, bf16[1,512,3584]{2,1,0:T(8,128)(2,1)} %param.13, f32[512]{0:T(512)S(1)} %multiply_reduce_fusion), kind=kOutput, calls=%fused_computation.14 | convolution fusion | flops 1879310336 | bytes 8390656 | tf_op jit(solution)/shard_map/dot_general | solution.py:56
  143.1 0.0 copy-done
  143.1 0.0 copy-start.2
  143.1 2.3 fusion.6
  145.4 0.0 copy-done.2
  145.4 4.0 add_convert_fusion
  149.4 0.0 reduce-scatter.5.cloned.1.call-update
  149.5 129.7 %reduce-scatter.3.cloned.1.call-done = bf16[16,3584]{1,0:T(8,128)(2,1)} async-done(((bf16[512,3584]{1,0:T(8,128)(2,1)}), bf16[16,3584]{1,0:T(8,128)(2,1)}) %reduce-scatter.3.cloned.1.call-update) | async-done | bytes 114704 | tf_op jit(solution)/shard_map/reduce_scatter | solution.py:52
  279.1 138.4 %reduce-scatter.5.cloned.1.call-done = bf16[16,3584]{1,0:T(8,128)(2,1)} async-done(((bf16[512,3584]{1,0:T(8,128)(2,1)}), bf16[16,3584]{1,0:T(8,128)(2,1)}) %reduce-scatter.5.cloned.1.call-update) | async-done | bytes 114704 | tf_op jit(solution)/shard_map/reduce_scatter | solution.py:61
  (5 shorter events, 0.1 us)
Async XLA Ops:
  7.2 68.5 %all-gather.3.cloned.1.call-start = ((), (), s32[]{:S(2)}) async-start(), calls=%async_computation.2 | async-start | bytes 3919872 | tf_op jit(solution)/shard_map/all_gather | solution.py:35
  11.9 125.8 %all-gather.5.cloned.1.call-start = ((), (), s32[]{:S(2)}) async-start(), calls=%async_computation.4 | async-start | bytes 3784704 | tf_op jit(solution)/shard_map/all_gather | solution.py:36
  12.7 266.5 %reduce-scatter.3.cloned.1.call-start = ((), (), s32[]{:S(2)}) async-start(), calls=%async_computation.3 | async-start | bytes 3784704 | tf_op jit(solution)/shard_map/reduce_scatter | solution.py:52
  76.8 5.4 %copy-start.1 = (bf16[1,3584,512]{2,1,0:T(8,128)(2,1)S(1)}, bf16[1,3584,512]{2,1,0:T(8,128)(2,1)}, u32[]{:S(2)}) copy-start(bf16[1,3584,512]{2,1,0:T(8,128)(2,1)} %param.12) | copy-start | bytes 11010052
  76.8 5.4 %copy-start.3 = (bf16[512,3712]{1,0:T(8,128)(2,1)S(1)}, bf16[512,3712]{1,0:T(8,128)(2,1)}, u32[]{:S(2)}) copy-start(bf16[512,3712]{1,0:T(8,128)(2,1)} %all-gather.3.cloned.1.call-done) | copy-start | bytes 11403268
  82.2 2.1 copy-start.4
  88.3 329.3 %reduce-scatter.5.cloned.1.call-start = ((), (), s32[]{:S(2)}) async-start(), calls=%async_computation.5 | async-start | bytes 3784704 | tf_op jit(solution)/shard_map/reduce_scatter | solution.py:61
  137.7 5.4 %copy-start = (bf16[1,3584,512]{2,1,0:T(8,128)(2,1)S(1)}, bf16[1,3584,512]{2,1,0:T(8,128)(2,1)}, u32[]{:S(2)}) copy-start(bf16[1,3584,512]{2,1,0:T(8,128)(2,1)} %param.11) | copy-start | bytes 11010052
  143.1 2.3 copy-start.2
Sparse Core Ops, SparseCore 0:
  12.0 63.5 all-gather.2
  78.5 59.0 all-gather.4
  140.5 138.5 reduce-scatter.2
  282.0 135.5 reduce-scatter.4

commit v2 on v1

v2 whole, which is shorter than its diff:
```python
import jax
import jax.numpy as jnp
from jax import lax
from jax.sharding import PartitionSpec as P

CORE, X, Y, Z = 1, 2, 4, 8
f32, bf16 = jnp.float32, jnp.bfloat16
CONTRACT_COLS = (((1,), (1,)), ((), ()))


def swap(value, offset):
    devices = lax.axis_size("expert")
    return lax.ppermute(value, "expert", [(i, i ^ offset) for i in range(devices)])


def far_offsets():
    return range(Z, lax.axis_size("expert"), Z)


def gather_half(block, first, second):
    held = jnp.concatenate([block] + [swap(block, offset) for offset in far_offsets()], axis=0)
    held = jnp.concatenate([held, swap(held, first)], axis=0)
    return jnp.concatenate([held, swap(held, second)], axis=0)


def scatter_half(sums, first, second):
    for offset in (second, first):
        half = sums.shape[0] // 2
        sums = (sums[:half].astype(f32) + swap(sums[half:], offset).astype(f32)).astype(bf16)
    blocks = lax.axis_size("expert") // Z
    rows = sums.shape[0] // blocks
    total = sums[:rows].astype(f32)
    for at, offset in enumerate(far_offsets()):
        total = total + swap(sums[(at + 1) * rows : (at + 2) * rows], offset).astype(f32)
    return total.astype(bf16)


def reorder(rows_yx):
    quarter = rows_yx.shape[0] // 4
    parts = [rows_yx[i * quarter : (i + 1) * quarter] for i in (0, 2, 1, 3)]
    return jnp.concatenate(parts, axis=0)


def code_rows(tokens, blocks):
    blocked = tokens.astype(f32).reshape(tokens.shape[0], blocks, 128)
    scale = lax.reduce_precision(jnp.max(jnp.abs(blocked), axis=2) + 1e-06, 8, 7)[:, :, None]
    quantized = lax.reduce_precision(blocked / scale, 8, 7)
    dequant = (quantized * scale).astype(bf16)
    return dequant.reshape(tokens.shape)


def gate_columns(expert_ids, gate_values, experts):
    named = expert_ids[:, :, None] == jnp.arange(experts, dtype=jnp.int32)[None, None, :]
    rest = jnp.sum(jnp.where(named, gate_values[:, :, None], 0.0), axis=1)
    pieces = []
    for _ in range(3):
        piece = lax.reduce_precision(rest, 8, 7)
        pieces.append(piece.astype(bf16))
        rest = rest - piece
    columns = jnp.concatenate(pieces, axis=1)
    return jnp.pad(columns, ((0, 0), (0, -columns.shape[1] % 128)))


def on_device(tokens, expert_ids, gate_values, cotangent, gate_weight, up_weight, down_weight):
    width = tokens.shape[1]
    cut = width // 256 * 128
    devices = lax.axis_size("expert")
    experts = devices // 2
    expert = lax.axis_index("expert") // 2
    gate_slab, up_slab, down_slab = gate_weight[0], up_weight[0], down_weight[0]
    dequant = code_rows(tokens, width // 128)
    columns = gate_columns(expert_ids, gate_values, experts)
    low = gather_half(jnp.concatenate([dequant[:, :cut], columns], axis=1), X, Y)
    high = gather_half(dequant[:, cut:], Y, X)
    slabs = [
        (gate_slab, up_slab, down_slab),
        (swap(gate_slab, CORE), swap(up_slab, CORE), swap(down_slab, CORE)),
    ]
    cot_low = gather_half(cotangent[:, :cut], X, Y)
    cot_high = gather_half(cotangent[:, cut:], Y, X)
    cots = jnp.concatenate([cot_low, reorder(cot_high)], axis=1)

    x = jnp.concatenate([low[:, :cut], reorder(high)], axis=1)
    pieces = low[:, cut : cut + 3 * experts].astype(f32).reshape(-1, 3, experts)
    mine = (jnp.arange(experts, dtype=jnp.int32) == expert).astype(f32)
    gate = jnp.sum(jnp.sum(pieces, axis=1) * mine, axis=1, keepdims=True)

    kept, partial = [], 0.0
    for gate_w, up_w, down_w in slabs:
        pre_gate = jnp.dot(x, gate_w, preferred_element_type=f32)
        pre_up = jnp.dot(x, up_w, preferred_element_type=f32)
        sigma = jax.nn.sigmoid(pre_gate)
        activated = pre_gate * sigma
        slope = sigma * (1.0 + pre_gate * (1.0 - sigma))
        kept.append((activated * gate, pre_up * slope * gate))
        hidden = (activated * pre_up).astype(bf16)
        partial = partial + jnp.dot(hidden, down_w, preferred_element_type=f32)
    out = (partial * gate).astype(bf16)
    layer_out = jnp.concatenate(
        [
            scatter_half(out[:, :cut], X, Y),
            scatter_half(reorder(out[:, cut:]), Y, X),
        ],
        axis=1,
    )

    back = 0.0
    for (gate_w, up_w, down_w), (for_up, for_gate) in zip(slabs, kept):
        hidden_grad = lax.dot_general(cots, down_w, CONTRACT_COLS, preferred_element_type=f32)
        gate_grad = (hidden_grad * for_gate).astype(bf16)
        up_grad = (hidden_grad * for_up).astype(bf16)
        back = back + lax.dot_general(gate_grad, gate_w, CONTRACT_COLS, preferred_element_type=f32)
        back = back + lax.dot_general(up_grad, up_w, CONTRACT_COLS, preferred_element_type=f32)
    back = back.astype(bf16)
    token_grad = jnp.concatenate(
        [
            scatter_half(back[:, :cut], X, Y),
            scatter_half(reorder(back[:, cut:]), Y, X),
        ],
        axis=1,
    )
    return layer_out, token_grad


def solution(mesh):
    rows = P(("groups", "expert"), None)
    slabs = P("expert", None, None)
    return jax.shard_map(
        on_device,
        mesh=mesh,
        in_specs=(rows, rows, rows, rows, slabs, slabs, slabs),
        out_specs=(rows, rows),
        check_vma=False,
    )
```

time: 424 us -> 235 us (0.55)
  waiting for transfers between devices: 381 us -> 96 us
  starting transfers between devices: 0.16 us -> 62.1 us
  local copies, waits for them, and re-layouts: 2.71 us -> 34.9 us
  between operations: 13.9 us -> 1.17 us
  matrix products: 23.1 us -> 32.6 us
  other arithmetic: 3.06 us -> 7.59 us
    reduce_scatter x2 -> x0, waiting for transfers between devices: 268 us -> none  [the longest x1 138 us: on_device(): lax.psum_scatter(back.astype(jnp.bfloat16), 'expert', scatter_dimension=0...]
    all_gather x2 -> x0, waiting for transfers between devices: 112 us -> none  [the longest x1 62.9 us: on_device(): lax.all_gather(jnp.concatenate([dequant, columns], axis=1), 'expert', til...]
    ppermute x0 -> x43, waiting for transfers between devices: none -> 96 us  [swap(): lax.ppermute(value, 'expert', [(i, i ^ offset) for i in range(devices)])]
    ppermute x0 -> x43, starting transfers between devices: none -> 62.1 us  [swap(): lax.ppermute(value, 'expert', [(i, i ^ offset) for i in range(devices)])]
    concatenate x0 -> x9, local copies, waits for them, and re-layouts: none -> 20.1 us  [the longest x4 10.3 us: gather_half(): held = jnp.concatenate([held, swap(held, first)], axis=0)]
    unnamed x13 -> x39, local copies, waits for them, and re-layouts: 1.63 us -> 12 us
    dot_general x6 -> x12, matrix products: 23.1 us -> 32.6 us  [the longest x2 7.72 us: on_device(): lax.dot_general(cots, down_w, CONTRACT_COLS, preferred_element_type=f32)]
    concatenate x2 -> x10, other arithmetic: 0.73 us -> 5.93 us  [the longest x4 4.46 us: gather_half(): jnp.concatenate([block] + [swap(block, offset) for offset in far_offsets(...]
  transfers between devices with their start and end apart: 4 -> 43, of which waited for: 4 -> 13; matrix products, arithmetic and copies ran while one was open for 6% -> 28% of each run, Pallas kernels for 0% -> 0%
where the time goes in v2:
time: 235 us; the launch traced here: 234 us
  waiting for transfers between devices  96 us (41%)
  starting transfers between devices  62.1 us (26%)
  local copies, waits for them, and re-layouts  34.9 us (15%)
  matrix products  32.6 us (14%)
  other arithmetic  7.59 us (3%)
    ppermute x43, waiting for transfers between devices, swap(): lax.ppermute(value, 'expert', [(i, i ^ offset) for i in range(devices)])  96 us
    ppermute x43, starting transfers between devices, swap(): lax.ppermute(value, 'expert', [(i, i ^ offset) for i in range(devices)])  62.1 us
    unnamed x39, local copies, waits for them, and re-layouts  12 us
    concatenate x4, local copies, waits for them, and re-layouts, gather_half(): held = jnp.concatenate([held, swap(held, first)], axis=0)  10.3 us
    dot_general x2, matrix products, on_device(): lax.dot_general(cots, down_w, CONTRACT_COLS, preferred_element_type=f32)  7.72 us
    dot_general x2, matrix products, on_device(): pre_up = jnp.dot(x, up_w, preferred_element_type=f32)  6.75 us
    concatenate x2, local copies, waits for them, and re-layouts, reorder(): return jnp.concatenate(parts, axis=0)  5.7 us
    dot_general x2, matrix products, on_device(): lax.dot_general(gate_grad, gate_w, CONTRACT_COLS, preferred_element_type=...  4.79 us
  transfers between devices with their start and end apart: 43, of which 13 were waited for; matrix products, arithmetic and copies ran while one was open for 28% of the time, Pallas kernels for 0%

profile of v2, /device:TPU:0, one launch (start us, length us, event | category | flops | bytes accessed | tf_op | source)
XLA Modules:
  0.0 234.4 jit_solution(6662106900828939227)
XLA Ops:
  2.9 3.1 %collective-permute-start.5 = (bf16[16,1792]{0,1:T(8,128)(2,1)S(1)}, bf16[16,1792]{0,1:T(8,128)(2,1)S(1)}, u32[]{:S(2)}, u32[]{:S(2)}) collective-permute-start(bf16[16,1792]{0,1:T(8,128)(2,1)S(1)} %get-tuple-element.11), channel_id=1, source_target_pairs={{0,8},{1,9},{2,10},{3,11},{4,12},{5,13},{6,14},{7,15},{8,0},{9,1},... | collective-permute-start | bytes 172040 | tf_op jit(solution)/shard_map/ppermute | solution.py:13
  6.0 2.6 %collective-permute-start.6 = (bf16[16,1792]{0,1:T(8,128)(2,1)S(1)}, bf16[16,1792]{0,1:T(8,128)(2,1)S(1)}, u32[]{:S(2)}, u32[]{:S(2)}) collective-permute-start(bf16[16,1792]{0,1:T(8,128)(2,1)S(1)} %get-tuple-element.11), channel_id=1, source_target_pairs={{0,16},{1,17},{2,18},{3,19},{4,20},{5,21},{6,22},{7,23},{8,24},{9,... | collective-permute-start | bytes 172040 | tf_op jit(solution)/shard_map/ppermute | solution.py:13
  10.1 3.5 %collective-permute-start.29 = (bf16[16,1792]{1,0:T(8,128)(2,1)S(1)}, bf16[16,1792]{1,0:T(8,128)(2,1)S(1)}, u32[]{:S(2)}, u32[]{:S(2)}) collective-permute-start(bf16[16,1792]{1,0:T(8,128)(2,1)S(1)} %get-tuple-element.32), channel_id=1, source_target_pairs={{0,16},{1,17},{2,18},{3,19},{4,20},{5,21},{6,22},{7,23},{8,24},{9,... | collective-permute-start | bytes 172040 | tf_op jit(solution)/shard_map/ppermute | solution.py:13
  14.5 22.8 %collective-permute-done.28 = bf16[16,1792]{1,0:T(8,128)(2,1)S(1)} collective-permute-done((bf16[16,1792]{1,0:T(8,128)(2,1)S(1)}, bf16[16,1792]{1,0:T(8,128)(2,1)S(1)}, u32[]{:S(2)}, u32[]{:S(2)}) %collective-permute-start.28) | collective-permute-done | bytes 57376 | tf_op jit(solution)/shard_map/ppermute | solution.py:13
  37.3 2.6 %collective-permute-start.30 = (bf16[16,1792]{1,0:T(8,128)(2,1)S(1)}, bf16[16,1792]{1,0:T(8,128)(2,1)S(1)}, u32[]{:S(2)}, u32[]{:S(2)}) collective-permute-start(bf16[16,1792]{1,0:T(8,128)(2,1)S(1)} %get-tuple-element.32), channel_id=1, source_target_pairs={{0,24},{1,25},{2,26},{3,27},{4,28},{5,29},{6,30},{7,31},{8,16},{9,... | collective-permute-start | bytes 172040 | tf_op jit(solution)/shard_map/ppermute | solution.py:13
  40.5 12.2 %collective-permute-done.29 = bf16[16,1792]{1,0:T(8,128)(2,1)S(1)} collective-permute-done((bf16[16,1792]{1,0:T(8,128)(2,1)S(1)}, bf16[16,1792]{1,0:T(8,128)(2,1)S(1)}, u32[]{:S(2)}, u32[]{:S(2)}) %collective-permute-start.29) | collective-permute-done | bytes 57376 | tf_op jit(solution)/shard_map/ppermute | solution.py:13
  52.7 3.0 %collective-permute-start.24 = (bf16[16,1792]{1,0:T(8,128)(2,1)S(1)}, bf16[16,1792]{1,0:T(8,128)(2,1)S(1)}, u32[]{:S(2)}, u32[]{:S(2)}) collective-permute-start(bf16[16,1792]{1,0:T(8,128)(2,1)S(1)} %get-tuple-element.33), channel_id=1, source_target_pairs={{0,16},{1,17},{2,18},{3,19},{4,20},{5,21},{6,22},{7,23},{8,24},{9,... | collective-permute-start | bytes 172040 | tf_op jit(solution)/shard_map/ppermute | solution.py:13
  57.7 1.7 collective-permute-start.25
  60.0 4.5 %collective-permute-done.25 = bf16[16,1792]{1,0:T(8,128)(2,1)S(1)} collective-permute-done((bf16[16,1792]{1,0:T(8,128)(2,1)S(1)}, bf16[16,1792]{1,0:T(8,128)(2,1)S(1)}, u32[]{:S(2)}, u32[]{:S(2)}) %collective-permute-start.25) | collective-permute-done | bytes 57376 | tf_op jit(solution)/shard_map/ppermute | solution.py:13
  66.5 1.7 collective-permute-start.2
  68.7 1.6 pad_maximum_fusion.5
  71.0 7.2 %collective-permute-done = bf16[16,1920]{0,1:T(8,128)(2,1)S(1)} collective-permute-done((bf16[16,1920]{0,1:T(8,128)(2,1)S(1)}, bf16[16,1920]{0,1:T(8,128)(2,1)S(1)}, u32[]{:S(2)}, u32[]{:S(2)}) %collective-permute-start) | collective-permute-done | bytes 61472 | tf_op jit(solution)/shard_map/ppermute | solution.py:13
  78.2 1.5 collective-permute-start.8
  79.7 20.4 %collective-permute-done.1 = bf16[16,1920]{0,1:T(8,128)(2,1)S(1)} collective-permute-done((bf16[16,1920]{0,1:T(8,128)(2,1)S(1)}, bf16[16,1920]{0,1:T(8,128)(2,1)S(1)}, u32[]{:S(2)}, u32[]{:S(2)}) %collective-permute-start.1) | collective-permute-done | bytes 61472 | tf_op jit(solution)/shard_map/ppermute | solution.py:13
  100.1 1.5 collective-permute-start.31
  101.7 1.5 collective-permute-start.26
  105.1 3.7 %concatenate.82 = bf16[128,1792]{0,1:T(8,128)(2,1)} concatenate(bf16[16,1792]{0,1:T(8,128)(2,1)S(1)} %get-tuple-element.11, bf16[16,1792]{0,1:T(8,128)(2,1)S(1)} %collective-permute-done.5, bf16[16,1792]{0,1:T(8,128)(2,1)S(1)} %collective-permute-done.6, bf16[16,1792]{0,1:T(8,128)(2,1)} %collective-permute-done.7, bf16[64,1792]{0,1:T(8,128)(2,1)} %collective-permute-done.8), dimensions={0} | concatenate | bytes 917504 | tf_op jit(solution)/shard_map/concatenate | solution.py:22
  108.8 1.5 collective-permute-start.9
  110.3 1.7 constant_dynamic-update-slice_fusion.11
  112.0 1.8 constant_dynamic-update-slice_fusion
  114.7 3.2 %concatenate.79 = bf16[128,1920]{0,1:T(8,128)(2,1)} concatenate(bf16[16,1920]{0,1:T(8,128)(2,1)S(1)} %copy.40, bf16[16,1920]{0,1:T(8,128)(2,1)S(1)} %collective-permute-done, bf16[16,1920]{0,1:T(8,128)(2,1)S(1)} %collective-permute-done.1, bf16[16,1920]{0,1:T(8,128)(2,1)S(1)} %collective-permute-done.2, bf16[64,1920]{0,1:T(8,128)(2,1)} %collective-permute-done.3), dimensions={0} | concatenate | bytes 983040 | tf_op jit(solution)/shard_map/concatenate | solution.py:22
  117.9 2.1 collective-permute-done.9
  120.6 2.3 fusion.51
  122.8 5.7 %collective-permute-done.32 = bf16[128,1792]{1,0:T(8,128)(2,1)} collective-permute-done((bf16[128,1792]{1,0:T(8,128)(2,1)}, bf16[128,1792]{1,0:T(8,128)(2,1)}, u32[]{:S(2)}, u32[]{:S(2)}) %collective-permute-start.32) | collective-permute-done | bytes 458784 | tf_op jit(solution)/shard_map/ppermute | solution.py:13
  129.0 1.7 slice_dynamic-update-slice_fusion.1
  130.7 1.6 constant_dynamic-update-slice_fusion.16
  132.3 1.6 slice_dynamic-update-slice_fusion
  134.8 4.1 %concatenate.83 = bf16[256,1792]{0,1:T(8,128)(2,1)} concatenate(bf16[16,1792]{0,1:T(8,128)(2,1)S(1)} %get-tuple-element.11, bf16[16,1792]{0,1:T(8,128)(2,1)S(1)} %collective-permute-done.5, bf16[16,1792]{0,1:T(8,128)(2,1)S(1)} %collective-permute-done.6, bf16[16,1792]{0,1:T(8,128)(2,1)} %collective-permute-done.7, bf16[64,1792]{0,1:T(8,128)(2,1)} %get-tuple-element.13, ...), dimensions={0} | concatenate | bytes 1835008 | tf_op jit(solution)/shard_map/concatenate | solution.py:41
  138.8 4.5 %fusion.7 = f32[256,512]{1,0:T(8,128)} fusion(bf16[256,1792]{1,0:T(8,128)(2,1)} %slice_dynamic-update-slice_fusion, bf16[256,1792]{1,0:T(8,128)(2,1)} %constant_dynamic-update-slice_fusion.5, bf16[1,512,3584]{2,1,0:T(8,128)(2,1)} %param.13), kind=kOutput, calls=%fused_computation.15 | convolution fusion | flops 943194112 | bytes 6029312 | tf_op jit(solution)/shard_map/dot_general | solution.py:109
  143.4 3.0 %concatenate.80 = bf16[256,1920]{0,1:T(8,128)(2,1)S(1)} concatenate(bf16[16,1920]{0,1:T(8,128)(2,1)S(1)} %copy.40, bf16[16,1920]{0,1:T(8,128)(2,1)S(1)} %collective-permute-done, bf16[16,1920]{0,1:T(8,128)(2,1)S(1)} %collective-permute-done.1, bf16[16,1920]{0,1:T(8,128)(2,1)S(1)} %collective-permute-done.2, bf16[64,1920]{0,1:T(8,128)(2,1)} %collective-permute-done.3, ...), dimensions={0} | concatenate | bytes 1966080 | tf_op jit(solution)/shard_map/concatenate | solution.py:23
  146.5 3.6 %fusion.35 = f32[256,512]{1,0:T(8,128)S(1)} fusion(bf16[1,3584,512]{2,1,0:T(8,128)(2,1)} %param.12, bf16[256,1792]{0,1:T(8,128)(2,1)} %concatenate.83, bf16[256,1792]{0,1:T(8,128)(2,1)S(1)} %slice.209), kind=kOutput, calls=%fused_computation.102 | convolution fusion | flops 943194112 | bytes 6029312 | tf_op jit(solution)/shard_map/dot_general | solution.py:91
  156.7 3.2 %fusion.46 = f32[256,512]{1,0:T(8,128)S(1)} fusion(bf16[3584,512]{1,0:T(8,128)(2,1)} %collective-permute-done.11, bf16[256,1792]{0,1:T(8,128)(2,1)S(1)} %copy-done.4, bf16[256,1792]{0,1:T(8,128)(2,1)S(1)} %slice.209), kind=kOutput, calls=%fused_computation.113 | convolution fusion | flops 943194112 | bytes 6029312 | tf_op jit(solution)/shard_map/dot_general | solution.py:91
  159.9 3.2 %fusion.47 = f32[256,512]{1,0:T(8,128)S(1)} fusion(bf16[3584,512]{1,0:T(8,128)(2,1)} %collective-permute-done.10, bf16[256,1792]{0,1:T(8,128)(2,1)S(1)} %copy-done.4, bf16[256,1792]{0,1:T(8,128)(2,1)S(1)} %slice.209), kind=kOutput, calls=%fused_computation.114 | convolution fusion | flops 943194112 | bytes 6029312 | tf_op jit(solution)/shard_map/dot_general | solution.py:90
  163.1 3.4 %fusion.2 = bf16[256,3584]{1,0:T(8,128)(2,1)S(1)} fusion(f32[256,3584]{1,0:T(8,128)S(1)} %fusion.10, bf16[512,3584]{1,0:T(8,128)(2,1)} %collective-permute-done.12, f32[256]{0:T(256)S(1)} %multiply_reduce_fusion, f32[256,512]{1,0:T(8,128)S(1)} %fusion.46, f32[256,512]{1,0:T(8,128)S(1)} %fusion.47), kind=kOutput, calls=%fused_computation.5 | convolution fusion | flops 943063040 | bytes 10224640 | tf_op jit(solution)/shard_map/dot_general | solution.py:97
  168.0 3.2 %fusion.6 = f32[256,512]{1,0:T(8,128)S(1)} fusion(bf16[512,3584]{1,0:T(8,128)(2,1)} %collective-permute-done.12, bf16[256,1792]{1,0:T(8,128)(2,1)S(1)} %copy-done.11, bf16[256,1792]{1,0:T(8,128)(2,1)S(1)} %copy-done.10), kind=kOutput, calls=%fused_computation.14 | convolution fusion | flops 943194112 | bytes 6029312 | tf_op jit(solution)/shard_map/dot_general | solution.py:109
  171.2 3.3 %fusion.12 = f32[256,3584]{1,0:T(8,128)S(1)} fusion(bf16[3584,512]{1,0:T(8,128)(2,1)} %collective-permute-done.11, f32[256,512]{1,0:T(8,128)S(1)} %fusion.6, f32[256]{0:T(256)S(1)} %multiply_reduce_fusion, f32[256,512]{1,0:T(8,128)S(1)} %fusion.47), kind=kOutput, calls=%fused_computation.40 | convolution fusion | flops 940441600 | bytes 8389632 | tf_op jit(solution)/shard_map/dot_general | solution.py:113
  174.4 3.5 %fusion.3 = bf16[256,3584]{1,0:T(8,128)(2,1)S(1)} fusion(f32[256,3584]{1,0:T(8,128)S(1)} %fusion.12, f32[256,3584]{1,0:T(8,128)S(1)} %convolution_add_fusion.1, bf16[3584,512]{1,0:T(8,128)(2,1)} %collective-permute-done.10, f32[256,512]{1,0:T(8,128)S(1)} %fusion.6, f32[256,512]{1,0:T(8,128)S(1)} %fusion.46, f32[256,512]{1,0:T(8,128)S(1)} %fusion.47, ...), kind=kOutput, calls=%fused_computation.6 | convolution fusion | flops 943718400 | bytes 14418944 | tf_op jit(solution)/shard_map/dot_general | solution.py:112
  181.2 1.6 collective-permute-start.19
  182.7 8.9 %collective-permute-done.13 = bf16[128,1792]{1,0:T(8,128)(2,1)S(1)} collective-permute-done((bf16[128,1792]{1,0:T(8,128)(2,1)S(1)}, bf16[128,1792]{1,0:T(8,128)(2,1)S(1)}, u32[]{:S(2)}, u32[]{:S(2)}) %collective-permute-start.13) | collective-permute-done | bytes 458784 | tf_op jit(solution)/shard_map/ppermute | solution.py:13
  192.7 1.6 collective-permute-start.39
  194.3 7.2 %collective-permute-done.33 = bf16[128,1792]{1,0:T(8,128)(2,1)S(1)} collective-permute-done((bf16[128,1792]{1,0:T(8,128)(2,1)S(1)}, bf16[128,1792]{1,0:T(8,128)(2,1)S(1)}, u32[]{:S(2)}, u32[]{:S(2)}) %collective-permute-start.33) | collective-permute-done | bytes 458784 | tf_op jit(solution)/shard_map/ppermute | solution.py:13
  202.4 2.8 %collective-permute-done.19 = bf16[64,1792]{1,0:T(8,128)(2,1)S(1)} collective-permute-done((bf16[64,1792]{1,0:T(8,128)(2,1)S(1)}, bf16[64,1792]{1,0:T(8,128)(2,1)S(1)}, u32[]{:S(2)}, u32[]{:S(2)}) %collective-permute-start.19) | collective-permute-done | bytes 229408 | tf_op jit(solution)/shard_map/ppermute | solution.py:13
  205.3 2.1 collective-permute-start.22
  207.3 9.5 %collective-permute-start.21 = (bf16[16,1792]{1,0:T(8,128)(2,1)S(1)}, bf16[16,1792]{1,0:T(8,128)(2,1)S(1)}, u32[]{:S(2)}, u32[]{:S(2)}) collective-permute-start(bf16[16,1792]{1,0:T(8,128)(2,1)S(1)} %get-tuple-element.27), channel_id=1, source_target_pairs={{0,16},{1,17},{2,18},{3,19},{4,20},{5,21},{6,22},{7,23},{8,24},{9,... | collective-permute-start | bytes 172040 | tf_op jit(solution)/shard_map/ppermute | solution.py:13
  216.9 1.5 collective-permute-start.17
  218.5 2.1 collective-permute-start.16
  224.3 2.1 collective-permute-start.40
  228.0 2.9 %collective-permute-start.35 = (bf16[16,1792]{1,0:T(8,128)(2,1)S(1)}, bf16[16,1792]{1,0:T(8,128)(2,1)S(1)}, u32[]{:S(2)}, u32[]{:S(2)}) collective-permute-start(bf16[16,1792]{1,0:T(8,128)(2,1)S(1)} %get-tuple-element.14), channel_id=1, source_target_pairs={{0,8},{1,9},{2,10},{3,11},{4,12},{5,13},{6,14},{7,15},{8,0},{9,1},... | collective-permute-start | bytes 172040 | tf_op jit(solution)/shard_map/ppermute | solution.py:13
  (145 shorter events, 38.1 us)
Async XLA Ops:
  2.0 6.6 %copy-start.5 = (bf16[16,3584]{1,0:T(8,128)(2,1)S(1)}, bf16[16,3584]{1,0:T(8,128)(2,1)}, u32[]{:S(2)}) copy-start(bf16[16,3584]{1,0:T(8,128)(2,1)} %param.10) | copy-start | bytes 344068
  2.1 11.5 %copy-start.8 = (f32[16,8]{0,1:T(8,128)S(1)}, f32[16,8]{0,1:T(8,128)}, u32[]{:S(2)}) copy-start(f32[16,8]{0,1:T(8,128)} %param.9) | copy-start | bytes 1540
  2.1 11.6 %copy-start.9 = (s32[16,8]{0,1:T(8,128)S(1)}, s32[16,8]{0,1:T(8,128)}, u32[]{:S(2)}) copy-start(s32[16,8]{0,1:T(8,128)} %param.8) | copy-start | bytes 1540
  2.9 63.7 %collective-permute-start.5 = (bf16[16,1792]{0,1:T(8,128)(2,1)S(1)}, bf16[16,1792]{0,1:T(8,128)(2,1)S(1)}, u32[]{:S(2)}, u32[]{:S(2)}) collective-permute-start(bf16[16,1792]{0,1:T(8,128)(2,1)S(1)} %get-tuple-element.11), channel_id=1, source_target_pairs={{0,8},{1,9},{2,10},{3,11},{4,12},{5,13},{6,14},{7,15},{8,0},{9,1},... | collective-permute-start | bytes 172040 | tf_op jit(solution)/shard_map/ppermute | solution.py:13
  6.0 62.2 %collective-permute-start.6 = (bf16[16,1792]{0,1:T(8,128)(2,1)S(1)}, bf16[16,1792]{0,1:T(8,128)(2,1)S(1)}, u32[]{:S(2)}, u32[]{:S(2)}) collective-permute-start(bf16[16,1792]{0,1:T(8,128)(2,1)S(1)} %get-tuple-element.11), channel_id=1, source_target_pairs={{0,16},{1,17},{2,18},{3,19},{4,20},{5,21},{6,22},{7,23},{8,24},{9,... | collective-permute-start | bytes 172040 | tf_op jit(solution)/shard_map/ppermute | solution.py:13
  8.6 59.6 %collective-permute-start.7 = (bf16[16,1792]{0,1:T(8,128)(2,1)S(1)}, bf16[16,1792]{0,1:T(8,128)(2,1)}, u32[]{:S(2)}, u32[]{:S(2)}) collective-permute-start(bf16[16,1792]{0,1:T(8,128)(2,1)S(1)} %get-tuple-element.11), channel_id=1, source_target_pairs={{0,24},{1,25},{2,26},{3,27},{4,28},{5,29},{6,30},{7,31},{8,16},{9,... | collective-permute-start | bytes 172040 | tf_op jit(solution)/shard_map/ppermute | solution.py:13
  9.2 28.1 %collective-permute-start.28 = (bf16[16,1792]{1,0:T(8,128)(2,1)S(1)}, bf16[16,1792]{1,0:T(8,128)(2,1)S(1)}, u32[]{:S(2)}, u32[]{:S(2)}) collective-permute-start(bf16[16,1792]{1,0:T(8,128)(2,1)S(1)} %get-tuple-element.32), channel_id=1, source_target_pairs={{0,8},{1,9},{2,10},{3,11},{4,12},{5,13},{6,14},{7,15},{8,0},{9,1},... | collective-permute-start | bytes 172040 | tf_op jit(solution)/shard_map/ppermute | solution.py:13
  10.1 42.6 %collective-permute-start.29 = (bf16[16,1792]{1,0:T(8,128)(2,1)S(1)}, bf16[16,1792]{1,0:T(8,128)(2,1)S(1)}, u32[]{:S(2)}, u32[]{:S(2)}) collective-permute-start(bf16[16,1792]{1,0:T(8,128)(2,1)S(1)} %get-tuple-element.32), channel_id=1, source_target_pairs={{0,16},{1,17},{2,18},{3,19},{4,20},{5,21},{6,22},{7,23},{8,24},{9,... | collective-permute-start | bytes 172040 | tf_op jit(solution)/shard_map/ppermute | solution.py:13
  37.3 15.4 %collective-permute-start.30 = (bf16[16,1792]{1,0:T(8,128)(2,1)S(1)}, bf16[16,1792]{1,0:T(8,128)(2,1)S(1)}, u32[]{:S(2)}, u32[]{:S(2)}) collective-permute-start(bf16[16,1792]{1,0:T(8,128)(2,1)S(1)} %get-tuple-element.32), channel_id=1, source_target_pairs={{0,24},{1,25},{2,26},{3,27},{4,28},{5,29},{6,30},{7,31},{8,16},{9,... | collective-permute-start | bytes 172040 | tf_op jit(solution)/shard_map/ppermute | solution.py:13
  52.7 5.0 %collective-permute-start.23 = (bf16[16,1792]{1,0:T(8,128)(2,1)S(1)}, bf16[16,1792]{1,0:T(8,128)(2,1)S(1)}, u32[]{:S(2)}, u32[]{:S(2)}) collective-permute-start(bf16[16,1792]{1,0:T(8,128)(2,1)S(1)} %get-tuple-element.33), channel_id=1, source_target_pairs={{0,8},{1,9},{2,10},{3,11},{4,12},{5,13},{6,14},{7,15},{8,0},{9,1},... | collective-permute-start | bytes 172040 | tf_op jit(solution)/shard_map/ppermute | solution.py:13
  52.7 7.3 %collective-permute-start.24 = (bf16[16,1792]{1,0:T(8,128)(2,1)S(1)}, bf16[16,1792]{1,0:T(8,128)(2,1)S(1)}, u32[]{:S(2)}, u32[]{:S(2)}) collective-permute-start(bf16[16,1792]{1,0:T(8,128)(2,1)S(1)} %get-tuple-element.33), channel_id=1, source_target_pairs={{0,16},{1,17},{2,18},{3,19},{4,20},{5,21},{6,22},{7,23},{8,24},{9,... | collective-permute-start | bytes 172040 | tf_op jit(solution)/shard_map/ppermute | solution.py:13
  57.7 6.8 %collective-permute-start.25 = (bf16[16,1792]{1,0:T(8,128)(2,1)S(1)}, bf16[16,1792]{1,0:T(8,128)(2,1)S(1)}, u32[]{:S(2)}, u32[]{:S(2)}) collective-permute-start(bf16[16,1792]{1,0:T(8,128)(2,1)S(1)} %get-tuple-element.33), channel_id=1, source_target_pairs={{0,24},{1,25},{2,26},{3,27},{4,28},{5,29},{6,30},{7,31},{8,16},{9,... | collective-permute-start | bytes 172040 | tf_op jit(solution)/shard_map/ppermute | solution.py:13
  60.0 18.3 %collective-permute-start = (bf16[16,1920]{0,1:T(8,128)(2,1)S(1)}, bf16[16,1920]{0,1:T(8,128)(2,1)S(1)}, u32[]{:S(2)}, u32[]{:S(2)}) collective-permute-start(bf16[16,1920]{0,1:T(8,128)(2,1)S(1)} %copy.40), channel_id=1, source_target_pairs={{0,8},{1,9},{2,10},{3,11},{4,12},{5,13},{6,14},{7,15},{8,0},{9,1},... | collective-permute-start | bytes 184328 | tf_op jit(solution)/shard_map/ppermute | solution.py:13
  64.4 35.7 %collective-permute-start.1 = (bf16[16,1920]{0,1:T(8,128)(2,1)S(1)}, bf16[16,1920]{0,1:T(8,128)(2,1)S(1)}, u32[]{:S(2)}, u32[]{:S(2)}) collective-permute-start(bf16[16,1920]{0,1:T(8,128)(2,1)S(1)} %copy.40), channel_id=1, source_target_pairs={{0,16},{1,17},{2,18},{3,19},{4,20},{5,21},{6,22},{7,23},{8,24},{9,... | collective-permute-start | bytes 184328 | tf_op jit(solution)/shard_map/ppermute | solution.py:13
  66.5 35.1 %collective-permute-start.2 = (bf16[16,1920]{0,1:T(8,128)(2,1)S(1)}, bf16[16,1920]{0,1:T(8,128)(2,1)S(1)}, u32[]{:S(2)}, u32[]{:S(2)}) collective-permute-start(bf16[16,1920]{0,1:T(8,128)(2,1)S(1)} %copy.40), channel_id=1, source_target_pairs={{0,24},{1,25},{2,26},{3,27},{4,28},{5,29},{6,30},{7,31},{8,16},{9,... | collective-permute-start | bytes 184328 | tf_op jit(solution)/shard_map/ppermute | solution.py:13
  68.2 94.9 %collective-permute-start.12 = (bf16[512,3584]{1,0:T(8,128)(2,1)}, bf16[512,3584]{1,0:T(8,128)(2,1)}, u32[]{:S(2)}, u32[]{:S(2)}) collective-permute-start(bf16[512,3584]{1,0:T(8,128)(2,1)} %bitcast.36), channel_id=1, source_target_pairs={{0,1},{1,0},{2,3},{3,2},{4,5},{5,4},{6,7},{7,6},{8,9},{9,8},{10,11... | collective-permute-start | bytes 11010056 | tf_op jit(solution)/shard_map/ppermute | solution.py:13
  68.2 88.5 %collective-permute-start.11 = (bf16[3584,512]{1,0:T(8,128)(2,1)}, bf16[3584,512]{1,0:T(8,128)(2,1)}, u32[]{:S(2)}, u32[]{:S(2)}) collective-permute-start(bf16[3584,512]{1,0:T(8,128)(2,1)} %bitcast.34), channel_id=1, source_target_pairs={{0,1},{1,0},{2,3},{3,2},{4,5},{5,4},{6,7},{7,6},{8,9},{9,8},{10,11... | collective-permute-start | bytes 11010056 | tf_op jit(solution)/shard_map/ppermute | solution.py:13
  78.2 26.4 %collective-permute-start.8 = (bf16[64,1792]{0,1:T(8,128)(2,1)S(1)}, bf16[64,1792]{0,1:T(8,128)(2,1)}, u32[]{:S(2)}, u32[]{:S(2)}) collective-permute-start(bf16[64,1792]{0,1:T(8,128)(2,1)S(1)} %pad_maximum_fusion.5), channel_id=1, source_target_pairs={{0,4},{1,5},{2,6},{3,7},{4,0},{5,1},{6,2},{7,3},{8,12},{9,13},{10,... | collective-permute-start | bytes 688136 | tf_op jit(solution)/shard_map/ppermute | solution.py:13
  100.1 8.7 %collective-permute-start.31 = (bf16[64,1792]{1,0:T(8,128)(2,1)}, bf16[64,1792]{1,0:T(8,128)(2,1)}, u32[]{:S(2)}, u32[]{:S(2)}) collective-permute-start(bf16[64,1792]{1,0:T(8,128)(2,1)} %pad_maximum_fusion.9), channel_id=1, source_target_pairs={{0,4},{1,5},{2,6},{3,7},{4,0},{5,1},{6,2},{7,3},{8,12},{9,13},{10,... | collective-permute-start | bytes 688136 | tf_op jit(solution)/shard_map/ppermute | solution.py:13
  101.7 10.3 %collective-permute-start.26 = (bf16[64,1792]{1,0:T(8,128)(2,1)}, bf16[64,1792]{1,0:T(8,128)(2,1)}, u32[]{:S(2)}, u32[]{:S(2)}) collective-permute-start(bf16[64,1792]{1,0:T(8,128)(2,1)} %pad_maximum_fusion.8), channel_id=1, source_target_pairs={{0,2},{1,3},{2,0},{3,1},{4,6},{5,7},{6,4},{7,5},{8,10},{9,11},{10,... | collective-permute-start | bytes 688136 | tf_op jit(solution)/shard_map/ppermute | solution.py:13
  104.6 9.2 %collective-permute-start.3 = (bf16[64,1920]{0,1:T(8,128)(2,1)}, bf16[64,1920]{0,1:T(8,128)(2,1)}, u32[]{:S(2)}, u32[]{:S(2)}) collective-permute-start(bf16[64,1920]{0,1:T(8,128)(2,1)} %pad_maximum_fusion.4), channel_id=1, source_target_pairs={{0,2},{1,3},{2,0},{3,1},{4,6},{5,7},{6,4},{7,5},{8,10},{9,11},{10,... | collective-permute-start | bytes 737288 | tf_op jit(solution)/shard_map/ppermute | solution.py:13
  108.8 11.2 %collective-permute-start.9 = (bf16[128,1792]{0,1:T(8,128)(2,1)}, bf16[128,1792]{0,1:T(8,128)(2,1)}, u32[]{:S(2)}, u32[]{:S(2)}) collective-permute-start(bf16[128,1792]{0,1:T(8,128)(2,1)} %concatenate.82), channel_id=1, source_target_pairs={{0,2},{1,3},{2,0},{3,1},{4,6},{5,7},{6,4},{7,5},{8,10},{9,11},{10,... | collective-permute-start | bytes 1376264 | tf_op jit(solution)/shard_map/ppermute | solution.py:13
  112.0 47.9 %collective-permute-start.10 = (bf16[3584,512]{1,0:T(8,128)(2,1)}, bf16[3584,512]{1,0:T(8,128)(2,1)}, u32[]{:S(2)}, u32[]{:S(2)}) collective-permute-start(bf16[3584,512]{1,0:T(8,128)(2,1)} %bitcast.35), channel_id=1, source_target_pairs={{0,1},{1,0},{2,3},{3,2},{4,5},{5,4},{6,7},{7,6},{8,9},{9,8},{10,11... | collective-permute-start | bytes 11010056 | tf_op jit(solution)/shard_map/ppermute | solution.py:13
  113.8 14.7 %collective-permute-start.32 = (bf16[128,1792]{1,0:T(8,128)(2,1)}, bf16[128,1792]{1,0:T(8,128)(2,1)}, u32[]{:S(2)}, u32[]{:S(2)}) collective-permute-start(bf16[128,1792]{1,0:T(8,128)(2,1)} %constant_dynamic-update-slice_fusion.11), channel_id=1, source_target_pairs={{0,2},{1,3},{2,0},{3,1},{4,6},{5,7},{6,4},{7,5},{8,10},{9,11},{10,... | collective-permute-start | bytes 1376264 | tf_op jit(solution)/shard_map/ppermute | solution.py:13
  120.0 13.9 %collective-permute-start.27 = (bf16[128,1792]{1,0:T(8,128)(2,1)}, bf16[128,1792]{1,0:T(8,128)(2,1)S(1)}, u32[]{:S(2)}, u32[]{:S(2)}) collective-permute-start(bf16[128,1792]{1,0:T(8,128)(2,1)} %get-tuple-element.20), channel_id=1, source_target_pairs={{0,4},{1,5},{2,6},{3,7},{4,0},{5,1},{6,2},{7,3},{8,12},{9,13},{10,... | collective-permute-start | bytes 1376264 | tf_op jit(solution)/shard_map/ppermute | solution.py:13
  128.5 14.9 %collective-permute-start.4 = (bf16[128,1920]{0,1:T(8,128)(2,1)}, bf16[128,1920]{0,1:T(8,128)(2,1)}, u32[]{:S(2)}, u32[]{:S(2)}) collective-permute-start(bf16[128,1920]{0,1:T(8,128)(2,1)} %concatenate.79), channel_id=1, source_target_pairs={{0,4},{1,5},{2,6},{3,7},{4,0},{5,1},{6,2},{7,3},{8,12},{9,13},{10,... | collective-permute-start | bytes 1474568 | tf_op jit(solution)/shard_map/ppermute | solution.py:13
  163.1 4.9 %copy-start.10 = (bf16[256,1792]{1,0:T(8,128)(2,1)S(1)}, bf16[256,1792]{1,0:T(8,128)(2,1)}, u32[]{:S(2)}) copy-start(bf16[256,1792]{1,0:T(8,128)(2,1)} %constant_dynamic-update-slice_fusion.5) | copy-start | bytes 2752516
  163.1 4.9 %copy-start.11 = (bf16[256,1792]{1,0:T(8,128)(2,1)S(1)}, bf16[256,1792]{1,0:T(8,128)(2,1)}, u32[]{:S(2)}) copy-start(bf16[256,1792]{1,0:T(8,128)(2,1)} %slice_dynamic-update-slice_fusion) | copy-start | bytes 2752516
  166.6 14.4 %collective-permute-start.18 = (bf16[128,1792]{1,0:T(8,128)(2,1)S(1)}, bf16[128,1792]{1,0:T(8,128)(2,1)S(1)}, u32[]{:S(2)}, u32[]{:S(2)}) collective-permute-start(bf16[128,1792]{1,0:T(8,128)(2,1)S(1)} %pad_maximum_fusion.6), channel_id=1, source_target_pairs={{0,2},{1,3},{2,0},{3,1},{4,6},{5,7},{6,4},{7,5},{8,10},{9,11},{10,... | collective-permute-start | bytes 1376264 | tf_op jit(solution)/shard_map/ppermute | solution.py:13
  178.1 13.5 %collective-permute-start.13 = (bf16[128,1792]{1,0:T(8,128)(2,1)S(1)}, bf16[128,1792]{1,0:T(8,128)(2,1)S(1)}, u32[]{:S(2)}, u32[]{:S(2)}) collective-permute-start(bf16[128,1792]{1,0:T(8,128)(2,1)S(1)} %slice.215), channel_id=1, source_target_pairs={{0,4},{1,5},{2,6},{3,7},{4,0},{5,1},{6,2},{7,3},{8,12},{9,13},{10,... | collective-permute-start | bytes 1376264 | tf_op jit(solution)/shard_map/ppermute | solution.py:13
  179.4 13.1 %collective-permute-start.38 = (bf16[128,1792]{1,0:T(8,128)(2,1)S(1)}, bf16[128,1792]{1,0:T(8,128)(2,1)S(1)}, u32[]{:S(2)}, u32[]{:S(2)}) collective-permute-start(bf16[128,1792]{1,0:T(8,128)(2,1)S(1)} %pad_maximum_fusion.7), channel_id=1, source_target_pairs={{0,2},{1,3},{2,0},{3,1},{4,6},{5,7},{6,4},{7,5},{8,10},{9,11},{10,... | collective-permute-start | bytes 1376264 | tf_op jit(solution)/shard_map/ppermute | solution.py:13
  180.5 21.0 %collective-permute-start.33 = (bf16[128,1792]{1,0:T(8,128)(2,1)S(1)}, bf16[128,1792]{1,0:T(8,128)(2,1)S(1)}, u32[]{:S(2)}, u32[]{:S(2)}) collective-permute-start(bf16[128,1792]{1,0:T(8,128)(2,1)S(1)} %slice.235), channel_id=1, source_target_pairs={{0,4},{1,5},{2,6},{3,7},{4,0},{5,1},{6,2},{7,3},{8,12},{9,13},{10,... | collective-permute-start | bytes 1376264 | tf_op jit(solution)/shard_map/ppermute | solution.py:13
  181.2 24.0 %collective-permute-start.19 = (bf16[64,1792]{1,0:T(8,128)(2,1)S(1)}, bf16[64,1792]{1,0:T(8,128)(2,1)S(1)}, u32[]{:S(2)}, u32[]{:S(2)}) collective-permute-start(bf16[64,1792]{1,0:T(8,128)(2,1)S(1)} %slice.227), channel_id=1, source_target_pairs={{0,4},{1,5},{2,6},{3,7},{4,0},{5,1},{6,2},{7,3},{8,12},{9,13},{10,... | collective-permute-start | bytes 688136 | tf_op jit(solution)/shard_map/ppermute | solution.py:13
  191.8 25.0 %collective-permute-start.14 = (bf16[64,1792]{1,0:T(8,128)(2,1)S(1)}, bf16[64,1792]{1,0:T(8,128)(2,1)S(1)}, u32[]{:S(2)}, u32[]{:S(2)}) collective-permute-start(bf16[64,1792]{1,0:T(8,128)(2,1)S(1)} %slice.217), channel_id=1, source_target_pairs={{0,2},{1,3},{2,0},{3,1},{4,6},{5,7},{6,4},{7,5},{8,10},{9,11},{10,... | collective-permute-start | bytes 688136 | tf_op jit(solution)/shard_map/ppermute | solution.py:13
  192.7 24.2 %collective-permute-start.39 = (bf16[64,1792]{1,0:T(8,128)(2,1)S(1)}, bf16[64,1792]{1,0:T(8,128)(2,1)S(1)}, u32[]{:S(2)}, u32[]{:S(2)}) collective-permute-start(bf16[64,1792]{1,0:T(8,128)(2,1)S(1)} %slice.247), channel_id=1, source_target_pairs={{0,4},{1,5},{2,6},{3,7},{4,0},{5,1},{6,2},{7,3},{8,12},{9,13},{10,... | collective-permute-start | bytes 688136 | tf_op jit(solution)/shard_map/ppermute | solution.py:13
  201.6 16.9 %collective-permute-start.34 = (bf16[64,1792]{1,0:T(8,128)(2,1)S(1)}, bf16[64,1792]{1,0:T(8,128)(2,1)S(1)}, u32[]{:S(2)}, u32[]{:S(2)}) collective-permute-start(bf16[64,1792]{1,0:T(8,128)(2,1)S(1)} %slice.237), channel_id=1, source_target_pairs={{0,2},{1,3},{2,0},{3,1},{4,6},{5,7},{6,4},{7,5},{8,10},{9,11},{10,... | collective-permute-start | bytes 688136 | tf_op jit(solution)/shard_map/ppermute | solution.py:13
  205.3 15.4 %collective-permute-start.22 = (bf16[16,1792]{1,0:T(8,128)(2,1)S(1)}, bf16[16,1792]{1,0:T(8,128)(2,1)S(1)}, u32[]{:S(2)}, u32[]{:S(2)}) collective-permute-start(bf16[16,1792]{1,0:T(8,128)(2,1)S(1)} %get-tuple-element.26), channel_id=1, source_target_pairs={{0,24},{1,25},{2,26},{3,27},{4,28},{5,29},{6,30},{7,31},{8,16},{9,... | collective-permute-start | bytes 172040 | tf_op jit(solution)/shard_map/ppermute | solution.py:13
  207.3 14.6 %collective-permute-start.21 = (bf16[16,1792]{1,0:T(8,128)(2,1)S(1)}, bf16[16,1792]{1,0:T(8,128)(2,1)S(1)}, u32[]{:S(2)}, u32[]{:S(2)}) collective-permute-start(bf16[16,1792]{1,0:T(8,128)(2,1)S(1)} %get-tuple-element.27), channel_id=1, source_target_pairs={{0,16},{1,17},{2,18},{3,19},{4,20},{5,21},{6,22},{7,23},{8,24},{9,... | collective-permute-start | bytes 172040 | tf_op jit(solution)/shard_map/ppermute | solution.py:13
  216.8 6.6 %collective-permute-start.20 = (bf16[16,1792]{1,0:T(8,128)(2,1)S(1)}, bf16[16,1792]{1,0:T(8,128)(2,1)S(1)}, u32[]{:S(2)}, u32[]{:S(2)}) collective-permute-start(bf16[16,1792]{1,0:T(8,128)(2,1)S(1)} %get-tuple-element.25), channel_id=1, source_target_pairs={{0,8},{1,9},{2,10},{3,11},{4,12},{5,13},{6,14},{7,15},{8,0},{9,1},... | collective-permute-start | bytes 172040 | tf_op jit(solution)/shard_map/ppermute | solution.py:13
  216.9 7.4 %collective-permute-start.17 = (bf16[16,1792]{1,0:T(8,128)(2,1)S(1)}, bf16[16,1792]{1,0:T(8,128)(2,1)S(1)}, u32[]{:S(2)}, u32[]{:S(2)}) collective-permute-start(bf16[16,1792]{1,0:T(8,128)(2,1)S(1)} %get-tuple-element.23), channel_id=1, source_target_pairs={{0,24},{1,25},{2,26},{3,27},{4,28},{5,29},{6,30},{7,31},{8,16},{9,... | collective-permute-start | bytes 172040 | tf_op jit(solution)/shard_map/ppermute | solution.py:13
  218.5 7.9 %collective-permute-start.16 = (bf16[16,1792]{1,0:T(8,128)(2,1)S(1)}, bf16[16,1792]{1,0:T(8,128)(2,1)S(1)}, u32[]{:S(2)}, u32[]{:S(2)}) collective-permute-start(bf16[16,1792]{1,0:T(8,128)(2,1)S(1)} %get-tuple-element.24), channel_id=1, source_target_pairs={{0,16},{1,17},{2,18},{3,19},{4,20},{5,21},{6,22},{7,23},{8,24},{9,... | collective-permute-start | bytes 172040 | tf_op jit(solution)/shard_map/ppermute | solution.py:13
  220.7 7.2 %collective-permute-start.15 = (bf16[16,1792]{1,0:T(8,128)(2,1)S(1)}, bf16[16,1792]{1,0:T(8,128)(2,1)S(1)}, u32[]{:S(2)}, u32[]{:S(2)}) collective-permute-start(bf16[16,1792]{1,0:T(8,128)(2,1)S(1)} %get-tuple-element.22), channel_id=1, source_target_pairs={{0,8},{1,9},{2,10},{3,11},{4,12},{5,13},{6,14},{7,15},{8,0},{9,1},... | collective-permute-start | bytes 172040 | tf_op jit(solution)/shard_map/ppermute | solution.py:13
  221.9 6.1 %collective-permute-start.42 = (bf16[16,1792]{1,0:T(8,128)(2,1)S(1)}, bf16[16,1792]{1,0:T(8,128)(2,1)S(1)}, u32[]{:S(2)}, u32[]{:S(2)}) collective-permute-start(bf16[16,1792]{1,0:T(8,128)(2,1)S(1)} %get-tuple-element.18), channel_id=1, source_target_pairs={{0,24},{1,25},{2,26},{3,27},{4,28},{5,29},{6,30},{7,31},{8,16},{9,... | collective-permute-start | bytes 172040 | tf_op jit(solution)/shard_map/ppermute | solution.py:13
  223.4 7.5 %collective-permute-start.41 = (bf16[16,1792]{1,0:T(8,128)(2,1)S(1)}, bf16[16,1792]{1,0:T(8,128)(2,1)S(1)}, u32[]{:S(2)}, u32[]{:S(2)}) collective-permute-start(bf16[16,1792]{1,0:T(8,128)(2,1)S(1)} %get-tuple-element.19), channel_id=1, source_target_pairs={{0,16},{1,17},{2,18},{3,19},{4,20},{5,21},{6,22},{7,23},{8,24},{9,... | collective-permute-start | bytes 172040 | tf_op jit(solution)/shard_map/ppermute | solution.py:13
  224.3 6.6 %collective-permute-start.40 = (bf16[16,1792]{1,0:T(8,128)(2,1)S(1)}, bf16[16,1792]{1,0:T(8,128)(2,1)S(1)}, u32[]{:S(2)}, u32[]{:S(2)}) collective-permute-start(bf16[16,1792]{1,0:T(8,128)(2,1)S(1)} %get-tuple-element.17), channel_id=1, source_target_pairs={{0,8},{1,9},{2,10},{3,11},{4,12},{5,13},{6,14},{7,15},{8,0},{9,1},... | collective-permute-start | bytes 172040 | tf_op jit(solution)/shard_map/ppermute | solution.py:13
  226.4 6.0 %collective-permute-start.37 = (bf16[16,1792]{1,0:T(8,128)(2,1)S(1)}, bf16[16,1792]{1,0:T(8,128)(2,1)S(1)}, u32[]{:S(2)}, u32[]{:S(2)}) collective-permute-start(bf16[16,1792]{1,0:T(8,128)(2,1)S(1)} %get-tuple-element.15), channel_id=1, source_target_pairs={{0,24},{1,25},{2,26},{3,27},{4,28},{5,29},{6,30},{7,31},{8,16},{9,... | collective-permute-start | bytes 172040 | tf_op jit(solution)/shard_map/ppermute | solution.py:13
  227.9 5.8 %collective-permute-start.36 = (bf16[16,1792]{1,0:T(8,128)(2,1)S(1)}, bf16[16,1792]{1,0:T(8,128)(2,1)S(1)}, u32[]{:S(2)}, u32[]{:S(2)}) collective-permute-start(bf16[16,1792]{1,0:T(8,128)(2,1)S(1)} %get-tuple-element.16), channel_id=1, source_target_pairs={{0,16},{1,17},{2,18},{3,19},{4,20},{5,21},{6,22},{7,23},{8,24},{9,... | collective-permute-start | bytes 172040 | tf_op jit(solution)/shard_map/ppermute | solution.py:13
  228.0 5.7 %collective-permute-start.35 = (bf16[16,1792]{1,0:T(8,128)(2,1)S(1)}, bf16[16,1792]{1,0:T(8,128)(2,1)S(1)}, u32[]{:S(2)}, u32[]{:S(2)}) collective-permute-start(bf16[16,1792]{1,0:T(8,128)(2,1)S(1)} %get-tuple-element.14), channel_id=1, source_target_pairs={{0,8},{1,9},{2,10},{3,11},{4,12},{5,13},{6,14},{7,15},{8,0},{9,1},... | collective-permute-start | bytes 172040 | tf_op jit(solution)/shard_map/ppermute | solution.py:13
  (7 other events, 15.6 us)

commit v3 on v1

v3 whole, which is shorter than its diff:
```python
import functools
import math

import jax
import jax.numpy as jnp
from jax import lax
from jax.experimental import pallas as pl
from jax.experimental.pallas import tpu as pltpu
from jax.sharding import PartitionSpec as P

CORE, PLANE, FAR = 1, (0, 2, 4, 6), 8
f32, bf16 = jnp.float32, jnp.bfloat16
CONTRACT_COLS = (((1,), (1,)), ((), ()))
LANES = 128
PIECES = 3
VMEM_LIMIT = 48 * 1024 * 1024


def swap(value, offset):
    devices = lax.axis_size("expert")
    return lax.ppermute(value, "expert", [(i, i ^ offset) for i in range(devices)])


def padded(count):
    return -(-count // LANES) * LANES


def column_chunks(width):
    step = 512 if width % 512 == 0 else LANES
    return [slice(at, at + step) for at in range(0, width, step)]


def call(body, outs, args, flops=0, scratch=(), grid=(), in_specs=None, out_specs=None):
    size = sum(math.prod(a.shape) * a.dtype.itemsize for a in (*args, *outs))
    whole = pl.BlockSpec(memory_space=pltpu.VMEM)
    return pl.pallas_call(
        body,
        out_shape=outs,
        grid=grid,
        in_specs=[whole] * len(args) if in_specs is None else in_specs,
        out_specs=[whole] * len(outs) if out_specs is None else out_specs,
        scratch_shapes=scratch,
        compiler_params=pltpu.CompilerParams(vmem_limit_bytes=VMEM_LIMIT),
        cost_estimate=pl.CostEstimate(flops=flops, bytes_accessed=size, transcendentals=0),
    )(*args)


def code_kernel(experts, tokens, ids, gates, out):
    rows, width = tokens.shape
    for at in range(0, width, LANES):
        block = tokens[:, at : at + LANES].astype(f32)
        scale = jnp.max(jnp.abs(block), axis=1, keepdims=True) + 1e-06
        scale = scale.astype(bf16).astype(f32)
        quantized = (block / scale).astype(bf16).astype(f32)
        out[:, at : at + LANES] = (quantized * scale).astype(bf16)
    lane = lax.broadcasted_iota(jnp.int32, (rows, out.shape[1] - width), 1)
    rest = jnp.zeros(lane.shape, f32)
    for k in range(ids.shape[1]):
        rest = jnp.where(ids[:, k : k + 1] == lane % experts, gates[:, k : k + 1], rest)
    columns = jnp.zeros(lane.shape, f32)
    for number in range(PIECES):
        piece = rest.astype(bf16).astype(f32)
        columns = jnp.where(lane // experts == number, piece, columns)
        rest = rest - piece
    out[:, width:] = columns.astype(bf16)


def pack_tokens_kernel(experts, capacity, chip, *refs):
    *blocks, first, second, third, fourth, by_row, by_slot = refs
    tok_dev = blocks[0].shape[0]
    rows, slots = by_row.shape
    width = first.shape[1]
    taken = slots_of(len(blocks), capacity)
    columns = jnp.concatenate([block[:, width:].astype(f32) for block in blocks], axis=0)
    lane = lax.broadcasted_iota(jnp.int32, columns.shape, 1)
    pick = lax.broadcasted_iota(jnp.int32, (rows, LANES), 1)
    gates, named = [], jnp.zeros((rows, LANES), f32)
    for number in range(len(PLANE)):
        mine = (lane % experts == (chip[0] ^ number)) & (lane < PIECES * experts)
        gates.append(jnp.sum(jnp.where(mine, columns, 0.0), axis=1, keepdims=True))
        named = jnp.where((pick == number) & (gates[-1] > 0.0), 1.0, named)
    row = lax.broadcasted_iota(jnp.int32, (rows, rows), 0)
    other = lax.broadcasted_iota(jnp.int32, (rows, rows), 1)
    earlier = (row // tok_dev == other // tok_dev) & (other < row)
    earlier = jnp.where(earlier, 1.0, 0.0).astype(bf16)
    counts = jnp.dot(earlier, named.astype(bf16), preferred_element_type=f32)
    slot = lax.broadcasted_iota(jnp.int32, (rows, slots), 1)
    start = lax.broadcasted_iota(jnp.int32, (rows, 1), 0) // tok_dev * capacity
    weights = jnp.zeros((rows, slots), f32)
    for number, gate in enumerate(gates):
        count = jnp.sum(jnp.where(pick == number, counts, 0.0), axis=1, keepdims=True)
        place = number * taken + start + count.astype(jnp.int32)
        weights = jnp.where(slot == place, gate, weights)
    by_row[...] = weights
    by_slot[...] = weights.T
    chosen = jnp.where(by_slot[...] > 0.0, 1.0, 0.0).astype(bf16)
    for part in column_chunks(width):
        held = jnp.concatenate([block[:, part] for block in blocks], axis=0)
        packed = jnp.dot(chosen, held, preferred_element_type=f32)
        for number, out in enumerate((first, second, third, fourth)):
            out[:, part] = packed[number * taken : (number + 1) * taken].astype(bf16)


def pack_cots_kernel(capacity, by_slot, *refs):
    *blocks, first, second, third, fourth = refs
    width = first.shape[1]
    taken = slots_of(len(blocks), capacity)
    gate = jnp.sum(by_slot[...], axis=1, keepdims=True)
    chosen = jnp.where(by_slot[...] > 0.0, 1.0, 0.0).astype(bf16)
    for part in column_chunks(width):
        held = jnp.concatenate([block[:, part] for block in blocks], axis=0)
        packed = gate * jnp.dot(chosen, held, preferred_element_type=f32)
        for number, out in enumerate((first, second, third, fourth)):
            out[:, part] = packed[number * taken : (number + 1) * taken].astype(bf16)


def slots_of(blocks, capacity):
    return blocks * capacity


def joined(refs, part, height):
    taken = [ref[:, part].astype(f32) for ref in refs]
    rest = height - sum(value.shape[0] for value in taken)
    if rest:
        taken.append(jnp.zeros((rest, taken[0].shape[1]), f32))
    return jnp.concatenate(taken, axis=0).astype(bf16)


def unpack_kernel(weighted, by_row, first, second, third, fourth, *outs):
    rows, slots = by_row.shape
    tok_dev = outs[0].shape[0]
    if weighted:
        matrices, rest = [], by_row[...]
        for _ in range(PIECES):
            matrices.append(rest.astype(bf16))
            rest = rest - matrices[-1].astype(f32)
    else:
        matrices = [jnp.where(by_row[...] > 0.0, 1.0, 0.0).astype(bf16)]
    for part in column_chunks(first.shape[1]):
        packed = joined((first, second, third, fourth), part, slots)
        total = jnp.dot(matrices[0], packed, preferred_element_type=f32)
        for matrix in matrices[1:]:
            total = total + jnp.dot(matrix, packed, preferred_element_type=f32)
        for number, out in enumerate(outs):
            out[:, part] = total[number * tok_dev : (number + 1) * tok_dev].astype(bf16)


def sum_kernel(*refs):
    *blocks, out = refs
    for part in column_chunks(out.shape[1]):
        total = blocks[0][:, part].astype(f32)
        for block in blocks[1:]:
            total = total + block[:, part].astype(f32)
        out[:, part] = total.astype(bf16)


def each_slab(step, steps, own, other, work):
    pl.when(step < steps)(functools.partial(work, *own))
    pl.when(step >= steps)(functools.partial(work, *other))


def forward_kernel(steps, x0, x1, x2, x3, g0, u0, d0, g1, u1, d1, *refs):
    o0, o1, o2, o3, for_up, for_gate, x, total = refs
    step = pl.program_id(0)
    rows = x.shape[0]

    @pl.when(step == 0)
    def _():
        for part in column_chunks(x.shape[1]):
            x[:, part] = joined((x0, x1, x2, x3), part, rows)
        total[...] = jnp.zeros_like(total)

    def work(gate_w, up_w, down_w):
        pre_gate = jnp.dot(x[...], gate_w[0], preferred_element_type=f32)
        pre_up = jnp.dot(x[...], up_w[0], preferred_element_type=f32)
        sigma = jax.nn.sigmoid(pre_gate)
        activated = pre_gate * sigma
        for_up[...] = activated
        for_gate[...] = pre_up * sigma * (1.0 + pre_gate * (1.0 - sigma))
        hidden = (activated * pre_up).astype(bf16)
        for part in column_chunks(x.shape[1]):
            total[:, part] += jnp.dot(hidden, down_w[0, :, part], preferred_element_type=f32)

    each_slab(step, steps, (g0, u0, d0), (g1, u1, d1), work)

    @pl.when(step == 2 * steps - 1)
    def _():
        store_packed(total, (o0, o1, o2, o3))


def store_packed(total, outs):
    taken = outs[0].shape[0]
    for number, out in enumerate(outs):
        for part in column_chunks(out.shape[1]):
            out[:, part] = total[number * taken : (number + 1) * taken, part].astype(bf16)


def backward_kernel(steps, x0, x1, x2, x3, for_up, for_gate, g0, u0, d0, g1, u1, d1, *refs):
    o0, o1, o2, o3, x, total = refs
    step = pl.program_id(0)
    rows = x.shape[0]

    @pl.when(step == 0)
    def _():
        for part in column_chunks(x.shape[1]):
            x[:, part] = joined((x0, x1, x2, x3), part, rows)
        total[...] = jnp.zeros_like(total)

    def work(gate_w, up_w, down_w):
        hidden_grad = lax.dot_general(x[...], down_w[0], CONTRACT_COLS, preferred_element_type=f32)
        gate_grad = (hidden_grad * for_gate[...]).astype(bf16)
        up_grad = (hidden_grad * for_up[...]).astype(bf16)
        for part in column_chunks(x.shape[1]):
            total[:, part] += lax.dot_general(
                gate_grad, gate_w[0, part], CONTRACT_COLS, preferred_element_type=f32
            ) + lax.dot_general(
                up_grad, up_w[0, part], CONTRACT_COLS, preferred_element_type=f32
            )

    each_slab(step, steps, (g0, u0, d0), (g1, u1, d1), work)

    @pl.when(step == 2 * steps - 1)
    def _():
        store_packed(total, (o0, o1, o2, o3))


def expert_specs(width, hidden, tile):
    steps = hidden // tile
    own = lambda i: jnp.minimum(i, steps - 1)
    other = lambda i: jnp.maximum(i - steps, 0)
    specs = []
    for place in (own, other):
        into = pl.BlockSpec((1, width, tile), lambda i, place=place: (0, 0, place(i)))
        back = pl.BlockSpec((1, tile, width), lambda i, place=place: (0, place(i), 0))
        specs += [into, into, back]
    return specs, steps


def on_device(tokens, expert_ids, gate_values, cotangent, gate_weight, up_weight, down_weight):
    tok_dev, top = expert_ids.shape
    width, hidden = gate_weight.shape[1:]
    devices = lax.axis_size("expert")
    experts = devices // 2
    capacity = min(tok_dev, tok_dev * top * 5 // (4 * experts))
    far = range(FAR, devices, FAR)
    blocks = devices // FAR
    taken = slots_of(blocks, capacity)
    rows, slots = blocks * tok_dev, padded(len(PLANE) * taken)
    chip = (lax.axis_index("expert") // 2).reshape(1).astype(jnp.int32)
    shape = jax.ShapeDtypeStruct
    packed_shapes = [shape((taken, width), bf16)] * len(PLANE)

    own = (gate_weight, up_weight, down_weight)
    other = tuple(swap(slab, CORE) for slab in own)

    (coded,) = call(
        functools.partial(code_kernel, experts),
        [shape((tok_dev, width + padded(PIECES * experts)), bf16)],
        (tokens, expert_ids, gate_values),
    )
    held = [coded] + [swap(coded, offset) for offset in far]
    cots = [cotangent] + [swap(cotangent, offset) for offset in far]

    whole = pl.BlockSpec(memory_space=pltpu.VMEM)
    *packed, by_row, by_slot = call(
        functools.partial(pack_tokens_kernel, experts, capacity),
        packed_shapes + [shape((rows, slots), f32), shape((slots, rows), f32)],
        (chip, *held),
        in_specs=[pl.BlockSpec(memory_space=pltpu.SMEM)] + [whole] * blocks,
        flops=2 * rows * slots * width,
    )
    x = [packed[0]] + [swap(value, offset) for value, offset in zip(packed[1:], PLANE[1:])]

    packed = call(
        functools.partial(pack_cots_kernel, capacity),
        packed_shapes,
        (by_slot, *cots),
        flops=2 * rows * slots * width,
    )
    grads = [packed[0]] + [swap(value, offset) for value, offset in zip(packed[1:], PLANE[1:])]

    all_taken = len(PLANE) * taken
    tile = 256
    weight_specs, steps = expert_specs(width, hidden, tile)
    kept_spec = pl.BlockSpec((all_taken, tile), lambda i: (0, i))
    kept_shapes = [shape((all_taken, 2 * hidden), f32)] * 2
    scratch = [pltpu.VMEM((all_taken, width), bf16), pltpu.VMEM((all_taken, width), f32)]
    flops = 2 * 3 * all_taken * width * 2 * hidden
    *outs, for_up, for_gate = call(
        functools.partial(forward_kernel, steps),
        packed_shapes + kept_shapes,
        (*x, *own, *other),
        flops=flops,
        grid=(2 * steps,),
        in_specs=[whole] * 4 + weight_specs,
        out_specs=[whole] * 4 + [kept_spec] * 2,
        scratch=scratch,
    )

    def go_home(values, weighted):
        back = [values[0]] + [swap(value, offset) for value, offset in zip(values[1:], PLANE[1:])]
        sums = call(
            functools.partial(unpack_kernel, weighted),
            [shape((tok_dev, width), bf16)] * blocks,
            (by_row, *back),
            flops=2 * rows * slots * width * (PIECES if weighted else 1),
        )
        home = [sums[0]] + [swap(value, offset) for value, offset in zip(sums[1:], far)]
        (result,) = call(sum_kernel, [shape((tok_dev, width), bf16)], home)
        return result

    layer_out = go_home(outs, True)
    backs = call(
        functools.partial(backward_kernel, steps),
        packed_shapes,
        (*grads, for_up, for_gate, *own, *other),
        flops=flops,
        grid=(2 * steps,),
        in_specs=[whole] * 4 + [kept_spec] * 2 + weight_specs,
        scratch=scratch,
    )
    token_grad = go_home(backs, False)
    return layer_out, token_grad


def solution(mesh):
    rows = P(("groups", "expert"), None)
    slabs = P("expert", None, None)
    return jax.shard_map(
        on_device,
        mesh=mesh,
        in_specs=(rows, rows, rows, rows, slabs, slabs, slabs),
        out_specs=(rows, rows),
        check_vma=False,
    )
```

time: 424 us -> 107 us (0.25)
  waiting for transfers between devices: 381 us -> 31.3 us
  starting transfers between devices: 0.16 us -> 40.8 us
  Pallas kernels: 0 us -> 30.7 us
  matrix products: 23.1 us -> 0 us
  between operations: 13.9 us -> 0.71 us
    reduce_scatter x2 -> x0, waiting for transfers between devices: 268 us -> none  [the longest x1 138 us: on_device(): lax.psum_scatter(back.astype(jnp.bfloat16), 'expert', scatter_dimension=0...]
    all_gather x2 -> x0, waiting for transfers between devices: 112 us -> none  [the longest x1 62.9 us: on_device(): lax.all_gather(jnp.concatenate([dequant, columns], axis=1), 'expert', til...]
    ppermute x0 -> x27, starting transfers between devices: none -> 40.8 us  [swap(): lax.ppermute(value, 'expert', [(i, i ^ offset) for i in range(devices)])]
    ppermute x0 -> x27, waiting for transfers between devices: none -> 31.3 us  [swap(): lax.ppermute(value, 'expert', [(i, i ^ offset) for i in range(devices)])]
    pallas_call x0 -> x9, Pallas kernels: none -> 30.7 us  [call(): pl.pallas_call(body, out_shape=outs, grid=grid, in_specs=[whole] * len(ar...]
    dot_general x6 -> x0, matrix products: 23.1 us -> none  [the longest x1 5.37 us: on_device(): lax.dot_general(cots, down_slab, contract_cols, preferred_element_type=f32)]
  transfers between devices with their start and end apart: 4 -> 27, of which waited for: 4 -> 10; matrix products, arithmetic and copies ran while one was open for 6% -> 1% of each run, Pallas kernels for 0% -> 28%
where the time goes in v3:
time: 107 us
  starting transfers between devices  40.8 us (38%)
  waiting for transfers between devices  31.3 us (29%)
  Pallas kernels  30.7 us (29%)
  local copies, waits for them, and re-layouts  3.31 us (3%)
    ppermute x27, starting transfers between devices, swap(): lax.ppermute(value, 'expert', [(i, i ^ offset) for i in range(devices)])  40.8 us
    ppermute x27, waiting for transfers between devices, swap(): lax.ppermute(value, 'expert', [(i, i ^ offset) for i in range(devices)])  31.3 us
    pallas_call x9, Pallas kernels, call(): pl.pallas_call(body, out_shape=outs, grid=grid, in_specs=[whole] * len(ar...  30.7 us
    unnamed x6, local copies, waits for them, and re-layouts  3.31 us
  transfers between devices with their start and end apart: 27, of which 10 were waited for; matrix products, arithmetic and copies ran while one was open for 1% of the time, Pallas kernels for 28%

profile of v3, /device:TPU:0, one launch (start us, length us, event | category | flops | bytes accessed | tf_op | source)
XLA Modules:
  0.0 106.8 jit_solution(10853618388791773380)
XLA Ops:
  0.6 0.5 collective-permute-start.6
  1.1 0.1 collective-permute-start.7
  1.2 0.4 collective-permute-start.8
  1.7 0.8 copy.9.ids
  2.4 0.8 copy.10.gates
  3.2 0.9 copy-done.1
  4.1 0.2 shard_map.86.refs_0_
  4.3 2.7 %collective-permute-start = (bf16[16,3712]{1,0:T(8,128)(2,1)S(1)}, bf16[16,3712]{1,0:T(8,128)(2,1)S(1)}, u32[]{:S(2)}, u32[]{:S(2)}) collective-permute-start(bf16[16,3712]{1,0:T(8,128)(2,1)S(1)} %shard_map.86.refs_0_), channel_id=1, source_target_pairs={{0,8},{1,9},{2,10},{3,11},{4,12},{5,13},{6,14},{7,15},{8,0},{9,1},... | collective-permute-start | bytes 356360 | tf_op jit(solution)/shard_map/ppermute | solution.py:21
  7.0 2.6 %collective-permute-start.1 = (bf16[16,3712]{1,0:T(8,128)(2,1)S(1)}, bf16[16,3712]{1,0:T(8,128)(2,1)S(1)}, u32[]{:S(2)}, u32[]{:S(2)}) collective-permute-start(bf16[16,3712]{1,0:T(8,128)(2,1)S(1)} %shard_map.86.refs_0_), channel_id=1, source_target_pairs={{0,16},{1,17},{2,18},{3,19},{4,20},{5,21},{6,22},{7,23},{8,24},{9,... | collective-permute-start | bytes 356360 | tf_op jit(solution)/shard_map/ppermute | solution.py:21
  9.6 3.2 %collective-permute-done.refs_1_ = bf16[16,3712]{1,0:T(8,128)(2,1)S(1)} collective-permute-done((bf16[16,3712]{1,0:T(8,128)(2,1)S(1)}, bf16[16,3712]{1,0:T(8,128)(2,1)S(1)}, u32[]{:S(2)}, u32[]{:S(2)}) %collective-permute-start) | collective-permute-done | bytes 118816 | tf_op jit(solution)/shard_map/ppermute | solution.py:21
  12.8 3.1 %collective-permute-start.2 = (bf16[16,3712]{1,0:T(8,128)(2,1)S(1)}, bf16[16,3712]{1,0:T(8,128)(2,1)S(1)}, u32[]{:S(2)}, u32[]{:S(2)}) collective-permute-start(bf16[16,3712]{1,0:T(8,128)(2,1)S(1)} %shard_map.86.refs_0_), channel_id=1, source_target_pairs={{0,24},{1,25},{2,26},{3,27},{4,28},{5,29},{6,30},{7,31},{8,16},{9,... | collective-permute-start | bytes 356360 | tf_op jit(solution)/shard_map/ppermute | solution.py:21
  15.9 0.3 collective-permute-start.15
  16.2 4.1 %collective-permute-done.2.refs_3_ = bf16[16,3712]{1,0:T(8,128)(2,1)S(1)} collective-permute-done((bf16[16,3712]{1,0:T(8,128)(2,1)S(1)}, bf16[16,3712]{1,0:T(8,128)(2,1)S(1)}, u32[]{:S(2)}, u32[]{:S(2)}) %collective-permute-start.2) | collective-permute-done | bytes 118816 | tf_op jit(solution)/shard_map/ppermute | solution.py:21
  20.3 1.0 shard_map.87
  21.4 2.2 %collective-permute-start.3 = (bf16[40,3584]{1,0:T(8,128)(2,1)S(1)}, bf16[40,3584]{1,0:T(8,128)(2,1)S(1)}, u32[]{:S(2)}, u32[]{:S(2)}) collective-permute-start(bf16[40,3584]{1,0:T(8,128)(2,1)S(1)} %get-tuple-element.32), channel_id=1, source_target_pairs={{0,2},{1,3},{2,0},{3,1},{4,6},{5,7},{6,4},{7,5},{8,10},{9,11},{10,... | collective-permute-start | bytes 860168 | tf_op jit(solution)/shard_map/ppermute | solution.py:21
  23.5 1.0 collective-permute-start.16
  24.5 6.0 %collective-permute-done.16.refs_2_ = bf16[16,3584]{1,0:T(8,128)(2,1)S(1)} collective-permute-done((bf16[16,3584]{1,0:T(8,128)(2,1)}, bf16[16,3584]{1,0:T(8,128)(2,1)S(1)}, u32[]{:S(2)}, u32[]{:S(2)}) %collective-permute-start.16) | collective-permute-done | bytes 114720 | tf_op jit(solution)/shard_map/ppermute | solution.py:21
  30.6 2.7 %collective-permute-start.17 = (bf16[16,3584]{1,0:T(8,128)(2,1)}, bf16[16,3584]{1,0:T(8,128)(2,1)S(1)}, u32[]{:S(2)}, u32[]{:S(2)}) collective-permute-start(bf16[16,3584]{1,0:T(8,128)(2,1)} %refs_0_.1), channel_id=1, source_target_pairs={{0,24},{1,25},{2,26},{3,27},{4,28},{5,29},{6,30},{7,31},{8,16},{9,... | collective-permute-start | bytes 344072 | tf_op jit(solution)/shard_map/ppermute | solution.py:21
  33.3 4.1 %collective-permute-done.17.refs_3_ = bf16[16,3584]{1,0:T(8,128)(2,1)S(1)} collective-permute-done((bf16[16,3584]{1,0:T(8,128)(2,1)}, bf16[16,3584]{1,0:T(8,128)(2,1)S(1)}, u32[]{:S(2)}, u32[]{:S(2)}) %collective-permute-start.17) | collective-permute-done | bytes 114720 | tf_op jit(solution)/shard_map/ppermute | solution.py:21
  37.4 2.8 %collective-permute-start.4 = (bf16[40,3584]{1,0:T(8,128)(2,1)S(1)}, bf16[40,3584]{1,0:T(8,128)(2,1)S(1)}, u32[]{:S(2)}, u32[]{:S(2)}) collective-permute-start(bf16[40,3584]{1,0:T(8,128)(2,1)S(1)} %get-tuple-element.33), channel_id=1, source_target_pairs={{0,4},{1,5},{2,6},{3,7},{4,0},{5,1},{6,2},{7,3},{8,12},{9,13},{10,... | collective-permute-start | bytes 860168 | tf_op jit(solution)/shard_map/ppermute | solution.py:21
  40.2 0.9 copy-done
  41.1 0.6 shard_map.91
  41.7 6.2 %collective-permute-done.4.x2 = bf16[40,3584]{1,0:T(8,128)(2,1)S(1)} collective-permute-done((bf16[40,3584]{1,0:T(8,128)(2,1)S(1)}, bf16[40,3584]{1,0:T(8,128)(2,1)S(1)}, u32[]{:S(2)}, u32[]{:S(2)}) %collective-permute-start.4) | collective-permute-done | bytes 286752 | tf_op jit(solution)/shard_map/ppermute | solution.py:21
  47.9 1.6 %collective-permute-start.18 = (bf16[40,3584]{1,0:T(8,128)(2,1)S(1)}, bf16[40,3584]{1,0:T(8,128)(2,1)S(1)}, u32[]{:S(2)}, u32[]{:S(2)}) collective-permute-start(bf16[40,3584]{1,0:T(8,128)(2,1)S(1)} %get-tuple-element.45), channel_id=1, source_target_pairs={{0,2},{1,3},{2,0},{3,1},{4,6},{5,7},{6,4},{7,5},{8,10},{9,11},{10,... | collective-permute-start | bytes 860168 | tf_op jit(solution)/shard_map/ppermute | solution.py:21
  49.5 1.5 %collective-permute-start.19 = (bf16[40,3584]{1,0:T(8,128)(2,1)S(1)}, bf16[40,3584]{1,0:T(8,128)(2,1)S(1)}, u32[]{:S(2)}, u32[]{:S(2)}) collective-permute-start(bf16[40,3584]{1,0:T(8,128)(2,1)S(1)} %get-tuple-element.46), channel_id=1, source_target_pairs={{0,4},{1,5},{2,6},{3,7},{4,0},{5,1},{6,2},{7,3},{8,12},{9,13},{10,... | collective-permute-start | bytes 860168 | tf_op jit(solution)/shard_map/ppermute | solution.py:21
  51.0 0.4 collective-permute-start.20
  51.4 11.0 %shard_map.88 = (bf16[40,3584]{1,0:T(8,128)(2,1)S(1)}, bf16[40,3584]{1,0:T(8,128)(2,1)S(1)}, bf16[40,3584]{1,0:T(8,128)(2,1)S(1)}, bf16[40,3584]{1,0:T(8,128)(2,...) custom-call(bf16[40,3584]{1,0:T(8,128)(2,1)S(1)} %get-tuple-element.31.x0, ...), custom_call_target="tpu_custom_call" | custom-call | flops 3523215360 | bytes 25624576 | tf_op jit(solution)/shard_map/pallas_call | solution.py:36
  62.5 1.6 %collective-permute-start.9 = (bf16[40,3584]{1,0:T(8,128)(2,1)S(1)}, bf16[40,3584]{1,0:T(8,128)(2,1)S(1)}, u32[]{:S(2)}, u32[]{:S(2)}) collective-permute-start(bf16[40,3584]{1,0:T(8,128)(2,1)S(1)} %get-tuple-element.36), channel_id=1, source_target_pairs={{0,2},{1,3},{2,0},{3,1},{4,6},{5,7},{6,4},{7,5},{8,10},{9,11},{10,... | collective-permute-start | bytes 860168 | tf_op jit(solution)/shard_map/ppermute | solution.py:21
  64.1 1.5 %collective-permute-start.10 = (bf16[40,3584]{1,0:T(8,128)(2,1)S(1)}, bf16[40,3584]{1,0:T(8,128)(2,1)S(1)}, u32[]{:S(2)}, u32[]{:S(2)}) collective-permute-start(bf16[40,3584]{1,0:T(8,128)(2,1)S(1)} %get-tuple-element.37), channel_id=1, source_target_pairs={{0,4},{1,5},{2,6},{3,7},{4,0},{5,1},{6,2},{7,3},{8,12},{9,13},{10,... | collective-permute-start | bytes 860168 | tf_op jit(solution)/shard_map/ppermute | solution.py:21
  65.6 0.4 collective-permute-start.11
  66.0 15.5 %shard_map.92 = (bf16[40,3584]{1,0:T(8,128)(2,1)S(1)}, bf16[40,3584]{1,0:T(8,128)(2,1)S(1)}, bf16[40,3584]{1,0:T(8,128)(2,1)S(1)}, bf16[40,3584]{1,0:T(8,128)(2,1)S(1)}) custom-call(bf16[40,3584]{1,0:T(8,128)(2,1)S(1)} %get-tuple-element.44.x0, bf16[40,3584]{1,0:T(8,128)(2,1)S(1)} %collective-permute-done.18.x1, ...), custom_call_target="tpu_custom_call" | custom-call | flops 3523215360 | bytes 25624576 | tf_op jit(solution)/shard_map/pallas_call | solution.py:36
  81.5 1.6 %collective-permute-start.21 = (bf16[40,3584]{1,0:T(8,128)(2,1)S(1)}, bf16[40,3584]{1,0:T(8,128)(2,1)S(1)}, u32[]{:S(2)}, u32[]{:S(2)}) collective-permute-start(bf16[40,3584]{1,0:T(8,128)(2,1)S(1)} %get-tuple-element.51), channel_id=1, source_target_pairs={{0,2},{1,3},{2,0},{3,1},{4,6},{5,7},{6,4},{7,5},{8,10},{9,11},{10,... | collective-permute-start | bytes 860168 | tf_op jit(solution)/shard_map/ppermute | solution.py:21
  83.1 1.5 %collective-permute-start.22 = (bf16[40,3584]{1,0:T(8,128)(2,1)S(1)}, bf16[40,3584]{1,0:T(8,128)(2,1)S(1)}, u32[]{:S(2)}, u32[]{:S(2)}) collective-permute-start(bf16[40,3584]{1,0:T(8,128)(2,1)S(1)} %get-tuple-element.52), channel_id=1, source_target_pairs={{0,4},{1,5},{2,6},{3,7},{4,0},{5,1},{6,2},{7,3},{8,12},{9,13},{10,... | collective-permute-start | bytes 860168 | tf_op jit(solution)/shard_map/ppermute | solution.py:21
  84.7 0.4 collective-permute-start.23
  85.1 0.6 shard_map.89
  85.7 0.4 collective-permute-start.12
  86.1 3.3 %collective-permute-start.13 = (bf16[16,3584]{1,0:T(8,128)(2,1)S(1)}, bf16[16,3584]{1,0:T(8,128)(2,1)S(1)}, u32[]{:S(2)}, u32[]{:S(2)}) collective-permute-start(bf16[16,3584]{1,0:T(8,128)(2,1)S(1)} %get-tuple-element.41), channel_id=1, source_target_pairs={{0,16},{1,17},{2,18},{3,19},{4,20},{5,21},{6,22},{7,23},{8,24},{9,... | collective-permute-start | bytes 344072 | tf_op jit(solution)/shard_map/ppermute | solution.py:21
  89.4 1.0 collective-permute-done.21.second
  90.4 3.5 %collective-permute-start.14 = (bf16[16,3584]{1,0:T(8,128)(2,1)S(1)}, bf16[16,3584]{1,0:T(8,128)(2,1)S(1)}, u32[]{:S(2)}, u32[]{:S(2)}) collective-permute-start(bf16[16,3584]{1,0:T(8,128)(2,1)S(1)} %get-tuple-element.42), channel_id=1, source_target_pairs={{0,24},{1,25},{2,26},{3,27},{4,28},{5,29},{6,30},{7,31},{8,16},{9,... | collective-permute-start | bytes 344072 | tf_op jit(solution)/shard_map/ppermute | solution.py:21
  93.9 0.7 collective-permute-done.22.third
  94.6 0.3 shard_map.93
  95.0 0.3 collective-permute-start.24
  95.3 4.0 %collective-permute-start.25 = (bf16[16,3584]{1,0:T(8,128)(2,1)S(1)}, bf16[16,3584]{1,0:T(8,128)(2,1)S(1)}, u32[]{:S(2)}, u32[]{:S(2)}) collective-permute-start(bf16[16,3584]{1,0:T(8,128)(2,1)S(1)} %get-tuple-element.56), channel_id=1, source_target_pairs={{0,16},{1,17},{2,18},{3,19},{4,20},{5,21},{6,22},{7,23},{8,24},{9,... | collective-permute-start | bytes 344072 | tf_op jit(solution)/shard_map/ppermute | solution.py:21
  99.4 0.7 shard_map.90
  100.1 1.2 %collective-permute-done.24.refs_1_ = bf16[16,3584]{1,0:T(8,128)(2,1)S(1)} collective-permute-done((bf16[16,3584]{1,0:T(8,128)(2,1)S(1)}, bf16[16,3584]{1,0:T(8,128)(2,1)S(1)}, u32[]{:S(2)}, u32[]{:S(2)}) %collective-permute-start.24) | collective-permute-done | bytes 114720 | tf_op jit(solution)/shard_map/ppermute | solution.py:21
  101.3 3.2 %collective-permute-done.25.refs_2_ = bf16[16,3584]{1,0:T(8,128)(2,1)S(1)} collective-permute-done((bf16[16,3584]{1,0:T(8,128)(2,1)S(1)}, bf16[16,3584]{1,0:T(8,128)(2,1)S(1)}, u32[]{:S(2)}, u32[]{:S(2)}) %collective-permute-start.25) | collective-permute-done | bytes 114720 | tf_op jit(solution)/shard_map/ppermute | solution.py:21
  104.5 1.5 %collective-permute-done.26.refs_3_ = bf16[16,3584]{1,0:T(8,128)(2,1)S(1)} collective-permute-done((bf16[16,3584]{1,0:T(8,128)(2,1)S(1)}, bf16[16,3584]{1,0:T(8,128)(2,1)S(1)}, u32[]{:S(2)}, u32[]{:S(2)}) %collective-permute-start.26) | collective-permute-done | bytes 114720 | tf_op jit(solution)/shard_map/ppermute | solution.py:21
  106.1 0.7 shard_map.94
  (21 shorter events, 0.1 us)
Async XLA Ops:
  0.6 50.4 %collective-permute-start.6 = (bf16[1,3584,512]{2,1,0:T(8,128)(2,1)}, bf16[1,3584,512]{2,1,0:T(8,128)(2,1)}, u32[]{:S(2)}, u32[]{:S(2)}) collective-permute-start(bf16[1,3584,512]{2,1,0:T(8,128)(2,1)} %g0.3), channel_id=1, source_target_pairs={{0,1},{1,0},{2,3},{3,2},{4,5},{5,4},{6,7},{7,6},{8,9},{9,8},{10,11... | collective-permute-start | bytes 11010056 | tf_op jit(solution)/shard_map/ppermute | solution.py:21
  1.1 50.3 %collective-permute-start.7 = (bf16[1,3584,512]{2,1,0:T(8,128)(2,1)}, bf16[1,3584,512]{2,1,0:T(8,128)(2,1)}, u32[]{:S(2)}, u32[]{:S(2)}) collective-permute-start(bf16[1,3584,512]{2,1,0:T(8,128)(2,1)} %u0.3), channel_id=1, source_target_pairs={{0,1},{1,0},{2,3},{3,2},{4,5},{5,4},{6,7},{7,6},{8,9},{9,8},{10,11... | collective-permute-start | bytes 11010056 | tf_op jit(solution)/shard_map/ppermute | solution.py:21
  1.2 50.2 %collective-permute-start.8 = (bf16[1,512,3584]{2,1,0:T(8,128)(2,1)}, bf16[1,512,3584]{2,1,0:T(8,128)(2,1)}, u32[]{:S(2)}, u32[]{:S(2)}) collective-permute-start(bf16[1,512,3584]{2,1,0:T(8,128)(2,1)} %d0.3), channel_id=1, source_target_pairs={{0,1},{1,0},{2,3},{3,2},{4,5},{5,4},{6,7},{7,6},{8,9},{9,8},{10,11... | collective-permute-start | bytes 11010056 | tf_op jit(solution)/shard_map/ppermute | solution.py:21
  3.2 0.9 copy-start.1
  4.3 8.5 %collective-permute-start = (bf16[16,3712]{1,0:T(8,128)(2,1)S(1)}, bf16[16,3712]{1,0:T(8,128)(2,1)S(1)}, u32[]{:S(2)}, u32[]{:S(2)}) collective-permute-start(bf16[16,3712]{1,0:T(8,128)(2,1)S(1)} %shard_map.86.refs_0_), channel_id=1, source_target_pairs={{0,8},{1,9},{2,10},{3,11},{4,12},{5,13},{6,14},{7,15},{8,0},{9,1},... | collective-permute-start | bytes 356360 | tf_op jit(solution)/shard_map/ppermute | solution.py:21
  7.0 8.9 %collective-permute-start.1 = (bf16[16,3712]{1,0:T(8,128)(2,1)S(1)}, bf16[16,3712]{1,0:T(8,128)(2,1)S(1)}, u32[]{:S(2)}, u32[]{:S(2)}) collective-permute-start(bf16[16,3712]{1,0:T(8,128)(2,1)S(1)} %shard_map.86.refs_0_), channel_id=1, source_target_pairs={{0,16},{1,17},{2,18},{3,19},{4,20},{5,21},{6,22},{7,23},{8,24},{9,... | collective-permute-start | bytes 356360 | tf_op jit(solution)/shard_map/ppermute | solution.py:21
  12.8 7.5 %collective-permute-start.2 = (bf16[16,3712]{1,0:T(8,128)(2,1)S(1)}, bf16[16,3712]{1,0:T(8,128)(2,1)S(1)}, u32[]{:S(2)}, u32[]{:S(2)}) collective-permute-start(bf16[16,3712]{1,0:T(8,128)(2,1)S(1)} %shard_map.86.refs_0_), channel_id=1, source_target_pairs={{0,24},{1,25},{2,26},{3,27},{4,28},{5,29},{6,30},{7,31},{8,16},{9,... | collective-permute-start | bytes 356360 | tf_op jit(solution)/shard_map/ppermute | solution.py:21
  15.9 7.6 %collective-permute-start.15 = (bf16[16,3584]{1,0:T(8,128)(2,1)}, bf16[16,3584]{1,0:T(8,128)(2,1)S(1)}, u32[]{:S(2)}, u32[]{:S(2)}) collective-permute-start(bf16[16,3584]{1,0:T(8,128)(2,1)} %refs_0_.1), channel_id=1, source_target_pairs={{0,8},{1,9},{2,10},{3,11},{4,12},{5,13},{6,14},{7,15},{8,0},{9,1},... | collective-permute-start | bytes 344072 | tf_op jit(solution)/shard_map/ppermute | solution.py:21
  21.4 18.8 %collective-permute-start.3 = (bf16[40,3584]{1,0:T(8,128)(2,1)S(1)}, bf16[40,3584]{1,0:T(8,128)(2,1)S(1)}, u32[]{:S(2)}, u32[]{:S(2)}) collective-permute-start(bf16[40,3584]{1,0:T(8,128)(2,1)S(1)} %get-tuple-element.32), channel_id=1, source_target_pairs={{0,2},{1,3},{2,0},{3,1},{4,6},{5,7},{6,4},{7,5},{8,10},{9,11},{10,... | collective-permute-start | bytes 860168 | tf_op jit(solution)/shard_map/ppermute | solution.py:21
  23.5 7.0 %collective-permute-start.16 = (bf16[16,3584]{1,0:T(8,128)(2,1)}, bf16[16,3584]{1,0:T(8,128)(2,1)S(1)}, u32[]{:S(2)}, u32[]{:S(2)}) collective-permute-start(bf16[16,3584]{1,0:T(8,128)(2,1)} %refs_0_.1), channel_id=1, source_target_pairs={{0,16},{1,17},{2,18},{3,19},{4,20},{5,21},{6,22},{7,23},{8,24},{9,... | collective-permute-start | bytes 344072 | tf_op jit(solution)/shard_map/ppermute | solution.py:21
  30.6 6.8 %collective-permute-start.17 = (bf16[16,3584]{1,0:T(8,128)(2,1)}, bf16[16,3584]{1,0:T(8,128)(2,1)S(1)}, u32[]{:S(2)}, u32[]{:S(2)}) collective-permute-start(bf16[16,3584]{1,0:T(8,128)(2,1)} %refs_0_.1), channel_id=1, source_target_pairs={{0,24},{1,25},{2,26},{3,27},{4,28},{5,29},{6,30},{7,31},{8,16},{9,... | collective-permute-start | bytes 344072 | tf_op jit(solution)/shard_map/ppermute | solution.py:21
  37.4 10.5 %collective-permute-start.4 = (bf16[40,3584]{1,0:T(8,128)(2,1)S(1)}, bf16[40,3584]{1,0:T(8,128)(2,1)S(1)}, u32[]{:S(2)}, u32[]{:S(2)}) collective-permute-start(bf16[40,3584]{1,0:T(8,128)(2,1)S(1)} %get-tuple-element.33), channel_id=1, source_target_pairs={{0,4},{1,5},{2,6},{3,7},{4,0},{5,1},{6,2},{7,3},{8,12},{9,13},{10,... | collective-permute-start | bytes 860168 | tf_op jit(solution)/shard_map/ppermute | solution.py:21
  40.2 9.3 %collective-permute-start.5 = (bf16[40,3584]{1,0:T(8,128)(2,1)S(1)}, bf16[40,3584]{1,0:T(8,128)(2,1)S(1)}, u32[]{:S(2)}, u32[]{:S(2)}) collective-permute-start(bf16[40,3584]{1,0:T(8,128)(2,1)S(1)} %get-tuple-element.34), channel_id=1, source_target_pairs={{0,6},{1,7},{2,4},{3,5},{4,2},{5,3},{6,0},{7,1},{8,14},{9,15},{10,... | collective-permute-start | bytes 860168 | tf_op jit(solution)/shard_map/ppermute | solution.py:21
  40.2 0.9 copy-start
  47.9 17.7 %collective-permute-start.18 = (bf16[40,3584]{1,0:T(8,128)(2,1)S(1)}, bf16[40,3584]{1,0:T(8,128)(2,1)S(1)}, u32[]{:S(2)}, u32[]{:S(2)}) collective-permute-start(bf16[40,3584]{1,0:T(8,128)(2,1)S(1)} %get-tuple-element.45), channel_id=1, source_target_pairs={{0,2},{1,3},{2,0},{3,1},{4,6},{5,7},{6,4},{7,5},{8,10},{9,11},{10,... | collective-permute-start | bytes 860168 | tf_op jit(solution)/shard_map/ppermute | solution.py:21
  49.5 16.5 %collective-permute-start.19 = (bf16[40,3584]{1,0:T(8,128)(2,1)S(1)}, bf16[40,3584]{1,0:T(8,128)(2,1)S(1)}, u32[]{:S(2)}, u32[]{:S(2)}) collective-permute-start(bf16[40,3584]{1,0:T(8,128)(2,1)S(1)} %get-tuple-element.46), channel_id=1, source_target_pairs={{0,4},{1,5},{2,6},{3,7},{4,0},{5,1},{6,2},{7,3},{8,12},{9,13},{10,... | collective-permute-start | bytes 860168 | tf_op jit(solution)/shard_map/ppermute | solution.py:21
  51.0 15.0 %collective-permute-start.20 = (bf16[40,3584]{1,0:T(8,128)(2,1)S(1)}, bf16[40,3584]{1,0:T(8,128)(2,1)S(1)}, u32[]{:S(2)}, u32[]{:S(2)}) collective-permute-start(bf16[40,3584]{1,0:T(8,128)(2,1)S(1)} %get-tuple-element.47), channel_id=1, source_target_pairs={{0,6},{1,7},{2,4},{3,5},{4,2},{5,3},{6,0},{7,1},{8,14},{9,15},{10,... | collective-permute-start | bytes 860168 | tf_op jit(solution)/shard_map/ppermute | solution.py:21
  62.5 22.2 %collective-permute-start.9 = (bf16[40,3584]{1,0:T(8,128)(2,1)S(1)}, bf16[40,3584]{1,0:T(8,128)(2,1)S(1)}, u32[]{:S(2)}, u32[]{:S(2)}) collective-permute-start(bf16[40,3584]{1,0:T(8,128)(2,1)S(1)} %get-tuple-element.36), channel_id=1, source_target_pairs={{0,2},{1,3},{2,0},{3,1},{4,6},{5,7},{6,4},{7,5},{8,10},{9,11},{10,... | collective-permute-start | bytes 860168 | tf_op jit(solution)/shard_map/ppermute | solution.py:21
  64.1 21.0 %collective-permute-start.10 = (bf16[40,3584]{1,0:T(8,128)(2,1)S(1)}, bf16[40,3584]{1,0:T(8,128)(2,1)S(1)}, u32[]{:S(2)}, u32[]{:S(2)}) collective-permute-start(bf16[40,3584]{1,0:T(8,128)(2,1)S(1)} %get-tuple-element.37), channel_id=1, source_target_pairs={{0,4},{1,5},{2,6},{3,7},{4,0},{5,1},{6,2},{7,3},{8,12},{9,13},{10,... | collective-permute-start | bytes 860168 | tf_op jit(solution)/shard_map/ppermute | solution.py:21
  65.6 19.5 %collective-permute-start.11 = (bf16[40,3584]{1,0:T(8,128)(2,1)S(1)}, bf16[40,3584]{1,0:T(8,128)(2,1)S(1)}, u32[]{:S(2)}, u32[]{:S(2)}) collective-permute-start(bf16[40,3584]{1,0:T(8,128)(2,1)S(1)} %get-tuple-element.38), channel_id=1, source_target_pairs={{0,6},{1,7},{2,4},{3,5},{4,2},{5,3},{6,0},{7,1},{8,14},{9,15},{10,... | collective-permute-start | bytes 860168 | tf_op jit(solution)/shard_map/ppermute | solution.py:21
  81.5 8.9 %collective-permute-start.21 = (bf16[40,3584]{1,0:T(8,128)(2,1)S(1)}, bf16[40,3584]{1,0:T(8,128)(2,1)S(1)}, u32[]{:S(2)}, u32[]{:S(2)}) collective-permute-start(bf16[40,3584]{1,0:T(8,128)(2,1)S(1)} %get-tuple-element.51), channel_id=1, source_target_pairs={{0,2},{1,3},{2,0},{3,1},{4,6},{5,7},{6,4},{7,5},{8,10},{9,11},{10,... | collective-permute-start | bytes 860168 | tf_op jit(solution)/shard_map/ppermute | solution.py:21
  83.1 11.5 %collective-permute-start.22 = (bf16[40,3584]{1,0:T(8,128)(2,1)S(1)}, bf16[40,3584]{1,0:T(8,128)(2,1)S(1)}, u32[]{:S(2)}, u32[]{:S(2)}) collective-permute-start(bf16[40,3584]{1,0:T(8,128)(2,1)S(1)} %get-tuple-element.52), channel_id=1, source_target_pairs={{0,4},{1,5},{2,6},{3,7},{4,0},{5,1},{6,2},{7,3},{8,12},{9,13},{10,... | collective-permute-start | bytes 860168 | tf_op jit(solution)/shard_map/ppermute | solution.py:21
  84.7 10.0 %collective-permute-start.23 = (bf16[40,3584]{1,0:T(8,128)(2,1)S(1)}, bf16[40,3584]{1,0:T(8,128)(2,1)S(1)}, u32[]{:S(2)}, u32[]{:S(2)}) collective-permute-start(bf16[40,3584]{1,0:T(8,128)(2,1)S(1)} %get-tuple-element.53), channel_id=1, source_target_pairs={{0,6},{1,7},{2,4},{3,5},{4,2},{5,3},{6,0},{7,1},{8,14},{9,15},{10,... | collective-permute-start | bytes 860168 | tf_op jit(solution)/shard_map/ppermute | solution.py:21
  85.7 13.6 %collective-permute-start.12 = (bf16[16,3584]{1,0:T(8,128)(2,1)S(1)}, bf16[16,3584]{1,0:T(8,128)(2,1)S(1)}, u32[]{:S(2)}, u32[]{:S(2)}) collective-permute-start(bf16[16,3584]{1,0:T(8,128)(2,1)S(1)} %get-tuple-element.40), channel_id=1, source_target_pairs={{0,8},{1,9},{2,10},{3,11},{4,12},{5,13},{6,14},{7,15},{8,0},{9,1},... | collective-permute-start | bytes 344072 | tf_op jit(solution)/shard_map/ppermute | solution.py:21
  86.1 13.3 %collective-permute-start.13 = (bf16[16,3584]{1,0:T(8,128)(2,1)S(1)}, bf16[16,3584]{1,0:T(8,128)(2,1)S(1)}, u32[]{:S(2)}, u32[]{:S(2)}) collective-permute-start(bf16[16,3584]{1,0:T(8,128)(2,1)S(1)} %get-tuple-element.41), channel_id=1, source_target_pairs={{0,16},{1,17},{2,18},{3,19},{4,20},{5,21},{6,22},{7,23},{8,24},{9,... | collective-permute-start | bytes 344072 | tf_op jit(solution)/shard_map/ppermute | solution.py:21
  90.4 9.0 %collective-permute-start.14 = (bf16[16,3584]{1,0:T(8,128)(2,1)S(1)}, bf16[16,3584]{1,0:T(8,128)(2,1)S(1)}, u32[]{:S(2)}, u32[]{:S(2)}) collective-permute-start(bf16[16,3584]{1,0:T(8,128)(2,1)S(1)} %get-tuple-element.42), channel_id=1, source_target_pairs={{0,24},{1,25},{2,26},{3,27},{4,28},{5,29},{6,30},{7,31},{8,16},{9,... | collective-permute-start | bytes 344072 | tf_op jit(solution)/shard_map/ppermute | solution.py:21
  95.0 6.4 %collective-permute-start.24 = (bf16[16,3584]{1,0:T(8,128)(2,1)S(1)}, bf16[16,3584]{1,0:T(8,128)(2,1)S(1)}, u32[]{:S(2)}, u32[]{:S(2)}) collective-permute-start(bf16[16,3584]{1,0:T(8,128)(2,1)S(1)} %get-tuple-element.55), channel_id=1, source_target_pairs={{0,8},{1,9},{2,10},{3,11},{4,12},{5,13},{6,14},{7,15},{8,0},{9,1},... | collective-permute-start | bytes 344072 | tf_op jit(solution)/shard_map/ppermute | solution.py:21
  95.3 9.2 %collective-permute-start.25 = (bf16[16,3584]{1,0:T(8,128)(2,1)S(1)}, bf16[16,3584]{1,0:T(8,128)(2,1)S(1)}, u32[]{:S(2)}, u32[]{:S(2)}) collective-permute-start(bf16[16,3584]{1,0:T(8,128)(2,1)S(1)} %get-tuple-element.56), channel_id=1, source_target_pairs={{0,16},{1,17},{2,18},{3,19},{4,20},{5,21},{6,22},{7,23},{8,24},{9,... | collective-permute-start | bytes 344072 | tf_op jit(solution)/shard_map/ppermute | solution.py:21
  99.4 6.7 %collective-permute-start.26 = (bf16[16,3584]{1,0:T(8,128)(2,1)S(1)}, bf16[16,3584]{1,0:T(8,128)(2,1)S(1)}, u32[]{:S(2)}, u32[]{:S(2)}) collective-permute-start(bf16[16,3584]{1,0:T(8,128)(2,1)S(1)} %get-tuple-element.57), channel_id=1, source_target_pairs={{0,24},{1,25},{2,26},{3,27},{4,28},{5,29},{6,30},{7,31},{8,16},{9,... | collective-permute-start | bytes 344072 | tf_op jit(solution)/shard_map/ppermute | solution.py:21

commit v4 on v3

--- a/solution.py
+++ b/solution.py
@@ -13,7 +13,8 @@
 CONTRACT_COLS = (((1,), (1,)), ((), ()))
 LANES = 128
 PIECES = 3
-VMEM_LIMIT = 48 * 1024 * 1024
+VMEM_LIMIT = 16 * 1024 * 1024
+VMEM_LIMIT_EXPERT = 48 * 1024 * 1024
 
 
 def swap(value, offset):
@@ -21,26 +22,37 @@
     return lax.ppermute(value, "expert", [(i, i ^ offset) for i in range(devices)])
 
 
+def gather_far(block):
+    held, offset = {0: block}, lax.axis_size("expert") // 2
+    while offset >= FAR:
+        held.update({at ^ offset: swap(value, offset) for at, value in held.items()})
+        offset //= 2
+    return [held[at] for at in sorted(held)]
+
+
 def padded(count):
     return -(-count // LANES) * LANES
 
 
+def chunk_of(width):
+    return 512 if width % 512 == 0 else LANES
+
+
 def column_chunks(width):
-    step = 512 if width % 512 == 0 else LANES
+    step = chunk_of(width)
     return [slice(at, at + step) for at in range(0, width, step)]
 
 
-def call(body, outs, args, flops=0, scratch=(), grid=(), in_specs=None, out_specs=None):
+def call(body, outs, args, flops=0, scratch=(), in_specs=None, limit=VMEM_LIMIT):
     size = sum(math.prod(a.shape) * a.dtype.itemsize for a in (*args, *outs))
     whole = pl.BlockSpec(memory_space=pltpu.VMEM)
     return pl.pallas_call(
         body,
         out_shape=outs,
-        grid=grid,
         in_specs=[whole] * len(args) if in_specs is None else in_specs,
-        out_specs=[whole] * len(outs) if out_specs is None else out_specs,
+        out_specs=[whole] * len(outs),
         scratch_shapes=scratch,
-        compiler_params=pltpu.CompilerParams(vmem_limit_bytes=VMEM_LIMIT),
+        compiler_params=pltpu.CompilerParams(vmem_limit_bytes=limit),
         cost_estimate=pl.CostEstimate(flops=flops, bytes_accessed=size, transcendentals=0),
     )(*args)
 
@@ -53,16 +65,16 @@
         scale = scale.astype(bf16).astype(f32)
         quantized = (block / scale).astype(bf16).astype(f32)
         out[:, at : at + LANES] = (quantized * scale).astype(bf16)
-    lane = lax.broadcasted_iota(jnp.int32, (rows, out.shape[1] - width), 1)
-    rest = jnp.zeros(lane.shape, f32)
-    for k in range(ids.shape[1]):
-        rest = jnp.where(ids[:, k : k + 1] == lane % experts, gates[:, k : k + 1], rest)
-    columns = jnp.zeros(lane.shape, f32)
+    line = lax.broadcasted_iota(jnp.int32, (out.shape[1] - width, rows), 0)
+    rest = jnp.zeros(line.shape, f32)
+    for k in range(ids.shape[0]):
+        rest = jnp.where(ids[k : k + 1] == line % experts, gates[k : k + 1], rest)
+    columns = jnp.zeros(line.shape, f32)
     for number in range(PIECES):
         piece = rest.astype(bf16).astype(f32)
-        columns = jnp.where(lane // experts == number, piece, columns)
+        columns = jnp.where(line // experts == number, piece, columns)
         rest = rest - piece
-    out[:, width:] = columns.astype(bf16)
+    out[:, width:] = columns.T.astype(bf16)
 
 
 def pack_tokens_kernel(experts, capacity, chip, *refs):
@@ -118,12 +130,12 @@
     return blocks * capacity
 
 
-def joined(refs, part, height):
+def joined(refs, part, height, kind=bf16):
     taken = [ref[:, part].astype(f32) for ref in refs]
     rest = height - sum(value.shape[0] for value in taken)
     if rest:
         taken.append(jnp.zeros((rest, taken[0].shape[1]), f32))
-    return jnp.concatenate(taken, axis=0).astype(bf16)
+    return jnp.concatenate(taken, axis=0).astype(kind)
 
 
 def unpack_kernel(weighted, by_row, first, second, third, fourth, *outs):
@@ -154,86 +166,100 @@
         out[:, part] = total.astype(bf16)
 
 
-def each_slab(step, steps, own, other, work):
-    pl.when(step < steps)(functools.partial(work, *own))
-    pl.when(step >= steps)(functools.partial(work, *other))
-
-
-def forward_kernel(steps, x0, x1, x2, x3, g0, u0, d0, g1, u1, d1, *refs):
-    o0, o1, o2, o3, for_up, for_gate, x, total = refs
-    step = pl.program_id(0)
-    rows = x.shape[0]
-
-    @pl.when(step == 0)
-    def _():
-        for part in column_chunks(x.shape[1]):
-            x[:, part] = joined((x0, x1, x2, x3), part, rows)
-        total[...] = jnp.zeros_like(total)
-
-    def work(gate_w, up_w, down_w):
-        pre_gate = jnp.dot(x[...], gate_w[0], preferred_element_type=f32)
-        pre_up = jnp.dot(x[...], up_w[0], preferred_element_type=f32)
+def streams(pairs, sems):
+    copies = [
+        pltpu.make_async_copy(source, place, sems.at[number])
+        for number, (source, place) in enumerate(pairs)
+    ]
+    for copy in copies:
+        copy.start()
+    return copies
+
+
+def forward_kernel(tile, x0, x1, x2, x3, *refs):
+    *slabs, o0, o1, o2, o3, for_up, for_gate, x, hidden, g0, u0, d0, g1, u1, d1, sems = refs
+    places = (g0, u0, d0, g1, u1, d1)
+    rows, width = x.shape
+    units = g0.shape[2]
+    step, chunk = min(tile, units), chunk_of(width)
+    pairs, tiles = [], []
+    for slab in (0, 3):
+        for at in range(0, units, step):
+            tiles.append((slab, at))
+            for matrix in (slab, slab + 1):
+                pairs.append([ref.at[0, :, pl.ds(at, step)] for ref in (slabs[matrix], places[matrix])])
+    for at in range(0, width, chunk):
+        for matrix in (2, 5):
+            pairs.append([ref.at[0, :, pl.ds(at, chunk)] for ref in (slabs[matrix], places[matrix])])
+    copies = iter(streams(pairs, sems))
+    for part in column_chunks(width):
+        x[:, part] = joined((x0, x1, x2, x3), part, rows)
+
+    for slab, at in tiles:
+        gate_w, up_w = places[slab : slab + 2]
+        next(copies).wait()
+        pre_gate = jnp.dot(x[...], gate_w[0, :, at : at + step], preferred_element_type=f32)
+        next(copies).wait()
+        pre_up = jnp.dot(x[...], up_w[0, :, at : at + step], preferred_element_type=f32)
         sigma = jax.nn.sigmoid(pre_gate)
         activated = pre_gate * sigma
-        for_up[...] = activated
-        for_gate[...] = pre_up * sigma * (1.0 + pre_gate * (1.0 - sigma))
-        hidden = (activated * pre_up).astype(bf16)
-        for part in column_chunks(x.shape[1]):
-            total[:, part] += jnp.dot(hidden, down_w[0, :, part], preferred_element_type=f32)
-
-    each_slab(step, steps, (g0, u0, d0), (g1, u1, d1), work)
-
-    @pl.when(step == 2 * steps - 1)
-    def _():
-        store_packed(total, (o0, o1, o2, o3))
-
-
-def store_packed(total, outs):
+        slope = pre_up * sigma * (1.0 + pre_gate * (1.0 - sigma))
+        into = slice(slab // 3 * units + at, slab // 3 * units + at + step)
+        hidden[:, into] = (activated * pre_up).astype(bf16)
+        for_up[into] = activated.T
+        for_gate[into] = slope.T
+
+    for part in column_chunks(width):
+        next(copies).wait()
+        total = jnp.dot(hidden[:, :units], d0[0, :, part], preferred_element_type=f32)
+        next(copies).wait()
+        total = total + jnp.dot(hidden[:, units:], d1[0, :, part], preferred_element_type=f32)
+        store_packed(total, (o0, o1, o2, o3), part)
+
+
+def store_packed(total, outs, at):
     taken = outs[0].shape[0]
     for number, out in enumerate(outs):
-        for part in column_chunks(out.shape[1]):
-            out[:, part] = total[number * taken : (number + 1) * taken, part].astype(bf16)
-
-
-def backward_kernel(steps, x0, x1, x2, x3, for_up, for_gate, g0, u0, d0, g1, u1, d1, *refs):
-    o0, o1, o2, o3, x, total = refs
-    step = pl.program_id(0)
-    rows = x.shape[0]
-
-    @pl.when(step == 0)
-    def _():
-        for part in column_chunks(x.shape[1]):
-            x[:, part] = joined((x0, x1, x2, x3), part, rows)
-        total[...] = jnp.zeros_like(total)
-
-    def work(gate_w, up_w, down_w):
-        hidden_grad = lax.dot_general(x[...], down_w[0], CONTRACT_COLS, preferred_element_type=f32)
-        gate_grad = (hidden_grad * for_gate[...]).astype(bf16)
-        up_grad = (hidden_grad * for_up[...]).astype(bf16)
-        for part in column_chunks(x.shape[1]):
-            total[:, part] += lax.dot_general(
-                gate_grad, gate_w[0, part], CONTRACT_COLS, preferred_element_type=f32
-            ) + lax.dot_general(
-                up_grad, up_w[0, part], CONTRACT_COLS, preferred_element_type=f32
-            )
-
-    each_slab(step, steps, (g0, u0, d0), (g1, u1, d1), work)
-
-    @pl.when(step == 2 * steps - 1)
-    def _():
-        store_packed(total, (o0, o1, o2, o3))
-
-
-def expert_specs(width, hidden, tile):
-    steps = hidden // tile
-    own = lambda i: jnp.minimum(i, steps - 1)
-    other = lambda i: jnp.maximum(i - steps, 0)
-    specs = []
-    for place in (own, other):
-        into = pl.BlockSpec((1, width, tile), lambda i, place=place: (0, 0, place(i)))
-        back = pl.BlockSpec((1, tile, width), lambda i, place=place: (0, place(i), 0))
-        specs += [into, into, back]
-    return specs, steps
+        out[:, at] = total[number * taken : (number + 1) * taken].astype(bf16)
+
+
+def backward_kernel(tile, x0, x1, x2, x3, for_up, for_gate, *refs):
+    *slabs, o0, o1, o2, o3, x, gate_grad, up_grad, g0, u0, d0, g1, u1, d1, sems = refs
+    places = (g0, u0, d0, g1, u1, d1)
+    width, rows = x.shape
+    units = g0.shape[2]
+    step, chunk = min(tile, units), chunk_of(width)
+    pairs, tiles = [], []
+    for slab in (0, 3):
+        for at in range(0, units, step):
+            tiles.append((slab, at))
+            pairs.append([ref.at[0, pl.ds(at, step)] for ref in (slabs[slab + 2], places[slab + 2])])
+    for at in range(0, width, chunk):
+        for matrix in (0, 1, 3, 4):
+            pairs.append([ref.at[0, pl.ds(at, chunk)] for ref in (slabs[matrix], places[matrix])])
+    copies = iter(streams(pairs, sems))
+    for part in column_chunks(width):
+        x[part] = joined((x0, x1, x2, x3), part, rows, f32).T.astype(bf16)
+
+    for slab, at in tiles:
+        next(copies).wait()
+        into = slice(slab // 3 * units + at, slab // 3 * units + at + step)
+        down_w = places[slab + 2]
+        hidden_grad = jnp.dot(down_w[0, at : at + step], x[...], preferred_element_type=f32)
+        gate_grad[into] = (hidden_grad * for_gate[into]).astype(bf16)
+        up_grad[into] = (hidden_grad * for_up[into]).astype(bf16)
+
+    own, other = slice(0, units), slice(units, 2 * units)
+    for part in column_chunks(width):
+        total = jnp.zeros((chunk, rows), f32)
+        for matrix, grad in ((g0, gate_grad[own]), (u0, up_grad[own]), (g1, gate_grad[other]), (u1, up_grad[other])):
+            next(copies).wait()
+            total = total + jnp.dot(matrix[0, part], grad, preferred_element_type=f32)
+        store_packed(total.T, (o0, o1, o2, o3), part)
+
+
+def after(value, *others):
+    return lax.optimization_barrier((value, *others))[0]
 
 
 def on_device(tokens, expert_ids, gate_values, cotangent, gate_weight, up_weight, down_weight):
@@ -250,16 +276,13 @@
     shape = jax.ShapeDtypeStruct
     packed_shapes = [shape((taken, width), bf16)] * len(PLANE)
 
-    own = (gate_weight, up_weight, down_weight)
-    other = tuple(swap(slab, CORE) for slab in own)
-
     (coded,) = call(
         functools.partial(code_kernel, experts),
         [shape((tok_dev, width + padded(PIECES * experts)), bf16)],
-        (tokens, expert_ids, gate_values),
-    )
-    held = [coded] + [swap(coded, offset) for offset in far]
-    cots = [cotangent] + [swap(cotangent, offset) for offset in far]
+        (tokens, expert_ids.T, gate_values.T),
+    )
+    held = gather_far(coded)
+    gate_other, up_other = swap(gate_weight, CORE), swap(up_weight, CORE)
 
     whole = pl.BlockSpec(memory_space=pltpu.VMEM)
     *packed, by_row, by_slot = call(
@@ -271,6 +294,11 @@
     )
     x = [packed[0]] + [swap(value, offset) for value, offset in zip(packed[1:], PLANE[1:])]
 
+    down_other = swap(after(down_weight, gate_other, up_other, packed[0]), CORE)
+    own = (gate_weight, up_weight, down_weight)
+    other = (gate_other, up_other, down_other)
+    cots = gather_far(after(cotangent, held[len(held) // 2]))
+
     packed = call(
         functools.partial(pack_cots_kernel, capacity),
         packed_shapes,
@@ -280,21 +308,24 @@
     grads = [packed[0]] + [swap(value, offset) for value, offset in zip(packed[1:], PLANE[1:])]
 
     all_taken = len(PLANE) * taken
-    tile = 256
-    weight_specs, steps = expert_specs(width, hidden, tile)
-    kept_spec = pl.BlockSpec((all_taken, tile), lambda i: (0, i))
-    kept_shapes = [shape((all_taken, 2 * hidden), f32)] * 2
-    scratch = [pltpu.VMEM((all_taken, width), bf16), pltpu.VMEM((all_taken, width), f32)]
+    in_place = pl.BlockSpec(memory_space=pl.ANY)
+    tile = 256 if hidden % 256 == 0 else LANES
+    tiles, chunks = 2 * hidden // tile, width // chunk_of(width)
+    slab_room = [pltpu.VMEM(slab.shape, bf16) for slab in (*own, *other)]
     flops = 2 * 3 * all_taken * width * 2 * hidden
     *outs, for_up, for_gate = call(
-        functools.partial(forward_kernel, steps),
-        packed_shapes + kept_shapes,
+        functools.partial(forward_kernel, tile),
+        packed_shapes + [shape((2 * hidden, all_taken), f32)] * 2,
         (*x, *own, *other),
         flops=flops,
-        grid=(2 * steps,),
-        in_specs=[whole] * 4 + weight_specs,
-        out_specs=[whole] * 4 + [kept_spec] * 2,
-        scratch=scratch,
+        in_specs=[whole] * 4 + [in_place] * 6,
+        limit=VMEM_LIMIT_EXPERT,
+        scratch=[
+            pltpu.VMEM((all_taken, width), bf16),
+            pltpu.VMEM((all_taken, 2 * hidden), bf16),
+            *slab_room,
+            pltpu.SemaphoreType.DMA((2 * tiles + 2 * chunks,)),
+        ],
     )
 
     def go_home(values, weighted):
@@ -311,13 +342,18 @@
 
     layer_out = go_home(outs, True)
     backs = call(
-        functools.partial(backward_kernel, steps),
+        functools.partial(backward_kernel, tile),
         packed_shapes,
         (*grads, for_up, for_gate, *own, *other),
         flops=flops,
-        grid=(2 * steps,),
-        in_specs=[whole] * 4 + [kept_spec] * 2 + weight_specs,
-        scratch=scratch,
+        in_specs=[whole] * 6 + [in_place] * 6,
+        limit=VMEM_LIMIT_EXPERT,
+        scratch=[
+            pltpu.VMEM((width, all_taken), bf16),
+            *[pltpu.VMEM((2 * hidden, all_taken), bf16)] * 2,
+            *slab_room,
+            pltpu.SemaphoreType.DMA((tiles + 4 * chunks,)),
+        ],
     )
     token_grad = go_home(backs, False)
     return layer_out, token_grad

time: 107 us -> 103 us (0.963)
  waiting for transfers between devices: 31.3 us -> 25.8 us
  local copies, waits for them, and re-layouts: 3.31 us -> 5.09 us
  starting transfers between devices: 40.8 us -> 39.3 us
  Pallas kernels: 30.7 us -> 31.8 us
    ppermute x27, waiting for transfers between devices: 31.3 us -> 25.8 us  [swap(): lax.ppermute(value, 'expert', [(i, i ^ offset) for i in range(devices)])]
    unnamed x6 -> x10, local copies, waits for them, and re-layouts: 3.31 us -> 5.09 us
    ppermute x27, starting transfers between devices: 40.8 us -> 39.3 us  [swap(): lax.ppermute(value, 'expert', [(i, i ^ offset) for i in range(devices)])]
    pallas_call x9, Pallas kernels: 30.7 us -> 31.8 us  [call(): pl.pallas_call(body, out_shape=outs, in_specs=[whole] * len(args) if in_s...]
  transfers between devices with their start and end apart: 27 -> 27, of which waited for: 10 -> 7; matrix products, arithmetic and copies ran while one was open for 1% -> 0% of each run, Pallas kernels for 28% -> 30%
where the time goes in v4:
time: 103 us
  starting transfers between devices  39.3 us (38%)
  Pallas kernels  31.8 us (31%)
  waiting for transfers between devices  25.8 us (25%)
  local copies, waits for them, and re-layouts  5.09 us (5%)
    ppermute x27, starting transfers between devices, swap(): lax.ppermute(value, 'expert', [(i, i ^ offset) for i in range(devices)])  39.3 us
    pallas_call x9, Pallas kernels, call(): pl.pallas_call(body, out_shape=outs, in_specs=[whole] * len(args) if in_s...  31.8 us
    ppermute x27, waiting for transfers between devices, swap(): lax.ppermute(value, 'expert', [(i, i ^ offset) for i in range(devices)])  25.8 us
    unnamed x10, local copies, waits for them, and re-layouts  5.09 us
  transfers between devices with their start and end apart: 27, of which 7 were waited for; matrix products, arithmetic and copies ran while one was open for 0% of the time, Pallas kernels for 30%

profile of v4, /device:TPU:0, one launch (start us, length us, event | category | flops | bytes accessed | tf_op | source)
XLA Modules:
  0.0 102.7 jit_solution(6438741420276829675)
XLA Ops:
  0.6 0.5 collective-permute-start.6
  1.1 0.1 collective-permute-start.7
  1.2 0.9 copy-done.1
  2.1 0.7 copy-done.2
  2.8 0.7 copy-done.3
  3.5 0.2 shard_map.86.refs_0_
  3.7 4.1 %collective-permute-start.1 = (bf16[16,3712]{1,0:T(8,128)(2,1)S(1)}, bf16[16,3712]{1,0:T(8,128)(2,1)S(1)}, u32[]{:S(2)}, u32[]{:S(2)}) collective-permute-start(bf16[16,3712]{1,0:T(8,128)(2,1)S(1)} %shard_map.86.refs_0_), channel_id=1, source_target_pairs={{0,16},{1,17},{2,18},{3,19},{4,20},{5,21},{6,22},{7,23},{8,24},{9,... | collective-permute-start | bytes 356360 | tf_op jit(solution)/shard_map/ppermute | solution.py:22
  7.7 1.6 %collective-permute-start = (bf16[16,3712]{1,0:T(8,128)(2,1)S(1)}, bf16[16,3712]{1,0:T(8,128)(2,1)S(1)}, u32[]{:S(2)}, u32[]{:S(2)}) collective-permute-start(bf16[16,3712]{1,0:T(8,128)(2,1)S(1)} %shard_map.86.refs_0_), channel_id=1, source_target_pairs={{0,8},{1,9},{2,10},{3,11},{4,12},{5,13},{6,14},{7,15},{8,0},{9,1},... | collective-permute-start | bytes 356360 | tf_op jit(solution)/shard_map/ppermute | solution.py:22
  9.3 4.6 %collective-permute-done.1.refs_2_ = bf16[16,3712]{1,0:T(8,128)(2,1)S(1)} collective-permute-done((bf16[16,3712]{1,0:T(8,128)(2,1)S(1)}, bf16[16,3712]{1,0:T(8,128)(2,1)S(1)}, u32[]{:S(2)}, u32[]{:S(2)}) %collective-permute-start.1) | collective-permute-done | bytes 118816 | tf_op jit(solution)/shard_map/ppermute | solution.py:22
  13.9 0.6 collective-permute-start.2
  14.5 4.2 %collective-permute-done.2.refs_3_ = bf16[16,3712]{1,0:T(8,128)(2,1)S(1)} collective-permute-done((bf16[16,3712]{1,0:T(8,128)(2,1)S(1)}, bf16[16,3712]{1,0:T(8,128)(2,1)S(1)}, u32[]{:S(2)}, u32[]{:S(2)}) %collective-permute-start.2) | collective-permute-done | bytes 118816 | tf_op jit(solution)/shard_map/ppermute | solution.py:22
  18.7 1.0 %shard_map.87 = (bf16[40,3584]{1,0:T(8,128)(2,1)S(1)}, bf16[40,3584]{1,0:T(8,128)(2,1)S(1)}, bf16[40,3584]{1,0:T(8,128)(2,1)S(1)}, bf16[40,3584]{1,0:T(8,128)(2,...) custom-call(s32[1]{0:T(128)} %bitcast.chip, bf16[16,3712]{1,0:T(8,128)(2,1)S(1)} %shard_map.86.refs_0_, ...), custom_call_target="tpu_custom_call" | custom-call | flops 117440512 | bytes 1753092 | tf_op jit(solution)/shard_map/pallas_call | solution.py:49
  19.8 0.1 collective-permute-start.8
  19.8 1.0 collective-permute-start.15
  20.9 1.5 %collective-permute-start.3 = (bf16[40,3584]{1,0:T(8,128)(2,1)S(1)}, bf16[40,3584]{1,0:T(8,128)(2,1)S(1)}, u32[]{:S(2)}, u32[]{:S(2)}) collective-permute-start(bf16[40,3584]{1,0:T(8,128)(2,1)S(1)} %get-tuple-element.34), channel_id=1, source_target_pairs={{0,2},{1,3},{2,0},{3,1},{4,6},{5,7},{6,4},{7,5},{8,10},{9,11},{10,... | collective-permute-start | bytes 860168 | tf_op jit(solution)/shard_map/ppermute | solution.py:22
  22.3 1.5 %collective-permute-start.4 = (bf16[40,3584]{1,0:T(8,128)(2,1)S(1)}, bf16[40,3584]{1,0:T(8,128)(2,1)S(1)}, u32[]{:S(2)}, u32[]{:S(2)}) collective-permute-start(bf16[40,3584]{1,0:T(8,128)(2,1)S(1)} %get-tuple-element.35), channel_id=1, source_target_pairs={{0,4},{1,5},{2,6},{3,7},{4,0},{5,1},{6,2},{7,3},{8,12},{9,13},{10,... | collective-permute-start | bytes 860168 | tf_op jit(solution)/shard_map/ppermute | solution.py:22
  23.9 0.5 collective-permute-start.5
  24.3 1.3 %collective-permute-done.15.refs_1_ = bf16[16,3584]{1,0:T(8,128)(2,1)S(1)} collective-permute-done((bf16[16,3584]{1,0:T(8,128)(2,1)}, bf16[16,3584]{1,0:T(8,128)(2,1)S(1)}, u32[]{:S(2)}, u32[]{:S(2)}) %collective-permute-start.15) | collective-permute-done | bytes 114720 | tf_op jit(solution)/shard_map/ppermute | solution.py:22
  25.6 2.6 %collective-permute-start.16 = (bf16[16,3584]{1,0:T(8,128)(2,1)}, bf16[16,3584]{1,0:T(8,128)(2,1)S(1)}, u32[]{:S(2)}, u32[]{:S(2)}) collective-permute-start(bf16[16,3584]{1,0:T(8,128)(2,1)} %refs_0_.3), channel_id=1, source_target_pairs={{0,16},{1,17},{2,18},{3,19},{4,20},{5,21},{6,22},{7,23},{8,24},{9,... | collective-permute-start | bytes 344072 | tf_op jit(solution)/shard_map/ppermute | solution.py:22
  28.2 5.7 %collective-permute-done.16.refs_2_ = bf16[16,3584]{1,0:T(8,128)(2,1)S(1)} collective-permute-done((bf16[16,3584]{1,0:T(8,128)(2,1)}, bf16[16,3584]{1,0:T(8,128)(2,1)S(1)}, u32[]{:S(2)}, u32[]{:S(2)}) %collective-permute-start.16) | collective-permute-done | bytes 114720 | tf_op jit(solution)/shard_map/ppermute | solution.py:22
  33.9 0.8 collective-permute-start.17
  34.7 4.0 %collective-permute-done.17.refs_3_ = bf16[16,3584]{1,0:T(8,128)(2,1)S(1)} collective-permute-done((bf16[16,3584]{1,0:T(8,128)(2,1)S(1)}, bf16[16,3584]{1,0:T(8,128)(2,1)S(1)}, u32[]{:S(2)}, u32[]{:S(2)}) %collective-permute-start.17) | collective-permute-done | bytes 114720 | tf_op jit(solution)/shard_map/ppermute | solution.py:22
  38.7 0.9 copy-done
  39.6 0.6 shard_map.91
  40.2 1.6 %collective-permute-start.18 = (bf16[40,3584]{1,0:T(8,128)(2,1)S(1)}, bf16[40,3584]{1,0:T(8,128)(2,1)S(1)}, u32[]{:S(2)}, u32[]{:S(2)}) collective-permute-start(bf16[40,3584]{1,0:T(8,128)(2,1)S(1)} %get-tuple-element.49), channel_id=1, source_target_pairs={{0,2},{1,3},{2,0},{3,1},{4,6},{5,7},{6,4},{7,5},{8,10},{9,11},{10,... | collective-permute-start | bytes 860168 | tf_op jit(solution)/shard_map/ppermute | solution.py:22
  41.8 1.5 %collective-permute-start.19 = (bf16[40,3584]{1,0:T(8,128)(2,1)S(1)}, bf16[40,3584]{1,0:T(8,128)(2,1)S(1)}, u32[]{:S(2)}, u32[]{:S(2)}) collective-permute-start(bf16[40,3584]{1,0:T(8,128)(2,1)S(1)} %get-tuple-element.50), channel_id=1, source_target_pairs={{0,4},{1,5},{2,6},{3,7},{4,0},{5,1},{6,2},{7,3},{8,12},{9,13},{10,... | collective-permute-start | bytes 860168 | tf_op jit(solution)/shard_map/ppermute | solution.py:22
  43.3 0.4 collective-permute-start.20
  43.8 1.9 %copy-done.4 = bf16[1,512,3584]{2,1,0:T(8,128)(2,1)} copy-done((bf16[1,512,3584]{2,1,0:T(8,128)(2,1)}, bf16[1,512,3584]{2,1,0:T(8,128)(2,1)S(1)}, u32[]{:S(2)}) %copy-start.4) | copy-done | bytes 3670040
  45.7 10.6 %shard_map.88 = (bf16[40,3584]{1,0:T(8,128)(2,1)S(1)}, bf16[40,3584]{1,0:T(8,128)(2,1)S(1)}, bf16[40,3584]{1,0:T(8,128)(2,1)S(1)}, bf16[40,3584]{1,0:T(8,128)(2,...) custom-call(bf16[40,3584]{1,0:T(8,128)(2,1)S(1)} %get-tuple-element.33.x0, ...), custom_call_target="tpu_custom_call" | custom-call | flops 3523215360 | bytes 25624576 | tf_op jit(solution)/shard_map/pallas_call | solution.py:49
  56.3 1.6 %collective-permute-start.9 = (bf16[40,3584]{1,0:T(8,128)(2,1)S(1)}, bf16[40,3584]{1,0:T(8,128)(2,1)S(1)}, u32[]{:S(2)}, u32[]{:S(2)}) collective-permute-start(bf16[40,3584]{1,0:T(8,128)(2,1)S(1)} %get-tuple-element.39), channel_id=1, source_target_pairs={{0,2},{1,3},{2,0},{3,1},{4,6},{5,7},{6,4},{7,5},{8,10},{9,11},{10,... | collective-permute-start | bytes 860168 | tf_op jit(solution)/shard_map/ppermute | solution.py:22
  57.9 1.5 %collective-permute-start.10 = (bf16[40,3584]{1,0:T(8,128)(2,1)S(1)}, bf16[40,3584]{1,0:T(8,128)(2,1)S(1)}, u32[]{:S(2)}, u32[]{:S(2)}) collective-permute-start(bf16[40,3584]{1,0:T(8,128)(2,1)S(1)} %get-tuple-element.40), channel_id=1, source_target_pairs={{0,4},{1,5},{2,6},{3,7},{4,0},{5,1},{6,2},{7,3},{8,12},{9,13},{10,... | collective-permute-start | bytes 860168 | tf_op jit(solution)/shard_map/ppermute | solution.py:22
  59.5 0.4 collective-permute-start.11
  59.9 17.0 %shard_map.92 = (bf16[40,3584]{1,0:T(8,128)(2,1)S(1)}, bf16[40,3584]{1,0:T(8,128)(2,1)S(1)}, bf16[40,3584]{1,0:T(8,128)(2,1)S(1)}, bf16[40,3584]{1,0:T(8,128)(2,1)S(1)}) custom-call(bf16[40,3584]{1,0:T(8,128)(2,1)S(1)} %get-tuple-element.48.x0, bf16[40,3584]{1,0:T(8,128)(2,1)S(1)} %collective-permute-done.18.x1, ...), custom_call_target="tpu_custom_call" | custom-call | flops 3523215360 | bytes 25624576 | tf_op jit(solution)/shard_map/pallas_call | solution.py:49
  76.9 1.6 %collective-permute-start.21 = (bf16[40,3584]{1,0:T(8,128)(2,1)S(1)}, bf16[40,3584]{1,0:T(8,128)(2,1)S(1)}, u32[]{:S(2)}, u32[]{:S(2)}) collective-permute-start(bf16[40,3584]{1,0:T(8,128)(2,1)S(1)} %get-tuple-element.55), channel_id=1, source_target_pairs={{0,2},{1,3},{2,0},{3,1},{4,6},{5,7},{6,4},{7,5},{8,10},{9,11},{10,... | collective-permute-start | bytes 860168 | tf_op jit(solution)/shard_map/ppermute | solution.py:22
  78.5 1.5 %collective-permute-start.22 = (bf16[40,3584]{1,0:T(8,128)(2,1)S(1)}, bf16[40,3584]{1,0:T(8,128)(2,1)S(1)}, u32[]{:S(2)}, u32[]{:S(2)}) collective-permute-start(bf16[40,3584]{1,0:T(8,128)(2,1)S(1)} %get-tuple-element.56), channel_id=1, source_target_pairs={{0,4},{1,5},{2,6},{3,7},{4,0},{5,1},{6,2},{7,3},{8,12},{9,13},{10,... | collective-permute-start | bytes 860168 | tf_op jit(solution)/shard_map/ppermute | solution.py:22
  80.0 0.4 collective-permute-start.23
  80.5 0.6 shard_map.89
  81.1 1.1 %collective-permute-start.12 = (bf16[16,3584]{1,0:T(8,128)(2,1)S(1)}, bf16[16,3584]{1,0:T(8,128)(2,1)S(1)}, u32[]{:S(2)}, u32[]{:S(2)}) collective-permute-start(bf16[16,3584]{1,0:T(8,128)(2,1)S(1)} %get-tuple-element.43), channel_id=1, source_target_pairs={{0,8},{1,9},{2,10},{3,11},{4,12},{5,13},{6,14},{7,15},{8,0},{9,1},... | collective-permute-start | bytes 344072 | tf_op jit(solution)/shard_map/ppermute | solution.py:22
  82.2 3.3 %collective-permute-start.13 = (bf16[16,3584]{1,0:T(8,128)(2,1)S(1)}, bf16[16,3584]{1,0:T(8,128)(2,1)S(1)}, u32[]{:S(2)}, u32[]{:S(2)}) collective-permute-start(bf16[16,3584]{1,0:T(8,128)(2,1)S(1)} %get-tuple-element.44), channel_id=1, source_target_pairs={{0,16},{1,17},{2,18},{3,19},{4,20},{5,21},{6,22},{7,23},{8,24},{9,... | collective-permute-start | bytes 344072 | tf_op jit(solution)/shard_map/ppermute | solution.py:22
  85.5 4.5 %collective-permute-start.14 = (bf16[16,3584]{1,0:T(8,128)(2,1)S(1)}, bf16[16,3584]{1,0:T(8,128)(2,1)S(1)}, u32[]{:S(2)}, u32[]{:S(2)}) collective-permute-start(bf16[16,3584]{1,0:T(8,128)(2,1)S(1)} %get-tuple-element.45), channel_id=1, source_target_pairs={{0,24},{1,25},{2,26},{3,27},{4,28},{5,29},{6,30},{7,31},{8,16},{9,... | collective-permute-start | bytes 344072 | tf_op jit(solution)/shard_map/ppermute | solution.py:22
  90.0 0.3 shard_map.93
  90.4 1.6 %collective-permute-start.24 = (bf16[16,3584]{1,0:T(8,128)(2,1)S(1)}, bf16[16,3584]{1,0:T(8,128)(2,1)S(1)}, u32[]{:S(2)}, u32[]{:S(2)}) collective-permute-start(bf16[16,3584]{1,0:T(8,128)(2,1)S(1)} %get-tuple-element.59), channel_id=1, source_target_pairs={{0,8},{1,9},{2,10},{3,11},{4,12},{5,13},{6,14},{7,15},{8,0},{9,1},... | collective-permute-start | bytes 344072 | tf_op jit(solution)/shard_map/ppermute | solution.py:22
  92.0 3.3 %collective-permute-start.25 = (bf16[16,3584]{1,0:T(8,128)(2,1)S(1)}, bf16[16,3584]{1,0:T(8,128)(2,1)S(1)}, u32[]{:S(2)}, u32[]{:S(2)}) collective-permute-start(bf16[16,3584]{1,0:T(8,128)(2,1)S(1)} %get-tuple-element.60), channel_id=1, source_target_pairs={{0,16},{1,17},{2,18},{3,19},{4,20},{5,21},{6,22},{7,23},{8,24},{9,... | collective-permute-start | bytes 344072 | tf_op jit(solution)/shard_map/ppermute | solution.py:22
  95.3 0.0 collective-permute-start.26
  95.3 0.7 shard_map.90
  96.0 4.5 %collective-permute-done.25.refs_2_ = bf16[16,3584]{1,0:T(8,128)(2,1)S(1)} collective-permute-done((bf16[16,3584]{1,0:T(8,128)(2,1)S(1)}, bf16[16,3584]{1,0:T(8,128)(2,1)S(1)}, u32[]{:S(2)}, u32[]{:S(2)}) %collective-permute-start.25) | collective-permute-done | bytes 114720 | tf_op jit(solution)/shard_map/ppermute | solution.py:22
  100.6 1.4 %collective-permute-done.26.refs_3_ = bf16[16,3584]{1,0:T(8,128)(2,1)S(1)} collective-permute-done((bf16[16,3584]{1,0:T(8,128)(2,1)S(1)}, bf16[16,3584]{1,0:T(8,128)(2,1)S(1)}, u32[]{:S(2)}, u32[]{:S(2)}) %collective-permute-start.26) | collective-permute-done | bytes 114720 | tf_op jit(solution)/shard_map/ppermute | solution.py:22
  102.0 0.7 shard_map.94
  (25 shorter events, 0.1 us)
Async XLA Ops:
  0.6 19.1 %collective-permute-start.6 = (bf16[1,3584,512]{2,1,0:T(8,128)(2,1)}, bf16[1,3584,512]{2,1,0:T(8,128)(2,1)}, u32[]{:S(2)}, u32[]{:S(2)}) collective-permute-start(bf16[1,3584,512]{2,1,0:T(8,128)(2,1)} %refs_0_.4), channel_id=1, source_target_pairs={{0,1},{1,0},{2,3},{3,2},{4,5},{5,4},{6,7},{7,6},{8,9},{9,8},{10,11... | collective-permute-start | bytes 11010056 | tf_op jit(solution)/shard_map/ppermute | solution.py:22
  1.1 18.6 %collective-permute-start.7 = (bf16[1,3584,512]{2,1,0:T(8,128)(2,1)}, bf16[1,3584,512]{2,1,0:T(8,128)(2,1)}, u32[]{:S(2)}, u32[]{:S(2)}) collective-permute-start(bf16[1,3584,512]{2,1,0:T(8,128)(2,1)} %refs_1_.3), channel_id=1, source_target_pairs={{0,1},{1,0},{2,3},{3,2},{4,5},{5,4},{6,7},{7,6},{8,9},{9,8},{10,11... | collective-permute-start | bytes 11010056 | tf_op jit(solution)/shard_map/ppermute | solution.py:22
  1.2 0.9 copy-start.1
  2.1 0.7 copy-start.2
  2.8 0.7 copy-start.3
  3.7 10.2 %collective-permute-start.1 = (bf16[16,3712]{1,0:T(8,128)(2,1)S(1)}, bf16[16,3712]{1,0:T(8,128)(2,1)S(1)}, u32[]{:S(2)}, u32[]{:S(2)}) collective-permute-start(bf16[16,3712]{1,0:T(8,128)(2,1)S(1)} %shard_map.86.refs_0_), channel_id=1, source_target_pairs={{0,16},{1,17},{2,18},{3,19},{4,20},{5,21},{6,22},{7,23},{8,24},{9,... | collective-permute-start | bytes 356360 | tf_op jit(solution)/shard_map/ppermute | solution.py:22
  7.7 6.8 %collective-permute-start = (bf16[16,3712]{1,0:T(8,128)(2,1)S(1)}, bf16[16,3712]{1,0:T(8,128)(2,1)S(1)}, u32[]{:S(2)}, u32[]{:S(2)}) collective-permute-start(bf16[16,3712]{1,0:T(8,128)(2,1)S(1)} %shard_map.86.refs_0_), channel_id=1, source_target_pairs={{0,8},{1,9},{2,10},{3,11},{4,12},{5,13},{6,14},{7,15},{8,0},{9,1},... | collective-permute-start | bytes 356360 | tf_op jit(solution)/shard_map/ppermute | solution.py:22
  13.9 4.8 %collective-permute-start.2 = (bf16[16,3712]{1,0:T(8,128)(2,1)S(1)}, bf16[16,3712]{1,0:T(8,128)(2,1)S(1)}, u32[]{:S(2)}, u32[]{:S(2)}) collective-permute-start(bf16[16,3712]{1,0:T(8,128)(2,1)S(1)} %collective-permute-done.1.refs_2_), channel_id=1, source_target_pairs={{0,8},{1,9},{2,10},{3,11},{4,12},{5,13},{6,14},{7,15},{8,0},{9,1},... | collective-permute-start | bytes 356360 | tf_op jit(solution)/shard_map/ppermute | solution.py:22
  19.8 24.0 %collective-permute-start.8 = (bf16[1,512,3584]{2,1,0:T(8,128)(2,1)}, bf16[1,512,3584]{2,1,0:T(8,128)(2,1)S(1)}, u32[]{:S(2)}, u32[]{:S(2)}) collective-permute-start(bf16[1,512,3584]{2,1,0:T(8,128)(2,1)} %refs_2_.3), channel_id=1, source_target_pairs={{0,1},{1,0},{2,3},{3,2},{4,5},{5,4},{6,7},{7,6},{8,9},{9,8},{10,11... | collective-permute-start | bytes 11010056 | tf_op jit(solution)/shard_map/ppermute | solution.py:22
  19.8 5.8 %collective-permute-start.15 = (bf16[16,3584]{1,0:T(8,128)(2,1)}, bf16[16,3584]{1,0:T(8,128)(2,1)S(1)}, u32[]{:S(2)}, u32[]{:S(2)}) collective-permute-start(bf16[16,3584]{1,0:T(8,128)(2,1)} %refs_0_.3), channel_id=1, source_target_pairs={{0,8},{1,9},{2,10},{3,11},{4,12},{5,13},{6,14},{7,15},{8,0},{9,1},... | collective-permute-start | bytes 344072 | tf_op jit(solution)/shard_map/ppermute | solution.py:22
  20.9 20.9 %collective-permute-start.3 = (bf16[40,3584]{1,0:T(8,128)(2,1)S(1)}, bf16[40,3584]{1,0:T(8,128)(2,1)S(1)}, u32[]{:S(2)}, u32[]{:S(2)}) collective-permute-start(bf16[40,3584]{1,0:T(8,128)(2,1)S(1)} %get-tuple-element.34), channel_id=1, source_target_pairs={{0,2},{1,3},{2,0},{3,1},{4,6},{5,7},{6,4},{7,5},{8,10},{9,11},{10,... | collective-permute-start | bytes 860168 | tf_op jit(solution)/shard_map/ppermute | solution.py:22
  22.3 21.0 %collective-permute-start.4 = (bf16[40,3584]{1,0:T(8,128)(2,1)S(1)}, bf16[40,3584]{1,0:T(8,128)(2,1)S(1)}, u32[]{:S(2)}, u32[]{:S(2)}) collective-permute-start(bf16[40,3584]{1,0:T(8,128)(2,1)S(1)} %get-tuple-element.35), channel_id=1, source_target_pairs={{0,4},{1,5},{2,6},{3,7},{4,0},{5,1},{6,2},{7,3},{8,12},{9,13},{10,... | collective-permute-start | bytes 860168 | tf_op jit(solution)/shard_map/ppermute | solution.py:22
  23.9 19.9 %collective-permute-start.5 = (bf16[40,3584]{1,0:T(8,128)(2,1)S(1)}, bf16[40,3584]{1,0:T(8,128)(2,1)S(1)}, u32[]{:S(2)}, u32[]{:S(2)}) collective-permute-start(bf16[40,3584]{1,0:T(8,128)(2,1)S(1)} %get-tuple-element.36), channel_id=1, source_target_pairs={{0,6},{1,7},{2,4},{3,5},{4,2},{5,3},{6,0},{7,1},{8,14},{9,15},{10,... | collective-permute-start | bytes 860168 | tf_op jit(solution)/shard_map/ppermute | solution.py:22
  25.6 8.3 %collective-permute-start.16 = (bf16[16,3584]{1,0:T(8,128)(2,1)}, bf16[16,3584]{1,0:T(8,128)(2,1)S(1)}, u32[]{:S(2)}, u32[]{:S(2)}) collective-permute-start(bf16[16,3584]{1,0:T(8,128)(2,1)} %refs_0_.3), channel_id=1, source_target_pairs={{0,16},{1,17},{2,18},{3,19},{4,20},{5,21},{6,22},{7,23},{8,24},{9,... | collective-permute-start | bytes 344072 | tf_op jit(solution)/shard_map/ppermute | solution.py:22
  33.9 4.8 %collective-permute-start.17 = (bf16[16,3584]{1,0:T(8,128)(2,1)S(1)}, bf16[16,3584]{1,0:T(8,128)(2,1)S(1)}, u32[]{:S(2)}, u32[]{:S(2)}) collective-permute-start(bf16[16,3584]{1,0:T(8,128)(2,1)S(1)} %collective-permute-done.16.refs_2_), channel_id=1, source_target_pairs={{0,8},{1,9},{2,10},{3,11},{4,12},{5,13},{6,14},{7,15},{8,0},{9,1},... | collective-permute-start | bytes 344072 | tf_op jit(solution)/shard_map/ppermute | solution.py:22
  38.7 0.9 copy-start
  40.2 19.3 %collective-permute-start.18 = (bf16[40,3584]{1,0:T(8,128)(2,1)S(1)}, bf16[40,3584]{1,0:T(8,128)(2,1)S(1)}, u32[]{:S(2)}, u32[]{:S(2)}) collective-permute-start(bf16[40,3584]{1,0:T(8,128)(2,1)S(1)} %get-tuple-element.49), channel_id=1, source_target_pairs={{0,2},{1,3},{2,0},{3,1},{4,6},{5,7},{6,4},{7,5},{8,10},{9,11},{10,... | collective-permute-start | bytes 860168 | tf_op jit(solution)/shard_map/ppermute | solution.py:22
  41.8 18.1 %collective-permute-start.19 = (bf16[40,3584]{1,0:T(8,128)(2,1)S(1)}, bf16[40,3584]{1,0:T(8,128)(2,1)S(1)}, u32[]{:S(2)}, u32[]{:S(2)}) collective-permute-start(bf16[40,3584]{1,0:T(8,128)(2,1)S(1)} %get-tuple-element.50), channel_id=1, source_target_pairs={{0,4},{1,5},{2,6},{3,7},{4,0},{5,1},{6,2},{7,3},{8,12},{9,13},{10,... | collective-permute-start | bytes 860168 | tf_op jit(solution)/shard_map/ppermute | solution.py:22
  43.3 16.6 %collective-permute-start.20 = (bf16[40,3584]{1,0:T(8,128)(2,1)S(1)}, bf16[40,3584]{1,0:T(8,128)(2,1)S(1)}, u32[]{:S(2)}, u32[]{:S(2)}) collective-permute-start(bf16[40,3584]{1,0:T(8,128)(2,1)S(1)} %get-tuple-element.51), channel_id=1, source_target_pairs={{0,6},{1,7},{2,4},{3,5},{4,2},{5,3},{6,0},{7,1},{8,14},{9,15},{10,... | collective-permute-start | bytes 860168 | tf_op jit(solution)/shard_map/ppermute | solution.py:22
  43.8 1.9 %copy-start.4 = (bf16[1,512,3584]{2,1,0:T(8,128)(2,1)}, bf16[1,512,3584]{2,1,0:T(8,128)(2,1)S(1)}, u32[]{:S(2)}) copy-start(bf16[1,512,3584]{2,1,0:T(8,128)(2,1)S(1)} %collective-permute-done.8.refs_5_) | copy-start | bytes 11010052
  56.3 23.7 %collective-permute-start.9 = (bf16[40,3584]{1,0:T(8,128)(2,1)S(1)}, bf16[40,3584]{1,0:T(8,128)(2,1)S(1)}, u32[]{:S(2)}, u32[]{:S(2)}) collective-permute-start(bf16[40,3584]{1,0:T(8,128)(2,1)S(1)} %get-tuple-element.39), channel_id=1, source_target_pairs={{0,2},{1,3},{2,0},{3,1},{4,6},{5,7},{6,4},{7,5},{8,10},{9,11},{10,... | collective-permute-start | bytes 860168 | tf_op jit(solution)/shard_map/ppermute | solution.py:22
  57.9 22.5 %collective-permute-start.10 = (bf16[40,3584]{1,0:T(8,128)(2,1)S(1)}, bf16[40,3584]{1,0:T(8,128)(2,1)S(1)}, u32[]{:S(2)}, u32[]{:S(2)}) collective-permute-start(bf16[40,3584]{1,0:T(8,128)(2,1)S(1)} %get-tuple-element.40), channel_id=1, source_target_pairs={{0,4},{1,5},{2,6},{3,7},{4,0},{5,1},{6,2},{7,3},{8,12},{9,13},{10,... | collective-permute-start | bytes 860168 | tf_op jit(solution)/shard_map/ppermute | solution.py:22
  59.5 21.0 %collective-permute-start.11 = (bf16[40,3584]{1,0:T(8,128)(2,1)S(1)}, bf16[40,3584]{1,0:T(8,128)(2,1)S(1)}, u32[]{:S(2)}, u32[]{:S(2)}) collective-permute-start(bf16[40,3584]{1,0:T(8,128)(2,1)S(1)} %get-tuple-element.41), channel_id=1, source_target_pairs={{0,6},{1,7},{2,4},{3,5},{4,2},{5,3},{6,0},{7,1},{8,14},{9,15},{10,... | collective-permute-start | bytes 860168 | tf_op jit(solution)/shard_map/ppermute | solution.py:22
  76.9 8.6 %collective-permute-start.21 = (bf16[40,3584]{1,0:T(8,128)(2,1)S(1)}, bf16[40,3584]{1,0:T(8,128)(2,1)S(1)}, u32[]{:S(2)}, u32[]{:S(2)}) collective-permute-start(bf16[40,3584]{1,0:T(8,128)(2,1)S(1)} %get-tuple-element.55), channel_id=1, source_target_pairs={{0,2},{1,3},{2,0},{3,1},{4,6},{5,7},{6,4},{7,5},{8,10},{9,11},{10,... | collective-permute-start | bytes 860168 | tf_op jit(solution)/shard_map/ppermute | solution.py:22
  78.5 11.5 %collective-permute-start.22 = (bf16[40,3584]{1,0:T(8,128)(2,1)S(1)}, bf16[40,3584]{1,0:T(8,128)(2,1)S(1)}, u32[]{:S(2)}, u32[]{:S(2)}) collective-permute-start(bf16[40,3584]{1,0:T(8,128)(2,1)S(1)} %get-tuple-element.56), channel_id=1, source_target_pairs={{0,4},{1,5},{2,6},{3,7},{4,0},{5,1},{6,2},{7,3},{8,12},{9,13},{10,... | collective-permute-start | bytes 860168 | tf_op jit(solution)/shard_map/ppermute | solution.py:22
  80.0 10.0 %collective-permute-start.23 = (bf16[40,3584]{1,0:T(8,128)(2,1)S(1)}, bf16[40,3584]{1,0:T(8,128)(2,1)S(1)}, u32[]{:S(2)}, u32[]{:S(2)}) collective-permute-start(bf16[40,3584]{1,0:T(8,128)(2,1)S(1)} %get-tuple-element.57), channel_id=1, source_target_pairs={{0,6},{1,7},{2,4},{3,5},{4,2},{5,3},{6,0},{7,1},{8,14},{9,15},{10,... | collective-permute-start | bytes 860168 | tf_op jit(solution)/shard_map/ppermute | solution.py:22
  81.1 14.2 %collective-permute-start.12 = (bf16[16,3584]{1,0:T(8,128)(2,1)S(1)}, bf16[16,3584]{1,0:T(8,128)(2,1)S(1)}, u32[]{:S(2)}, u32[]{:S(2)}) collective-permute-start(bf16[16,3584]{1,0:T(8,128)(2,1)S(1)} %get-tuple-element.43), channel_id=1, source_target_pairs={{0,8},{1,9},{2,10},{3,11},{4,12},{5,13},{6,14},{7,15},{8,0},{9,1},... | collective-permute-start | bytes 344072 | tf_op jit(solution)/shard_map/ppermute | solution.py:22
  82.2 13.1 %collective-permute-start.13 = (bf16[16,3584]{1,0:T(8,128)(2,1)S(1)}, bf16[16,3584]{1,0:T(8,128)(2,1)S(1)}, u32[]{:S(2)}, u32[]{:S(2)}) collective-permute-start(bf16[16,3584]{1,0:T(8,128)(2,1)S(1)} %get-tuple-element.44), channel_id=1, source_target_pairs={{0,16},{1,17},{2,18},{3,19},{4,20},{5,21},{6,22},{7,23},{8,24},{9,... | collective-permute-start | bytes 344072 | tf_op jit(solution)/shard_map/ppermute | solution.py:22
  85.5 9.8 %collective-permute-start.14 = (bf16[16,3584]{1,0:T(8,128)(2,1)S(1)}, bf16[16,3584]{1,0:T(8,128)(2,1)S(1)}, u32[]{:S(2)}, u32[]{:S(2)}) collective-permute-start(bf16[16,3584]{1,0:T(8,128)(2,1)S(1)} %get-tuple-element.45), channel_id=1, source_target_pairs={{0,24},{1,25},{2,26},{3,27},{4,28},{5,29},{6,30},{7,31},{8,16},{9,... | collective-permute-start | bytes 344072 | tf_op jit(solution)/shard_map/ppermute | solution.py:22
  90.4 5.7 %collective-permute-start.24 = (bf16[16,3584]{1,0:T(8,128)(2,1)S(1)}, bf16[16,3584]{1,0:T(8,128)(2,1)S(1)}, u32[]{:S(2)}, u32[]{:S(2)}) collective-permute-start(bf16[16,3584]{1,0:T(8,128)(2,1)S(1)} %get-tuple-element.59), channel_id=1, source_target_pairs={{0,8},{1,9},{2,10},{3,11},{4,12},{5,13},{6,14},{7,15},{8,0},{9,1},... | collective-permute-start | bytes 344072 | tf_op jit(solution)/shard_map/ppermute | solution.py:22
  92.0 8.6 %collective-permute-start.25 = (bf16[16,3584]{1,0:T(8,128)(2,1)S(1)}, bf16[16,3584]{1,0:T(8,128)(2,1)S(1)}, u32[]{:S(2)}, u32[]{:S(2)}) collective-permute-start(bf16[16,3584]{1,0:T(8,128)(2,1)S(1)} %get-tuple-element.60), channel_id=1, source_target_pairs={{0,16},{1,17},{2,18},{3,19},{4,20},{5,21},{6,22},{7,23},{8,24},{9,... | collective-permute-start | bytes 344072 | tf_op jit(solution)/shard_map/ppermute | solution.py:22
  95.3 6.7 %collective-permute-start.26 = (bf16[16,3584]{1,0:T(8,128)(2,1)S(1)}, bf16[16,3584]{1,0:T(8,128)(2,1)S(1)}, u32[]{:S(2)}, u32[]{:S(2)}) collective-permute-start(bf16[16,3584]{1,0:T(8,128)(2,1)S(1)} %get-tuple-element.61), channel_id=1, source_target_pairs={{0,24},{1,25},{2,26},{3,27},{4,28},{5,29},{6,30},{7,31},{8,16},{9,... | collective-permute-start | bytes 344072 | tf_op jit(solution)/shard_map/ppermute | solution.py:22

commit v5 on v4

--- a/solution.py
+++ b/solution.py
@@ -22,12 +22,13 @@
     return lax.ppermute(value, "expert", [(i, i ^ offset) for i in range(devices)])
 
 
-def gather_far(block):
-    held, offset = {0: block}, lax.axis_size("expert") // 2
-    while offset >= FAR:
-        held.update({at ^ offset: swap(value, offset) for at, value in held.items()})
-        offset //= 2
-    return [held[at] for at in sorted(held)]
+def after(value, *others):
+    return lax.optimization_barrier((value, *others))[0]
+
+
+def double(held, offset, wait):
+    ready = {at: after(value, wait) for at, value in held.items()}
+    return held | {at ^ offset: swap(value, offset) for at, value in ready.items()}
 
 
 def padded(count):
@@ -177,43 +178,41 @@
 
 
 def forward_kernel(tile, x0, x1, x2, x3, *refs):
-    *slabs, o0, o1, o2, o3, for_up, for_gate, x, hidden, g0, u0, d0, g1, u1, d1, sems = refs
-    places = (g0, u0, d0, g1, u1, d1)
+    *slabs, o0, o1, o2, o3, for_up, for_gate, x, hidden, into, back, sems = refs
     rows, width = x.shape
-    units = g0.shape[2]
-    step, chunk = min(tile, units), chunk_of(width)
-    pairs, tiles = [], []
-    for slab in (0, 3):
-        for at in range(0, units, step):
-            tiles.append((slab, at))
-            for matrix in (slab, slab + 1):
-                pairs.append([ref.at[0, :, pl.ds(at, step)] for ref in (slabs[matrix], places[matrix])])
+    units = back.shape[0] // 2
+    chunk, tiles = chunk_of(width), 2 * units // tile
+    pairs = []
+    for number in range(tiles):
+        slab, at = divmod(number * tile, units)
+        for half, source in enumerate(slabs[3 * slab : 3 * slab + 2]):
+            place = into.at[:, pl.ds((2 * number + half) * tile, tile)]
+            pairs.append((source.at[0, :, pl.ds(at, tile)], place))
     for at in range(0, width, chunk):
-        for matrix in (2, 5):
-            pairs.append([ref.at[0, :, pl.ds(at, chunk)] for ref in (slabs[matrix], places[matrix])])
+        for slab in range(2):
+            place = back.at[pl.ds(slab * units, units), pl.ds(at, chunk)]
+            pairs.append((slabs[3 * slab + 2].at[0, :, pl.ds(at, chunk)], place))
     copies = iter(streams(pairs, sems))
     for part in column_chunks(width):
         x[:, part] = joined((x0, x1, x2, x3), part, rows)
 
-    for slab, at in tiles:
-        gate_w, up_w = places[slab : slab + 2]
-        next(copies).wait()
-        pre_gate = jnp.dot(x[...], gate_w[0, :, at : at + step], preferred_element_type=f32)
-        next(copies).wait()
-        pre_up = jnp.dot(x[...], up_w[0, :, at : at + step], preferred_element_type=f32)
+    for number in range(tiles):
+        next(copies).wait()
+        next(copies).wait()
+        columns = slice(2 * number * tile, 2 * (number + 1) * tile)
+        pre = jnp.dot(x[...], into[:, columns], preferred_element_type=f32)
+        pre_gate, pre_up = pre[:, :tile], pre[:, tile:]
         sigma = jax.nn.sigmoid(pre_gate)
         activated = pre_gate * sigma
-        slope = pre_up * sigma * (1.0 + pre_gate * (1.0 - sigma))
-        into = slice(slab // 3 * units + at, slab // 3 * units + at + step)
-        hidden[:, into] = (activated * pre_up).astype(bf16)
-        for_up[into] = activated.T
-        for_gate[into] = slope.T
-
-    for part in column_chunks(width):
-        next(copies).wait()
-        total = jnp.dot(hidden[:, :units], d0[0, :, part], preferred_element_type=f32)
-        next(copies).wait()
-        total = total + jnp.dot(hidden[:, units:], d1[0, :, part], preferred_element_type=f32)
+        at = slice(number * tile, (number + 1) * tile)
+        hidden[:, at] = (activated * pre_up).astype(bf16)
+        for_up[:, at] = activated
+        for_gate[:, at] = pre_up * sigma * (1.0 + pre_gate * (1.0 - sigma))
+
+    for part in column_chunks(width):
+        next(copies).wait()
+        next(copies).wait()
+        total = jnp.dot(hidden[...], back[:, part], preferred_element_type=f32)
         store_packed(total, (o0, o1, o2, o3), part)
 
 
@@ -223,43 +222,37 @@
         out[:, at] = total[number * taken : (number + 1) * taken].astype(bf16)
 
 
-def backward_kernel(tile, x0, x1, x2, x3, for_up, for_gate, *refs):
-    *slabs, o0, o1, o2, o3, x, gate_grad, up_grad, g0, u0, d0, g1, u1, d1, sems = refs
-    places = (g0, u0, d0, g1, u1, d1)
-    width, rows = x.shape
-    units = g0.shape[2]
-    step, chunk = min(tile, units), chunk_of(width)
-    pairs, tiles = [], []
-    for slab in (0, 3):
-        for at in range(0, units, step):
-            tiles.append((slab, at))
-            pairs.append([ref.at[0, pl.ds(at, step)] for ref in (slabs[slab + 2], places[slab + 2])])
+def backward_kernel(x0, x1, x2, x3, for_up, for_gate, *refs):
+    *slabs, o0, o1, o2, o3, x, grads, into, back, sems = refs
+    rows, width = x.shape
+    units = back.shape[0] // 2
+    chunk = chunk_of(width)
+    pairs = []
+    for slab in range(2):
+        pairs.append((slabs[3 * slab + 2].at[0], back.at[pl.ds(slab * units, units)]))
     for at in range(0, width, chunk):
-        for matrix in (0, 1, 3, 4):
-            pairs.append([ref.at[0, pl.ds(at, chunk)] for ref in (slabs[matrix], places[matrix])])
+        for number, matrix in enumerate((0, 1, 3, 4)):
+            place = into.at[pl.ds(at, chunk), pl.ds(number * units, units)]
+            pairs.append((slabs[matrix].at[0, pl.ds(at, chunk)], place))
     copies = iter(streams(pairs, sems))
     for part in column_chunks(width):
-        x[part] = joined((x0, x1, x2, x3), part, rows, f32).T.astype(bf16)
-
-    for slab, at in tiles:
-        next(copies).wait()
-        into = slice(slab // 3 * units + at, slab // 3 * units + at + step)
-        down_w = places[slab + 2]
-        hidden_grad = jnp.dot(down_w[0, at : at + step], x[...], preferred_element_type=f32)
-        gate_grad[into] = (hidden_grad * for_gate[into]).astype(bf16)
-        up_grad[into] = (hidden_grad * for_up[into]).astype(bf16)
-
-    own, other = slice(0, units), slice(units, 2 * units)
-    for part in column_chunks(width):
-        total = jnp.zeros((chunk, rows), f32)
-        for matrix, grad in ((g0, gate_grad[own]), (u0, up_grad[own]), (g1, gate_grad[other]), (u1, up_grad[other])):
+        x[:, part] = joined((x0, x1, x2, x3), part, rows)
+
+    for slab in range(2):
+        next(copies).wait()
+        at = slice(slab * units, (slab + 1) * units)
+        hidden_grad = lax.dot_general(x[...], back[at], CONTRACT_COLS, preferred_element_type=f32)
+        start = 2 * slab * units
+        grads[:, start : start + units] = (hidden_grad * for_gate[:, at]).astype(bf16)
+        grads[:, start + units : start + 2 * units] = (hidden_grad * for_up[:, at]).astype(bf16)
+
+    for part in column_chunks(width):
+        for _ in range(4):
             next(copies).wait()
-            total = total + jnp.dot(matrix[0, part], grad, preferred_element_type=f32)
-        store_packed(total.T, (o0, o1, o2, o3), part)
-
-
-def after(value, *others):
-    return lax.optimization_barrier((value, *others))[0]
+        total = lax.dot_general(
+            grads[...], into[part], CONTRACT_COLS, preferred_element_type=f32
+        )
+        store_packed(total, (o0, o1, o2, o3), part)
 
 
 def on_device(tokens, expert_ids, gate_values, cotangent, gate_weight, up_weight, down_weight):
@@ -281,7 +274,14 @@
         [shape((tok_dev, width + padded(PIECES * experts)), bf16)],
         (tokens, expert_ids.T, gate_values.T),
     )
-    held = gather_far(coded)
+    held, cots = {0: coded}, {0: cotangent}
+    offset = devices // 2
+    while offset > FAR:
+        cots = double(cots, offset, cotangent)
+        held = double(held, offset, coded)
+        offset //= 2
+    held = double(held, FAR, cots[max(cots)])
+    held = [held[at] for at in sorted(held)]
     gate_other, up_other = swap(gate_weight, CORE), swap(up_weight, CORE)
 
     whole = pl.BlockSpec(memory_space=pltpu.VMEM)
@@ -297,7 +297,8 @@
     down_other = swap(after(down_weight, gate_other, up_other, packed[0]), CORE)
     own = (gate_weight, up_weight, down_weight)
     other = (gate_other, up_other, down_other)
-    cots = gather_far(after(cotangent, held[len(held) // 2]))
+    cots = double(cots, FAR, packed[0])
+    cots = [cots[at] for at in sorted(cots)]
 
     packed = call(
         functools.partial(pack_cots_kernel, capacity),
@@ -311,11 +312,11 @@
     in_place = pl.BlockSpec(memory_space=pl.ANY)
     tile = 256 if hidden % 256 == 0 else LANES
     tiles, chunks = 2 * hidden // tile, width // chunk_of(width)
-    slab_room = [pltpu.VMEM(slab.shape, bf16) for slab in (*own, *other)]
+    slab_room = [pltpu.VMEM((width, 4 * hidden), bf16), pltpu.VMEM((2 * hidden, width), bf16)]
     flops = 2 * 3 * all_taken * width * 2 * hidden
     *outs, for_up, for_gate = call(
         functools.partial(forward_kernel, tile),
-        packed_shapes + [shape((2 * hidden, all_taken), f32)] * 2,
+        packed_shapes + [shape((all_taken, 2 * hidden), f32)] * 2,
         (*x, *own, *other),
         flops=flops,
         in_specs=[whole] * 4 + [in_place] * 6,
@@ -342,17 +343,17 @@
 
     layer_out = go_home(outs, True)
     backs = call(
-        functools.partial(backward_kernel, tile),
+        backward_kernel,
         packed_shapes,
         (*grads, for_up, for_gate, *own, *other),
         flops=flops,
         in_specs=[whole] * 6 + [in_place] * 6,
         limit=VMEM_LIMIT_EXPERT,
         scratch=[
-            pltpu.VMEM((width, all_taken), bf16),
-            *[pltpu.VMEM((2 * hidden, all_taken), bf16)] * 2,
+            pltpu.VMEM((all_taken, width), bf16),
+            pltpu.VMEM((all_taken, 4 * hidden), bf16),
             *slab_room,
-            pltpu.SemaphoreType.DMA((tiles + 4 * chunks,)),
+            pltpu.SemaphoreType.DMA((2 + 4 * chunks,)),
         ],
     )
     token_grad = go_home(backs, False)

time: 103 us -> 97.2 us (0.944)
  Pallas kernels: 31.8 us -> 23.6 us
  waiting for transfers between devices: 25.8 us -> 30 us
  starting transfers between devices: 39.3 us -> 37.4 us
    pallas_call x9, Pallas kernels: 31.8 us -> 23.6 us  [call(): pl.pallas_call(body, out_shape=outs, in_specs=[whole] * len(args) if in_s...]
    ppermute x27, waiting for transfers between devices: 25.8 us -> 30 us  [swap(): lax.ppermute(value, 'expert', [(i, i ^ offset) for i in range(devices)])]
    ppermute x27, starting transfers between devices: 39.3 us -> 37.4 us  [swap(): lax.ppermute(value, 'expert', [(i, i ^ offset) for i in range(devices)])]
  transfers between devices with their start and end apart: 27 -> 27, of which waited for: 7 -> 10; matrix products, arithmetic and copies ran while one was open for 0% -> 0% of each run, Pallas kernels for 30% -> 24%
where the time goes in v5:
time: 97.2 us; the launch traced here: 96.9 us
  starting transfers between devices  37.4 us (38%)
  waiting for transfers between devices  30 us (31%)
  Pallas kernels  23.6 us (24%)
  local copies, waits for them, and re-layouts  5.09 us (5%)
    ppermute x27, starting transfers between devices, swap(): lax.ppermute(value, 'expert', [(i, i ^ offset) for i in range(devices)])  37.4 us
    ppermute x27, waiting for transfers between devices, swap(): lax.ppermute(value, 'expert', [(i, i ^ offset) for i in range(devices)])  30 us
    pallas_call x9, Pallas kernels, call(): pl.pallas_call(body, out_shape=outs, in_specs=[whole] * len(args) if in_s...  23.6 us
    unnamed x10, local copies, waits for them, and re-layouts  5.09 us
  transfers between devices with their start and end apart: 27, of which 10 were waited for; matrix products, arithmetic and copies ran while one was open for 0% of the time, Pallas kernels for 24%

profile of v5, /device:TPU:0, one launch (start us, length us, event | category | flops | bytes accessed | tf_op | source)
XLA Modules:
  0.0 96.9 jit_solution(18010355021054767597)
XLA Ops:
  0.6 0.5 collective-permute-start.7
  1.1 0.1 collective-permute-start.8
  1.2 0.9 copy-done.1
  2.1 0.7 copy-done.2
  2.8 0.7 copy-done.3
  3.5 0.2 shard_map.86.refs_0_
  3.7 4.1 %collective-permute-start.2 = (bf16[16,3712]{1,0:T(8,128)(2,1)S(1)}, bf16[16,3712]{1,0:T(8,128)(2,1)S(1)}, u32[]{:S(2)}, u32[]{:S(2)}) collective-permute-start(bf16[16,3712]{1,0:T(8,128)(2,1)S(1)} %shard_map.86.refs_0_), channel_id=1, source_target_pairs={{0,16},{1,17},{2,18},{3,19},{4,20},{5,21},{6,22},{7,23},{8,24},{9,... | collective-permute-start | bytes 356360 | tf_op jit(solution)/shard_map/ppermute | solution.py:22
  7.8 10.9 %collective-permute-done.refs_2_ = bf16[16,3584]{1,0:T(8,128)(2,1)S(1)} collective-permute-done((bf16[16,3584]{1,0:T(8,128)(2,1)}, bf16[16,3584]{1,0:T(8,128)(2,1)S(1)}, u32[]{:S(2)}, u32[]{:S(2)}) %collective-permute-start) | collective-permute-done | bytes 114720 | tf_op jit(solution)/shard_map/ppermute | solution.py:22
  18.7 0.8 collective-permute-start.1
  19.5 1.2 %collective-permute-start.3 = (bf16[16,3712]{1,0:T(8,128)(2,1)S(1)}, bf16[16,3712]{1,0:T(8,128)(2,1)S(1)}, u32[]{:S(2)}, u32[]{:S(2)}) collective-permute-start(bf16[16,3712]{1,0:T(8,128)(2,1)S(1)} %collective-permute-done.2.refs_2_), channel_id=1, source_target_pairs={{0,8},{1,9},{2,10},{3,11},{4,12},{5,13},{6,14},{7,15},{8,0},{9,1},... | collective-permute-start | bytes 356360 | tf_op jit(solution)/shard_map/ppermute | solution.py:22
  20.7 3.9 %collective-permute-done.1.refs_1_ = bf16[16,3712]{1,0:T(8,128)(2,1)S(1)} collective-permute-done((bf16[16,3712]{1,0:T(8,128)(2,1)S(1)}, bf16[16,3712]{1,0:T(8,128)(2,1)S(1)}, u32[]{:S(2)}, u32[]{:S(2)}) %collective-permute-start.1) | collective-permute-done | bytes 118816 | tf_op jit(solution)/shard_map/ppermute | solution.py:22
  24.7 1.3 %collective-permute-done.3.refs_3_ = bf16[16,3712]{1,0:T(8,128)(2,1)S(1)} collective-permute-done((bf16[16,3712]{1,0:T(8,128)(2,1)S(1)}, bf16[16,3712]{1,0:T(8,128)(2,1)S(1)}, u32[]{:S(2)}, u32[]{:S(2)}) %collective-permute-start.3) | collective-permute-done | bytes 118816 | tf_op jit(solution)/shard_map/ppermute | solution.py:22
  25.9 1.0 %shard_map.87 = (bf16[40,3584]{1,0:T(8,128)(2,1)S(1)}, bf16[40,3584]{1,0:T(8,128)(2,1)S(1)}, bf16[40,3584]{1,0:T(8,128)(2,1)S(1)}, bf16[40,3584]{1,0:T(8,128)(2,...) custom-call(s32[1]{0:T(128)} %bitcast.chip, bf16[16,3712]{1,0:T(8,128)(2,1)S(1)} %shard_map.86.refs_0_, ...), custom_call_target="tpu_custom_call" | custom-call | flops 117440512 | bytes 1753092 | tf_op jit(solution)/shard_map/pallas_call | solution.py:50
  27.1 1.3 %collective-permute-start.4 = (bf16[40,3584]{1,0:T(8,128)(2,1)S(1)}, bf16[40,3584]{1,0:T(8,128)(2,1)S(1)}, u32[]{:S(2)}, u32[]{:S(2)}) collective-permute-start(bf16[40,3584]{1,0:T(8,128)(2,1)S(1)} %get-tuple-element.43), channel_id=1, source_target_pairs={{0,2},{1,3},{2,0},{3,1},{4,6},{5,7},{6,4},{7,5},{8,10},{9,11},{10,... | collective-permute-start | bytes 860168 | tf_op jit(solution)/shard_map/ppermute | solution.py:22
  28.4 1.5 %collective-permute-start.5 = (bf16[40,3584]{1,0:T(8,128)(2,1)S(1)}, bf16[40,3584]{1,0:T(8,128)(2,1)S(1)}, u32[]{:S(2)}, u32[]{:S(2)}) collective-permute-start(bf16[40,3584]{1,0:T(8,128)(2,1)S(1)} %get-tuple-element.44), channel_id=1, source_target_pairs={{0,4},{1,5},{2,6},{3,7},{4,0},{5,1},{6,2},{7,3},{8,12},{9,13},{10,... | collective-permute-start | bytes 860168 | tf_op jit(solution)/shard_map/ppermute | solution.py:22
  29.9 0.7 collective-permute-start.6
  30.6 1.3 %collective-permute-start.16 = (bf16[16,3584]{1,0:T(8,128)(2,1)}, bf16[16,3584]{1,0:T(8,128)(2,1)S(1)}, u32[]{:S(2)}, u32[]{:S(2)}) collective-permute-start(bf16[16,3584]{1,0:T(8,128)(2,1)} %refs_0_.4), channel_id=1, source_target_pairs={{0,8},{1,9},{2,10},{3,11},{4,12},{5,13},{6,14},{7,15},{8,0},{9,1},... | collective-permute-start | bytes 344072 | tf_op jit(solution)/shard_map/ppermute | solution.py:22
  31.9 3.7 %collective-permute-done.16.refs_1_ = bf16[16,3584]{1,0:T(8,128)(2,1)S(1)} collective-permute-done((bf16[16,3584]{1,0:T(8,128)(2,1)}, bf16[16,3584]{1,0:T(8,128)(2,1)S(1)}, u32[]{:S(2)}, u32[]{:S(2)}) %collective-permute-start.16) | collective-permute-done | bytes 114720 | tf_op jit(solution)/shard_map/ppermute | solution.py:22
  35.6 1.3 %collective-permute-start.17 = (bf16[16,3584]{1,0:T(8,128)(2,1)S(1)}, bf16[16,3584]{1,0:T(8,128)(2,1)S(1)}, u32[]{:S(2)}, u32[]{:S(2)}) collective-permute-start(bf16[16,3584]{1,0:T(8,128)(2,1)S(1)} %collective-permute-done.refs_2_), channel_id=1, source_target_pairs={{0,8},{1,9},{2,10},{3,11},{4,12},{5,13},{6,14},{7,15},{8,0},{9,1},... | collective-permute-start | bytes 344072 | tf_op jit(solution)/shard_map/ppermute | solution.py:22
  36.9 3.5 %collective-permute-done.17.refs_3_ = bf16[16,3584]{1,0:T(8,128)(2,1)S(1)} collective-permute-done((bf16[16,3584]{1,0:T(8,128)(2,1)S(1)}, bf16[16,3584]{1,0:T(8,128)(2,1)S(1)}, u32[]{:S(2)}, u32[]{:S(2)}) %collective-permute-start.17) | collective-permute-done | bytes 114720 | tf_op jit(solution)/shard_map/ppermute | solution.py:22
  40.4 0.9 copy-done
  41.3 0.6 shard_map.91
  41.9 1.3 %collective-permute-start.18 = (bf16[40,3584]{1,0:T(8,128)(2,1)S(1)}, bf16[40,3584]{1,0:T(8,128)(2,1)S(1)}, u32[]{:S(2)}, u32[]{:S(2)}) collective-permute-start(bf16[40,3584]{1,0:T(8,128)(2,1)S(1)} %get-tuple-element.59), channel_id=1, source_target_pairs={{0,2},{1,3},{2,0},{3,1},{4,6},{5,7},{6,4},{7,5},{8,10},{9,11},{10,... | collective-permute-start | bytes 860168 | tf_op jit(solution)/shard_map/ppermute | solution.py:22
  43.2 1.5 %collective-permute-start.19 = (bf16[40,3584]{1,0:T(8,128)(2,1)S(1)}, bf16[40,3584]{1,0:T(8,128)(2,1)S(1)}, u32[]{:S(2)}, u32[]{:S(2)}) collective-permute-start(bf16[40,3584]{1,0:T(8,128)(2,1)S(1)} %get-tuple-element.60), channel_id=1, source_target_pairs={{0,4},{1,5},{2,6},{3,7},{4,0},{5,1},{6,2},{7,3},{8,12},{9,13},{10,... | collective-permute-start | bytes 860168 | tf_op jit(solution)/shard_map/ppermute | solution.py:22
  44.8 0.7 collective-permute-start.20
  45.5 1.9 %copy-done.4 = bf16[1,512,3584]{2,1,0:T(8,128)(2,1)} copy-done((bf16[1,512,3584]{2,1,0:T(8,128)(2,1)}, bf16[1,512,3584]{2,1,0:T(8,128)(2,1)S(1)}, u32[]{:S(2)}) %copy-start.4) | copy-done | bytes 3670040
  47.4 8.6 %shard_map.88 = (bf16[40,3584]{1,0:T(8,128)(2,1)S(1)}, bf16[40,3584]{1,0:T(8,128)(2,1)S(1)}, bf16[40,3584]{1,0:T(8,128)(2,1)S(1)}, bf16[40,3584]{1,0:T(8,128)(2,...) custom-call(bf16[40,3584]{1,0:T(8,128)(2,1)S(1)} %get-tuple-element.42.x0, ...), custom_call_target="tpu_custom_call" | custom-call | flops 3523215360 | bytes 25624576 | tf_op jit(solution)/shard_map/pallas_call | solution.py:50
  56.1 1.3 %collective-permute-start.10 = (bf16[40,3584]{1,0:T(8,128)(2,1)S(1)}, bf16[40,3584]{1,0:T(8,128)(2,1)S(1)}, u32[]{:S(2)}, u32[]{:S(2)}) collective-permute-start(bf16[40,3584]{1,0:T(8,128)(2,1)S(1)} %get-tuple-element.48), channel_id=1, source_target_pairs={{0,2},{1,3},{2,0},{3,1},{4,6},{5,7},{6,4},{7,5},{8,10},{9,11},{10,... | collective-permute-start | bytes 860168 | tf_op jit(solution)/shard_map/ppermute | solution.py:22
  57.4 1.5 %collective-permute-start.11 = (bf16[40,3584]{1,0:T(8,128)(2,1)S(1)}, bf16[40,3584]{1,0:T(8,128)(2,1)S(1)}, u32[]{:S(2)}, u32[]{:S(2)}) collective-permute-start(bf16[40,3584]{1,0:T(8,128)(2,1)S(1)} %get-tuple-element.49), channel_id=1, source_target_pairs={{0,4},{1,5},{2,6},{3,7},{4,0},{5,1},{6,2},{7,3},{8,12},{9,13},{10,... | collective-permute-start | bytes 860168 | tf_op jit(solution)/shard_map/ppermute | solution.py:22
  58.9 0.7 collective-permute-start.12
  59.6 10.9 %shard_map.92 = (bf16[40,3584]{1,0:T(8,128)(2,1)S(1)}, bf16[40,3584]{1,0:T(8,128)(2,1)S(1)}, bf16[40,3584]{1,0:T(8,128)(2,1)S(1)}, bf16[40,3584]{1,0:T(8,128)(2,1)S(1)}) custom-call(bf16[40,3584]{1,0:T(8,128)(2,1)S(1)} %get-tuple-element.58.x0, bf16[40,3584]{1,0:T(8,128)(2,1)S(1)} %collective-permute-done.18.x1, ...), custom_call_target="tpu_custom_call" | custom-call | flops 3523215360 | bytes 25624576 | tf_op jit(solution)/shard_map/pallas_call | solution.py:50
  70.5 1.3 %collective-permute-start.21 = (bf16[40,3584]{1,0:T(8,128)(2,1)S(1)}, bf16[40,3584]{1,0:T(8,128)(2,1)S(1)}, u32[]{:S(2)}, u32[]{:S(2)}) collective-permute-start(bf16[40,3584]{1,0:T(8,128)(2,1)S(1)} %get-tuple-element.65), channel_id=1, source_target_pairs={{0,2},{1,3},{2,0},{3,1},{4,6},{5,7},{6,4},{7,5},{8,10},{9,11},{10,... | collective-permute-start | bytes 860168 | tf_op jit(solution)/shard_map/ppermute | solution.py:22
  71.8 1.5 %collective-permute-start.22 = (bf16[40,3584]{1,0:T(8,128)(2,1)S(1)}, bf16[40,3584]{1,0:T(8,128)(2,1)S(1)}, u32[]{:S(2)}, u32[]{:S(2)}) collective-permute-start(bf16[40,3584]{1,0:T(8,128)(2,1)S(1)} %get-tuple-element.66), channel_id=1, source_target_pairs={{0,4},{1,5},{2,6},{3,7},{4,0},{5,1},{6,2},{7,3},{8,12},{9,13},{10,... | collective-permute-start | bytes 860168 | tf_op jit(solution)/shard_map/ppermute | solution.py:22
  73.4 0.7 collective-permute-start.23
  74.1 0.6 shard_map.89
  74.7 1.4 %collective-permute-start.13 = (bf16[16,3584]{1,0:T(8,128)(2,1)S(1)}, bf16[16,3584]{1,0:T(8,128)(2,1)S(1)}, u32[]{:S(2)}, u32[]{:S(2)}) collective-permute-start(bf16[16,3584]{1,0:T(8,128)(2,1)S(1)} %get-tuple-element.52), channel_id=1, source_target_pairs={{0,8},{1,9},{2,10},{3,11},{4,12},{5,13},{6,14},{7,15},{8,0},{9,1},... | collective-permute-start | bytes 344072 | tf_op jit(solution)/shard_map/ppermute | solution.py:22
  76.1 3.3 %collective-permute-start.14 = (bf16[16,3584]{1,0:T(8,128)(2,1)S(1)}, bf16[16,3584]{1,0:T(8,128)(2,1)S(1)}, u32[]{:S(2)}, u32[]{:S(2)}) collective-permute-start(bf16[16,3584]{1,0:T(8,128)(2,1)S(1)} %get-tuple-element.53), channel_id=1, source_target_pairs={{0,16},{1,17},{2,18},{3,19},{4,20},{5,21},{6,22},{7,23},{8,24},{9,... | collective-permute-start | bytes 344072 | tf_op jit(solution)/shard_map/ppermute | solution.py:22
  79.3 0.5 collective-permute-done.21.second
  79.9 4.3 %collective-permute-start.15 = (bf16[16,3584]{1,0:T(8,128)(2,1)S(1)}, bf16[16,3584]{1,0:T(8,128)(2,1)S(1)}, u32[]{:S(2)}, u32[]{:S(2)}) collective-permute-start(bf16[16,3584]{1,0:T(8,128)(2,1)S(1)} %get-tuple-element.54), channel_id=1, source_target_pairs={{0,24},{1,25},{2,26},{3,27},{4,28},{5,29},{6,30},{7,31},{8,16},{9,... | collective-permute-start | bytes 344072 | tf_op jit(solution)/shard_map/ppermute | solution.py:22
  84.1 0.2 collective-permute-done.22.third
  84.3 0.3 shard_map.93
  84.6 1.6 %collective-permute-start.24 = (bf16[16,3584]{1,0:T(8,128)(2,1)S(1)}, bf16[16,3584]{1,0:T(8,128)(2,1)S(1)}, u32[]{:S(2)}, u32[]{:S(2)}) collective-permute-start(bf16[16,3584]{1,0:T(8,128)(2,1)S(1)} %get-tuple-element.69), channel_id=1, source_target_pairs={{0,8},{1,9},{2,10},{3,11},{4,12},{5,13},{6,14},{7,15},{8,0},{9,1},... | collective-permute-start | bytes 344072 | tf_op jit(solution)/shard_map/ppermute | solution.py:22
  86.2 3.3 %collective-permute-start.25 = (bf16[16,3584]{1,0:T(8,128)(2,1)S(1)}, bf16[16,3584]{1,0:T(8,128)(2,1)S(1)}, u32[]{:S(2)}, u32[]{:S(2)}) collective-permute-start(bf16[16,3584]{1,0:T(8,128)(2,1)S(1)} %get-tuple-element.70), channel_id=1, source_target_pairs={{0,16},{1,17},{2,18},{3,19},{4,20},{5,21},{6,22},{7,23},{8,24},{9,... | collective-permute-start | bytes 344072 | tf_op jit(solution)/shard_map/ppermute | solution.py:22
  89.5 0.7 shard_map.90
  90.3 1.5 %collective-permute-done.24.refs_1_ = bf16[16,3584]{1,0:T(8,128)(2,1)S(1)} collective-permute-done((bf16[16,3584]{1,0:T(8,128)(2,1)S(1)}, bf16[16,3584]{1,0:T(8,128)(2,1)S(1)}, u32[]{:S(2)}, u32[]{:S(2)}) %collective-permute-start.24) | collective-permute-done | bytes 114720 | tf_op jit(solution)/shard_map/ppermute | solution.py:22
  91.8 2.6 %collective-permute-done.25.refs_2_ = bf16[16,3584]{1,0:T(8,128)(2,1)S(1)} collective-permute-done((bf16[16,3584]{1,0:T(8,128)(2,1)S(1)}, bf16[16,3584]{1,0:T(8,128)(2,1)S(1)}, u32[]{:S(2)}, u32[]{:S(2)}) %collective-permute-start.25) | collective-permute-done | bytes 114720 | tf_op jit(solution)/shard_map/ppermute | solution.py:22
  94.4 1.8 %collective-permute-done.26.refs_3_ = bf16[16,3584]{1,0:T(8,128)(2,1)S(1)} collective-permute-done((bf16[16,3584]{1,0:T(8,128)(2,1)S(1)}, bf16[16,3584]{1,0:T(8,128)(2,1)S(1)}, u32[]{:S(2)}, u32[]{:S(2)}) %collective-permute-start.26) | collective-permute-done | bytes 114720 | tf_op jit(solution)/shard_map/ppermute | solution.py:22
  96.2 0.7 shard_map.94
  (25 shorter events, 0.2 us)
Async XLA Ops:
  0.6 26.3 %collective-permute-start.7 = (bf16[1,3584,512]{2,1,0:T(8,128)(2,1)}, bf16[1,3584,512]{2,1,0:T(8,128)(2,1)}, u32[]{:S(2)}, u32[]{:S(2)}) collective-permute-start(bf16[1,3584,512]{2,1,0:T(8,128)(2,1)} %refs_0_.5), channel_id=1, source_target_pairs={{0,1},{1,0},{2,3},{3,2},{4,5},{5,4},{6,7},{7,6},{8,9},{9,8},{10,11... | collective-permute-start | bytes 11010056 | tf_op jit(solution)/shard_map/ppermute | solution.py:22
  1.1 25.8 %collective-permute-start.8 = (bf16[1,3584,512]{2,1,0:T(8,128)(2,1)}, bf16[1,3584,512]{2,1,0:T(8,128)(2,1)}, u32[]{:S(2)}, u32[]{:S(2)}) collective-permute-start(bf16[1,3584,512]{2,1,0:T(8,128)(2,1)} %refs_1_.3), channel_id=1, source_target_pairs={{0,1},{1,0},{2,3},{3,2},{4,5},{5,4},{6,7},{7,6},{8,9},{9,8},{10,11... | collective-permute-start | bytes 11010056 | tf_op jit(solution)/shard_map/ppermute | solution.py:22
  1.2 0.9 copy-start.1
  2.1 0.7 copy-start.2
  2.8 0.7 copy-start.3
  3.7 15.8 %collective-permute-start.2 = (bf16[16,3712]{1,0:T(8,128)(2,1)S(1)}, bf16[16,3712]{1,0:T(8,128)(2,1)S(1)}, u32[]{:S(2)}, u32[]{:S(2)}) collective-permute-start(bf16[16,3712]{1,0:T(8,128)(2,1)S(1)} %shard_map.86.refs_0_), channel_id=1, source_target_pairs={{0,16},{1,17},{2,18},{3,19},{4,20},{5,21},{6,22},{7,23},{8,24},{9,... | collective-permute-start | bytes 356360 | tf_op jit(solution)/shard_map/ppermute | solution.py:22
  7.7 10.9 %collective-permute-start = (bf16[16,3584]{1,0:T(8,128)(2,1)}, bf16[16,3584]{1,0:T(8,128)(2,1)S(1)}, u32[]{:S(2)}, u32[]{:S(2)}) collective-permute-start(bf16[16,3584]{1,0:T(8,128)(2,1)} %refs_0_.4), channel_id=1, source_target_pairs={{0,16},{1,17},{2,18},{3,19},{4,20},{5,21},{6,22},{7,23},{8,24},{9,... | collective-permute-start | bytes 344072 | tf_op jit(solution)/shard_map/ppermute | solution.py:22
  18.7 6.0 %collective-permute-start.1 = (bf16[16,3712]{1,0:T(8,128)(2,1)S(1)}, bf16[16,3712]{1,0:T(8,128)(2,1)S(1)}, u32[]{:S(2)}, u32[]{:S(2)}) collective-permute-start(bf16[16,3712]{1,0:T(8,128)(2,1)S(1)} %shard_map.86.refs_0_), channel_id=1, source_target_pairs={{0,8},{1,9},{2,10},{3,11},{4,12},{5,13},{6,14},{7,15},{8,0},{9,1},... | collective-permute-start | bytes 356360 | tf_op jit(solution)/shard_map/ppermute | solution.py:22
  19.5 6.4 %collective-permute-start.3 = (bf16[16,3712]{1,0:T(8,128)(2,1)S(1)}, bf16[16,3712]{1,0:T(8,128)(2,1)S(1)}, u32[]{:S(2)}, u32[]{:S(2)}) collective-permute-start(bf16[16,3712]{1,0:T(8,128)(2,1)S(1)} %collective-permute-done.2.refs_2_), channel_id=1, source_target_pairs={{0,8},{1,9},{2,10},{3,11},{4,12},{5,13},{6,14},{7,15},{8,0},{9,1},... | collective-permute-start | bytes 356360 | tf_op jit(solution)/shard_map/ppermute | solution.py:22
  27.0 18.5 %collective-permute-start.9 = (bf16[1,512,3584]{2,1,0:T(8,128)(2,1)}, bf16[1,512,3584]{2,1,0:T(8,128)(2,1)S(1)}, u32[]{:S(2)}, u32[]{:S(2)}) collective-permute-start(bf16[1,512,3584]{2,1,0:T(8,128)(2,1)} %refs_2_.3), channel_id=1, source_target_pairs={{0,1},{1,0},{2,3},{3,2},{4,5},{5,4},{6,7},{7,6},{8,9},{9,8},{10,11... | collective-permute-start | bytes 11010056 | tf_op jit(solution)/shard_map/ppermute | solution.py:22
  27.1 16.2 %collective-permute-start.4 = (bf16[40,3584]{1,0:T(8,128)(2,1)S(1)}, bf16[40,3584]{1,0:T(8,128)(2,1)S(1)}, u32[]{:S(2)}, u32[]{:S(2)}) collective-permute-start(bf16[40,3584]{1,0:T(8,128)(2,1)S(1)} %get-tuple-element.43), channel_id=1, source_target_pairs={{0,2},{1,3},{2,0},{3,1},{4,6},{5,7},{6,4},{7,5},{8,10},{9,11},{10,... | collective-permute-start | bytes 860168 | tf_op jit(solution)/shard_map/ppermute | solution.py:22
  28.4 16.4 %collective-permute-start.5 = (bf16[40,3584]{1,0:T(8,128)(2,1)S(1)}, bf16[40,3584]{1,0:T(8,128)(2,1)S(1)}, u32[]{:S(2)}, u32[]{:S(2)}) collective-permute-start(bf16[40,3584]{1,0:T(8,128)(2,1)S(1)} %get-tuple-element.44), channel_id=1, source_target_pairs={{0,4},{1,5},{2,6},{3,7},{4,0},{5,1},{6,2},{7,3},{8,12},{9,13},{10,... | collective-permute-start | bytes 860168 | tf_op jit(solution)/shard_map/ppermute | solution.py:22
  29.9 15.6 %collective-permute-start.6 = (bf16[40,3584]{1,0:T(8,128)(2,1)S(1)}, bf16[40,3584]{1,0:T(8,128)(2,1)S(1)}, u32[]{:S(2)}, u32[]{:S(2)}) collective-permute-start(bf16[40,3584]{1,0:T(8,128)(2,1)S(1)} %get-tuple-element.45), channel_id=1, source_target_pairs={{0,6},{1,7},{2,4},{3,5},{4,2},{5,3},{6,0},{7,1},{8,14},{9,15},{10,... | collective-permute-start | bytes 860168 | tf_op jit(solution)/shard_map/ppermute | solution.py:22
  30.6 5.0 %collective-permute-start.16 = (bf16[16,3584]{1,0:T(8,128)(2,1)}, bf16[16,3584]{1,0:T(8,128)(2,1)S(1)}, u32[]{:S(2)}, u32[]{:S(2)}) collective-permute-start(bf16[16,3584]{1,0:T(8,128)(2,1)} %refs_0_.4), channel_id=1, source_target_pairs={{0,8},{1,9},{2,10},{3,11},{4,12},{5,13},{6,14},{7,15},{8,0},{9,1},... | collective-permute-start | bytes 344072 | tf_op jit(solution)/shard_map/ppermute | solution.py:22
  35.6 4.8 %collective-permute-start.17 = (bf16[16,3584]{1,0:T(8,128)(2,1)S(1)}, bf16[16,3584]{1,0:T(8,128)(2,1)S(1)}, u32[]{:S(2)}, u32[]{:S(2)}) collective-permute-start(bf16[16,3584]{1,0:T(8,128)(2,1)S(1)} %collective-permute-done.refs_2_), channel_id=1, source_target_pairs={{0,8},{1,9},{2,10},{3,11},{4,12},{5,13},{6,14},{7,15},{8,0},{9,1},... | collective-permute-start | bytes 344072 | tf_op jit(solution)/shard_map/ppermute | solution.py:22
  40.4 0.9 copy-start
  41.9 17.0 %collective-permute-start.18 = (bf16[40,3584]{1,0:T(8,128)(2,1)S(1)}, bf16[40,3584]{1,0:T(8,128)(2,1)S(1)}, u32[]{:S(2)}, u32[]{:S(2)}) collective-permute-start(bf16[40,3584]{1,0:T(8,128)(2,1)S(1)} %get-tuple-element.59), channel_id=1, source_target_pairs={{0,2},{1,3},{2,0},{3,1},{4,6},{5,7},{6,4},{7,5},{8,10},{9,11},{10,... | collective-permute-start | bytes 860168 | tf_op jit(solution)/shard_map/ppermute | solution.py:22
  43.2 16.4 %collective-permute-start.19 = (bf16[40,3584]{1,0:T(8,128)(2,1)S(1)}, bf16[40,3584]{1,0:T(8,128)(2,1)S(1)}, u32[]{:S(2)}, u32[]{:S(2)}) collective-permute-start(bf16[40,3584]{1,0:T(8,128)(2,1)S(1)} %get-tuple-element.60), channel_id=1, source_target_pairs={{0,4},{1,5},{2,6},{3,7},{4,0},{5,1},{6,2},{7,3},{8,12},{9,13},{10,... | collective-permute-start | bytes 860168 | tf_op jit(solution)/shard_map/ppermute | solution.py:22
  44.8 14.9 %collective-permute-start.20 = (bf16[40,3584]{1,0:T(8,128)(2,1)S(1)}, bf16[40,3584]{1,0:T(8,128)(2,1)S(1)}, u32[]{:S(2)}, u32[]{:S(2)}) collective-permute-start(bf16[40,3584]{1,0:T(8,128)(2,1)S(1)} %get-tuple-element.61), channel_id=1, source_target_pairs={{0,6},{1,7},{2,4},{3,5},{4,2},{5,3},{6,0},{7,1},{8,14},{9,15},{10,... | collective-permute-start | bytes 860168 | tf_op jit(solution)/shard_map/ppermute | solution.py:22
  45.5 1.9 %copy-start.4 = (bf16[1,512,3584]{2,1,0:T(8,128)(2,1)}, bf16[1,512,3584]{2,1,0:T(8,128)(2,1)S(1)}, u32[]{:S(2)}) copy-start(bf16[1,512,3584]{2,1,0:T(8,128)(2,1)S(1)} %collective-permute-done.9.refs_5_) | copy-start | bytes 11010052
  56.1 17.3 %collective-permute-start.10 = (bf16[40,3584]{1,0:T(8,128)(2,1)S(1)}, bf16[40,3584]{1,0:T(8,128)(2,1)S(1)}, u32[]{:S(2)}, u32[]{:S(2)}) collective-permute-start(bf16[40,3584]{1,0:T(8,128)(2,1)S(1)} %get-tuple-element.48), channel_id=1, source_target_pairs={{0,2},{1,3},{2,0},{3,1},{4,6},{5,7},{6,4},{7,5},{8,10},{9,11},{10,... | collective-permute-start | bytes 860168 | tf_op jit(solution)/shard_map/ppermute | solution.py:22
  57.4 16.7 %collective-permute-start.11 = (bf16[40,3584]{1,0:T(8,128)(2,1)S(1)}, bf16[40,3584]{1,0:T(8,128)(2,1)S(1)}, u32[]{:S(2)}, u32[]{:S(2)}) collective-permute-start(bf16[40,3584]{1,0:T(8,128)(2,1)S(1)} %get-tuple-element.49), channel_id=1, source_target_pairs={{0,4},{1,5},{2,6},{3,7},{4,0},{5,1},{6,2},{7,3},{8,12},{9,13},{10,... | collective-permute-start | bytes 860168 | tf_op jit(solution)/shard_map/ppermute | solution.py:22
  58.9 15.2 %collective-permute-start.12 = (bf16[40,3584]{1,0:T(8,128)(2,1)S(1)}, bf16[40,3584]{1,0:T(8,128)(2,1)S(1)}, u32[]{:S(2)}, u32[]{:S(2)}) collective-permute-start(bf16[40,3584]{1,0:T(8,128)(2,1)S(1)} %get-tuple-element.50), channel_id=1, source_target_pairs={{0,6},{1,7},{2,4},{3,5},{4,2},{5,3},{6,0},{7,1},{8,14},{9,15},{10,... | collective-permute-start | bytes 860168 | tf_op jit(solution)/shard_map/ppermute | solution.py:22
  70.5 9.3 %collective-permute-start.21 = (bf16[40,3584]{1,0:T(8,128)(2,1)S(1)}, bf16[40,3584]{1,0:T(8,128)(2,1)S(1)}, u32[]{:S(2)}, u32[]{:S(2)}) collective-permute-start(bf16[40,3584]{1,0:T(8,128)(2,1)S(1)} %get-tuple-element.65), channel_id=1, source_target_pairs={{0,2},{1,3},{2,0},{3,1},{4,6},{5,7},{6,4},{7,5},{8,10},{9,11},{10,... | collective-permute-start | bytes 860168 | tf_op jit(solution)/shard_map/ppermute | solution.py:22
  71.8 12.5 %collective-permute-start.22 = (bf16[40,3584]{1,0:T(8,128)(2,1)S(1)}, bf16[40,3584]{1,0:T(8,128)(2,1)S(1)}, u32[]{:S(2)}, u32[]{:S(2)}) collective-permute-start(bf16[40,3584]{1,0:T(8,128)(2,1)S(1)} %get-tuple-element.66), channel_id=1, source_target_pairs={{0,4},{1,5},{2,6},{3,7},{4,0},{5,1},{6,2},{7,3},{8,12},{9,13},{10,... | collective-permute-start | bytes 860168 | tf_op jit(solution)/shard_map/ppermute | solution.py:22
  73.4 11.0 %collective-permute-start.23 = (bf16[40,3584]{1,0:T(8,128)(2,1)S(1)}, bf16[40,3584]{1,0:T(8,128)(2,1)S(1)}, u32[]{:S(2)}, u32[]{:S(2)}) collective-permute-start(bf16[40,3584]{1,0:T(8,128)(2,1)S(1)} %get-tuple-element.67), channel_id=1, source_target_pairs={{0,6},{1,7},{2,4},{3,5},{4,2},{5,3},{6,0},{7,1},{8,14},{9,15},{10,... | collective-permute-start | bytes 860168 | tf_op jit(solution)/shard_map/ppermute | solution.py:22
  74.7 14.8 %collective-permute-start.13 = (bf16[16,3584]{1,0:T(8,128)(2,1)S(1)}, bf16[16,3584]{1,0:T(8,128)(2,1)S(1)}, u32[]{:S(2)}, u32[]{:S(2)}) collective-permute-start(bf16[16,3584]{1,0:T(8,128)(2,1)S(1)} %get-tuple-element.52), channel_id=1, source_target_pairs={{0,8},{1,9},{2,10},{3,11},{4,12},{5,13},{6,14},{7,15},{8,0},{9,1},... | collective-permute-start | bytes 344072 | tf_op jit(solution)/shard_map/ppermute | solution.py:22
  76.1 13.5 %collective-permute-start.14 = (bf16[16,3584]{1,0:T(8,128)(2,1)S(1)}, bf16[16,3584]{1,0:T(8,128)(2,1)S(1)}, u32[]{:S(2)}, u32[]{:S(2)}) collective-permute-start(bf16[16,3584]{1,0:T(8,128)(2,1)S(1)} %get-tuple-element.53), channel_id=1, source_target_pairs={{0,16},{1,17},{2,18},{3,19},{4,20},{5,21},{6,22},{7,23},{8,24},{9,... | collective-permute-start | bytes 344072 | tf_op jit(solution)/shard_map/ppermute | solution.py:22
  79.9 9.7 %collective-permute-start.15 = (bf16[16,3584]{1,0:T(8,128)(2,1)S(1)}, bf16[16,3584]{1,0:T(8,128)(2,1)S(1)}, u32[]{:S(2)}, u32[]{:S(2)}) collective-permute-start(bf16[16,3584]{1,0:T(8,128)(2,1)S(1)} %get-tuple-element.54), channel_id=1, source_target_pairs={{0,24},{1,25},{2,26},{3,27},{4,28},{5,29},{6,30},{7,31},{8,16},{9,... | collective-permute-start | bytes 344072 | tf_op jit(solution)/shard_map/ppermute | solution.py:22
  84.6 7.1 %collective-permute-start.24 = (bf16[16,3584]{1,0:T(8,128)(2,1)S(1)}, bf16[16,3584]{1,0:T(8,128)(2,1)S(1)}, u32[]{:S(2)}, u32[]{:S(2)}) collective-permute-start(bf16[16,3584]{1,0:T(8,128)(2,1)S(1)} %get-tuple-element.69), channel_id=1, source_target_pairs={{0,8},{1,9},{2,10},{3,11},{4,12},{5,13},{6,14},{7,15},{8,0},{9,1},... | collective-permute-start | bytes 344072 | tf_op jit(solution)/shard_map/ppermute | solution.py:22
  86.2 8.1 %collective-permute-start.25 = (bf16[16,3584]{1,0:T(8,128)(2,1)S(1)}, bf16[16,3584]{1,0:T(8,128)(2,1)S(1)}, u32[]{:S(2)}, u32[]{:S(2)}) collective-permute-start(bf16[16,3584]{1,0:T(8,128)(2,1)S(1)} %get-tuple-element.70), channel_id=1, source_target_pairs={{0,16},{1,17},{2,18},{3,19},{4,20},{5,21},{6,22},{7,23},{8,24},{9,... | collective-permute-start | bytes 344072 | tf_op jit(solution)/shard_map/ppermute | solution.py:22
  89.5 6.7 %collective-permute-start.26 = (bf16[16,3584]{1,0:T(8,128)(2,1)S(1)}, bf16[16,3584]{1,0:T(8,128)(2,1)S(1)}, u32[]{:S(2)}, u32[]{:S(2)}) collective-permute-start(bf16[16,3584]{1,0:T(8,128)(2,1)S(1)} %get-tuple-element.71), channel_id=1, source_target_pairs={{0,24},{1,25},{2,26},{3,27},{4,28},{5,29},{6,30},{7,31},{8,16},{9,... | collective-permute-start | bytes 344072 | tf_op jit(solution)/shard_map/ppermute | solution.py:22

commit v6 on v5

--- a/solution.py
+++ b/solution.py
@@ -13,8 +13,14 @@
 CONTRACT_COLS = (((1,), (1,)), ((), ()))
 LANES = 128
 PIECES = 3
+CHUNK = 512
 VMEM_LIMIT = 16 * 1024 * 1024
 VMEM_LIMIT_EXPERT = 48 * 1024 * 1024
+VMEM_LIMIT_ALL = 58 * 1024 * 1024
+
+
+def after(value, *others):
+    return lax.optimization_barrier((value, *others))[0]
 
 
 def swap(value, offset):
@@ -22,26 +28,12 @@
     return lax.ppermute(value, "expert", [(i, i ^ offset) for i in range(devices)])
 
 
-def after(value, *others):
-    return lax.optimization_barrier((value, *others))[0]
-
-
-def double(held, offset, wait):
-    ready = {at: after(value, wait) for at, value in held.items()}
-    return held | {at ^ offset: swap(value, offset) for at, value in ready.items()}
-
-
 def padded(count):
     return -(-count // LANES) * LANES
 
 
-def chunk_of(width):
-    return 512 if width % 512 == 0 else LANES
-
-
 def column_chunks(width):
-    step = chunk_of(width)
-    return [slice(at, at + step) for at in range(0, width, step)]
+    return [slice(at, min(at + CHUNK, width)) for at in range(0, width, CHUNK)]
 
 
 def call(body, outs, args, flops=0, scratch=(), in_specs=None, limit=VMEM_LIMIT):
@@ -58,15 +50,26 @@
     )(*args)
 
 
-def code_kernel(experts, tokens, ids, gates, out):
+def streams(pairs, sems):
+    copies = [
+        pltpu.make_async_copy(source, place, sems.at[number])
+        for number, (source, place) in enumerate(pairs)
+    ]
+    for copy in copies:
+        copy.start()
+    return copies
+
+
+def code_kernel(experts, tokens_in, ids_in, gates_in, cots_in, out, tokens, ids, gates, sems):
     rows, width = tokens.shape
-    for at in range(0, width, LANES):
-        block = tokens[:, at : at + LANES].astype(f32)
-        scale = jnp.max(jnp.abs(block), axis=1, keepdims=True) + 1e-06
-        scale = scale.astype(bf16).astype(f32)
-        quantized = (block / scale).astype(bf16).astype(f32)
-        out[:, at : at + LANES] = (quantized * scale).astype(bf16)
-    line = lax.broadcasted_iota(jnp.int32, (out.shape[1] - width, rows), 0)
+    copies = streams(((ids_in, ids), (gates_in, gates), (tokens_in, tokens)), sems)
+    gate_width = out.shape[1] - 2 * width
+    place = out.at[:, pl.ds(width + gate_width, width)]
+    cots_copy = pltpu.make_async_copy(cots_in, place, sems.at[len(copies)])
+    cots_copy.start()
+    copies[0].wait()
+    copies[1].wait()
+    line = lax.broadcasted_iota(jnp.int32, (gate_width, rows), 0)
     rest = jnp.zeros(line.shape, f32)
     for k in range(ids.shape[0]):
         rest = jnp.where(ids[k : k + 1] == line % experts, gates[k : k + 1], rest)
@@ -75,7 +78,15 @@
         piece = rest.astype(bf16).astype(f32)
         columns = jnp.where(line // experts == number, piece, columns)
         rest = rest - piece
-    out[:, width:] = columns.T.astype(bf16)
+    out[:, width : width + gate_width] = columns.T.astype(bf16)
+    copies[2].wait()
+    for at in range(0, width, LANES):
+        block = tokens[:, at : at + LANES].astype(f32)
+        scale = jnp.max(jnp.abs(block), axis=1, keepdims=True) + 1e-06
+        scale = scale.astype(bf16).astype(f32)
+        quantized = (block / scale).astype(bf16).astype(f32)
+        out[:, at : at + LANES] = (quantized * scale).astype(bf16)
+    cots_copy.wait()
 
 
 def pack_tokens_kernel(experts, capacity, chip, *refs):
@@ -84,7 +95,8 @@
     rows, slots = by_row.shape
     width = first.shape[1]
     taken = slots_of(len(blocks), capacity)
-    columns = jnp.concatenate([block[:, width:].astype(f32) for block in blocks], axis=0)
+    gate_columns = slice(width, blocks[0].shape[1] - width)
+    columns = jnp.concatenate([block[:, gate_columns].astype(f32) for block in blocks], axis=0)
     lane = lax.broadcasted_iota(jnp.int32, columns.shape, 1)
     pick = lax.broadcasted_iota(jnp.int32, (rows, LANES), 1)
     gates, named = [], jnp.zeros((rows, LANES), f32)
@@ -120,8 +132,10 @@
     taken = slots_of(len(blocks), capacity)
     gate = jnp.sum(by_slot[...], axis=1, keepdims=True)
     chosen = jnp.where(by_slot[...] > 0.0, 1.0, 0.0).astype(bf16)
-    for part in column_chunks(width):
-        held = jnp.concatenate([block[:, part] for block in blocks], axis=0)
+    first_column = blocks[0].shape[1] - width
+    for part in column_chunks(width):
+        source = slice(first_column + part.start, first_column + part.stop)
+        held = jnp.concatenate([block[:, source] for block in blocks], axis=0)
         packed = gate * jnp.dot(chosen, held, preferred_element_type=f32)
         for number, out in enumerate((first, second, third, fourth)):
             out[:, part] = packed[number * taken : (number + 1) * taken].astype(bf16)
@@ -158,40 +172,35 @@
             out[:, part] = total[number * tok_dev : (number + 1) * tok_dev].astype(bf16)
 
 
-def sum_kernel(*refs):
+def sum_kernel(count, *refs):
     *blocks, out = refs
-    for part in column_chunks(out.shape[1]):
-        total = blocks[0][:, part].astype(f32)
-        for block in blocks[1:]:
-            total = total + block[:, part].astype(f32)
-        out[:, part] = total.astype(bf16)
-
-
-def streams(pairs, sems):
-    copies = [
-        pltpu.make_async_copy(source, place, sems.at[number])
-        for number, (source, place) in enumerate(pairs)
-    ]
-    for copy in copies:
-        copy.start()
-    return copies
+    start = 0
+    for at in range(0, len(blocks), count):
+        columns = blocks[at].shape[1]
+        for part in column_chunks(columns):
+            total = blocks[at][:, part].astype(f32)
+            for block in blocks[at + 1 : at + count]:
+                total = total + block[:, part].astype(f32)
+            out[:, start + part.start : start + part.stop] = total.astype(bf16)
+        start += columns
 
 
 def forward_kernel(tile, x0, x1, x2, x3, *refs):
     *slabs, o0, o1, o2, o3, for_up, for_gate, x, hidden, into, back, sems = refs
     rows, width = x.shape
     units = back.shape[0] // 2
-    chunk, tiles = chunk_of(width), 2 * units // tile
+    tiles = 2 * units // tile
     pairs = []
     for number in range(tiles):
         slab, at = divmod(number * tile, units)
         for half, source in enumerate(slabs[3 * slab : 3 * slab + 2]):
             place = into.at[:, pl.ds((2 * number + half) * tile, tile)]
             pairs.append((source.at[0, :, pl.ds(at, tile)], place))
-    for at in range(0, width, chunk):
+    for part in column_chunks(width):
+        columns = pl.ds(part.start, part.stop - part.start)
         for slab in range(2):
-            place = back.at[pl.ds(slab * units, units), pl.ds(at, chunk)]
-            pairs.append((slabs[3 * slab + 2].at[0, :, pl.ds(at, chunk)], place))
+            place = back.at[pl.ds(slab * units, units), columns]
+            pairs.append((slabs[3 * slab + 2].at[0, :, columns], place))
     copies = iter(streams(pairs, sems))
     for part in column_chunks(width):
         x[:, part] = joined((x0, x1, x2, x3), part, rows)
@@ -222,19 +231,35 @@
         out[:, at] = total[number * taken : (number + 1) * taken].astype(bf16)
 
 
+def into_pairs(slabs, into, first):
+    pairs, units = [], into.shape[1] // len(slabs)
+    for part in column_chunks(into.shape[0]):
+        height = part.stop - part.start
+        for number, source in enumerate(slabs):
+            place = into.at[pl.ds(part.start, height), pl.ds(number * units, units)]
+            pairs.append((source.at[0, pl.ds(first + part.start, height)], place))
+    return pairs
+
+
+def project_back(copies, matrices, grads, into, outs):
+    for part in column_chunks(into.shape[0]):
+        for _ in range(matrices):
+            next(copies).wait()
+        total = lax.dot_general(
+            grads[...], into[part], CONTRACT_COLS, preferred_element_type=f32
+        )
+        store_packed(total, outs, part)
+
+
 def backward_kernel(x0, x1, x2, x3, for_up, for_gate, *refs):
-    *slabs, o0, o1, o2, o3, x, grads, into, back, sems = refs
+    *slabs, o0, o1, o2, o3, grads, x, into, back, sems = refs
     rows, width = x.shape
     units = back.shape[0] // 2
-    chunk = chunk_of(width)
+    into_slabs = (*slabs[:2], *slabs[3:5])
     pairs = []
     for slab in range(2):
         pairs.append((slabs[3 * slab + 2].at[0], back.at[pl.ds(slab * units, units)]))
-    for at in range(0, width, chunk):
-        for number, matrix in enumerate((0, 1, 3, 4)):
-            place = into.at[pl.ds(at, chunk), pl.ds(number * units, units)]
-            pairs.append((slabs[matrix].at[0, pl.ds(at, chunk)], place))
-    copies = iter(streams(pairs, sems))
+    copies = iter(streams(pairs + into_pairs(into_slabs, into, 0), sems))
     for part in column_chunks(width):
         x[:, part] = joined((x0, x1, x2, x3), part, rows)
 
@@ -246,13 +271,13 @@
         grads[:, start : start + units] = (hidden_grad * for_gate[:, at]).astype(bf16)
         grads[:, start + units : start + 2 * units] = (hidden_grad * for_up[:, at]).astype(bf16)
 
-    for part in column_chunks(width):
-        for _ in range(4):
-            next(copies).wait()
-        total = lax.dot_general(
-            grads[...], into[part], CONTRACT_COLS, preferred_element_type=f32
-        )
-        store_packed(total, (o0, o1, o2, o3), part)
+    project_back(copies, len(into_slabs), grads, into, (o0, o1, o2, o3))
+
+
+def backward_rest_kernel(first, grads, *refs):
+    *slabs, o0, o1, o2, o3, into, sems = refs
+    copies = iter(streams(into_pairs(slabs, into, first), sems))
+    project_back(copies, len(slabs), grads, into, (o0, o1, o2, o3))
 
 
 def on_device(tokens, expert_ids, gate_values, cotangent, gate_weight, up_weight, down_weight):
@@ -269,20 +294,28 @@
     shape = jax.ShapeDtypeStruct
     packed_shapes = [shape((taken, width), bf16)] * len(PLANE)
 
+    own = (gate_weight, up_weight, down_weight)
+    other = tuple(swap(slab, CORE) for slab in own)
+
+    in_place = pl.BlockSpec(memory_space=pl.ANY)
     (coded,) = call(
         functools.partial(code_kernel, experts),
-        [shape((tok_dev, width + padded(PIECES * experts)), bf16)],
-        (tokens, expert_ids.T, gate_values.T),
-    )
-    held, cots = {0: coded}, {0: cotangent}
-    offset = devices // 2
-    while offset > FAR:
-        cots = double(cots, offset, cotangent)
-        held = double(held, offset, coded)
+        [shape((tok_dev, 2 * width + padded(PIECES * experts)), bf16)],
+        (tokens, expert_ids.T, gate_values.T, cotangent),
+        in_specs=[in_place] * 4,
+        scratch=[
+            pltpu.VMEM((tok_dev, width), bf16),
+            pltpu.VMEM((top, tok_dev), jnp.int32),
+            pltpu.VMEM((top, tok_dev), f32),
+            pltpu.SemaphoreType.DMA((4,)),
+        ],
+        limit=VMEM_LIMIT_ALL,
+    )
+    held, offset = {0: coded}, devices // 2
+    while offset >= FAR:
+        held.update({at ^ offset: swap(value, offset) for at, value in held.items()})
         offset //= 2
-    held = double(held, FAR, cots[max(cots)])
     held = [held[at] for at in sorted(held)]
-    gate_other, up_other = swap(gate_weight, CORE), swap(up_weight, CORE)
 
     whole = pl.BlockSpec(memory_space=pltpu.VMEM)
     *packed, by_row, by_slot = call(
@@ -292,26 +325,20 @@
         in_specs=[pl.BlockSpec(memory_space=pltpu.SMEM)] + [whole] * blocks,
         flops=2 * rows * slots * width,
     )
+    packed = [after(value, *other[:2]) for value in packed]
     x = [packed[0]] + [swap(value, offset) for value, offset in zip(packed[1:], PLANE[1:])]
-
-    down_other = swap(after(down_weight, gate_other, up_other, packed[0]), CORE)
-    own = (gate_weight, up_weight, down_weight)
-    other = (gate_other, up_other, down_other)
-    cots = double(cots, FAR, packed[0])
-    cots = [cots[at] for at in sorted(cots)]
 
     packed = call(
         functools.partial(pack_cots_kernel, capacity),
         packed_shapes,
-        (by_slot, *cots),
+        (by_slot, *held),
         flops=2 * rows * slots * width,
     )
     grads = [packed[0]] + [swap(value, offset) for value, offset in zip(packed[1:], PLANE[1:])]
 
     all_taken = len(PLANE) * taken
-    in_place = pl.BlockSpec(memory_space=pl.ANY)
     tile = 256 if hidden % 256 == 0 else LANES
-    tiles, chunks = 2 * hidden // tile, width // chunk_of(width)
+    tiles, chunks = 2 * hidden // tile, len(column_chunks(width))
     slab_room = [pltpu.VMEM((width, 4 * hidden), bf16), pltpu.VMEM((2 * hidden, width), bf16)]
     flops = 2 * 3 * all_taken * width * 2 * hidden
     *outs, for_up, for_gate = call(
@@ -331,32 +358,50 @@
 
     def go_home(values, weighted):
         back = [values[0]] + [swap(value, offset) for value, offset in zip(values[1:], PLANE[1:])]
+        columns = values[0].shape[1]
         sums = call(
             functools.partial(unpack_kernel, weighted),
-            [shape((tok_dev, width), bf16)] * blocks,
+            [shape((tok_dev, columns), bf16)] * blocks,
             (by_row, *back),
-            flops=2 * rows * slots * width * (PIECES if weighted else 1),
+            flops=2 * rows * slots * columns * (PIECES if weighted else 1),
         )
-        home = [sums[0]] + [swap(value, offset) for value, offset in zip(sums[1:], far)]
-        (result,) = call(sum_kernel, [shape((tok_dev, width), bf16)], home)
-        return result
-
-    layer_out = go_home(outs, True)
-    backs = call(
+        return [sums[0]] + [swap(value, offset) for value, offset in zip(sums[1:], far)]
+
+    result_shape = [shape((tok_dev, width), bf16)]
+    out_homes = go_home(outs, True)
+    (layer_out,) = call(functools.partial(sum_kernel, blocks), result_shape, out_homes)
+
+    half = padded(width // 2)
+    grads_shape = shape((all_taken, 4 * hidden), bf16)
+    *backs, unit_grads = call(
         backward_kernel,
-        packed_shapes,
+        [shape((taken, half), bf16)] * len(PLANE) + [grads_shape],
         (*grads, for_up, for_gate, *own, *other),
-        flops=flops,
+        flops=2 * all_taken * 2 * hidden * (width + 2 * half),
         in_specs=[whole] * 6 + [in_place] * 6,
         limit=VMEM_LIMIT_EXPERT,
         scratch=[
             pltpu.VMEM((all_taken, width), bf16),
-            pltpu.VMEM((all_taken, 4 * hidden), bf16),
-            *slab_room,
-            pltpu.SemaphoreType.DMA((2 + 4 * chunks,)),
+            pltpu.VMEM((half, 4 * hidden), bf16),
+            pltpu.VMEM((2 * hidden, width), bf16),
+            pltpu.SemaphoreType.DMA((2 + 4 * len(column_chunks(half)),)),
         ],
     )
-    token_grad = go_home(backs, False)
+    homes = go_home(backs, False)
+    backs = call(
+        functools.partial(backward_rest_kernel, half),
+        [shape((taken, width - half), bf16)] * len(PLANE),
+        (after(unit_grads, out_homes[0]), *own[:2], *other[:2]),
+        flops=2 * all_taken * 2 * hidden * 2 * (width - half),
+        in_specs=[whole] + [in_place] * 4,
+        limit=VMEM_LIMIT_EXPERT,
+        scratch=[
+            pltpu.VMEM((width - half, 4 * hidden), bf16),
+            pltpu.SemaphoreType.DMA((4 * len(column_chunks(width - half)),)),
+        ],
+    )
+    homes = homes + go_home(backs, False)
+    (token_grad,) = call(functools.partial(sum_kernel, blocks), result_shape, homes)
     return layer_out, token_grad
 
 

time: 97.2 us -> 104 us (1.070)
  Pallas kernels: 23.6 us -> 28.3 us
  local copies, waits for them, and re-layouts: 5.09 us -> 0.94 us
  starting transfers between devices: 37.4 us -> 41.4 us
  waiting for transfers between devices: 30 us -> 32.6 us
    pallas_call x9 -> x11, Pallas kernels: 23.6 us -> 28.3 us  [call(): pl.pallas_call(body, out_shape=outs, in_specs=[whole] * len(args) if in_s...]
    unnamed x10 -> x4, local copies, waits for them, and re-layouts: 5.09 us -> 0.94 us
    ppermute x27 -> x30, starting transfers between devices: 37.4 us -> 41.4 us  [swap(): lax.ppermute(value, 'expert', [(i, i ^ offset) for i in range(devices)])]
    ppermute x27 -> x30, waiting for transfers between devices: 30 us -> 32.6 us  [swap(): lax.ppermute(value, 'expert', [(i, i ^ offset) for i in range(devices)])]
  transfers between devices with their start and end apart: 27 -> 30, of which waited for: 10 -> 8; matrix products, arithmetic and copies ran while one was open for 0% -> 0% of each run, Pallas kernels for 24% -> 27%
where the time goes in v6:
time: 104 us
  starting transfers between devices  41.4 us (40%)
  waiting for transfers between devices  32.6 us (31%)
  Pallas kernels  28.3 us (27%)
    ppermute x30, starting transfers between devices, swap(): lax.ppermute(value, 'expert', [(i, i ^ offset) for i in range(devices)])  41.4 us
    ppermute x30, waiting for transfers between devices, swap(): lax.ppermute(value, 'expert', [(i, i ^ offset) for i in range(devices)])  32.6 us
    pallas_call x11, Pallas kernels, call(): pl.pallas_call(body, out_shape=outs, in_specs=[whole] * len(args) if in_s...  28.3 us
  transfers between devices with their start and end apart: 30, of which 8 were waited for; matrix products, arithmetic and copies ran while one was open for 0% of the time, Pallas kernels for 27%

profile of v6, /device:TPU:0, one launch (start us, length us, event | category | flops | bytes accessed | tf_op | source)
XLA Modules:
  0.0 104.1 jit_solution(15159320346937667613)
XLA Ops:
  0.6 0.5 collective-permute-start.3
  1.1 0.1 collective-permute-start.4
  1.2 0.4 collective-permute-start.8
  1.7 1.8 %shard_map.86.refs_0_ = bf16[16,7296]{1,0:T(8,128)(2,1)} custom-call(bf16[16,3584]{1,0:T(8,128)(2,1)} %tokens_in.1, s32[8,16]{1,0:T(8,128)} %bitcast.3, f32[8,16]{1,0:T(8,128)} %bitcast.4, bf16[16,3584]{1,0:T(8,128)(2,1)} %cots_in.1), custom_call_target="tpu_custom_call" | custom-call | bytes 463872 | tf_op jit(solution)/shard_map/pallas_call | solution.py:42
  3.5 3.7 %collective-permute-start.1 = (bf16[16,7296]{1,0:T(8,128)(2,1)}, bf16[16,7296]{1,0:T(8,128)(2,1)S(1)}, u32[]{:S(2)}, u32[]{:S(2)}) collective-permute-start(bf16[16,7296]{1,0:T(8,128)(2,1)} %shard_map.86.refs_0_), channel_id=1, source_target_pairs={{0,16},{1,17},{2,18},{3,19},{4,20},{5,21},{6,22},{7,23},{8,24},{9,... | collective-permute-start | bytes 700424 | tf_op jit(solution)/shard_map/ppermute | solution.py:28
  7.2 1.6 %collective-permute-start = (bf16[16,7296]{1,0:T(8,128)(2,1)}, bf16[16,7296]{1,0:T(8,128)(2,1)S(1)}, u32[]{:S(2)}, u32[]{:S(2)}) collective-permute-start(bf16[16,7296]{1,0:T(8,128)(2,1)} %shard_map.86.refs_0_), channel_id=1, source_target_pairs={{0,8},{1,9},{2,10},{3,11},{4,12},{5,13},{6,14},{7,15},{8,0},{9,1},... | collective-permute-start | bytes 700424 | tf_op jit(solution)/shard_map/ppermute | solution.py:28
  8.8 10.0 %collective-permute-done.1.refs_2_ = bf16[16,7296]{1,0:T(8,128)(2,1)S(1)} collective-permute-done((bf16[16,7296]{1,0:T(8,128)(2,1)}, bf16[16,7296]{1,0:T(8,128)(2,1)S(1)}, u32[]{:S(2)}, u32[]{:S(2)}) %collective-permute-start.1) | collective-permute-done | bytes 233504 | tf_op jit(solution)/shard_map/ppermute | solution.py:28
  18.8 0.7 collective-permute-start.2
  19.5 6.7 %collective-permute-done.2.refs_3_ = bf16[16,7296]{1,0:T(8,128)(2,1)S(1)} collective-permute-done((bf16[16,7296]{1,0:T(8,128)(2,1)S(1)}, bf16[16,7296]{1,0:T(8,128)(2,1)S(1)}, u32[]{:S(2)}, u32[]{:S(2)}) %collective-permute-start.2) | collective-permute-done | bytes 233504 | tf_op jit(solution)/shard_map/ppermute | solution.py:28
  26.2 0.9 copy-done.1
  27.1 1.0 shard_map.87
  28.2 1.4 %collective-permute-start.5 = (bf16[40,3584]{1,0:T(8,128)(2,1)S(1)}, bf16[40,3584]{1,0:T(8,128)(2,1)S(1)}, u32[]{:S(2)}, u32[]{:S(2)}) collective-permute-start(bf16[40,3584]{1,0:T(8,128)(2,1)S(1)} %get-tuple-element.48), channel_id=1, source_target_pairs={{0,2},{1,3},{2,0},{3,1},{4,6},{5,7},{6,4},{7,5},{8,10},{9,11},{10,... | collective-permute-start | bytes 860168 | tf_op jit(solution)/shard_map/ppermute | solution.py:28
  29.6 1.5 %collective-permute-start.6 = (bf16[40,3584]{1,0:T(8,128)(2,1)S(1)}, bf16[40,3584]{1,0:T(8,128)(2,1)S(1)}, u32[]{:S(2)}, u32[]{:S(2)}) collective-permute-start(bf16[40,3584]{1,0:T(8,128)(2,1)S(1)} %get-tuple-element.50), channel_id=1, source_target_pairs={{0,4},{1,5},{2,6},{3,7},{4,0},{5,1},{6,2},{7,3},{8,12},{9,13},{10,... | collective-permute-start | bytes 860168 | tf_op jit(solution)/shard_map/ppermute | solution.py:28
  31.1 0.6 collective-permute-start.7
  31.8 0.6 shard_map.91
  32.4 1.4 %collective-permute-start.15 = (bf16[40,3584]{1,0:T(8,128)(2,1)S(1)}, bf16[40,3584]{1,0:T(8,128)(2,1)S(1)}, u32[]{:S(2)}, u32[]{:S(2)}) collective-permute-start(bf16[40,3584]{1,0:T(8,128)(2,1)S(1)} %get-tuple-element.63), channel_id=1, source_target_pairs={{0,2},{1,3},{2,0},{3,1},{4,6},{5,7},{6,4},{7,5},{8,10},{9,11},{10,... | collective-permute-start | bytes 860168 | tf_op jit(solution)/shard_map/ppermute | solution.py:28
  33.8 1.5 %collective-permute-start.16 = (bf16[40,3584]{1,0:T(8,128)(2,1)S(1)}, bf16[40,3584]{1,0:T(8,128)(2,1)S(1)}, u32[]{:S(2)}, u32[]{:S(2)}) collective-permute-start(bf16[40,3584]{1,0:T(8,128)(2,1)S(1)} %get-tuple-element.64), channel_id=1, source_target_pairs={{0,4},{1,5},{2,6},{3,7},{4,0},{5,1},{6,2},{7,3},{8,12},{9,13},{10,... | collective-permute-start | bytes 860168 | tf_op jit(solution)/shard_map/ppermute | solution.py:28
  35.3 2.7 %collective-permute-done.5.x1 = bf16[40,3584]{1,0:T(8,128)(2,1)S(1)} collective-permute-done((bf16[40,3584]{1,0:T(8,128)(2,1)S(1)}, bf16[40,3584]{1,0:T(8,128)(2,1)S(1)}, u32[]{:S(2)}, u32[]{:S(2)}) %collective-permute-start.5) | collective-permute-done | bytes 286752 | tf_op jit(solution)/shard_map/ppermute | solution.py:28
  38.0 2.3 %collective-permute-start.17 = (bf16[40,3584]{1,0:T(8,128)(2,1)S(1)}, bf16[40,3584]{1,0:T(8,128)(2,1)S(1)}, u32[]{:S(2)}, u32[]{:S(2)}) collective-permute-start(bf16[40,3584]{1,0:T(8,128)(2,1)S(1)} %get-tuple-element.65), channel_id=1, source_target_pairs={{0,6},{1,7},{2,4},{3,5},{4,2},{5,3},{6,0},{7,1},{8,14},{9,15},{10,... | collective-permute-start | bytes 860168 | tf_op jit(solution)/shard_map/ppermute | solution.py:28
  40.3 5.2 %collective-permute-done.6.x2 = bf16[40,3584]{1,0:T(8,128)(2,1)S(1)} collective-permute-done((bf16[40,3584]{1,0:T(8,128)(2,1)S(1)}, bf16[40,3584]{1,0:T(8,128)(2,1)S(1)}, u32[]{:S(2)}, u32[]{:S(2)}) %collective-permute-start.6) | collective-permute-done | bytes 286752 | tf_op jit(solution)/shard_map/ppermute | solution.py:28
  45.5 8.6 %shard_map.88 = (bf16[40,3584]{1,0:T(8,128)(2,1)S(1)}, bf16[40,3584]{1,0:T(8,128)(2,1)S(1)}, bf16[40,3584]{1,0:T(8,128)(2,1)S(1)}, bf16[40,3584]{1,0:T(8,128)(2,...) custom-call(bf16[40,3584]{1,0:T(8,128)(2,1)S(1)} %get-tuple-element.46.x0, ...), custom_call_target="tpu_custom_call" | custom-call | flops 3523215360 | bytes 25624576 | tf_op jit(solution)/shard_map/pallas_call | solution.py:42
  54.2 1.1 %collective-permute-start.9 = (bf16[40,3584]{1,0:T(8,128)(2,1)S(1)}, bf16[40,3584]{1,0:T(8,128)(2,1)S(1)}, u32[]{:S(2)}, u32[]{:S(2)}) collective-permute-start(bf16[40,3584]{1,0:T(8,128)(2,1)S(1)} %get-tuple-element.54), channel_id=1, source_target_pairs={{0,2},{1,3},{2,0},{3,1},{4,6},{5,7},{6,4},{7,5},{8,10},{9,11},{10,... | collective-permute-start | bytes 860168 | tf_op jit(solution)/shard_map/ppermute | solution.py:28
  55.2 1.1 %collective-permute-start.10 = (bf16[40,3584]{1,0:T(8,128)(2,1)S(1)}, bf16[40,3584]{1,0:T(8,128)(2,1)S(1)}, u32[]{:S(2)}, u32[]{:S(2)}) collective-permute-start(bf16[40,3584]{1,0:T(8,128)(2,1)S(1)} %get-tuple-element.55), channel_id=1, source_target_pairs={{0,4},{1,5},{2,6},{3,7},{4,0},{5,1},{6,2},{7,3},{8,12},{9,13},{10,... | collective-permute-start | bytes 860168 | tf_op jit(solution)/shard_map/ppermute | solution.py:28
  56.3 1.4 %collective-permute-start.11 = (bf16[40,3584]{1,0:T(8,128)(2,1)S(1)}, bf16[40,3584]{1,0:T(8,128)(2,1)S(1)}, u32[]{:S(2)}, u32[]{:S(2)}) collective-permute-start(bf16[40,3584]{1,0:T(8,128)(2,1)S(1)} %get-tuple-element.56), channel_id=1, source_target_pairs={{0,6},{1,7},{2,4},{3,5},{4,2},{5,3},{6,0},{7,1},{8,14},{9,15},{10,... | collective-permute-start | bytes 860168 | tf_op jit(solution)/shard_map/ppermute | solution.py:28
  57.7 8.5 %shard_map.92 = (bf16[40,1792]{1,0:T(8,128)(2,1)S(1)}, bf16[40,1792]{1,0:T(8,128)(2,1)S(1)}, bf16[40,1792]{1,0:T(8,128)(2,1)S(1)}, bf16[40,1792]{1,0:T(8,128)(2,1)S(1)}, bf16[160,2048]{1,0:T(8,128)(2,1)S(1)}) custom-call(bf16[40,3584]{1,0:T(8,128)(2,1)S(1)} %get-tuple-element.62.x0, bf16[40,3584]{1,0:T(8,128)(2,1)S(1)} %collective-permute-done.15.x1, ...), custom_call_target="tpu_custom_call" | custom-call | flops 2348810240 | bytes 25706496 | tf_op jit(solution)/shard_map/pallas_call | solution.py:42
  66.3 1.1 %collective-permute-start.18 = (bf16[40,1792]{1,0:T(8,128)(2,1)S(1)}, bf16[40,1792]{1,0:T(8,128)(2,1)S(1)}, u32[]{:S(2)}, u32[]{:S(2)}) collective-permute-start(bf16[40,1792]{1,0:T(8,128)(2,1)S(1)} %get-tuple-element.69), channel_id=1, source_target_pairs={{0,2},{1,3},{2,0},{3,1},{4,6},{5,7},{6,4},{7,5},{8,10},{9,11},{10,... | collective-permute-start | bytes 430088 | tf_op jit(solution)/shard_map/ppermute | solution.py:28
  67.4 1.0 collective-permute-start.19
  68.4 1.4 %collective-permute-start.20 = (bf16[40,1792]{1,0:T(8,128)(2,1)S(1)}, bf16[40,1792]{1,0:T(8,128)(2,1)S(1)}, u32[]{:S(2)}, u32[]{:S(2)}) collective-permute-start(bf16[40,1792]{1,0:T(8,128)(2,1)S(1)} %get-tuple-element.71), channel_id=1, source_target_pairs={{0,6},{1,7},{2,4},{3,5},{4,2},{5,3},{6,0},{7,1},{8,14},{9,15},{10,... | collective-permute-start | bytes 430088 | tf_op jit(solution)/shard_map/ppermute | solution.py:28
  69.8 0.2 collective-permute-done.11.fourth
  70.1 0.6 shard_map.89
  70.7 5.2 %shard_map.94 = (bf16[40,1792]{1,0:T(8,128)(2,1)S(1)}, bf16[40,1792]{1,0:T(8,128)(2,1)S(1)}, bf16[40,1792]{1,0:T(8,128)(2,1)S(1)}, bf16[40,1792]{1,0:T(8,128)(2,1)S(1)}) custom-call(bf16[160,2048]{1,0:T(8,128)(2,1)S(1)} %get-tuple-element.77.grads, bf16[1,3584,512]{2,1,0:T(8,128)(2,1)S(1)} %copy-done, bf16[1,3584,512]{2,1,0:T(8,128)(2,1)} %refs_1_.5, ...), custom_call_target="tpu_custom_call" | custom-call | flops 1174405120 | bytes 15908864 | tf_op jit(solution)/shard_map/pallas_call | solution.py:42
  75.9 1.7 %collective-permute-start.24 = (bf16[40,1792]{1,0:T(8,128)(2,1)S(1)}, bf16[40,1792]{1,0:T(8,128)(2,1)S(1)}, u32[]{:S(2)}, u32[]{:S(2)}) collective-permute-start(bf16[40,1792]{1,0:T(8,128)(2,1)S(1)} %get-tuple-element.79), channel_id=1, source_target_pairs={{0,2},{1,3},{2,0},{3,1},{4,6},{5,7},{6,4},{7,5},{8,10},{9,11},{10,... | collective-permute-start | bytes 430088 | tf_op jit(solution)/shard_map/ppermute | solution.py:28
  77.7 0.2 collective-permute-start.25
  77.9 1.6 %collective-permute-start.26 = (bf16[40,1792]{1,0:T(8,128)(2,1)S(1)}, bf16[40,1792]{1,0:T(8,128)(2,1)S(1)}, u32[]{:S(2)}, u32[]{:S(2)}) collective-permute-start(bf16[40,1792]{1,0:T(8,128)(2,1)S(1)} %get-tuple-element.81), channel_id=1, source_target_pairs={{0,6},{1,7},{2,4},{3,5},{4,2},{5,3},{6,0},{7,1},{8,14},{9,15},{10,... | collective-permute-start | bytes 430088 | tf_op jit(solution)/shard_map/ppermute | solution.py:28
  79.5 1.7 %collective-permute-start.12 = (bf16[16,3584]{1,0:T(8,128)(2,1)S(1)}, bf16[16,3584]{1,0:T(8,128)(2,1)S(1)}, u32[]{:S(2)}, u32[]{:S(2)}) collective-permute-start(bf16[16,3584]{1,0:T(8,128)(2,1)S(1)} %get-tuple-element.58), channel_id=1, source_target_pairs={{0,8},{1,9},{2,10},{3,11},{4,12},{5,13},{6,14},{7,15},{8,0},{9,1},... | collective-permute-start | bytes 344072 | tf_op jit(solution)/shard_map/ppermute | solution.py:28
  81.3 3.3 %collective-permute-start.13 = (bf16[16,3584]{1,0:T(8,128)(2,1)S(1)}, bf16[16,3584]{1,0:T(8,128)(2,1)S(1)}, u32[]{:S(2)}, u32[]{:S(2)}) collective-permute-start(bf16[16,3584]{1,0:T(8,128)(2,1)S(1)} %get-tuple-element.59), channel_id=1, source_target_pairs={{0,16},{1,17},{2,18},{3,19},{4,20},{5,21},{6,22},{7,23},{8,24},{9,... | collective-permute-start | bytes 344072 | tf_op jit(solution)/shard_map/ppermute | solution.py:28
  84.5 1.0 collective-permute-start.14
  85.6 0.2 shard_map.93
  85.9 3.3 %collective-permute-start.22 = (bf16[16,1792]{1,0:T(8,128)(2,1)S(1)}, bf16[16,1792]{1,0:T(8,128)(2,1)S(1)}, u32[]{:S(2)}, u32[]{:S(2)}) collective-permute-start(bf16[16,1792]{1,0:T(8,128)(2,1)S(1)} %get-tuple-element.74), channel_id=1, source_target_pairs={{0,16},{1,17},{2,18},{3,19},{4,20},{5,21},{6,22},{7,23},{8,24},{9,... | collective-permute-start | bytes 172040 | tf_op jit(solution)/shard_map/ppermute | solution.py:28
  89.2 0.2 shard_map.95
  89.5 3.6 %collective-permute-done.21.refs_1_ = bf16[16,1792]{1,0:T(8,128)(2,1)S(1)} collective-permute-done((bf16[16,1792]{1,0:T(8,128)(2,1)S(1)}, bf16[16,1792]{1,0:T(8,128)(2,1)S(1)}, u32[]{:S(2)}, u32[]{:S(2)}) %collective-permute-start.21) | collective-permute-done | bytes 57376 | tf_op jit(solution)/shard_map/ppermute | solution.py:28
  93.0 1.1 %collective-permute-start.23 = (bf16[16,1792]{1,0:T(8,128)(2,1)S(1)}, bf16[16,1792]{1,0:T(8,128)(2,1)S(1)}, u32[]{:S(2)}, u32[]{:S(2)}) collective-permute-start(bf16[16,1792]{1,0:T(8,128)(2,1)S(1)} %get-tuple-element.75), channel_id=1, source_target_pairs={{0,24},{1,25},{2,26},{3,27},{4,28},{5,29},{6,30},{7,31},{8,16},{9,... | collective-permute-start | bytes 172040 | tf_op jit(solution)/shard_map/ppermute | solution.py:28
  94.1 3.3 %collective-permute-start.28 = (bf16[16,1792]{1,0:T(8,128)(2,1)S(1)}, bf16[16,1792]{1,0:T(8,128)(2,1)S(1)}, u32[]{:S(2)}, u32[]{:S(2)}) collective-permute-start(bf16[16,1792]{1,0:T(8,128)(2,1)S(1)} %get-tuple-element.84), channel_id=1, source_target_pairs={{0,16},{1,17},{2,18},{3,19},{4,20},{5,21},{6,22},{7,23},{8,24},{9,... | collective-permute-start | bytes 172040 | tf_op jit(solution)/shard_map/ppermute | solution.py:28
  97.4 1.1 %collective-permute-start.29 = (bf16[16,1792]{1,0:T(8,128)(2,1)S(1)}, bf16[16,1792]{1,0:T(8,128)(2,1)S(1)}, u32[]{:S(2)}, u32[]{:S(2)}) collective-permute-start(bf16[16,1792]{1,0:T(8,128)(2,1)S(1)} %get-tuple-element.85), channel_id=1, source_target_pairs={{0,24},{1,25},{2,26},{3,27},{4,28},{5,29},{6,30},{7,31},{8,16},{9,... | collective-permute-start | bytes 172040 | tf_op jit(solution)/shard_map/ppermute | solution.py:28
  98.5 0.7 shard_map.90
  99.3 0.4 collective-permute-done.28.refs_6_
  99.6 3.8 %collective-permute-done.29.refs_7_ = bf16[16,1792]{1,0:T(8,128)(2,1)S(1)} collective-permute-done((bf16[16,1792]{1,0:T(8,128)(2,1)S(1)}, bf16[16,1792]{1,0:T(8,128)(2,1)S(1)}, u32[]{:S(2)}, u32[]{:S(2)}) %collective-permute-start.29) | collective-permute-done | bytes 57376 | tf_op jit(solution)/shard_map/ppermute | solution.py:28
  103.4 0.7 shard_map.96
  (27 shorter events, 0.1 us)
Async XLA Ops:
  0.6 27.5 %collective-permute-start.3 = (bf16[1,3584,512]{2,1,0:T(8,128)(2,1)}, bf16[1,3584,512]{2,1,0:T(8,128)(2,1)}, u32[]{:S(2)}, u32[]{:S(2)}) collective-permute-start(bf16[1,3584,512]{2,1,0:T(8,128)(2,1)} %refs_0_.5), channel_id=1, source_target_pairs={{0,1},{1,0},{2,3},{3,2},{4,5},{5,4},{6,7},{7,6},{8,9},{9,8},{10,11... | collective-permute-start | bytes 11010056 | tf_op jit(solution)/shard_map/ppermute | solution.py:28
  1.1 27.0 %collective-permute-start.4 = (bf16[1,3584,512]{2,1,0:T(8,128)(2,1)}, bf16[1,3584,512]{2,1,0:T(8,128)(2,1)}, u32[]{:S(2)}, u32[]{:S(2)}) collective-permute-start(bf16[1,3584,512]{2,1,0:T(8,128)(2,1)} %refs_1_.5), channel_id=1, source_target_pairs={{0,1},{1,0},{2,3},{3,2},{4,5},{5,4},{6,7},{7,6},{8,9},{9,8},{10,11... | collective-permute-start | bytes 11010056 | tf_op jit(solution)/shard_map/ppermute | solution.py:28
  1.2 32.5 %collective-permute-start.8 = (bf16[1,512,3584]{2,1,0:T(8,128)(2,1)}, bf16[1,512,3584]{2,1,0:T(8,128)(2,1)}, u32[]{:S(2)}, u32[]{:S(2)}) collective-permute-start(bf16[1,512,3584]{2,1,0:T(8,128)(2,1)} %refs_2_.3), channel_id=1, source_target_pairs={{0,1},{1,0},{2,3},{3,2},{4,5},{5,4},{6,7},{7,6},{8,9},{9,8},{10,11... | collective-permute-start | bytes 11010056 | tf_op jit(solution)/shard_map/ppermute | solution.py:28
  3.5 15.3 %collective-permute-start.1 = (bf16[16,7296]{1,0:T(8,128)(2,1)}, bf16[16,7296]{1,0:T(8,128)(2,1)S(1)}, u32[]{:S(2)}, u32[]{:S(2)}) collective-permute-start(bf16[16,7296]{1,0:T(8,128)(2,1)} %shard_map.86.refs_0_), channel_id=1, source_target_pairs={{0,16},{1,17},{2,18},{3,19},{4,20},{5,21},{6,22},{7,23},{8,24},{9,... | collective-permute-start | bytes 700424 | tf_op jit(solution)/shard_map/ppermute | solution.py:28
  7.2 12.3 %collective-permute-start = (bf16[16,7296]{1,0:T(8,128)(2,1)}, bf16[16,7296]{1,0:T(8,128)(2,1)S(1)}, u32[]{:S(2)}, u32[]{:S(2)}) collective-permute-start(bf16[16,7296]{1,0:T(8,128)(2,1)} %shard_map.86.refs_0_), channel_id=1, source_target_pairs={{0,8},{1,9},{2,10},{3,11},{4,12},{5,13},{6,14},{7,15},{8,0},{9,1},... | collective-permute-start | bytes 700424 | tf_op jit(solution)/shard_map/ppermute | solution.py:28
  18.8 7.4 %collective-permute-start.2 = (bf16[16,7296]{1,0:T(8,128)(2,1)S(1)}, bf16[16,7296]{1,0:T(8,128)(2,1)S(1)}, u32[]{:S(2)}, u32[]{:S(2)}) collective-permute-start(bf16[16,7296]{1,0:T(8,128)(2,1)S(1)} %collective-permute-done.1.refs_2_), channel_id=1, source_target_pairs={{0,8},{1,9},{2,10},{3,11},{4,12},{5,13},{6,14},{7,15},{8,0},{9,1},... | collective-permute-start | bytes 700424 | tf_op jit(solution)/shard_map/ppermute | solution.py:28
  26.2 0.9 copy-start.1
  28.2 9.8 %collective-permute-start.5 = (bf16[40,3584]{1,0:T(8,128)(2,1)S(1)}, bf16[40,3584]{1,0:T(8,128)(2,1)S(1)}, u32[]{:S(2)}, u32[]{:S(2)}) collective-permute-start(bf16[40,3584]{1,0:T(8,128)(2,1)S(1)} %get-tuple-element.48), channel_id=1, source_target_pairs={{0,2},{1,3},{2,0},{3,1},{4,6},{5,7},{6,4},{7,5},{8,10},{9,11},{10,... | collective-permute-start | bytes 860168 | tf_op jit(solution)/shard_map/ppermute | solution.py:28
  29.6 15.9 %collective-permute-start.6 = (bf16[40,3584]{1,0:T(8,128)(2,1)S(1)}, bf16[40,3584]{1,0:T(8,128)(2,1)S(1)}, u32[]{:S(2)}, u32[]{:S(2)}) collective-permute-start(bf16[40,3584]{1,0:T(8,128)(2,1)S(1)} %get-tuple-element.50), channel_id=1, source_target_pairs={{0,4},{1,5},{2,6},{3,7},{4,0},{5,1},{6,2},{7,3},{8,12},{9,13},{10,... | collective-permute-start | bytes 860168 | tf_op jit(solution)/shard_map/ppermute | solution.py:28
  31.1 14.4 %collective-permute-start.7 = (bf16[40,3584]{1,0:T(8,128)(2,1)S(1)}, bf16[40,3584]{1,0:T(8,128)(2,1)S(1)}, u32[]{:S(2)}, u32[]{:S(2)}) collective-permute-start(bf16[40,3584]{1,0:T(8,128)(2,1)S(1)} %get-tuple-element.52), channel_id=1, source_target_pairs={{0,6},{1,7},{2,4},{3,5},{4,2},{5,3},{6,0},{7,1},{8,14},{9,15},{10,... | collective-permute-start | bytes 860168 | tf_op jit(solution)/shard_map/ppermute | solution.py:28
  32.4 23.9 %collective-permute-start.15 = (bf16[40,3584]{1,0:T(8,128)(2,1)S(1)}, bf16[40,3584]{1,0:T(8,128)(2,1)S(1)}, u32[]{:S(2)}, u32[]{:S(2)}) collective-permute-start(bf16[40,3584]{1,0:T(8,128)(2,1)S(1)} %get-tuple-element.63), channel_id=1, source_target_pairs={{0,2},{1,3},{2,0},{3,1},{4,6},{5,7},{6,4},{7,5},{8,10},{9,11},{10,... | collective-permute-start | bytes 860168 | tf_op jit(solution)/shard_map/ppermute | solution.py:28
  33.8 24.0 %collective-permute-start.16 = (bf16[40,3584]{1,0:T(8,128)(2,1)S(1)}, bf16[40,3584]{1,0:T(8,128)(2,1)S(1)}, u32[]{:S(2)}, u32[]{:S(2)}) collective-permute-start(bf16[40,3584]{1,0:T(8,128)(2,1)S(1)} %get-tuple-element.64), channel_id=1, source_target_pairs={{0,4},{1,5},{2,6},{3,7},{4,0},{5,1},{6,2},{7,3},{8,12},{9,13},{10,... | collective-permute-start | bytes 860168 | tf_op jit(solution)/shard_map/ppermute | solution.py:28
  38.0 19.7 %collective-permute-start.17 = (bf16[40,3584]{1,0:T(8,128)(2,1)S(1)}, bf16[40,3584]{1,0:T(8,128)(2,1)S(1)}, u32[]{:S(2)}, u32[]{:S(2)}) collective-permute-start(bf16[40,3584]{1,0:T(8,128)(2,1)S(1)} %get-tuple-element.65), channel_id=1, source_target_pairs={{0,6},{1,7},{2,4},{3,5},{4,2},{5,3},{6,0},{7,1},{8,14},{9,15},{10,... | collective-permute-start | bytes 860168 | tf_op jit(solution)/shard_map/ppermute | solution.py:28
  54.2 14.3 %collective-permute-start.9 = (bf16[40,3584]{1,0:T(8,128)(2,1)S(1)}, bf16[40,3584]{1,0:T(8,128)(2,1)S(1)}, u32[]{:S(2)}, u32[]{:S(2)}) collective-permute-start(bf16[40,3584]{1,0:T(8,128)(2,1)S(1)} %get-tuple-element.54), channel_id=1, source_target_pairs={{0,2},{1,3},{2,0},{3,1},{4,6},{5,7},{6,4},{7,5},{8,10},{9,11},{10,... | collective-permute-start | bytes 860168 | tf_op jit(solution)/shard_map/ppermute | solution.py:28
  55.2 14.6 %collective-permute-start.10 = (bf16[40,3584]{1,0:T(8,128)(2,1)S(1)}, bf16[40,3584]{1,0:T(8,128)(2,1)S(1)}, u32[]{:S(2)}, u32[]{:S(2)}) collective-permute-start(bf16[40,3584]{1,0:T(8,128)(2,1)S(1)} %get-tuple-element.55), channel_id=1, source_target_pairs={{0,4},{1,5},{2,6},{3,7},{4,0},{5,1},{6,2},{7,3},{8,12},{9,13},{10,... | collective-permute-start | bytes 860168 | tf_op jit(solution)/shard_map/ppermute | solution.py:28
  56.3 13.8 %collective-permute-start.11 = (bf16[40,3584]{1,0:T(8,128)(2,1)S(1)}, bf16[40,3584]{1,0:T(8,128)(2,1)S(1)}, u32[]{:S(2)}, u32[]{:S(2)}) collective-permute-start(bf16[40,3584]{1,0:T(8,128)(2,1)S(1)} %get-tuple-element.56), channel_id=1, source_target_pairs={{0,6},{1,7},{2,4},{3,5},{4,2},{5,3},{6,0},{7,1},{8,14},{9,15},{10,... | collective-permute-start | bytes 860168 | tf_op jit(solution)/shard_map/ppermute | solution.py:28
  57.7 13.0 %copy-start = (bf16[1,3584,512]{2,1,0:T(8,128)(2,1)S(1)}, bf16[1,3584,512]{2,1,0:T(8,128)(2,1)}, u32[]{:S(2)}) copy-start(bf16[1,3584,512]{2,1,0:T(8,128)(2,1)} %refs_0_.5) | copy-start | bytes 11010052
  66.3 11.6 %collective-permute-start.18 = (bf16[40,1792]{1,0:T(8,128)(2,1)S(1)}, bf16[40,1792]{1,0:T(8,128)(2,1)S(1)}, u32[]{:S(2)}, u32[]{:S(2)}) collective-permute-start(bf16[40,1792]{1,0:T(8,128)(2,1)S(1)} %get-tuple-element.69), channel_id=1, source_target_pairs={{0,2},{1,3},{2,0},{3,1},{4,6},{5,7},{6,4},{7,5},{8,10},{9,11},{10,... | collective-permute-start | bytes 430088 | tf_op jit(solution)/shard_map/ppermute | solution.py:28
  67.4 12.1 %collective-permute-start.19 = (bf16[40,1792]{1,0:T(8,128)(2,1)S(1)}, bf16[40,1792]{1,0:T(8,128)(2,1)S(1)}, u32[]{:S(2)}, u32[]{:S(2)}) collective-permute-start(bf16[40,1792]{1,0:T(8,128)(2,1)S(1)} %get-tuple-element.70), channel_id=1, source_target_pairs={{0,4},{1,5},{2,6},{3,7},{4,0},{5,1},{6,2},{7,3},{8,12},{9,13},{10,... | collective-permute-start | bytes 430088 | tf_op jit(solution)/shard_map/ppermute | solution.py:28
  68.4 12.8 %collective-permute-start.20 = (bf16[40,1792]{1,0:T(8,128)(2,1)S(1)}, bf16[40,1792]{1,0:T(8,128)(2,1)S(1)}, u32[]{:S(2)}, u32[]{:S(2)}) collective-permute-start(bf16[40,1792]{1,0:T(8,128)(2,1)S(1)} %get-tuple-element.71), channel_id=1, source_target_pairs={{0,6},{1,7},{2,4},{3,5},{4,2},{5,3},{6,0},{7,1},{8,14},{9,15},{10,... | collective-permute-start | bytes 430088 | tf_op jit(solution)/shard_map/ppermute | solution.py:28
  75.9 8.6 %collective-permute-start.24 = (bf16[40,1792]{1,0:T(8,128)(2,1)S(1)}, bf16[40,1792]{1,0:T(8,128)(2,1)S(1)}, u32[]{:S(2)}, u32[]{:S(2)}) collective-permute-start(bf16[40,1792]{1,0:T(8,128)(2,1)S(1)} %get-tuple-element.79), channel_id=1, source_target_pairs={{0,2},{1,3},{2,0},{3,1},{4,6},{5,7},{6,4},{7,5},{8,10},{9,11},{10,... | collective-permute-start | bytes 430088 | tf_op jit(solution)/shard_map/ppermute | solution.py:28
  77.7 8.1 %collective-permute-start.25 = (bf16[40,1792]{1,0:T(8,128)(2,1)S(1)}, bf16[40,1792]{1,0:T(8,128)(2,1)S(1)}, u32[]{:S(2)}, u32[]{:S(2)}) collective-permute-start(bf16[40,1792]{1,0:T(8,128)(2,1)S(1)} %get-tuple-element.80), channel_id=1, source_target_pairs={{0,4},{1,5},{2,6},{3,7},{4,0},{5,1},{6,2},{7,3},{8,12},{9,13},{10,... | collective-permute-start | bytes 430088 | tf_op jit(solution)/shard_map/ppermute | solution.py:28
  77.9 8.0 %collective-permute-start.26 = (bf16[40,1792]{1,0:T(8,128)(2,1)S(1)}, bf16[40,1792]{1,0:T(8,128)(2,1)S(1)}, u32[]{:S(2)}, u32[]{:S(2)}) collective-permute-start(bf16[40,1792]{1,0:T(8,128)(2,1)S(1)} %get-tuple-element.81), channel_id=1, source_target_pairs={{0,6},{1,7},{2,4},{3,5},{4,2},{5,3},{6,0},{7,1},{8,14},{9,15},{10,... | collective-permute-start | bytes 430088 | tf_op jit(solution)/shard_map/ppermute | solution.py:28
  79.5 14.6 %collective-permute-start.12 = (bf16[16,3584]{1,0:T(8,128)(2,1)S(1)}, bf16[16,3584]{1,0:T(8,128)(2,1)S(1)}, u32[]{:S(2)}, u32[]{:S(2)}) collective-permute-start(bf16[16,3584]{1,0:T(8,128)(2,1)S(1)} %get-tuple-element.58), channel_id=1, source_target_pairs={{0,8},{1,9},{2,10},{3,11},{4,12},{5,13},{6,14},{7,15},{8,0},{9,1},... | collective-permute-start | bytes 344072 | tf_op jit(solution)/shard_map/ppermute | solution.py:28
  81.3 12.9 %collective-permute-start.13 = (bf16[16,3584]{1,0:T(8,128)(2,1)S(1)}, bf16[16,3584]{1,0:T(8,128)(2,1)S(1)}, u32[]{:S(2)}, u32[]{:S(2)}) collective-permute-start(bf16[16,3584]{1,0:T(8,128)(2,1)S(1)} %get-tuple-element.59), channel_id=1, source_target_pairs={{0,16},{1,17},{2,18},{3,19},{4,20},{5,21},{6,22},{7,23},{8,24},{9,... | collective-permute-start | bytes 344072 | tf_op jit(solution)/shard_map/ppermute | solution.py:28
  84.5 12.9 %collective-permute-start.14 = (bf16[16,3584]{1,0:T(8,128)(2,1)S(1)}, bf16[16,3584]{1,0:T(8,128)(2,1)S(1)}, u32[]{:S(2)}, u32[]{:S(2)}) collective-permute-start(bf16[16,3584]{1,0:T(8,128)(2,1)S(1)} %get-tuple-element.60), channel_id=1, source_target_pairs={{0,24},{1,25},{2,26},{3,27},{4,28},{5,29},{6,30},{7,31},{8,16},{9,... | collective-permute-start | bytes 344072 | tf_op jit(solution)/shard_map/ppermute | solution.py:28
  85.8 7.2 %collective-permute-start.21 = (bf16[16,1792]{1,0:T(8,128)(2,1)S(1)}, bf16[16,1792]{1,0:T(8,128)(2,1)S(1)}, u32[]{:S(2)}, u32[]{:S(2)}) collective-permute-start(bf16[16,1792]{1,0:T(8,128)(2,1)S(1)} %get-tuple-element.73), channel_id=1, source_target_pairs={{0,8},{1,9},{2,10},{3,11},{4,12},{5,13},{6,14},{7,15},{8,0},{9,1},... | collective-permute-start | bytes 172040 | tf_op jit(solution)/shard_map/ppermute | solution.py:28
  85.9 13.3 %collective-permute-start.22 = (bf16[16,1792]{1,0:T(8,128)(2,1)S(1)}, bf16[16,1792]{1,0:T(8,128)(2,1)S(1)}, u32[]{:S(2)}, u32[]{:S(2)}) collective-permute-start(bf16[16,1792]{1,0:T(8,128)(2,1)S(1)} %get-tuple-element.74), channel_id=1, source_target_pairs={{0,16},{1,17},{2,18},{3,19},{4,20},{5,21},{6,22},{7,23},{8,24},{9,... | collective-permute-start | bytes 172040 | tf_op jit(solution)/shard_map/ppermute | solution.py:28
  93.0 6.2 %collective-permute-start.23 = (bf16[16,1792]{1,0:T(8,128)(2,1)S(1)}, bf16[16,1792]{1,0:T(8,128)(2,1)S(1)}, u32[]{:S(2)}, u32[]{:S(2)}) collective-permute-start(bf16[16,1792]{1,0:T(8,128)(2,1)S(1)} %get-tuple-element.75), channel_id=1, source_target_pairs={{0,24},{1,25},{2,26},{3,27},{4,28},{5,29},{6,30},{7,31},{8,16},{9,... | collective-permute-start | bytes 172040 | tf_op jit(solution)/shard_map/ppermute | solution.py:28
  94.1 5.1 %collective-permute-start.27 = (bf16[16,1792]{1,0:T(8,128)(2,1)S(1)}, bf16[16,1792]{1,0:T(8,128)(2,1)S(1)}, u32[]{:S(2)}, u32[]{:S(2)}) collective-permute-start(bf16[16,1792]{1,0:T(8,128)(2,1)S(1)} %get-tuple-element.83), channel_id=1, source_target_pairs={{0,8},{1,9},{2,10},{3,11},{4,12},{5,13},{6,14},{7,15},{8,0},{9,1},... | collective-permute-start | bytes 172040 | tf_op jit(solution)/shard_map/ppermute | solution.py:28
  94.1 5.5 %collective-permute-start.28 = (bf16[16,1792]{1,0:T(8,128)(2,1)S(1)}, bf16[16,1792]{1,0:T(8,128)(2,1)S(1)}, u32[]{:S(2)}, u32[]{:S(2)}) collective-permute-start(bf16[16,1792]{1,0:T(8,128)(2,1)S(1)} %get-tuple-element.84), channel_id=1, source_target_pairs={{0,16},{1,17},{2,18},{3,19},{4,20},{5,21},{6,22},{7,23},{8,24},{9,... | collective-permute-start | bytes 172040 | tf_op jit(solution)/shard_map/ppermute | solution.py:28
  97.4 6.0 %collective-permute-start.29 = (bf16[16,1792]{1,0:T(8,128)(2,1)S(1)}, bf16[16,1792]{1,0:T(8,128)(2,1)S(1)}, u32[]{:S(2)}, u32[]{:S(2)}) collective-permute-start(bf16[16,1792]{1,0:T(8,128)(2,1)S(1)} %get-tuple-element.85), channel_id=1, source_target_pairs={{0,24},{1,25},{2,26},{3,27},{4,28},{5,29},{6,30},{7,31},{8,16},{9,... | collective-permute-start | bytes 172040 | tf_op jit(solution)/shard_map/ppermute | solution.py:28

commit v7 on v5

--- a/solution.py
+++ b/solution.py
@@ -15,6 +15,7 @@
 PIECES = 3
 VMEM_LIMIT = 16 * 1024 * 1024
 VMEM_LIMIT_EXPERT = 48 * 1024 * 1024
+VMEM_LIMIT_ALL = 58 * 1024 * 1024
 
 
 def swap(value, offset):
@@ -26,11 +27,6 @@
     return lax.optimization_barrier((value, *others))[0]
 
 
-def double(held, offset, wait):
-    ready = {at: after(value, wait) for at, value in held.items()}
-    return held | {at ^ offset: swap(value, offset) for at, value in ready.items()}
-
-
 def padded(count):
     return -(-count // LANES) * LANES
 
@@ -40,8 +36,7 @@
 
 
 def column_chunks(width):
-    step = chunk_of(width)
-    return [slice(at, at + step) for at in range(0, width, step)]
+    return [slice(at, at + chunk_of(width)) for at in range(0, width, chunk_of(width))]
 
 
 def call(body, outs, args, flops=0, scratch=(), in_specs=None, limit=VMEM_LIMIT):
@@ -58,15 +53,25 @@
     )(*args)
 
 
-def code_kernel(experts, tokens, ids, gates, out):
+def streams(triples):
+    copies = [pltpu.make_async_copy(*triple) for triple in triples]
+    for copy in copies:
+        copy.start()
+    return copies
+
+
+def await_place(place, sem):
+    pltpu.make_async_copy(place, place, sem).wait()
+
+
+def code_kernel(experts, tokens_in, ids_in, gates_in, out, tokens, ids, gates, sems):
     rows, width = tokens.shape
-    for at in range(0, width, LANES):
-        block = tokens[:, at : at + LANES].astype(f32)
-        scale = jnp.max(jnp.abs(block), axis=1, keepdims=True) + 1e-06
-        scale = scale.astype(bf16).astype(f32)
-        quantized = (block / scale).astype(bf16).astype(f32)
-        out[:, at : at + LANES] = (quantized * scale).astype(bf16)
-    line = lax.broadcasted_iota(jnp.int32, (out.shape[1] - width, rows), 0)
+    sources, places = (ids_in, gates_in, tokens_in), (ids, gates, tokens)
+    copies = streams(zip(sources, places, (sems.at[number] for number in range(3))))
+    gate_width = out.shape[1] - width
+    copies[0].wait()
+    copies[1].wait()
+    line = lax.broadcasted_iota(jnp.int32, (gate_width, rows), 0)
     rest = jnp.zeros(line.shape, f32)
     for k in range(ids.shape[0]):
         rest = jnp.where(ids[k : k + 1] == line % experts, gates[k : k + 1], rest)
@@ -76,6 +81,13 @@
         columns = jnp.where(line // experts == number, piece, columns)
         rest = rest - piece
     out[:, width:] = columns.T.astype(bf16)
+    copies[2].wait()
+    for at in range(0, width, LANES):
+        block = tokens[:, at : at + LANES].astype(f32)
+        scale = jnp.max(jnp.abs(block), axis=1, keepdims=True) + 1e-06
+        scale = scale.astype(bf16).astype(f32)
+        quantized = (block / scale).astype(bf16).astype(f32)
+        out[:, at : at + LANES] = (quantized * scale).astype(bf16)
 
 
 def pack_tokens_kernel(experts, capacity, chip, *refs):
@@ -167,51 +179,44 @@
         out[:, part] = total.astype(bf16)
 
 
-def streams(pairs, sems):
-    copies = [
-        pltpu.make_async_copy(source, place, sems.at[number])
-        for number, (source, place) in enumerate(pairs)
-    ]
-    for copy in copies:
-        copy.start()
-    return copies
-
-
 def forward_kernel(tile, x0, x1, x2, x3, *refs):
     *slabs, o0, o1, o2, o3, for_up, for_gate, x, hidden, into, back, sems = refs
     rows, width = x.shape
     units = back.shape[0] // 2
-    chunk, tiles = chunk_of(width), 2 * units // tile
-    pairs = []
+    chunk, tiles, chunks = chunk_of(width), 2 * units // tile, width // chunk_of(width)
+    triples = []
     for number in range(tiles):
         slab, at = divmod(number * tile, units)
         for half, source in enumerate(slabs[3 * slab : 3 * slab + 2]):
             place = into.at[:, pl.ds((2 * number + half) * tile, tile)]
-            pairs.append((source.at[0, :, pl.ds(at, tile)], place))
-    for at in range(0, width, chunk):
+            triples.append((source.at[0, :, pl.ds(at, tile)], place, sems.at[number]))
+    for number in range(chunks):
+        columns = pl.ds(number * chunk, chunk)
         for slab in range(2):
-            place = back.at[pl.ds(slab * units, units), pl.ds(at, chunk)]
-            pairs.append((slabs[3 * slab + 2].at[0, :, pl.ds(at, chunk)], place))
-    copies = iter(streams(pairs, sems))
+            place = back.at[pl.ds(slab * units, units), columns]
+            source = slabs[3 * slab + 2].at[0, :, columns]
+            triples.append((source, place, sems.at[tiles + number]))
+    streams(triples)
     for part in column_chunks(width):
         x[:, part] = joined((x0, x1, x2, x3), part, rows)
 
-    for number in range(tiles):
-        next(copies).wait()
-        next(copies).wait()
-        columns = slice(2 * number * tile, 2 * (number + 1) * tile)
+    @pl.loop(0, tiles)
+    def _(number):
+        columns = pl.ds(pl.multiple_of(number * 2 * tile, 2 * tile), 2 * tile)
+        await_place(into.at[:, columns], sems.at[number])
         pre = jnp.dot(x[...], into[:, columns], preferred_element_type=f32)
         pre_gate, pre_up = pre[:, :tile], pre[:, tile:]
         sigma = jax.nn.sigmoid(pre_gate)
         activated = pre_gate * sigma
-        at = slice(number * tile, (number + 1) * tile)
+        at = pl.ds(pl.multiple_of(number * tile, tile), tile)
         hidden[:, at] = (activated * pre_up).astype(bf16)
         for_up[:, at] = activated
         for_gate[:, at] = pre_up * sigma * (1.0 + pre_gate * (1.0 - sigma))
 
-    for part in column_chunks(width):
-        next(copies).wait()
-        next(copies).wait()
+    @pl.loop(0, chunks)
+    def _(number):
+        part = pl.ds(pl.multiple_of(number * chunk, chunk), chunk)
+        await_place(back.at[:, part], sems.at[tiles + number])
         total = jnp.dot(hidden[...], back[:, part], preferred_element_type=f32)
         store_packed(total, (o0, o1, o2, o3), part)
 
@@ -226,29 +231,34 @@
     *slabs, o0, o1, o2, o3, x, grads, into, back, sems = refs
     rows, width = x.shape
     units = back.shape[0] // 2
-    chunk = chunk_of(width)
-    pairs = []
+    chunk, chunks = chunk_of(width), width // chunk_of(width)
+    triples = []
     for slab in range(2):
-        pairs.append((slabs[3 * slab + 2].at[0], back.at[pl.ds(slab * units, units)]))
-    for at in range(0, width, chunk):
-        for number, matrix in enumerate((0, 1, 3, 4)):
-            place = into.at[pl.ds(at, chunk), pl.ds(number * units, units)]
-            pairs.append((slabs[matrix].at[0, pl.ds(at, chunk)], place))
-    copies = iter(streams(pairs, sems))
+        place = back.at[pl.ds(slab * units, units)]
+        triples.append((slabs[3 * slab + 2].at[0], place, sems.at[slab]))
+    for number in range(chunks):
+        lines = pl.ds(number * chunk, chunk)
+        for column, matrix in enumerate((0, 1, 3, 4)):
+            place = into.at[lines, pl.ds(column * units, units)]
+            triples.append((slabs[matrix].at[0, lines], place, sems.at[2 + number]))
+    streams(triples)
     for part in column_chunks(width):
         x[:, part] = joined((x0, x1, x2, x3), part, rows)
 
-    for slab in range(2):
-        next(copies).wait()
-        at = slice(slab * units, (slab + 1) * units)
+    @pl.loop(0, 2)
+    def _(slab):
+        at = pl.ds(pl.multiple_of(slab * units, units), units)
+        await_place(back.at[at], sems.at[slab])
         hidden_grad = lax.dot_general(x[...], back[at], CONTRACT_COLS, preferred_element_type=f32)
-        start = 2 * slab * units
-        grads[:, start : start + units] = (hidden_grad * for_gate[:, at]).astype(bf16)
-        grads[:, start + units : start + 2 * units] = (hidden_grad * for_up[:, at]).astype(bf16)
-
-    for part in column_chunks(width):
-        for _ in range(4):
-            next(copies).wait()
+        start = pl.multiple_of(2 * slab * units, 2 * units)
+        gate_at, up_at = pl.ds(start, units), pl.ds(start + units, units)
+        grads[:, gate_at] = (hidden_grad * for_gate[:, at]).astype(bf16)
+        grads[:, up_at] = (hidden_grad * for_up[:, at]).astype(bf16)
+
+    @pl.loop(0, chunks)
+    def _(number):
+        part = pl.ds(pl.multiple_of(number * chunk, chunk), chunk)
+        await_place(into.at[part], sems.at[2 + number])
         total = lax.dot_general(
             grads[...], into[part], CONTRACT_COLS, preferred_element_type=f32
         )
@@ -269,20 +279,28 @@
     shape = jax.ShapeDtypeStruct
     packed_shapes = [shape((taken, width), bf16)] * len(PLANE)
 
+    own = (gate_weight, up_weight, down_weight)
+    other = tuple(swap(slab, CORE) for slab in own)
+
+    in_place = pl.BlockSpec(memory_space=pl.ANY)
     (coded,) = call(
         functools.partial(code_kernel, experts),
         [shape((tok_dev, width + padded(PIECES * experts)), bf16)],
         (tokens, expert_ids.T, gate_values.T),
-    )
-    held, cots = {0: coded}, {0: cotangent}
-    offset = devices // 2
-    while offset > FAR:
-        cots = double(cots, offset, cotangent)
-        held = double(held, offset, coded)
+        in_specs=[in_place] * 3,
+        scratch=[
+            pltpu.VMEM((tok_dev, width), bf16),
+            pltpu.VMEM((top, tok_dev), jnp.int32),
+            pltpu.VMEM((top, tok_dev), f32),
+            pltpu.SemaphoreType.DMA((3,)),
+        ],
+        limit=VMEM_LIMIT_ALL,
+    )
+    held, offset = {0: coded}, devices // 2
+    while offset >= FAR:
+        held.update({at ^ offset: swap(value, offset) for at, value in held.items()})
         offset //= 2
-    held = double(held, FAR, cots[max(cots)])
     held = [held[at] for at in sorted(held)]
-    gate_other, up_other = swap(gate_weight, CORE), swap(up_weight, CORE)
 
     whole = pl.BlockSpec(memory_space=pltpu.VMEM)
     *packed, by_row, by_slot = call(
@@ -292,12 +310,15 @@
         in_specs=[pl.BlockSpec(memory_space=pltpu.SMEM)] + [whole] * blocks,
         flops=2 * rows * slots * width,
     )
+    packed = [after(value, *other[:2]) for value in packed]
     x = [packed[0]] + [swap(value, offset) for value, offset in zip(packed[1:], PLANE[1:])]
 
-    down_other = swap(after(down_weight, gate_other, up_other, packed[0]), CORE)
-    own = (gate_weight, up_weight, down_weight)
-    other = (gate_other, up_other, down_other)
-    cots = double(cots, FAR, packed[0])
+    cots, offset = {0: after(cotangent, held[blocks // 2])}, devices // 2
+    while offset >= FAR:
+        wait = other[2] if offset == FAR else cotangent
+        ready = {at: after(value, wait) for at, value in cots.items()}
+        cots.update({at ^ offset: swap(value, offset) for at, value in ready.items()})
+        offset //= 2
     cots = [cots[at] for at in sorted(cots)]
 
     packed = call(
@@ -309,7 +330,6 @@
     grads = [packed[0]] + [swap(value, offset) for value, offset in zip(packed[1:], PLANE[1:])]
 
     all_taken = len(PLANE) * taken
-    in_place = pl.BlockSpec(memory_space=pl.ANY)
     tile = 256 if hidden % 256 == 0 else LANES
     tiles, chunks = 2 * hidden // tile, width // chunk_of(width)
     slab_room = [pltpu.VMEM((width, 4 * hidden), bf16), pltpu.VMEM((2 * hidden, width), bf16)]
@@ -325,7 +345,7 @@
             pltpu.VMEM((all_taken, width), bf16),
             pltpu.VMEM((all_taken, 2 * hidden), bf16),
             *slab_room,
-            pltpu.SemaphoreType.DMA((2 * tiles + 2 * chunks,)),
+            pltpu.SemaphoreType.DMA((tiles + chunks,)),
         ],
     )
 
@@ -353,7 +373,7 @@
             pltpu.VMEM((all_taken, width), bf16),
             pltpu.VMEM((all_taken, 4 * hidden), bf16),
             *slab_room,
-            pltpu.SemaphoreType.DMA((2 + 4 * chunks,)),
+            pltpu.SemaphoreType.DMA((2 + chunks,)),
         ],
     )
     token_grad = go_home(backs, False)

time: 97.2 us -> 88.9 us (0.915)
  waiting for transfers between devices: 30 us -> 24.4 us
  local copies, waits for them, and re-layouts: 5.09 us -> 1.8 us
  Pallas kernels: 23.6 us -> 25 us
    ppermute x27, waiting for transfers between devices: 30 us -> 24.4 us  [swap(): lax.ppermute(value, 'expert', [(i, i ^ offset) for i in range(devices)])]
    unnamed x10 -> x4, local copies, waits for them, and re-layouts: 5.09 us -> 1.8 us
    pallas_call x9, Pallas kernels: 23.6 us -> 25 us  [call(): pl.pallas_call(body, out_shape=outs, in_specs=[whole] * len(args) if in_s...]
  transfers between devices with their start and end apart: 27 -> 27, of which waited for: 10 -> 8; matrix products, arithmetic and copies ran while one was open for 0% -> 0% of each run, Pallas kernels for 24% -> 27%
where the time goes in v7:
time: 88.9 us; the launch traced here: 88.7 us
  starting transfers between devices  36.7 us (41%)
  Pallas kernels  25 us (28%)
  waiting for transfers between devices  24.4 us (27%)
  local copies, waits for them, and re-layouts  1.8 us (2%)
    ppermute x27, starting transfers between devices, swap(): lax.ppermute(value, 'expert', [(i, i ^ offset) for i in range(devices)])  36.7 us
    pallas_call x9, Pallas kernels, call(): pl.pallas_call(body, out_shape=outs, in_specs=[whole] * len(args) if in_s...  25 us
    ppermute x27, waiting for transfers between devices, swap(): lax.ppermute(value, 'expert', [(i, i ^ offset) for i in range(devices)])  24.4 us
    unnamed x4, local copies, waits for them, and re-layouts  1.8 us
  transfers between devices with their start and end apart: 27, of which 8 were waited for; matrix products, arithmetic and copies ran while one was open for 0% of the time, Pallas kernels for 27%

profile of v7, /device:TPU:0, one launch (start us, length us, event | category | flops | bytes accessed | tf_op | source)
XLA Modules:
  0.0 88.7 jit_solution(3210695947935334925)
XLA Ops:
  0.6 0.5 collective-permute-start.3
  1.1 0.1 collective-permute-start.4
  1.2 0.4 collective-permute-start.8
  1.7 1.7 %shard_map.86.refs_0_ = bf16[16,3712]{1,0:T(8,128)(2,1)} custom-call(bf16[16,3584]{1,0:T(8,128)(2,1)} %tokens_in.1, s32[8,16]{1,0:T(8,128)} %bitcast.3, f32[8,16]{1,0:T(8,128)} %bitcast.4), custom_call_target="tpu_custom_call" | custom-call | bytes 234496 | tf_op jit(solution)/shard_map/pallas_call | solution.py:45
  3.4 3.7 %collective-permute-start.1 = (bf16[16,3712]{1,0:T(8,128)(2,1)}, bf16[16,3712]{1,0:T(8,128)(2,1)S(1)}, u32[]{:S(2)}, u32[]{:S(2)}) collective-permute-start(bf16[16,3712]{1,0:T(8,128)(2,1)} %shard_map.86.refs_0_), channel_id=1, source_target_pairs={{0,16},{1,17},{2,18},{3,19},{4,20},{5,21},{6,22},{7,23},{8,24},{9,... | collective-permute-start | bytes 356360 | tf_op jit(solution)/shard_map/ppermute | solution.py:23
  7.1 1.6 %collective-permute-start = (bf16[16,3712]{1,0:T(8,128)(2,1)}, bf16[16,3712]{1,0:T(8,128)(2,1)S(1)}, u32[]{:S(2)}, u32[]{:S(2)}) collective-permute-start(bf16[16,3712]{1,0:T(8,128)(2,1)} %shard_map.86.refs_0_), channel_id=1, source_target_pairs={{0,8},{1,9},{2,10},{3,11},{4,12},{5,13},{6,14},{7,15},{8,0},{9,1},... | collective-permute-start | bytes 356360 | tf_op jit(solution)/shard_map/ppermute | solution.py:23
  8.7 5.1 %collective-permute-done.1.refs_2_ = bf16[16,3712]{1,0:T(8,128)(2,1)S(1)} collective-permute-done((bf16[16,3712]{1,0:T(8,128)(2,1)}, bf16[16,3712]{1,0:T(8,128)(2,1)S(1)}, u32[]{:S(2)}, u32[]{:S(2)}) %collective-permute-start.1) | collective-permute-done | bytes 118816 | tf_op jit(solution)/shard_map/ppermute | solution.py:23
  13.8 0.7 collective-permute-start.2
  14.6 0.0 collective-permute-done.refs_1_
  14.6 4.1 %collective-permute-done.2.refs_3_ = bf16[16,3712]{1,0:T(8,128)(2,1)S(1)} collective-permute-done((bf16[16,3712]{1,0:T(8,128)(2,1)S(1)}, bf16[16,3712]{1,0:T(8,128)(2,1)S(1)}, u32[]{:S(2)}, u32[]{:S(2)}) %collective-permute-start.2) | collective-permute-done | bytes 118816 | tf_op jit(solution)/shard_map/ppermute | solution.py:23
  18.7 0.9 %copy-done = bf16[16,3712]{1,0:T(8,128)(2,1)S(1)} copy-done((bf16[16,3712]{1,0:T(8,128)(2,1)S(1)}, bf16[16,3712]{1,0:T(8,128)(2,1)}, u32[]{:S(2)}) %copy-start) | copy-done | bytes 118808
  19.6 1.0 %shard_map.87 = (bf16[40,3584]{1,0:T(8,128)(2,1)S(1)}, bf16[40,3584]{1,0:T(8,128)(2,1)S(1)}, bf16[40,3584]{1,0:T(8,128)(2,1)S(1)}, bf16[40,3584]{1,0:T(8,128)(2,...) custom-call(s32[1]{0:T(128)} %bitcast.chip, bf16[16,3712]{1,0:T(8,128)(2,1)S(1)} %copy-done, ...), custom_call_target="tpu_custom_call" | custom-call | flops 117440512 | bytes 1753092 | tf_op jit(solution)/shard_map/pallas_call | solution.py:45
  20.7 1.6 %collective-permute-start.5 = (bf16[40,3584]{1,0:T(8,128)(2,1)S(1)}, bf16[40,3584]{1,0:T(8,128)(2,1)S(1)}, u32[]{:S(2)}, u32[]{:S(2)}) collective-permute-start(bf16[40,3584]{1,0:T(8,128)(2,1)S(1)} %get-tuple-element.42), channel_id=1, source_target_pairs={{0,2},{1,3},{2,0},{3,1},{4,6},{5,7},{6,4},{7,5},{8,10},{9,11},{10,... | collective-permute-start | bytes 860168 | tf_op jit(solution)/shard_map/ppermute | solution.py:23
  22.2 1.5 %collective-permute-start.6 = (bf16[40,3584]{1,0:T(8,128)(2,1)S(1)}, bf16[40,3584]{1,0:T(8,128)(2,1)S(1)}, u32[]{:S(2)}, u32[]{:S(2)}) collective-permute-start(bf16[40,3584]{1,0:T(8,128)(2,1)S(1)} %get-tuple-element.44), channel_id=1, source_target_pairs={{0,4},{1,5},{2,6},{3,7},{4,0},{5,1},{6,2},{7,3},{8,12},{9,13},{10,... | collective-permute-start | bytes 860168 | tf_op jit(solution)/shard_map/ppermute | solution.py:23
  23.8 0.5 collective-permute-start.7
  24.2 2.6 %collective-permute-start.16 = (bf16[16,3584]{1,0:T(8,128)(2,1)}, bf16[16,3584]{1,0:T(8,128)(2,1)S(1)}, u32[]{:S(2)}, u32[]{:S(2)}) collective-permute-start(bf16[16,3584]{1,0:T(8,128)(2,1)} %refs_0_.3), channel_id=1, source_target_pairs={{0,16},{1,17},{2,18},{3,19},{4,20},{5,21},{6,22},{7,23},{8,24},{9,... | collective-permute-start | bytes 344072 | tf_op jit(solution)/shard_map/ppermute | solution.py:23
  26.8 1.8 %collective-permute-start.15 = (bf16[16,3584]{1,0:T(8,128)(2,1)}, bf16[16,3584]{1,0:T(8,128)(2,1)S(1)}, u32[]{:S(2)}, u32[]{:S(2)}) collective-permute-start(bf16[16,3584]{1,0:T(8,128)(2,1)} %refs_0_.3), channel_id=1, source_target_pairs={{0,8},{1,9},{2,10},{3,11},{4,12},{5,13},{6,14},{7,15},{8,0},{9,1},... | collective-permute-start | bytes 344072 | tf_op jit(solution)/shard_map/ppermute | solution.py:23
  28.6 3.1 %collective-permute-done.16.refs_2_ = bf16[16,3584]{1,0:T(8,128)(2,1)S(1)} collective-permute-done((bf16[16,3584]{1,0:T(8,128)(2,1)}, bf16[16,3584]{1,0:T(8,128)(2,1)S(1)}, u32[]{:S(2)}, u32[]{:S(2)}) %collective-permute-start.16) | collective-permute-done | bytes 114720 | tf_op jit(solution)/shard_map/ppermute | solution.py:23
  31.6 0.7 collective-permute-start.17
  32.3 0.0 collective-permute-done.15.refs_1_
  32.3 4.1 %collective-permute-done.17.refs_3_ = bf16[16,3584]{1,0:T(8,128)(2,1)S(1)} collective-permute-done((bf16[16,3584]{1,0:T(8,128)(2,1)S(1)}, bf16[16,3584]{1,0:T(8,128)(2,1)S(1)}, u32[]{:S(2)}, u32[]{:S(2)}) %collective-permute-start.17) | collective-permute-done | bytes 114720 | tf_op jit(solution)/shard_map/ppermute | solution.py:23
  36.4 0.9 %copy-done.1 = bf16[16,3584]{1,0:T(8,128)(2,1)S(1)} copy-done((bf16[16,3584]{1,0:T(8,128)(2,1)S(1)}, bf16[16,3584]{1,0:T(8,128)(2,1)}, u32[]{:S(2)}) %copy-start.1) | copy-done | bytes 114712
  37.3 0.6 shard_map.91
  37.9 1.6 %collective-permute-start.18 = (bf16[40,3584]{1,0:T(8,128)(2,1)S(1)}, bf16[40,3584]{1,0:T(8,128)(2,1)S(1)}, u32[]{:S(2)}, u32[]{:S(2)}) collective-permute-start(bf16[40,3584]{1,0:T(8,128)(2,1)S(1)} %get-tuple-element.61), channel_id=1, source_target_pairs={{0,2},{1,3},{2,0},{3,1},{4,6},{5,7},{6,4},{7,5},{8,10},{9,11},{10,... | collective-permute-start | bytes 860168 | tf_op jit(solution)/shard_map/ppermute | solution.py:23
  39.5 1.5 %collective-permute-start.19 = (bf16[40,3584]{1,0:T(8,128)(2,1)S(1)}, bf16[40,3584]{1,0:T(8,128)(2,1)S(1)}, u32[]{:S(2)}, u32[]{:S(2)}) collective-permute-start(bf16[40,3584]{1,0:T(8,128)(2,1)S(1)} %get-tuple-element.62), channel_id=1, source_target_pairs={{0,4},{1,5},{2,6},{3,7},{4,0},{5,1},{6,2},{7,3},{8,12},{9,13},{10,... | collective-permute-start | bytes 860168 | tf_op jit(solution)/shard_map/ppermute | solution.py:23
  41.0 0.5 collective-permute-start.20
  41.5 8.5 %shard_map.88 = (bf16[40,3584]{1,0:T(8,128)(2,1)S(1)}, bf16[40,3584]{1,0:T(8,128)(2,1)S(1)}, bf16[40,3584]{1,0:T(8,128)(2,1)S(1)}, bf16[40,3584]{1,0:T(8,128)(2,...) custom-call(bf16[40,3584]{1,0:T(8,128)(2,1)S(1)} %get-tuple-element.40.x0, ...), custom_call_target="tpu_custom_call" | custom-call | flops 3523215360 | bytes 25624576 | tf_op jit(solution)/shard_map/pallas_call | solution.py:45
  50.1 1.6 %collective-permute-start.9 = (bf16[40,3584]{1,0:T(8,128)(2,1)S(1)}, bf16[40,3584]{1,0:T(8,128)(2,1)S(1)}, u32[]{:S(2)}, u32[]{:S(2)}) collective-permute-start(bf16[40,3584]{1,0:T(8,128)(2,1)S(1)} %get-tuple-element.48), channel_id=1, source_target_pairs={{0,2},{1,3},{2,0},{3,1},{4,6},{5,7},{6,4},{7,5},{8,10},{9,11},{10,... | collective-permute-start | bytes 860168 | tf_op jit(solution)/shard_map/ppermute | solution.py:23
  51.6 1.5 %collective-permute-start.10 = (bf16[40,3584]{1,0:T(8,128)(2,1)S(1)}, bf16[40,3584]{1,0:T(8,128)(2,1)S(1)}, u32[]{:S(2)}, u32[]{:S(2)}) collective-permute-start(bf16[40,3584]{1,0:T(8,128)(2,1)S(1)} %get-tuple-element.49), channel_id=1, source_target_pairs={{0,4},{1,5},{2,6},{3,7},{4,0},{5,1},{6,2},{7,3},{8,12},{9,13},{10,... | collective-permute-start | bytes 860168 | tf_op jit(solution)/shard_map/ppermute | solution.py:23
  53.2 0.5 collective-permute-start.11
  53.6 10.8 %shard_map.92 = (bf16[40,3584]{1,0:T(8,128)(2,1)S(1)}, bf16[40,3584]{1,0:T(8,128)(2,1)S(1)}, bf16[40,3584]{1,0:T(8,128)(2,1)S(1)}, bf16[40,3584]{1,0:T(8,128)(2,1)S(1)}) custom-call(bf16[40,3584]{1,0:T(8,128)(2,1)S(1)} %get-tuple-element.60.x0, bf16[40,3584]{1,0:T(8,128)(2,1)S(1)} %collective-permute-done.18.x1, ...), custom_call_target="tpu_custom_call" | custom-call | flops 3523215360 | bytes 25624576 | tf_op jit(solution)/shard_map/pallas_call | solution.py:45
  64.4 1.6 %collective-permute-start.21 = (bf16[40,3584]{1,0:T(8,128)(2,1)S(1)}, bf16[40,3584]{1,0:T(8,128)(2,1)S(1)}, u32[]{:S(2)}, u32[]{:S(2)}) collective-permute-start(bf16[40,3584]{1,0:T(8,128)(2,1)S(1)} %get-tuple-element.67), channel_id=1, source_target_pairs={{0,2},{1,3},{2,0},{3,1},{4,6},{5,7},{6,4},{7,5},{8,10},{9,11},{10,... | collective-permute-start | bytes 860168 | tf_op jit(solution)/shard_map/ppermute | solution.py:23
  66.0 1.5 %collective-permute-start.22 = (bf16[40,3584]{1,0:T(8,128)(2,1)S(1)}, bf16[40,3584]{1,0:T(8,128)(2,1)S(1)}, u32[]{:S(2)}, u32[]{:S(2)}) collective-permute-start(bf16[40,3584]{1,0:T(8,128)(2,1)S(1)} %get-tuple-element.68), channel_id=1, source_target_pairs={{0,4},{1,5},{2,6},{3,7},{4,0},{5,1},{6,2},{7,3},{8,12},{9,13},{10,... | collective-permute-start | bytes 860168 | tf_op jit(solution)/shard_map/ppermute | solution.py:23
  67.5 0.5 collective-permute-start.23
  68.0 0.6 shard_map.89
  68.6 0.7 collective-permute-start.12
  69.3 3.3 %collective-permute-start.13 = (bf16[16,3584]{1,0:T(8,128)(2,1)S(1)}, bf16[16,3584]{1,0:T(8,128)(2,1)S(1)}, u32[]{:S(2)}, u32[]{:S(2)}) collective-permute-start(bf16[16,3584]{1,0:T(8,128)(2,1)S(1)} %get-tuple-element.53), channel_id=1, source_target_pairs={{0,16},{1,17},{2,18},{3,19},{4,20},{5,21},{6,22},{7,23},{8,24},{9,... | collective-permute-start | bytes 344072 | tf_op jit(solution)/shard_map/ppermute | solution.py:23
  72.6 2.0 %collective-permute-start.14 = (bf16[16,3584]{1,0:T(8,128)(2,1)S(1)}, bf16[16,3584]{1,0:T(8,128)(2,1)S(1)}, u32[]{:S(2)}, u32[]{:S(2)}) collective-permute-start(bf16[16,3584]{1,0:T(8,128)(2,1)S(1)} %get-tuple-element.54), channel_id=1, source_target_pairs={{0,24},{1,25},{2,26},{3,27},{4,28},{5,29},{6,30},{7,31},{8,16},{9,... | collective-permute-start | bytes 344072 | tf_op jit(solution)/shard_map/ppermute | solution.py:23
  74.6 1.3 %collective-permute-done.22.third = bf16[40,3584]{1,0:T(8,128)(2,1)S(1)} collective-permute-done((bf16[40,3584]{1,0:T(8,128)(2,1)S(1)}, bf16[40,3584]{1,0:T(8,128)(2,1)S(1)}, u32[]{:S(2)}, u32[]{:S(2)}) %collective-permute-start.22) | collective-permute-done | bytes 286752 | tf_op jit(solution)/shard_map/ppermute | solution.py:23
  75.9 0.3 shard_map.93
  76.2 1.6 %collective-permute-start.24 = (bf16[16,3584]{1,0:T(8,128)(2,1)S(1)}, bf16[16,3584]{1,0:T(8,128)(2,1)S(1)}, u32[]{:S(2)}, u32[]{:S(2)}) collective-permute-start(bf16[16,3584]{1,0:T(8,128)(2,1)S(1)} %get-tuple-element.71), channel_id=1, source_target_pairs={{0,8},{1,9},{2,10},{3,11},{4,12},{5,13},{6,14},{7,15},{8,0},{9,1},... | collective-permute-start | bytes 344072 | tf_op jit(solution)/shard_map/ppermute | solution.py:23
  77.8 2.2 %collective-permute-start.25 = (bf16[16,3584]{1,0:T(8,128)(2,1)S(1)}, bf16[16,3584]{1,0:T(8,128)(2,1)S(1)}, u32[]{:S(2)}, u32[]{:S(2)}) collective-permute-start(bf16[16,3584]{1,0:T(8,128)(2,1)S(1)} %get-tuple-element.72), channel_id=1, source_target_pairs={{0,16},{1,17},{2,18},{3,19},{4,20},{5,21},{6,22},{7,23},{8,24},{9,... | collective-permute-start | bytes 344072 | tf_op jit(solution)/shard_map/ppermute | solution.py:23
  80.0 0.7 collective-permute-start.26
  80.7 0.1 collective-permute-done.14.refs_3_
  80.7 0.7 shard_map.90
  81.4 1.5 %collective-permute-done.24.refs_1_ = bf16[16,3584]{1,0:T(8,128)(2,1)S(1)} collective-permute-done((bf16[16,3584]{1,0:T(8,128)(2,1)S(1)}, bf16[16,3584]{1,0:T(8,128)(2,1)S(1)}, u32[]{:S(2)}, u32[]{:S(2)}) %collective-permute-start.24) | collective-permute-done | bytes 114720 | tf_op jit(solution)/shard_map/ppermute | solution.py:23
  82.9 5.0 %collective-permute-done.25.refs_2_ = bf16[16,3584]{1,0:T(8,128)(2,1)S(1)} collective-permute-done((bf16[16,3584]{1,0:T(8,128)(2,1)S(1)}, bf16[16,3584]{1,0:T(8,128)(2,1)S(1)}, u32[]{:S(2)}, u32[]{:S(2)}) %collective-permute-start.25) | collective-permute-done | bytes 114720 | tf_op jit(solution)/shard_map/ppermute | solution.py:23
  88.0 0.7 shard_map.94
  (19 shorter events, 0.0 us)
Async XLA Ops:
  0.6 20.0 %collective-permute-start.3 = (bf16[1,3584,512]{2,1,0:T(8,128)(2,1)}, bf16[1,3584,512]{2,1,0:T(8,128)(2,1)}, u32[]{:S(2)}, u32[]{:S(2)}) collective-permute-start(bf16[1,3584,512]{2,1,0:T(8,128)(2,1)} %refs_0_.4), channel_id=1, source_target_pairs={{0,1},{1,0},{2,3},{3,2},{4,5},{5,4},{6,7},{7,6},{8,9},{9,8},{10,11... | collective-permute-start | bytes 11010056 | tf_op jit(solution)/shard_map/ppermute | solution.py:23
  1.1 19.5 %collective-permute-start.4 = (bf16[1,3584,512]{2,1,0:T(8,128)(2,1)}, bf16[1,3584,512]{2,1,0:T(8,128)(2,1)}, u32[]{:S(2)}, u32[]{:S(2)}) collective-permute-start(bf16[1,3584,512]{2,1,0:T(8,128)(2,1)} %refs_1_.3), channel_id=1, source_target_pairs={{0,1},{1,0},{2,3},{3,2},{4,5},{5,4},{6,7},{7,6},{8,9},{9,8},{10,11... | collective-permute-start | bytes 11010056 | tf_op jit(solution)/shard_map/ppermute | solution.py:23
  1.2 25.6 %collective-permute-start.8 = (bf16[1,512,3584]{2,1,0:T(8,128)(2,1)}, bf16[1,512,3584]{2,1,0:T(8,128)(2,1)}, u32[]{:S(2)}, u32[]{:S(2)}) collective-permute-start(bf16[1,512,3584]{2,1,0:T(8,128)(2,1)} %refs_2_.3), channel_id=1, source_target_pairs={{0,1},{1,0},{2,3},{3,2},{4,5},{5,4},{6,7},{7,6},{8,9},{9,8},{10,11... | collective-permute-start | bytes 11010056 | tf_op jit(solution)/shard_map/ppermute | solution.py:23
  3.4 10.4 %collective-permute-start.1 = (bf16[16,3712]{1,0:T(8,128)(2,1)}, bf16[16,3712]{1,0:T(8,128)(2,1)S(1)}, u32[]{:S(2)}, u32[]{:S(2)}) collective-permute-start(bf16[16,3712]{1,0:T(8,128)(2,1)} %shard_map.86.refs_0_), channel_id=1, source_target_pairs={{0,16},{1,17},{2,18},{3,19},{4,20},{5,21},{6,22},{7,23},{8,24},{9,... | collective-permute-start | bytes 356360 | tf_op jit(solution)/shard_map/ppermute | solution.py:23
  7.1 7.4 %collective-permute-start = (bf16[16,3712]{1,0:T(8,128)(2,1)}, bf16[16,3712]{1,0:T(8,128)(2,1)S(1)}, u32[]{:S(2)}, u32[]{:S(2)}) collective-permute-start(bf16[16,3712]{1,0:T(8,128)(2,1)} %shard_map.86.refs_0_), channel_id=1, source_target_pairs={{0,8},{1,9},{2,10},{3,11},{4,12},{5,13},{6,14},{7,15},{8,0},{9,1},... | collective-permute-start | bytes 356360 | tf_op jit(solution)/shard_map/ppermute | solution.py:23
  13.8 4.9 %collective-permute-start.2 = (bf16[16,3712]{1,0:T(8,128)(2,1)S(1)}, bf16[16,3712]{1,0:T(8,128)(2,1)S(1)}, u32[]{:S(2)}, u32[]{:S(2)}) collective-permute-start(bf16[16,3712]{1,0:T(8,128)(2,1)S(1)} %collective-permute-done.1.refs_2_), channel_id=1, source_target_pairs={{0,8},{1,9},{2,10},{3,11},{4,12},{5,13},{6,14},{7,15},{8,0},{9,1},... | collective-permute-start | bytes 356360 | tf_op jit(solution)/shard_map/ppermute | solution.py:23
  18.7 0.9 %copy-start = (bf16[16,3712]{1,0:T(8,128)(2,1)S(1)}, bf16[16,3712]{1,0:T(8,128)(2,1)}, u32[]{:S(2)}) copy-start(bf16[16,3712]{1,0:T(8,128)(2,1)} %shard_map.86.refs_0_) | copy-start | bytes 356356
  20.7 20.4 %collective-permute-start.5 = (bf16[40,3584]{1,0:T(8,128)(2,1)S(1)}, bf16[40,3584]{1,0:T(8,128)(2,1)S(1)}, u32[]{:S(2)}, u32[]{:S(2)}) collective-permute-start(bf16[40,3584]{1,0:T(8,128)(2,1)S(1)} %get-tuple-element.42), channel_id=1, source_target_pairs={{0,2},{1,3},{2,0},{3,1},{4,6},{5,7},{6,4},{7,5},{8,10},{9,11},{10,... | collective-permute-start | bytes 860168 | tf_op jit(solution)/shard_map/ppermute | solution.py:23
  22.2 19.3 %collective-permute-start.6 = (bf16[40,3584]{1,0:T(8,128)(2,1)S(1)}, bf16[40,3584]{1,0:T(8,128)(2,1)S(1)}, u32[]{:S(2)}, u32[]{:S(2)}) collective-permute-start(bf16[40,3584]{1,0:T(8,128)(2,1)S(1)} %get-tuple-element.44), channel_id=1, source_target_pairs={{0,4},{1,5},{2,6},{3,7},{4,0},{5,1},{6,2},{7,3},{8,12},{9,13},{10,... | collective-permute-start | bytes 860168 | tf_op jit(solution)/shard_map/ppermute | solution.py:23
  23.8 17.8 %collective-permute-start.7 = (bf16[40,3584]{1,0:T(8,128)(2,1)S(1)}, bf16[40,3584]{1,0:T(8,128)(2,1)S(1)}, u32[]{:S(2)}, u32[]{:S(2)}) collective-permute-start(bf16[40,3584]{1,0:T(8,128)(2,1)S(1)} %get-tuple-element.46), channel_id=1, source_target_pairs={{0,6},{1,7},{2,4},{3,5},{4,2},{5,3},{6,0},{7,1},{8,14},{9,15},{10,... | collective-permute-start | bytes 860168 | tf_op jit(solution)/shard_map/ppermute | solution.py:23
  24.2 7.4 %collective-permute-start.16 = (bf16[16,3584]{1,0:T(8,128)(2,1)}, bf16[16,3584]{1,0:T(8,128)(2,1)S(1)}, u32[]{:S(2)}, u32[]{:S(2)}) collective-permute-start(bf16[16,3584]{1,0:T(8,128)(2,1)} %refs_0_.3), channel_id=1, source_target_pairs={{0,16},{1,17},{2,18},{3,19},{4,20},{5,21},{6,22},{7,23},{8,24},{9,... | collective-permute-start | bytes 344072 | tf_op jit(solution)/shard_map/ppermute | solution.py:23
  26.8 5.5 %collective-permute-start.15 = (bf16[16,3584]{1,0:T(8,128)(2,1)}, bf16[16,3584]{1,0:T(8,128)(2,1)S(1)}, u32[]{:S(2)}, u32[]{:S(2)}) collective-permute-start(bf16[16,3584]{1,0:T(8,128)(2,1)} %refs_0_.3), channel_id=1, source_target_pairs={{0,8},{1,9},{2,10},{3,11},{4,12},{5,13},{6,14},{7,15},{8,0},{9,1},... | collective-permute-start | bytes 344072 | tf_op jit(solution)/shard_map/ppermute | solution.py:23
  31.6 4.8 %collective-permute-start.17 = (bf16[16,3584]{1,0:T(8,128)(2,1)S(1)}, bf16[16,3584]{1,0:T(8,128)(2,1)S(1)}, u32[]{:S(2)}, u32[]{:S(2)}) collective-permute-start(bf16[16,3584]{1,0:T(8,128)(2,1)S(1)} %collective-permute-done.16.refs_2_), channel_id=1, source_target_pairs={{0,8},{1,9},{2,10},{3,11},{4,12},{5,13},{6,14},{7,15},{8,0},{9,1},... | collective-permute-start | bytes 344072 | tf_op jit(solution)/shard_map/ppermute | solution.py:23
  36.4 0.9 %copy-start.1 = (bf16[16,3584]{1,0:T(8,128)(2,1)S(1)}, bf16[16,3584]{1,0:T(8,128)(2,1)}, u32[]{:S(2)}) copy-start(bf16[16,3584]{1,0:T(8,128)(2,1)} %refs_0_.3) | copy-start | bytes 344068
  37.9 15.2 %collective-permute-start.18 = (bf16[40,3584]{1,0:T(8,128)(2,1)S(1)}, bf16[40,3584]{1,0:T(8,128)(2,1)S(1)}, u32[]{:S(2)}, u32[]{:S(2)}) collective-permute-start(bf16[40,3584]{1,0:T(8,128)(2,1)S(1)} %get-tuple-element.61), channel_id=1, source_target_pairs={{0,2},{1,3},{2,0},{3,1},{4,6},{5,7},{6,4},{7,5},{8,10},{9,11},{10,... | collective-permute-start | bytes 860168 | tf_op jit(solution)/shard_map/ppermute | solution.py:23
  39.5 14.1 %collective-permute-start.19 = (bf16[40,3584]{1,0:T(8,128)(2,1)S(1)}, bf16[40,3584]{1,0:T(8,128)(2,1)S(1)}, u32[]{:S(2)}, u32[]{:S(2)}) collective-permute-start(bf16[40,3584]{1,0:T(8,128)(2,1)S(1)} %get-tuple-element.62), channel_id=1, source_target_pairs={{0,4},{1,5},{2,6},{3,7},{4,0},{5,1},{6,2},{7,3},{8,12},{9,13},{10,... | collective-permute-start | bytes 860168 | tf_op jit(solution)/shard_map/ppermute | solution.py:23
  41.0 12.6 %collective-permute-start.20 = (bf16[40,3584]{1,0:T(8,128)(2,1)S(1)}, bf16[40,3584]{1,0:T(8,128)(2,1)S(1)}, u32[]{:S(2)}, u32[]{:S(2)}) collective-permute-start(bf16[40,3584]{1,0:T(8,128)(2,1)S(1)} %get-tuple-element.63), channel_id=1, source_target_pairs={{0,6},{1,7},{2,4},{3,5},{4,2},{5,3},{6,0},{7,1},{8,14},{9,15},{10,... | collective-permute-start | bytes 860168 | tf_op jit(solution)/shard_map/ppermute | solution.py:23
  50.1 17.4 %collective-permute-start.9 = (bf16[40,3584]{1,0:T(8,128)(2,1)S(1)}, bf16[40,3584]{1,0:T(8,128)(2,1)S(1)}, u32[]{:S(2)}, u32[]{:S(2)}) collective-permute-start(bf16[40,3584]{1,0:T(8,128)(2,1)S(1)} %get-tuple-element.48), channel_id=1, source_target_pairs={{0,2},{1,3},{2,0},{3,1},{4,6},{5,7},{6,4},{7,5},{8,10},{9,11},{10,... | collective-permute-start | bytes 860168 | tf_op jit(solution)/shard_map/ppermute | solution.py:23
  51.6 16.3 %collective-permute-start.10 = (bf16[40,3584]{1,0:T(8,128)(2,1)S(1)}, bf16[40,3584]{1,0:T(8,128)(2,1)S(1)}, u32[]{:S(2)}, u32[]{:S(2)}) collective-permute-start(bf16[40,3584]{1,0:T(8,128)(2,1)S(1)} %get-tuple-element.49), channel_id=1, source_target_pairs={{0,4},{1,5},{2,6},{3,7},{4,0},{5,1},{6,2},{7,3},{8,12},{9,13},{10,... | collective-permute-start | bytes 860168 | tf_op jit(solution)/shard_map/ppermute | solution.py:23
  53.2 14.8 %collective-permute-start.11 = (bf16[40,3584]{1,0:T(8,128)(2,1)S(1)}, bf16[40,3584]{1,0:T(8,128)(2,1)S(1)}, u32[]{:S(2)}, u32[]{:S(2)}) collective-permute-start(bf16[40,3584]{1,0:T(8,128)(2,1)S(1)} %get-tuple-element.50), channel_id=1, source_target_pairs={{0,6},{1,7},{2,4},{3,5},{4,2},{5,3},{6,0},{7,1},{8,14},{9,15},{10,... | collective-permute-start | bytes 860168 | tf_op jit(solution)/shard_map/ppermute | solution.py:23
  64.4 8.2 %collective-permute-start.21 = (bf16[40,3584]{1,0:T(8,128)(2,1)S(1)}, bf16[40,3584]{1,0:T(8,128)(2,1)S(1)}, u32[]{:S(2)}, u32[]{:S(2)}) collective-permute-start(bf16[40,3584]{1,0:T(8,128)(2,1)S(1)} %get-tuple-element.67), channel_id=1, source_target_pairs={{0,2},{1,3},{2,0},{3,1},{4,6},{5,7},{6,4},{7,5},{8,10},{9,11},{10,... | collective-permute-start | bytes 860168 | tf_op jit(solution)/shard_map/ppermute | solution.py:23
  66.0 9.9 %collective-permute-start.22 = (bf16[40,3584]{1,0:T(8,128)(2,1)S(1)}, bf16[40,3584]{1,0:T(8,128)(2,1)S(1)}, u32[]{:S(2)}, u32[]{:S(2)}) collective-permute-start(bf16[40,3584]{1,0:T(8,128)(2,1)S(1)} %get-tuple-element.68), channel_id=1, source_target_pairs={{0,4},{1,5},{2,6},{3,7},{4,0},{5,1},{6,2},{7,3},{8,12},{9,13},{10,... | collective-permute-start | bytes 860168 | tf_op jit(solution)/shard_map/ppermute | solution.py:23
  67.5 8.4 %collective-permute-start.23 = (bf16[40,3584]{1,0:T(8,128)(2,1)S(1)}, bf16[40,3584]{1,0:T(8,128)(2,1)S(1)}, u32[]{:S(2)}, u32[]{:S(2)}) collective-permute-start(bf16[40,3584]{1,0:T(8,128)(2,1)S(1)} %get-tuple-element.69), channel_id=1, source_target_pairs={{0,6},{1,7},{2,4},{3,5},{4,2},{5,3},{6,0},{7,1},{8,14},{9,15},{10,... | collective-permute-start | bytes 860168 | tf_op jit(solution)/shard_map/ppermute | solution.py:23
  68.6 11.4 %collective-permute-start.12 = (bf16[16,3584]{1,0:T(8,128)(2,1)S(1)}, bf16[16,3584]{1,0:T(8,128)(2,1)S(1)}, u32[]{:S(2)}, u32[]{:S(2)}) collective-permute-start(bf16[16,3584]{1,0:T(8,128)(2,1)S(1)} %get-tuple-element.52), channel_id=1, source_target_pairs={{0,8},{1,9},{2,10},{3,11},{4,12},{5,13},{6,14},{7,15},{8,0},{9,1},... | collective-permute-start | bytes 344072 | tf_op jit(solution)/shard_map/ppermute | solution.py:23
  69.3 11.4 %collective-permute-start.13 = (bf16[16,3584]{1,0:T(8,128)(2,1)S(1)}, bf16[16,3584]{1,0:T(8,128)(2,1)S(1)}, u32[]{:S(2)}, u32[]{:S(2)}) collective-permute-start(bf16[16,3584]{1,0:T(8,128)(2,1)S(1)} %get-tuple-element.53), channel_id=1, source_target_pairs={{0,16},{1,17},{2,18},{3,19},{4,20},{5,21},{6,22},{7,23},{8,24},{9,... | collective-permute-start | bytes 344072 | tf_op jit(solution)/shard_map/ppermute | solution.py:23
  72.6 8.2 %collective-permute-start.14 = (bf16[16,3584]{1,0:T(8,128)(2,1)S(1)}, bf16[16,3584]{1,0:T(8,128)(2,1)S(1)}, u32[]{:S(2)}, u32[]{:S(2)}) collective-permute-start(bf16[16,3584]{1,0:T(8,128)(2,1)S(1)} %get-tuple-element.54), channel_id=1, source_target_pairs={{0,24},{1,25},{2,26},{3,27},{4,28},{5,29},{6,30},{7,31},{8,16},{9,... | collective-permute-start | bytes 344072 | tf_op jit(solution)/shard_map/ppermute | solution.py:23
  76.2 6.7 %collective-permute-start.24 = (bf16[16,3584]{1,0:T(8,128)(2,1)S(1)}, bf16[16,3584]{1,0:T(8,128)(2,1)S(1)}, u32[]{:S(2)}, u32[]{:S(2)}) collective-permute-start(bf16[16,3584]{1,0:T(8,128)(2,1)S(1)} %get-tuple-element.71), channel_id=1, source_target_pairs={{0,8},{1,9},{2,10},{3,11},{4,12},{5,13},{6,14},{7,15},{8,0},{9,1},... | collective-permute-start | bytes 344072 | tf_op jit(solution)/shard_map/ppermute | solution.py:23
  77.8 10.2 %collective-permute-start.25 = (bf16[16,3584]{1,0:T(8,128)(2,1)S(1)}, bf16[16,3584]{1,0:T(8,128)(2,1)S(1)}, u32[]{:S(2)}, u32[]{:S(2)}) collective-permute-start(bf16[16,3584]{1,0:T(8,128)(2,1)S(1)} %get-tuple-element.72), channel_id=1, source_target_pairs={{0,16},{1,17},{2,18},{3,19},{4,20},{5,21},{6,22},{7,23},{8,24},{9,... | collective-permute-start | bytes 344072 | tf_op jit(solution)/shard_map/ppermute | solution.py:23
  80.0 8.0 %collective-permute-start.26 = (bf16[16,3584]{1,0:T(8,128)(2,1)S(1)}, bf16[16,3584]{1,0:T(8,128)(2,1)S(1)}, u32[]{:S(2)}, u32[]{:S(2)}) collective-permute-start(bf16[16,3584]{1,0:T(8,128)(2,1)S(1)} %get-tuple-element.73), channel_id=1, source_target_pairs={{0,24},{1,25},{2,26},{3,27},{4,28},{5,29},{6,30},{7,31},{8,16},{9,... | collective-permute-start | bytes 344072 | tf_op jit(solution)/shard_map/ppermute | solution.py:23

commit v8 on v7

--- a/solution.py
+++ b/solution.py
@@ -15,7 +15,6 @@
 PIECES = 3
 VMEM_LIMIT = 16 * 1024 * 1024
 VMEM_LIMIT_EXPERT = 48 * 1024 * 1024
-VMEM_LIMIT_ALL = 58 * 1024 * 1024
 
 
 def swap(value, offset):
@@ -64,13 +63,9 @@
     pltpu.make_async_copy(place, place, sem).wait()
 
 
-def code_kernel(experts, tokens_in, ids_in, gates_in, out, tokens, ids, gates, sems):
+def code_kernel(experts, tokens, ids, gates, out):
     rows, width = tokens.shape
-    sources, places = (ids_in, gates_in, tokens_in), (ids, gates, tokens)
-    copies = streams(zip(sources, places, (sems.at[number] for number in range(3))))
     gate_width = out.shape[1] - width
-    copies[0].wait()
-    copies[1].wait()
     line = lax.broadcasted_iota(jnp.int32, (gate_width, rows), 0)
     rest = jnp.zeros(line.shape, f32)
     for k in range(ids.shape[0]):
@@ -81,7 +76,6 @@
         columns = jnp.where(line // experts == number, piece, columns)
         rest = rest - piece
     out[:, width:] = columns.T.astype(bf16)
-    copies[2].wait()
     for at in range(0, width, LANES):
         block = tokens[:, at : at + LANES].astype(f32)
         scale = jnp.max(jnp.abs(block), axis=1, keepdims=True) + 1e-06
@@ -282,19 +276,11 @@
     own = (gate_weight, up_weight, down_weight)
     other = tuple(swap(slab, CORE) for slab in own)
 
-    in_place = pl.BlockSpec(memory_space=pl.ANY)
+    in_place = pl.BlockSpec(memory_space=pltpu.HBM)
     (coded,) = call(
         functools.partial(code_kernel, experts),
         [shape((tok_dev, width + padded(PIECES * experts)), bf16)],
         (tokens, expert_ids.T, gate_values.T),
-        in_specs=[in_place] * 3,
-        scratch=[
-            pltpu.VMEM((tok_dev, width), bf16),
-            pltpu.VMEM((top, tok_dev), jnp.int32),
-            pltpu.VMEM((top, tok_dev), f32),
-            pltpu.SemaphoreType.DMA((3,)),
-        ],
-        limit=VMEM_LIMIT_ALL,
     )
     held, offset = {0: coded}, devices // 2
     while offset >= FAR:
@@ -310,14 +296,15 @@
         in_specs=[pl.BlockSpec(memory_space=pltpu.SMEM)] + [whole] * blocks,
         flops=2 * rows * slots * width,
     )
-    packed = [after(value, *other[:2]) for value in packed]
+    far_cots = swap(after(cotangent, held[blocks // 2], other[0]), devices // 2)
+    packed = [after(value, far_cots, *other[:2]) for value in packed]
     x = [packed[0]] + [swap(value, offset) for value, offset in zip(packed[1:], PLANE[1:])]
 
-    cots, offset = {0: after(cotangent, held[blocks // 2])}, devices // 2
+    cots, offset = {0: cotangent, blocks // 2: far_cots}, devices // 4
     while offset >= FAR:
         wait = other[2] if offset == FAR else cotangent
         ready = {at: after(value, wait) for at, value in cots.items()}
-        cots.update({at ^ offset: swap(value, offset) for at, value in ready.items()})
+        cots.update({at ^ offset // FAR: swap(value, offset) for at, value in ready.items()})
         offset //= 2
     cots = [cots[at] for at in sorted(cots)]
 

time: 88.9 us -> 87.9 us (0.989)
  waiting for transfers between devices: 24.4 us -> 20.5 us
  starting transfers between devices: 36.7 us -> 39.8 us
  Pallas kernels: 25 us -> 23.4 us
  local copies, waits for them, and re-layouts: 1.8 us -> 3.17 us
    ppermute x27, waiting for transfers between devices: 24.4 us -> 20.5 us  [swap(): lax.ppermute(value, 'expert', [(i, i ^ offset) for i in range(devices)])]
    ppermute x27, starting transfers between devices: 36.7 us -> 39.8 us  [swap(): lax.ppermute(value, 'expert', [(i, i ^ offset) for i in range(devices)])]
    pallas_call x9, Pallas kernels: 25 us -> 23.4 us  [call(): pl.pallas_call(body, out_shape=outs, in_specs=[whole] * len(args) if in_s...]
    unnamed x4 -> x8, local copies, waits for them, and re-layouts: 1.8 us -> 3.17 us
  transfers between devices with their start and end apart: 27 -> 27, of which waited for: 8 -> 8; matrix products, arithmetic and copies ran while one was open for 0% -> 0% of each run, Pallas kernels for 27% -> 26%
where the time goes in v8:
time: 87.9 us; the launch traced here: 87.7 us
  starting transfers between devices  39.8 us (45%)
  Pallas kernels  23.4 us (27%)
  waiting for transfers between devices  20.5 us (23%)
  local copies, waits for them, and re-layouts  3.17 us (4%)
    ppermute x27, starting transfers between devices, swap(): lax.ppermute(value, 'expert', [(i, i ^ offset) for i in range(devices)])  39.8 us
    pallas_call x9, Pallas kernels, call(): pl.pallas_call(body, out_shape=outs, in_specs=[whole] * len(args) if in_s...  23.4 us
    ppermute x27, waiting for transfers between devices, swap(): lax.ppermute(value, 'expert', [(i, i ^ offset) for i in range(devices)])  20.5 us
    unnamed x8, local copies, waits for them, and re-layouts  3.17 us
  transfers between devices with their start and end apart: 27, of which 8 were waited for; matrix products, arithmetic and copies ran while one was open for 0% of the time, Pallas kernels for 26%

profile of v8, /device:TPU:0, one launch (start us, length us, event | category | flops | bytes accessed | tf_op | source)
XLA Modules:
  0.0 87.7 jit_solution(6951322135331557520)
XLA Ops:
  0.6 0.5 collective-permute-start.3
  1.1 0.1 collective-permute-start.5
  1.2 0.4 collective-permute-start.9
  1.7 0.9 %copy-done.1 = bf16[16,3584]{1,0:T(8,128)(2,1)S(1)} copy-done((bf16[16,3584]{1,0:T(8,128)(2,1)S(1)}, bf16[16,3584]{1,0:T(8,128)(2,1)}, u32[]{:S(2)}) %copy-start.1) | copy-done | bytes 114712
  2.6 0.7 copy-done.2
  3.2 0.7 copy-done.3
  3.9 0.2 shard_map.86.refs_0_
  4.1 3.7 %collective-permute-start.1 = (bf16[16,3712]{1,0:T(8,128)(2,1)S(1)}, bf16[16,3712]{1,0:T(8,128)(2,1)S(1)}, u32[]{:S(2)}, u32[]{:S(2)}) collective-permute-start(bf16[16,3712]{1,0:T(8,128)(2,1)S(1)} %shard_map.86.refs_0_), channel_id=1, source_target_pairs={{0,16},{1,17},{2,18},{3,19},{4,20},{5,21},{6,22},{7,23},{8,24},{9,... | collective-permute-start | bytes 356360 | tf_op jit(solution)/shard_map/ppermute | solution.py:22
  7.9 1.6 %collective-permute-start = (bf16[16,3712]{1,0:T(8,128)(2,1)S(1)}, bf16[16,3712]{1,0:T(8,128)(2,1)S(1)}, u32[]{:S(2)}, u32[]{:S(2)}) collective-permute-start(bf16[16,3712]{1,0:T(8,128)(2,1)S(1)} %shard_map.86.refs_0_), channel_id=1, source_target_pairs={{0,8},{1,9},{2,10},{3,11},{4,12},{5,13},{6,14},{7,15},{8,0},{9,1},... | collective-permute-start | bytes 356360 | tf_op jit(solution)/shard_map/ppermute | solution.py:22
  9.4 4.9 %collective-permute-done.1.refs_2_ = bf16[16,3712]{1,0:T(8,128)(2,1)S(1)} collective-permute-done((bf16[16,3712]{1,0:T(8,128)(2,1)S(1)}, bf16[16,3712]{1,0:T(8,128)(2,1)S(1)}, u32[]{:S(2)}, u32[]{:S(2)}) %collective-permute-start.1) | collective-permute-done | bytes 118816 | tf_op jit(solution)/shard_map/ppermute | solution.py:22
  14.3 0.6 collective-permute-start.2
  15.0 3.4 %collective-permute-start.4 = (bf16[16,3584]{1,0:T(8,128)(2,1)}, bf16[16,3584]{1,0:T(8,128)(2,1)S(1)}, u32[]{:S(2)}, u32[]{:S(2)}) collective-permute-start(bf16[16,3584]{1,0:T(8,128)(2,1)} %refs_0_.4), channel_id=1, source_target_pairs={{0,16},{1,17},{2,18},{3,19},{4,20},{5,21},{6,22},{7,23},{8,24},{9,... | collective-permute-start | bytes 344072 | tf_op jit(solution)/shard_map/ppermute | solution.py:22
  18.4 0.9 %collective-permute-done.2.refs_3_ = bf16[16,3712]{1,0:T(8,128)(2,1)S(1)} collective-permute-done((bf16[16,3712]{1,0:T(8,128)(2,1)S(1)}, bf16[16,3712]{1,0:T(8,128)(2,1)S(1)}, u32[]{:S(2)}, u32[]{:S(2)}) %collective-permute-start.2) | collective-permute-done | bytes 118816 | tf_op jit(solution)/shard_map/ppermute | solution.py:22
  19.2 1.0 %shard_map.87 = (bf16[40,3584]{1,0:T(8,128)(2,1)S(1)}, bf16[40,3584]{1,0:T(8,128)(2,1)S(1)}, bf16[40,3584]{1,0:T(8,128)(2,1)S(1)}, bf16[40,3584]{1,0:T(8,128)(2,...) custom-call(s32[1]{0:T(128)} %bitcast.chip, bf16[16,3712]{1,0:T(8,128)(2,1)S(1)} %shard_map.86.refs_0_, ...), custom_call_target="tpu_custom_call" | custom-call | flops 117440512 | bytes 1753092 | tf_op jit(solution)/shard_map/pallas_call | solution.py:44
  20.3 3.8 %collective-permute-done.4.refs_2_ = bf16[16,3584]{1,0:T(8,128)(2,1)S(1)} collective-permute-done((bf16[16,3584]{1,0:T(8,128)(2,1)}, bf16[16,3584]{1,0:T(8,128)(2,1)S(1)}, u32[]{:S(2)}, u32[]{:S(2)}) %collective-permute-start.4) | collective-permute-done | bytes 114720 | tf_op jit(solution)/shard_map/ppermute | solution.py:22
  24.1 1.5 %collective-permute-start.6 = (bf16[40,3584]{1,0:T(8,128)(2,1)S(1)}, bf16[40,3584]{1,0:T(8,128)(2,1)S(1)}, u32[]{:S(2)}, u32[]{:S(2)}) collective-permute-start(bf16[40,3584]{1,0:T(8,128)(2,1)S(1)} %get-tuple-element.42), channel_id=1, source_target_pairs={{0,2},{1,3},{2,0},{3,1},{4,6},{5,7},{6,4},{7,5},{8,10},{9,11},{10,... | collective-permute-start | bytes 860168 | tf_op jit(solution)/shard_map/ppermute | solution.py:22
  25.6 1.5 %collective-permute-start.7 = (bf16[40,3584]{1,0:T(8,128)(2,1)S(1)}, bf16[40,3584]{1,0:T(8,128)(2,1)S(1)}, u32[]{:S(2)}, u32[]{:S(2)}) collective-permute-start(bf16[40,3584]{1,0:T(8,128)(2,1)S(1)} %get-tuple-element.44), channel_id=1, source_target_pairs={{0,4},{1,5},{2,6},{3,7},{4,0},{5,1},{6,2},{7,3},{8,12},{9,13},{10,... | collective-permute-start | bytes 860168 | tf_op jit(solution)/shard_map/ppermute | solution.py:22
  27.1 0.5 collective-permute-start.8
  27.6 0.3 collective-permute-start.16
  27.9 1.8 %collective-permute-start.17 = (bf16[16,3584]{1,0:T(8,128)(2,1)S(1)}, bf16[16,3584]{1,0:T(8,128)(2,1)S(1)}, u32[]{:S(2)}, u32[]{:S(2)}) collective-permute-start(bf16[16,3584]{1,0:T(8,128)(2,1)S(1)} %collective-permute-done.4.refs_2_), channel_id=1, source_target_pairs={{0,8},{1,9},{2,10},{3,11},{4,12},{5,13},{6,14},{7,15},{8,0},{9,1},... | collective-permute-start | bytes 344072 | tf_op jit(solution)/shard_map/ppermute | solution.py:22
  29.6 3.0 %collective-permute-done.16.refs_1_ = bf16[16,3584]{1,0:T(8,128)(2,1)S(1)} collective-permute-done((bf16[16,3584]{1,0:T(8,128)(2,1)}, bf16[16,3584]{1,0:T(8,128)(2,1)S(1)}, u32[]{:S(2)}, u32[]{:S(2)}) %collective-permute-start.16) | collective-permute-done | bytes 114720 | tf_op jit(solution)/shard_map/ppermute | solution.py:22
  32.6 1.2 %collective-permute-done.17.refs_3_ = bf16[16,3584]{1,0:T(8,128)(2,1)S(1)} collective-permute-done((bf16[16,3584]{1,0:T(8,128)(2,1)S(1)}, bf16[16,3584]{1,0:T(8,128)(2,1)S(1)}, u32[]{:S(2)}, u32[]{:S(2)}) %collective-permute-start.17) | collective-permute-done | bytes 114720 | tf_op jit(solution)/shard_map/ppermute | solution.py:22
  33.8 0.9 %copy-done = bf16[16,3584]{1,0:T(8,128)(2,1)S(1)} copy-done((bf16[16,3584]{1,0:T(8,128)(2,1)S(1)}, bf16[16,3584]{1,0:T(8,128)(2,1)}, u32[]{:S(2)}) %copy-start) | copy-done | bytes 114712
  34.7 0.6 shard_map.91
  35.3 1.6 %collective-permute-start.18 = (bf16[40,3584]{1,0:T(8,128)(2,1)S(1)}, bf16[40,3584]{1,0:T(8,128)(2,1)S(1)}, u32[]{:S(2)}, u32[]{:S(2)}) collective-permute-start(bf16[40,3584]{1,0:T(8,128)(2,1)S(1)} %get-tuple-element.59), channel_id=1, source_target_pairs={{0,2},{1,3},{2,0},{3,1},{4,6},{5,7},{6,4},{7,5},{8,10},{9,11},{10,... | collective-permute-start | bytes 860168 | tf_op jit(solution)/shard_map/ppermute | solution.py:22
  36.9 1.5 %collective-permute-start.19 = (bf16[40,3584]{1,0:T(8,128)(2,1)S(1)}, bf16[40,3584]{1,0:T(8,128)(2,1)S(1)}, u32[]{:S(2)}, u32[]{:S(2)}) collective-permute-start(bf16[40,3584]{1,0:T(8,128)(2,1)S(1)} %get-tuple-element.60), channel_id=1, source_target_pairs={{0,4},{1,5},{2,6},{3,7},{4,0},{5,1},{6,2},{7,3},{8,12},{9,13},{10,... | collective-permute-start | bytes 860168 | tf_op jit(solution)/shard_map/ppermute | solution.py:22
  38.4 0.5 collective-permute-start.20
  38.9 8.5 %shard_map.88 = (bf16[40,3584]{1,0:T(8,128)(2,1)S(1)}, bf16[40,3584]{1,0:T(8,128)(2,1)S(1)}, bf16[40,3584]{1,0:T(8,128)(2,1)S(1)}, bf16[40,3584]{1,0:T(8,128)(2,...) custom-call(bf16[40,3584]{1,0:T(8,128)(2,1)S(1)} %get-tuple-element.40.x0, ...), custom_call_target="tpu_custom_call" | custom-call | flops 3523215360 | bytes 25624576 | tf_op jit(solution)/shard_map/pallas_call | solution.py:44
  47.5 1.6 %collective-permute-start.10 = (bf16[40,3584]{1,0:T(8,128)(2,1)S(1)}, bf16[40,3584]{1,0:T(8,128)(2,1)S(1)}, u32[]{:S(2)}, u32[]{:S(2)}) collective-permute-start(bf16[40,3584]{1,0:T(8,128)(2,1)S(1)} %get-tuple-element.48), channel_id=1, source_target_pairs={{0,2},{1,3},{2,0},{3,1},{4,6},{5,7},{6,4},{7,5},{8,10},{9,11},{10,... | collective-permute-start | bytes 860168 | tf_op jit(solution)/shard_map/ppermute | solution.py:22
  49.0 1.5 %collective-permute-start.11 = (bf16[40,3584]{1,0:T(8,128)(2,1)S(1)}, bf16[40,3584]{1,0:T(8,128)(2,1)S(1)}, u32[]{:S(2)}, u32[]{:S(2)}) collective-permute-start(bf16[40,3584]{1,0:T(8,128)(2,1)S(1)} %get-tuple-element.49), channel_id=1, source_target_pairs={{0,4},{1,5},{2,6},{3,7},{4,0},{5,1},{6,2},{7,3},{8,12},{9,13},{10,... | collective-permute-start | bytes 860168 | tf_op jit(solution)/shard_map/ppermute | solution.py:22
  50.5 0.5 collective-permute-start.12
  51.0 0.7 collective-permute-done.20.x3
  51.7 10.8 %shard_map.92 = (bf16[40,3584]{1,0:T(8,128)(2,1)S(1)}, bf16[40,3584]{1,0:T(8,128)(2,1)S(1)}, bf16[40,3584]{1,0:T(8,128)(2,1)S(1)}, bf16[40,3584]{1,0:T(8,128)(2,1)S(1)}) custom-call(bf16[40,3584]{1,0:T(8,128)(2,1)S(1)} %get-tuple-element.58.x0, bf16[40,3584]{1,0:T(8,128)(2,1)S(1)} %collective-permute-done.18.x1, ...), custom_call_target="tpu_custom_call" | custom-call | flops 3523215360 | bytes 25624576 | tf_op jit(solution)/shard_map/pallas_call | solution.py:44
  62.5 1.4 %collective-permute-start.21 = (bf16[40,3584]{1,0:T(8,128)(2,1)S(1)}, bf16[40,3584]{1,0:T(8,128)(2,1)S(1)}, u32[]{:S(2)}, u32[]{:S(2)}) collective-permute-start(bf16[40,3584]{1,0:T(8,128)(2,1)S(1)} %get-tuple-element.65), channel_id=1, source_target_pairs={{0,2},{1,3},{2,0},{3,1},{4,6},{5,7},{6,4},{7,5},{8,10},{9,11},{10,... | collective-permute-start | bytes 860168 | tf_op jit(solution)/shard_map/ppermute | solution.py:22
  63.9 1.0 %collective-permute-start.22 = (bf16[40,3584]{1,0:T(8,128)(2,1)S(1)}, bf16[40,3584]{1,0:T(8,128)(2,1)S(1)}, u32[]{:S(2)}, u32[]{:S(2)}) collective-permute-start(bf16[40,3584]{1,0:T(8,128)(2,1)S(1)} %get-tuple-element.66), channel_id=1, source_target_pairs={{0,4},{1,5},{2,6},{3,7},{4,0},{5,1},{6,2},{7,3},{8,12},{9,13},{10,... | collective-permute-start | bytes 860168 | tf_op jit(solution)/shard_map/ppermute | solution.py:22
  64.9 1.2 %collective-permute-start.23 = (bf16[40,3584]{1,0:T(8,128)(2,1)S(1)}, bf16[40,3584]{1,0:T(8,128)(2,1)S(1)}, u32[]{:S(2)}, u32[]{:S(2)}) collective-permute-start(bf16[40,3584]{1,0:T(8,128)(2,1)S(1)} %get-tuple-element.67), channel_id=1, source_target_pairs={{0,6},{1,7},{2,4},{3,5},{4,2},{5,3},{6,0},{7,1},{8,14},{9,15},{10,... | collective-permute-start | bytes 860168 | tf_op jit(solution)/shard_map/ppermute | solution.py:22
  66.1 0.6 shard_map.89
  66.7 2.0 %collective-permute-start.13 = (bf16[16,3584]{1,0:T(8,128)(2,1)S(1)}, bf16[16,3584]{1,0:T(8,128)(2,1)S(1)}, u32[]{:S(2)}, u32[]{:S(2)}) collective-permute-start(bf16[16,3584]{1,0:T(8,128)(2,1)S(1)} %get-tuple-element.52), channel_id=1, source_target_pairs={{0,8},{1,9},{2,10},{3,11},{4,12},{5,13},{6,14},{7,15},{8,0},{9,1},... | collective-permute-start | bytes 344072 | tf_op jit(solution)/shard_map/ppermute | solution.py:22
  68.6 2.7 %collective-permute-start.14 = (bf16[16,3584]{1,0:T(8,128)(2,1)S(1)}, bf16[16,3584]{1,0:T(8,128)(2,1)S(1)}, u32[]{:S(2)}, u32[]{:S(2)}) collective-permute-start(bf16[16,3584]{1,0:T(8,128)(2,1)S(1)} %get-tuple-element.53), channel_id=1, source_target_pairs={{0,16},{1,17},{2,18},{3,19},{4,20},{5,21},{6,22},{7,23},{8,24},{9,... | collective-permute-start | bytes 344072 | tf_op jit(solution)/shard_map/ppermute | solution.py:22
  71.3 3.6 %collective-permute-start.15 = (bf16[16,3584]{1,0:T(8,128)(2,1)S(1)}, bf16[16,3584]{1,0:T(8,128)(2,1)S(1)}, u32[]{:S(2)}, u32[]{:S(2)}) collective-permute-start(bf16[16,3584]{1,0:T(8,128)(2,1)S(1)} %get-tuple-element.54), channel_id=1, source_target_pairs={{0,24},{1,25},{2,26},{3,27},{4,28},{5,29},{6,30},{7,31},{8,16},{9,... | collective-permute-start | bytes 344072 | tf_op jit(solution)/shard_map/ppermute | solution.py:22
  75.0 0.3 shard_map.93
  75.3 2.6 %collective-permute-start.24 = (bf16[16,3584]{1,0:T(8,128)(2,1)S(1)}, bf16[16,3584]{1,0:T(8,128)(2,1)S(1)}, u32[]{:S(2)}, u32[]{:S(2)}) collective-permute-start(bf16[16,3584]{1,0:T(8,128)(2,1)S(1)} %get-tuple-element.69), channel_id=1, source_target_pairs={{0,8},{1,9},{2,10},{3,11},{4,12},{5,13},{6,14},{7,15},{8,0},{9,1},... | collective-permute-start | bytes 344072 | tf_op jit(solution)/shard_map/ppermute | solution.py:22
  77.9 2.2 %collective-permute-start.25 = (bf16[16,3584]{1,0:T(8,128)(2,1)S(1)}, bf16[16,3584]{1,0:T(8,128)(2,1)S(1)}, u32[]{:S(2)}, u32[]{:S(2)}) collective-permute-start(bf16[16,3584]{1,0:T(8,128)(2,1)S(1)} %get-tuple-element.70), channel_id=1, source_target_pairs={{0,16},{1,17},{2,18},{3,19},{4,20},{5,21},{6,22},{7,23},{8,24},{9,... | collective-permute-start | bytes 344072 | tf_op jit(solution)/shard_map/ppermute | solution.py:22
  80.1 0.2 collective-permute-start.26
  80.3 0.7 shard_map.90
  81.1 1.3 %collective-permute-done.24.refs_1_ = bf16[16,3584]{1,0:T(8,128)(2,1)S(1)} collective-permute-done((bf16[16,3584]{1,0:T(8,128)(2,1)S(1)}, bf16[16,3584]{1,0:T(8,128)(2,1)S(1)}, u32[]{:S(2)}, u32[]{:S(2)}) %collective-permute-start.24) | collective-permute-done | bytes 114720 | tf_op jit(solution)/shard_map/ppermute | solution.py:22
  82.4 4.6 %collective-permute-done.25.refs_2_ = bf16[16,3584]{1,0:T(8,128)(2,1)S(1)} collective-permute-done((bf16[16,3584]{1,0:T(8,128)(2,1)S(1)}, bf16[16,3584]{1,0:T(8,128)(2,1)S(1)}, u32[]{:S(2)}, u32[]{:S(2)}) %collective-permute-start.25) | collective-permute-done | bytes 114720 | tf_op jit(solution)/shard_map/ppermute | solution.py:22
  87.0 0.7 shard_map.94
  (23 shorter events, 0.1 us)
Async XLA Ops:
  0.6 14.4 %collective-permute-start.3 = (bf16[1,3584,512]{2,1,0:T(8,128)(2,1)}, bf16[1,3584,512]{2,1,0:T(8,128)(2,1)}, u32[]{:S(2)}, u32[]{:S(2)}) collective-permute-start(bf16[1,3584,512]{2,1,0:T(8,128)(2,1)} %refs_0_.5), channel_id=1, source_target_pairs={{0,1},{1,0},{2,3},{3,2},{4,5},{5,4},{6,7},{7,6},{8,9},{9,8},{10,11... | collective-permute-start | bytes 11010056 | tf_op jit(solution)/shard_map/ppermute | solution.py:22
  1.1 19.1 %collective-permute-start.5 = (bf16[1,3584,512]{2,1,0:T(8,128)(2,1)}, bf16[1,3584,512]{2,1,0:T(8,128)(2,1)}, u32[]{:S(2)}, u32[]{:S(2)}) collective-permute-start(bf16[1,3584,512]{2,1,0:T(8,128)(2,1)} %refs_1_.3), channel_id=1, source_target_pairs={{0,1},{1,0},{2,3},{3,2},{4,5},{5,4},{6,7},{7,6},{8,9},{9,8},{10,11... | collective-permute-start | bytes 11010056 | tf_op jit(solution)/shard_map/ppermute | solution.py:22
  1.2 26.4 %collective-permute-start.9 = (bf16[1,512,3584]{2,1,0:T(8,128)(2,1)}, bf16[1,512,3584]{2,1,0:T(8,128)(2,1)}, u32[]{:S(2)}, u32[]{:S(2)}) collective-permute-start(bf16[1,512,3584]{2,1,0:T(8,128)(2,1)} %refs_2_.3), channel_id=1, source_target_pairs={{0,1},{1,0},{2,3},{3,2},{4,5},{5,4},{6,7},{7,6},{8,9},{9,8},{10,11... | collective-permute-start | bytes 11010056 | tf_op jit(solution)/shard_map/ppermute | solution.py:22
  1.7 0.9 %copy-start.1 = (bf16[16,3584]{1,0:T(8,128)(2,1)S(1)}, bf16[16,3584]{1,0:T(8,128)(2,1)}, u32[]{:S(2)}) copy-start(bf16[16,3584]{1,0:T(8,128)(2,1)} %tokens.1) | copy-start | bytes 344068
  2.6 0.7 copy-start.2
  3.2 0.7 copy-start.3
  4.1 10.2 %collective-permute-start.1 = (bf16[16,3712]{1,0:T(8,128)(2,1)S(1)}, bf16[16,3712]{1,0:T(8,128)(2,1)S(1)}, u32[]{:S(2)}, u32[]{:S(2)}) collective-permute-start(bf16[16,3712]{1,0:T(8,128)(2,1)S(1)} %shard_map.86.refs_0_), channel_id=1, source_target_pairs={{0,16},{1,17},{2,18},{3,19},{4,20},{5,21},{6,22},{7,23},{8,24},{9,... | collective-permute-start | bytes 356360 | tf_op jit(solution)/shard_map/ppermute | solution.py:22
  7.9 10.5 %collective-permute-start = (bf16[16,3712]{1,0:T(8,128)(2,1)S(1)}, bf16[16,3712]{1,0:T(8,128)(2,1)S(1)}, u32[]{:S(2)}, u32[]{:S(2)}) collective-permute-start(bf16[16,3712]{1,0:T(8,128)(2,1)S(1)} %shard_map.86.refs_0_), channel_id=1, source_target_pairs={{0,8},{1,9},{2,10},{3,11},{4,12},{5,13},{6,14},{7,15},{8,0},{9,1},... | collective-permute-start | bytes 356360 | tf_op jit(solution)/shard_map/ppermute | solution.py:22
  14.3 4.9 %collective-permute-start.2 = (bf16[16,3712]{1,0:T(8,128)(2,1)S(1)}, bf16[16,3712]{1,0:T(8,128)(2,1)S(1)}, u32[]{:S(2)}, u32[]{:S(2)}) collective-permute-start(bf16[16,3712]{1,0:T(8,128)(2,1)S(1)} %collective-permute-done.1.refs_2_), channel_id=1, source_target_pairs={{0,8},{1,9},{2,10},{3,11},{4,12},{5,13},{6,14},{7,15},{8,0},{9,1},... | collective-permute-start | bytes 356360 | tf_op jit(solution)/shard_map/ppermute | solution.py:22
  15.0 9.1 %collective-permute-start.4 = (bf16[16,3584]{1,0:T(8,128)(2,1)}, bf16[16,3584]{1,0:T(8,128)(2,1)S(1)}, u32[]{:S(2)}, u32[]{:S(2)}) collective-permute-start(bf16[16,3584]{1,0:T(8,128)(2,1)} %refs_0_.4), channel_id=1, source_target_pairs={{0,16},{1,17},{2,18},{3,19},{4,20},{5,21},{6,22},{7,23},{8,24},{9,... | collective-permute-start | bytes 344072 | tf_op jit(solution)/shard_map/ppermute | solution.py:22
  24.1 14.3 %collective-permute-start.6 = (bf16[40,3584]{1,0:T(8,128)(2,1)S(1)}, bf16[40,3584]{1,0:T(8,128)(2,1)S(1)}, u32[]{:S(2)}, u32[]{:S(2)}) collective-permute-start(bf16[40,3584]{1,0:T(8,128)(2,1)S(1)} %get-tuple-element.42), channel_id=1, source_target_pairs={{0,2},{1,3},{2,0},{3,1},{4,6},{5,7},{6,4},{7,5},{8,10},{9,11},{10,... | collective-permute-start | bytes 860168 | tf_op jit(solution)/shard_map/ppermute | solution.py:22
  25.6 13.3 %collective-permute-start.7 = (bf16[40,3584]{1,0:T(8,128)(2,1)S(1)}, bf16[40,3584]{1,0:T(8,128)(2,1)S(1)}, u32[]{:S(2)}, u32[]{:S(2)}) collective-permute-start(bf16[40,3584]{1,0:T(8,128)(2,1)S(1)} %get-tuple-element.44), channel_id=1, source_target_pairs={{0,4},{1,5},{2,6},{3,7},{4,0},{5,1},{6,2},{7,3},{8,12},{9,13},{10,... | collective-permute-start | bytes 860168 | tf_op jit(solution)/shard_map/ppermute | solution.py:22
  27.1 11.8 %collective-permute-start.8 = (bf16[40,3584]{1,0:T(8,128)(2,1)S(1)}, bf16[40,3584]{1,0:T(8,128)(2,1)S(1)}, u32[]{:S(2)}, u32[]{:S(2)}) collective-permute-start(bf16[40,3584]{1,0:T(8,128)(2,1)S(1)} %get-tuple-element.46), channel_id=1, source_target_pairs={{0,6},{1,7},{2,4},{3,5},{4,2},{5,3},{6,0},{7,1},{8,14},{9,15},{10,... | collective-permute-start | bytes 860168 | tf_op jit(solution)/shard_map/ppermute | solution.py:22
  27.6 5.0 %collective-permute-start.16 = (bf16[16,3584]{1,0:T(8,128)(2,1)}, bf16[16,3584]{1,0:T(8,128)(2,1)S(1)}, u32[]{:S(2)}, u32[]{:S(2)}) collective-permute-start(bf16[16,3584]{1,0:T(8,128)(2,1)} %refs_0_.4), channel_id=1, source_target_pairs={{0,8},{1,9},{2,10},{3,11},{4,12},{5,13},{6,14},{7,15},{8,0},{9,1},... | collective-permute-start | bytes 344072 | tf_op jit(solution)/shard_map/ppermute | solution.py:22
  27.9 6.0 %collective-permute-start.17 = (bf16[16,3584]{1,0:T(8,128)(2,1)S(1)}, bf16[16,3584]{1,0:T(8,128)(2,1)S(1)}, u32[]{:S(2)}, u32[]{:S(2)}) collective-permute-start(bf16[16,3584]{1,0:T(8,128)(2,1)S(1)} %collective-permute-done.4.refs_2_), channel_id=1, source_target_pairs={{0,8},{1,9},{2,10},{3,11},{4,12},{5,13},{6,14},{7,15},{8,0},{9,1},... | collective-permute-start | bytes 344072 | tf_op jit(solution)/shard_map/ppermute | solution.py:22
  33.8 0.9 %copy-start = (bf16[16,3584]{1,0:T(8,128)(2,1)S(1)}, bf16[16,3584]{1,0:T(8,128)(2,1)}, u32[]{:S(2)}) copy-start(bf16[16,3584]{1,0:T(8,128)(2,1)} %refs_0_.4) | copy-start | bytes 344068
  35.3 15.2 %collective-permute-start.18 = (bf16[40,3584]{1,0:T(8,128)(2,1)S(1)}, bf16[40,3584]{1,0:T(8,128)(2,1)S(1)}, u32[]{:S(2)}, u32[]{:S(2)}) collective-permute-start(bf16[40,3584]{1,0:T(8,128)(2,1)S(1)} %get-tuple-element.59), channel_id=1, source_target_pairs={{0,2},{1,3},{2,0},{3,1},{4,6},{5,7},{6,4},{7,5},{8,10},{9,11},{10,... | collective-permute-start | bytes 860168 | tf_op jit(solution)/shard_map/ppermute | solution.py:22
  36.9 14.1 %collective-permute-start.19 = (bf16[40,3584]{1,0:T(8,128)(2,1)S(1)}, bf16[40,3584]{1,0:T(8,128)(2,1)S(1)}, u32[]{:S(2)}, u32[]{:S(2)}) collective-permute-start(bf16[40,3584]{1,0:T(8,128)(2,1)S(1)} %get-tuple-element.60), channel_id=1, source_target_pairs={{0,4},{1,5},{2,6},{3,7},{4,0},{5,1},{6,2},{7,3},{8,12},{9,13},{10,... | collective-permute-start | bytes 860168 | tf_op jit(solution)/shard_map/ppermute | solution.py:22
  38.4 13.3 %collective-permute-start.20 = (bf16[40,3584]{1,0:T(8,128)(2,1)S(1)}, bf16[40,3584]{1,0:T(8,128)(2,1)S(1)}, u32[]{:S(2)}, u32[]{:S(2)}) collective-permute-start(bf16[40,3584]{1,0:T(8,128)(2,1)S(1)} %get-tuple-element.61), channel_id=1, source_target_pairs={{0,6},{1,7},{2,4},{3,5},{4,2},{5,3},{6,0},{7,1},{8,14},{9,15},{10,... | collective-permute-start | bytes 860168 | tf_op jit(solution)/shard_map/ppermute | solution.py:22
  47.5 17.4 %collective-permute-start.10 = (bf16[40,3584]{1,0:T(8,128)(2,1)S(1)}, bf16[40,3584]{1,0:T(8,128)(2,1)S(1)}, u32[]{:S(2)}, u32[]{:S(2)}) collective-permute-start(bf16[40,3584]{1,0:T(8,128)(2,1)S(1)} %get-tuple-element.48), channel_id=1, source_target_pairs={{0,2},{1,3},{2,0},{3,1},{4,6},{5,7},{6,4},{7,5},{8,10},{9,11},{10,... | collective-permute-start | bytes 860168 | tf_op jit(solution)/shard_map/ppermute | solution.py:22
  49.0 17.0 %collective-permute-start.11 = (bf16[40,3584]{1,0:T(8,128)(2,1)S(1)}, bf16[40,3584]{1,0:T(8,128)(2,1)S(1)}, u32[]{:S(2)}, u32[]{:S(2)}) collective-permute-start(bf16[40,3584]{1,0:T(8,128)(2,1)S(1)} %get-tuple-element.49), channel_id=1, source_target_pairs={{0,4},{1,5},{2,6},{3,7},{4,0},{5,1},{6,2},{7,3},{8,12},{9,13},{10,... | collective-permute-start | bytes 860168 | tf_op jit(solution)/shard_map/ppermute | solution.py:22
  50.5 15.5 %collective-permute-start.12 = (bf16[40,3584]{1,0:T(8,128)(2,1)S(1)}, bf16[40,3584]{1,0:T(8,128)(2,1)S(1)}, u32[]{:S(2)}, u32[]{:S(2)}) collective-permute-start(bf16[40,3584]{1,0:T(8,128)(2,1)S(1)} %get-tuple-element.50), channel_id=1, source_target_pairs={{0,6},{1,7},{2,4},{3,5},{4,2},{5,3},{6,0},{7,1},{8,14},{9,15},{10,... | collective-permute-start | bytes 860168 | tf_op jit(solution)/shard_map/ppermute | solution.py:22
  62.5 8.8 %collective-permute-start.21 = (bf16[40,3584]{1,0:T(8,128)(2,1)S(1)}, bf16[40,3584]{1,0:T(8,128)(2,1)S(1)}, u32[]{:S(2)}, u32[]{:S(2)}) collective-permute-start(bf16[40,3584]{1,0:T(8,128)(2,1)S(1)} %get-tuple-element.65), channel_id=1, source_target_pairs={{0,2},{1,3},{2,0},{3,1},{4,6},{5,7},{6,4},{7,5},{8,10},{9,11},{10,... | collective-permute-start | bytes 860168 | tf_op jit(solution)/shard_map/ppermute | solution.py:22
  63.9 11.1 %collective-permute-start.22 = (bf16[40,3584]{1,0:T(8,128)(2,1)S(1)}, bf16[40,3584]{1,0:T(8,128)(2,1)S(1)}, u32[]{:S(2)}, u32[]{:S(2)}) collective-permute-start(bf16[40,3584]{1,0:T(8,128)(2,1)S(1)} %get-tuple-element.66), channel_id=1, source_target_pairs={{0,4},{1,5},{2,6},{3,7},{4,0},{5,1},{6,2},{7,3},{8,12},{9,13},{10,... | collective-permute-start | bytes 860168 | tf_op jit(solution)/shard_map/ppermute | solution.py:22
  64.9 10.1 %collective-permute-start.23 = (bf16[40,3584]{1,0:T(8,128)(2,1)S(1)}, bf16[40,3584]{1,0:T(8,128)(2,1)S(1)}, u32[]{:S(2)}, u32[]{:S(2)}) collective-permute-start(bf16[40,3584]{1,0:T(8,128)(2,1)S(1)} %get-tuple-element.67), channel_id=1, source_target_pairs={{0,6},{1,7},{2,4},{3,5},{4,2},{5,3},{6,0},{7,1},{8,14},{9,15},{10,... | collective-permute-start | bytes 860168 | tf_op jit(solution)/shard_map/ppermute | solution.py:22
  66.7 13.4 %collective-permute-start.13 = (bf16[16,3584]{1,0:T(8,128)(2,1)S(1)}, bf16[16,3584]{1,0:T(8,128)(2,1)S(1)}, u32[]{:S(2)}, u32[]{:S(2)}) collective-permute-start(bf16[16,3584]{1,0:T(8,128)(2,1)S(1)} %get-tuple-element.52), channel_id=1, source_target_pairs={{0,8},{1,9},{2,10},{3,11},{4,12},{5,13},{6,14},{7,15},{8,0},{9,1},... | collective-permute-start | bytes 344072 | tf_op jit(solution)/shard_map/ppermute | solution.py:22
  68.6 11.7 %collective-permute-start.14 = (bf16[16,3584]{1,0:T(8,128)(2,1)S(1)}, bf16[16,3584]{1,0:T(8,128)(2,1)S(1)}, u32[]{:S(2)}, u32[]{:S(2)}) collective-permute-start(bf16[16,3584]{1,0:T(8,128)(2,1)S(1)} %get-tuple-element.53), channel_id=1, source_target_pairs={{0,16},{1,17},{2,18},{3,19},{4,20},{5,21},{6,22},{7,23},{8,24},{9,... | collective-permute-start | bytes 344072 | tf_op jit(solution)/shard_map/ppermute | solution.py:22
  71.3 9.0 %collective-permute-start.15 = (bf16[16,3584]{1,0:T(8,128)(2,1)S(1)}, bf16[16,3584]{1,0:T(8,128)(2,1)S(1)}, u32[]{:S(2)}, u32[]{:S(2)}) collective-permute-start(bf16[16,3584]{1,0:T(8,128)(2,1)S(1)} %get-tuple-element.54), channel_id=1, source_target_pairs={{0,24},{1,25},{2,26},{3,27},{4,28},{5,29},{6,30},{7,31},{8,16},{9,... | collective-permute-start | bytes 344072 | tf_op jit(solution)/shard_map/ppermute | solution.py:22
  75.3 7.1 %collective-permute-start.24 = (bf16[16,3584]{1,0:T(8,128)(2,1)S(1)}, bf16[16,3584]{1,0:T(8,128)(2,1)S(1)}, u32[]{:S(2)}, u32[]{:S(2)}) collective-permute-start(bf16[16,3584]{1,0:T(8,128)(2,1)S(1)} %get-tuple-element.69), channel_id=1, source_target_pairs={{0,8},{1,9},{2,10},{3,11},{4,12},{5,13},{6,14},{7,15},{8,0},{9,1},... | collective-permute-start | bytes 344072 | tf_op jit(solution)/shard_map/ppermute | solution.py:22
  77.9 9.1 %collective-permute-start.25 = (bf16[16,3584]{1,0:T(8,128)(2,1)S(1)}, bf16[16,3584]{1,0:T(8,128)(2,1)S(1)}, u32[]{:S(2)}, u32[]{:S(2)}) collective-permute-start(bf16[16,3584]{1,0:T(8,128)(2,1)S(1)} %get-tuple-element.70), channel_id=1, source_target_pairs={{0,16},{1,17},{2,18},{3,19},{4,20},{5,21},{6,22},{7,23},{8,24},{9,... | collective-permute-start | bytes 344072 | tf_op jit(solution)/shard_map/ppermute | solution.py:22
  80.1 6.9 %collective-permute-start.26 = (bf16[16,3584]{1,0:T(8,128)(2,1)S(1)}, bf16[16,3584]{1,0:T(8,128)(2,1)S(1)}, u32[]{:S(2)}, u32[]{:S(2)}) collective-permute-start(bf16[16,3584]{1,0:T(8,128)(2,1)S(1)} %get-tuple-element.71), channel_id=1, source_target_pairs={{0,24},{1,25},{2,26},{3,27},{4,28},{5,29},{6,30},{7,31},{8,16},{9,... | collective-permute-start | bytes 344072 | tf_op jit(solution)/shard_map/ppermute | solution.py:22

commit v9 on v8

--- a/solution.py
+++ b/solution.py
@@ -14,7 +14,6 @@
 LANES = 128
 PIECES = 3
 VMEM_LIMIT = 16 * 1024 * 1024
-VMEM_LIMIT_EXPERT = 48 * 1024 * 1024
 
 
 def swap(value, offset):
@@ -38,7 +37,7 @@
     return [slice(at, at + chunk_of(width)) for at in range(0, width, chunk_of(width))]
 
 
-def call(body, outs, args, flops=0, scratch=(), in_specs=None, limit=VMEM_LIMIT):
+def call(body, outs, args, flops=0, scratch=(), in_specs=None):
     size = sum(math.prod(a.shape) * a.dtype.itemsize for a in (*args, *outs))
     whole = pl.BlockSpec(memory_space=pltpu.VMEM)
     return pl.pallas_call(
@@ -47,20 +46,9 @@
         in_specs=[whole] * len(args) if in_specs is None else in_specs,
         out_specs=[whole] * len(outs),
         scratch_shapes=scratch,
-        compiler_params=pltpu.CompilerParams(vmem_limit_bytes=limit),
+        compiler_params=pltpu.CompilerParams(vmem_limit_bytes=VMEM_LIMIT),
         cost_estimate=pl.CostEstimate(flops=flops, bytes_accessed=size, transcendentals=0),
     )(*args)
-
-
-def streams(triples):
-    copies = [pltpu.make_async_copy(*triple) for triple in triples]
-    for copy in copies:
-        copy.start()
-    return copies
-
-
-def await_place(place, sem):
-    pltpu.make_async_copy(place, place, sem).wait()
 
 
 def code_kernel(experts, tokens, ids, gates, out):
@@ -173,45 +161,28 @@
         out[:, part] = total.astype(bf16)
 
 
-def forward_kernel(tile, x0, x1, x2, x3, *refs):
-    *slabs, o0, o1, o2, o3, for_up, for_gate, x, hidden, into, back, sems = refs
+def forward_kernel(x0, x1, x2, x3, g0, u0, d0, g1, u1, d1, *refs):
+    o0, o1, o2, o3, for_up, for_gate, x, hidden = refs
     rows, width = x.shape
-    units = back.shape[0] // 2
-    chunk, tiles, chunks = chunk_of(width), 2 * units // tile, width // chunk_of(width)
-    triples = []
-    for number in range(tiles):
-        slab, at = divmod(number * tile, units)
-        for half, source in enumerate(slabs[3 * slab : 3 * slab + 2]):
-            place = into.at[:, pl.ds((2 * number + half) * tile, tile)]
-            triples.append((source.at[0, :, pl.ds(at, tile)], place, sems.at[number]))
-    for number in range(chunks):
-        columns = pl.ds(number * chunk, chunk)
-        for slab in range(2):
-            place = back.at[pl.ds(slab * units, units), columns]
-            source = slabs[3 * slab + 2].at[0, :, columns]
-            triples.append((source, place, sems.at[tiles + number]))
-    streams(triples)
+    units = g0.shape[2]
     for part in column_chunks(width):
         x[:, part] = joined((x0, x1, x2, x3), part, rows)
 
-    @pl.loop(0, tiles)
-    def _(number):
-        columns = pl.ds(pl.multiple_of(number * 2 * tile, 2 * tile), 2 * tile)
-        await_place(into.at[:, columns], sems.at[number])
-        pre = jnp.dot(x[...], into[:, columns], preferred_element_type=f32)
-        pre_gate, pre_up = pre[:, :tile], pre[:, tile:]
+    for slab, (gate_w, up_w) in enumerate(((g0, u0), (g1, u1))):
+        at = slice(slab * units, (slab + 1) * units)
+        pre_gate = jnp.dot(x[...], gate_w[0], preferred_element_type=f32)
+        pre_up = jnp.dot(x[...], up_w[0], preferred_element_type=f32)
         sigma = jax.nn.sigmoid(pre_gate)
         activated = pre_gate * sigma
-        at = pl.ds(pl.multiple_of(number * tile, tile), tile)
         hidden[:, at] = (activated * pre_up).astype(bf16)
         for_up[:, at] = activated
         for_gate[:, at] = pre_up * sigma * (1.0 + pre_gate * (1.0 - sigma))
 
-    @pl.loop(0, chunks)
+    @pl.loop(0, width // chunk_of(width))
     def _(number):
-        part = pl.ds(pl.multiple_of(number * chunk, chunk), chunk)
-        await_place(back.at[:, part], sems.at[tiles + number])
-        total = jnp.dot(hidden[...], back[:, part], preferred_element_type=f32)
+        part = pl.ds(pl.multiple_of(number * chunk_of(width), LANES), chunk_of(width))
+        total = jnp.dot(hidden[:, :units], d0[0, :, part], preferred_element_type=f32)
+        total = total + jnp.dot(hidden[:, units:], d1[0, :, part], preferred_element_type=f32)
         store_packed(total, (o0, o1, o2, o3), part)
 
 
@@ -221,41 +192,29 @@
         out[:, at] = total[number * taken : (number + 1) * taken].astype(bf16)
 
 
-def backward_kernel(x0, x1, x2, x3, for_up, for_gate, *refs):
-    *slabs, o0, o1, o2, o3, x, grads, into, back, sems = refs
+def backward_kernel(x0, x1, x2, x3, for_up, for_gate, g0, u0, d0, g1, u1, d1, *refs):
+    o0, o1, o2, o3, x, gate_grad, up_grad = refs
     rows, width = x.shape
-    units = back.shape[0] // 2
-    chunk, chunks = chunk_of(width), width // chunk_of(width)
-    triples = []
-    for slab in range(2):
-        place = back.at[pl.ds(slab * units, units)]
-        triples.append((slabs[3 * slab + 2].at[0], place, sems.at[slab]))
-    for number in range(chunks):
-        lines = pl.ds(number * chunk, chunk)
-        for column, matrix in enumerate((0, 1, 3, 4)):
-            place = into.at[lines, pl.ds(column * units, units)]
-            triples.append((slabs[matrix].at[0, lines], place, sems.at[2 + number]))
-    streams(triples)
+    units = g0.shape[2]
     for part in column_chunks(width):
         x[:, part] = joined((x0, x1, x2, x3), part, rows)
 
-    @pl.loop(0, 2)
-    def _(slab):
-        at = pl.ds(pl.multiple_of(slab * units, units), units)
-        await_place(back.at[at], sems.at[slab])
-        hidden_grad = lax.dot_general(x[...], back[at], CONTRACT_COLS, preferred_element_type=f32)
-        start = pl.multiple_of(2 * slab * units, 2 * units)
-        gate_at, up_at = pl.ds(start, units), pl.ds(start + units, units)
-        grads[:, gate_at] = (hidden_grad * for_gate[:, at]).astype(bf16)
-        grads[:, up_at] = (hidden_grad * for_up[:, at]).astype(bf16)
-
-    @pl.loop(0, chunks)
+    def transposed(left, right):
+        return lax.dot_general(left, right, CONTRACT_COLS, preferred_element_type=f32)
+
+    for slab, down_w in enumerate((d0, d1)):
+        at = slice(slab * units, (slab + 1) * units)
+        hidden_grad = transposed(x[...], down_w[0])
+        gate_grad[:, at] = (hidden_grad * for_gate[:, at]).astype(bf16)
+        up_grad[:, at] = (hidden_grad * for_up[:, at]).astype(bf16)
+
+    @pl.loop(0, width // chunk_of(width))
     def _(number):
-        part = pl.ds(pl.multiple_of(number * chunk, chunk), chunk)
-        await_place(into.at[part], sems.at[2 + number])
-        total = lax.dot_general(
-            grads[...], into[part], CONTRACT_COLS, preferred_element_type=f32
-        )
+        part = pl.ds(pl.multiple_of(number * chunk_of(width), LANES), chunk_of(width))
+        total = transposed(gate_grad[:, :units], g0[0, part])
+        total = total + transposed(up_grad[:, :units], u0[0, part])
+        total = total + transposed(gate_grad[:, units:], g1[0, part])
+        total = total + transposed(up_grad[:, units:], u1[0, part])
         store_packed(total, (o0, o1, o2, o3), part)
 
 
@@ -276,7 +235,6 @@
     own = (gate_weight, up_weight, down_weight)
     other = tuple(swap(slab, CORE) for slab in own)
 
-    in_place = pl.BlockSpec(memory_space=pltpu.HBM)
     (coded,) = call(
         functools.partial(code_kernel, experts),
         [shape((tok_dev, width + padded(PIECES * experts)), bf16)],
@@ -297,7 +255,8 @@
         flops=2 * rows * slots * width,
     )
     far_cots = swap(after(cotangent, held[blocks // 2], other[0]), devices // 2)
-    packed = [after(value, far_cots, *other[:2]) for value in packed]
+    packed = packed_tokens = [after(value, *other[:2]) for value in packed]
+    packed[-1] = after(packed[-1], far_cots)
     x = [packed[0]] + [swap(value, offset) for value, offset in zip(packed[1:], PLANE[1:])]
 
     cots, offset = {0: cotangent, blocks // 2: far_cots}, devices // 4
@@ -317,22 +276,16 @@
     grads = [packed[0]] + [swap(value, offset) for value, offset in zip(packed[1:], PLANE[1:])]
 
     all_taken = len(PLANE) * taken
-    tile = 256 if hidden % 256 == 0 else LANES
-    tiles, chunks = 2 * hidden // tile, width // chunk_of(width)
-    slab_room = [pltpu.VMEM((width, 4 * hidden), bf16), pltpu.VMEM((2 * hidden, width), bf16)]
     flops = 2 * 3 * all_taken * width * 2 * hidden
+    own = [after(slab, packed_tokens[0]) for slab in own]
     *outs, for_up, for_gate = call(
-        functools.partial(forward_kernel, tile),
+        forward_kernel,
         packed_shapes + [shape((all_taken, 2 * hidden), f32)] * 2,
         (*x, *own, *other),
         flops=flops,
-        in_specs=[whole] * 4 + [in_place] * 6,
-        limit=VMEM_LIMIT_EXPERT,
         scratch=[
             pltpu.VMEM((all_taken, width), bf16),
             pltpu.VMEM((all_taken, 2 * hidden), bf16),
-            *slab_room,
-            pltpu.SemaphoreType.DMA((tiles + chunks,)),
         ],
     )
 
@@ -354,13 +307,10 @@
         packed_shapes,
         (*grads, for_up, for_gate, *own, *other),
         flops=flops,
-        in_specs=[whole] * 6 + [in_place] * 6,
-        limit=VMEM_LIMIT_EXPERT,
         scratch=[
             pltpu.VMEM((all_taken, width), bf16),
-            pltpu.VMEM((all_taken, 4 * hidden), bf16),
-            *slab_room,
-            pltpu.SemaphoreType.DMA((2 + chunks,)),
+            pltpu.VMEM((all_taken, 2 * hidden), bf16),
+            pltpu.VMEM((all_taken, 2 * hidden), bf16),
         ],
     )
     token_grad = go_home(backs, False)

time: 87.9 us -> 96.5 us (1.098)
  local copies, waits for them, and re-layouts: 3.17 us -> 13.2 us
  starting transfers between devices: 39.8 us -> 36.9 us
    unnamed x8 -> x26, local copies, waits for them, and re-layouts: 3.17 us -> 13.2 us
    ppermute x27, starting transfers between devices: 39.8 us -> 36.9 us  [swap(): lax.ppermute(value, 'expert', [(i, i ^ offset) for i in range(devices)])]
  transfers between devices with their start and end apart: 27 -> 27, of which waited for: 8 -> 8; matrix products, arithmetic and copies ran while one was open for 0% -> 0% of each run, Pallas kernels for 26% -> 24%
where the time goes in v9:
time: 96.5 us; the launch traced here: 96.1 us
  starting transfers between devices  36.9 us (38%)
  Pallas kernels  23.9 us (25%)
  waiting for transfers between devices  21.4 us (22%)
  local copies, waits for them, and re-layouts  13.2 us (14%)
    ppermute x27, starting transfers between devices, swap(): lax.ppermute(value, 'expert', [(i, i ^ offset) for i in range(devices)])  36.9 us
    pallas_call x9, Pallas kernels, call(): pl.pallas_call(body, out_shape=outs, in_specs=[whole] * len(args) if in_s...  23.9 us
    ppermute x27, waiting for transfers between devices, swap(): lax.ppermute(value, 'expert', [(i, i ^ offset) for i in range(devices)])  21.4 us
    unnamed x26, local copies, waits for them, and re-layouts  13.2 us
  transfers between devices with their start and end apart: 27, of which 8 were waited for; matrix products, arithmetic and copies ran while one was open for 0% of the time, Pallas kernels for 24%

profile of v9, /device:TPU:0, one launch (start us, length us, event | category | flops | bytes accessed | tf_op | source)
XLA Modules:
  0.0 96.1 jit_solution(15105253556406877222)
XLA Ops:
  0.6 0.5 collective-permute-start.3
  1.2 0.4 collective-permute-start.9
  1.7 0.9 copy-done.10
  2.6 0.7 copy-done.11
  3.2 0.7 copy-done.12
  4.1 3.7 %collective-permute-start.1 = (bf16[16,3712]{1,0:T(8,128)(2,1)S(1)}, bf16[16,3712]{1,0:T(8,128)(2,1)S(1)}, u32[]{:S(2)}, u32[]{:S(2)}) collective-permute-start(bf16[16,3712]{1,0:T(8,128)(2,1)S(1)} %shard_map.86.refs_0_), channel_id=1, source_target_pairs={{0,16},{1,17},{2,18},{3,19},{4,20},{5,21},{6,22},{7,23},{8,24},{9,... | collective-permute-start | bytes 356360 | tf_op jit(solution)/shard_map/ppermute | solution.py:21
  7.9 1.6 %collective-permute-start = (bf16[16,3712]{1,0:T(8,128)(2,1)S(1)}, bf16[16,3712]{1,0:T(8,128)(2,1)S(1)}, u32[]{:S(2)}, u32[]{:S(2)}) collective-permute-start(bf16[16,3712]{1,0:T(8,128)(2,1)S(1)} %shard_map.86.refs_0_), channel_id=1, source_target_pairs={{0,8},{1,9},{2,10},{3,11},{4,12},{5,13},{6,14},{7,15},{8,0},{9,1},... | collective-permute-start | bytes 356360 | tf_op jit(solution)/shard_map/ppermute | solution.py:21
  9.4 4.9 %collective-permute-done.1.refs_2_ = bf16[16,3712]{1,0:T(8,128)(2,1)S(1)} collective-permute-done((bf16[16,3712]{1,0:T(8,128)(2,1)S(1)}, bf16[16,3712]{1,0:T(8,128)(2,1)S(1)}, u32[]{:S(2)}, u32[]{:S(2)}) %collective-permute-start.1) | collective-permute-done | bytes 118816 | tf_op jit(solution)/shard_map/ppermute | solution.py:21
  14.3 0.6 collective-permute-start.2
  15.0 1.9 %copy-done.6 = bf16[1,3584,512]{2,1,0:T(8,128)(2,1)} copy-done((bf16[1,3584,512]{2,1,0:T(8,128)(2,1)}, bf16[1,3584,512]{2,1,0:T(8,128)(2,1)S(1)}, u32[]{:S(2)}) %copy-start.6) | copy-done | bytes 3670040
  16.9 3.4 %collective-permute-start.7 = (bf16[16,3584]{1,0:T(8,128)(2,1)}, bf16[16,3584]{1,0:T(8,128)(2,1)S(1)}, u32[]{:S(2)}, u32[]{:S(2)}) collective-permute-start(bf16[16,3584]{1,0:T(8,128)(2,1)} %refs_0_.1), channel_id=1, source_target_pairs={{0,16},{1,17},{2,18},{3,19},{4,20},{5,21},{6,22},{7,23},{8,24},{9,... | collective-permute-start | bytes 344072 | tf_op jit(solution)/shard_map/ppermute | solution.py:21
  20.3 1.0 %shard_map.87 = (bf16[40,3584]{1,0:T(8,128)(2,1)S(1)}, bf16[40,3584]{1,0:T(8,128)(2,1)S(1)}, bf16[40,3584]{1,0:T(8,128)(2,1)S(1)}, bf16[40,3584]{1,0:T(8,128)(2,...) custom-call(s32[1]{0:T(128)} %bitcast.chip, bf16[16,3712]{1,0:T(8,128)(2,1)S(1)} %shard_map.86.refs_0_, ...), custom_call_target="tpu_custom_call" | custom-call | flops 117440512 | bytes 1753092 | tf_op jit(solution)/shard_map/pallas_call | solution.py:43
  21.3 1.6 %collective-permute-start.5 = (bf16[40,3584]{1,0:T(8,128)(2,1)S(1)}, bf16[40,3584]{1,0:T(8,128)(2,1)S(1)}, u32[]{:S(2)}, u32[]{:S(2)}) collective-permute-start(bf16[40,3584]{1,0:T(8,128)(2,1)S(1)} %get-tuple-element.45), channel_id=1, source_target_pairs={{0,2},{1,3},{2,0},{3,1},{4,6},{5,7},{6,4},{7,5},{8,10},{9,11},{10,... | collective-permute-start | bytes 860168 | tf_op jit(solution)/shard_map/ppermute | solution.py:21
  22.9 1.5 %collective-permute-start.6 = (bf16[40,3584]{1,0:T(8,128)(2,1)S(1)}, bf16[40,3584]{1,0:T(8,128)(2,1)S(1)}, u32[]{:S(2)}, u32[]{:S(2)}) collective-permute-start(bf16[40,3584]{1,0:T(8,128)(2,1)S(1)} %get-tuple-element.47), channel_id=1, source_target_pairs={{0,4},{1,5},{2,6},{3,7},{4,0},{5,1},{6,2},{7,3},{8,12},{9,13},{10,... | collective-permute-start | bytes 860168 | tf_op jit(solution)/shard_map/ppermute | solution.py:21
  24.4 1.6 %collective-permute-done.7.refs_2_ = bf16[16,3584]{1,0:T(8,128)(2,1)S(1)} collective-permute-done((bf16[16,3584]{1,0:T(8,128)(2,1)}, bf16[16,3584]{1,0:T(8,128)(2,1)S(1)}, u32[]{:S(2)}, u32[]{:S(2)}) %collective-permute-start.7) | collective-permute-done | bytes 114720 | tf_op jit(solution)/shard_map/ppermute | solution.py:21
  25.9 2.4 %collective-permute-start.8 = (bf16[40,3584]{1,0:T(8,128)(2,1)S(1)}, bf16[40,3584]{1,0:T(8,128)(2,1)S(1)}, u32[]{:S(2)}, u32[]{:S(2)}) collective-permute-start(bf16[40,3584]{1,0:T(8,128)(2,1)S(1)} %get-tuple-element.51), channel_id=1, source_target_pairs={{0,6},{1,7},{2,4},{3,5},{4,2},{5,3},{6,0},{7,1},{8,14},{9,15},{10,... | collective-permute-start | bytes 860168 | tf_op jit(solution)/shard_map/ppermute | solution.py:21
  28.4 2.0 %collective-permute-start.17 = (bf16[16,3584]{1,0:T(8,128)(2,1)S(1)}, bf16[16,3584]{1,0:T(8,128)(2,1)S(1)}, u32[]{:S(2)}, u32[]{:S(2)}) collective-permute-start(bf16[16,3584]{1,0:T(8,128)(2,1)S(1)} %collective-permute-done.7.refs_2_), channel_id=1, source_target_pairs={{0,8},{1,9},{2,10},{3,11},{4,12},{5,13},{6,14},{7,15},{8,0},{9,1},... | collective-permute-start | bytes 344072 | tf_op jit(solution)/shard_map/ppermute | solution.py:21
  30.4 4.0 %collective-permute-done.16.refs_1_ = bf16[16,3584]{1,0:T(8,128)(2,1)S(1)} collective-permute-done((bf16[16,3584]{1,0:T(8,128)(2,1)}, bf16[16,3584]{1,0:T(8,128)(2,1)S(1)}, u32[]{:S(2)}, u32[]{:S(2)}) %collective-permute-start.16) | collective-permute-done | bytes 114720 | tf_op jit(solution)/shard_map/ppermute | solution.py:21
  34.3 1.2 %collective-permute-done.17.refs_3_ = bf16[16,3584]{1,0:T(8,128)(2,1)S(1)} collective-permute-done((bf16[16,3584]{1,0:T(8,128)(2,1)S(1)}, bf16[16,3584]{1,0:T(8,128)(2,1)S(1)}, u32[]{:S(2)}, u32[]{:S(2)}) %collective-permute-start.17) | collective-permute-done | bytes 114720 | tf_op jit(solution)/shard_map/ppermute | solution.py:21
  35.6 0.9 copy-done.9
  36.5 0.6 shard_map.91
  37.1 0.6 collective-permute-start.18
  37.7 0.6 collective-permute-start.19
  38.2 2.4 %collective-permute-start.20 = (bf16[40,3584]{1,0:T(8,128)(2,1)S(1)}, bf16[40,3584]{1,0:T(8,128)(2,1)S(1)}, u32[]{:S(2)}, u32[]{:S(2)}) collective-permute-start(bf16[40,3584]{1,0:T(8,128)(2,1)S(1)} %get-tuple-element.69), channel_id=1, source_target_pairs={{0,6},{1,7},{2,4},{3,5},{4,2},{5,3},{6,0},{7,1},{8,14},{9,15},{10,... | collective-permute-start | bytes 860168 | tf_op jit(solution)/shard_map/ppermute | solution.py:21
  40.6 2.0 %copy-done = bf16[1,3584,512]{2,1,0:T(8,128)(2,1)S(1)} copy-done((bf16[1,3584,512]{2,1,0:T(8,128)(2,1)S(1)}, bf16[1,3584,512]{2,1,0:T(8,128)(2,1)}, u32[]{:S(2)}) %copy-start) | copy-done | bytes 3670040
  42.7 2.0 %copy-done.2 = bf16[1,3584,512]{2,1,0:T(8,128)(2,1)S(1)} copy-done((bf16[1,3584,512]{2,1,0:T(8,128)(2,1)S(1)}, bf16[1,3584,512]{2,1,0:T(8,128)(2,1)}, u32[]{:S(2)}) %copy-start.2) | copy-done | bytes 3670040
  44.7 2.0 %copy-done.4 = bf16[1,512,3584]{2,1,0:T(8,128)(2,1)S(1)} copy-done((bf16[1,512,3584]{2,1,0:T(8,128)(2,1)S(1)}, bf16[1,512,3584]{2,1,0:T(8,128)(2,1)}, u32[]{:S(2)}) %copy-start.4) | copy-done | bytes 3670040
  46.8 2.0 %copy-done.7 = bf16[1,3584,512]{2,1,0:T(8,128)(2,1)S(1)} copy-done((bf16[1,3584,512]{2,1,0:T(8,128)(2,1)S(1)}, bf16[1,3584,512]{2,1,0:T(8,128)(2,1)}, u32[]{:S(2)}) %copy-start.7) | copy-done | bytes 3670040
  48.8 8.3 %shard_map.88 = (bf16[40,3584]{1,0:T(8,128)(2,1)S(1)}, bf16[40,3584]{1,0:T(8,128)(2,1)S(1)}, bf16[40,3584]{1,0:T(8,128)(2,1)S(1)}, bf16[40,3584]{1,0:T(8,128)(2,...) custom-call(bf16[40,3584]{1,0:T(8,128)(2,1)S(1)} %get-tuple-element.43.x0, ...), custom_call_target="tpu_custom_call" | custom-call | flops 3523215360 | bytes 25624576 | tf_op jit(solution)/shard_map/pallas_call | solution.py:43
  57.1 0.6 collective-permute-start.10
  57.7 0.6 collective-permute-start.11
  58.3 2.4 %collective-permute-start.12 = (bf16[40,3584]{1,0:T(8,128)(2,1)S(1)}, bf16[40,3584]{1,0:T(8,128)(2,1)S(1)}, u32[]{:S(2)}, u32[]{:S(2)}) collective-permute-start(bf16[40,3584]{1,0:T(8,128)(2,1)S(1)} %get-tuple-element.58), channel_id=1, source_target_pairs={{0,6},{1,7},{2,4},{3,5},{4,2},{5,3},{6,0},{7,1},{8,14},{9,15},{10,... | collective-permute-start | bytes 860168 | tf_op jit(solution)/shard_map/ppermute | solution.py:21
  60.7 11.4 %shard_map.92 = (bf16[40,3584]{1,0:T(8,128)(2,1)S(1)}, bf16[40,3584]{1,0:T(8,128)(2,1)S(1)}, bf16[40,3584]{1,0:T(8,128)(2,1)S(1)}, bf16[40,3584]{1,0:T(8,128)(2,1)S(1)}) custom-call(bf16[40,3584]{1,0:T(8,128)(2,1)S(1)} %get-tuple-element.66.x0, bf16[40,3584]{1,0:T(8,128)(2,1)S(1)} %collective-permute-done.18.x1, ...), custom_call_target="tpu_custom_call" | custom-call | flops 3523215360 | bytes 25624576 | tf_op jit(solution)/shard_map/pallas_call | solution.py:43
  72.2 0.6 collective-permute-start.21
  72.8 0.6 collective-permute-start.22
  73.3 2.4 %collective-permute-start.23 = (bf16[40,3584]{1,0:T(8,128)(2,1)S(1)}, bf16[40,3584]{1,0:T(8,128)(2,1)S(1)}, u32[]{:S(2)}, u32[]{:S(2)}) collective-permute-start(bf16[40,3584]{1,0:T(8,128)(2,1)S(1)} %get-tuple-element.75), channel_id=1, source_target_pairs={{0,6},{1,7},{2,4},{3,5},{4,2},{5,3},{6,0},{7,1},{8,14},{9,15},{10,... | collective-permute-start | bytes 860168 | tf_op jit(solution)/shard_map/ppermute | solution.py:21
  75.7 0.6 shard_map.89
  76.7 2.2 %collective-permute-start.14 = (bf16[16,3584]{1,0:T(8,128)(2,1)S(1)}, bf16[16,3584]{1,0:T(8,128)(2,1)S(1)}, u32[]{:S(2)}, u32[]{:S(2)}) collective-permute-start(bf16[16,3584]{1,0:T(8,128)(2,1)S(1)} %get-tuple-element.61), channel_id=1, source_target_pairs={{0,16},{1,17},{2,18},{3,19},{4,20},{5,21},{6,22},{7,23},{8,24},{9,... | collective-permute-start | bytes 344072 | tf_op jit(solution)/shard_map/ppermute | solution.py:21
  78.9 2.1 %collective-permute-done.21.second = bf16[40,3584]{1,0:T(8,128)(2,1)S(1)} collective-permute-done((bf16[40,3584]{1,0:T(8,128)(2,1)S(1)}, bf16[40,3584]{1,0:T(8,128)(2,1)S(1)}, u32[]{:S(2)}, u32[]{:S(2)}) %collective-permute-start.21) | collective-permute-done | bytes 286752 | tf_op jit(solution)/shard_map/ppermute | solution.py:21
  81.0 1.4 %collective-permute-start.15 = (bf16[16,3584]{1,0:T(8,128)(2,1)S(1)}, bf16[16,3584]{1,0:T(8,128)(2,1)S(1)}, u32[]{:S(2)}, u32[]{:S(2)}) collective-permute-start(bf16[16,3584]{1,0:T(8,128)(2,1)S(1)} %get-tuple-element.62), channel_id=1, source_target_pairs={{0,24},{1,25},{2,26},{3,27},{4,28},{5,29},{6,30},{7,31},{8,16},{9,... | collective-permute-start | bytes 344072 | tf_op jit(solution)/shard_map/ppermute | solution.py:21
  82.3 2.0 %collective-permute-done.22.third = bf16[40,3584]{1,0:T(8,128)(2,1)S(1)} collective-permute-done((bf16[40,3584]{1,0:T(8,128)(2,1)S(1)}, bf16[40,3584]{1,0:T(8,128)(2,1)S(1)}, u32[]{:S(2)}, u32[]{:S(2)}) %collective-permute-start.22) | collective-permute-done | bytes 286752 | tf_op jit(solution)/shard_map/ppermute | solution.py:21
  84.6 0.7 collective-permute-start.24
  85.3 1.3 %collective-permute-start.25 = (bf16[16,3584]{1,0:T(8,128)(2,1)S(1)}, bf16[16,3584]{1,0:T(8,128)(2,1)S(1)}, u32[]{:S(2)}, u32[]{:S(2)}) collective-permute-start(bf16[16,3584]{1,0:T(8,128)(2,1)S(1)} %get-tuple-element.78), channel_id=1, source_target_pairs={{0,16},{1,17},{2,18},{3,19},{4,20},{5,21},{6,22},{7,23},{8,24},{9,... | collective-permute-start | bytes 344072 | tf_op jit(solution)/shard_map/ppermute | solution.py:21
  86.6 2.5 %collective-permute-start.26 = (bf16[16,3584]{1,0:T(8,128)(2,1)S(1)}, bf16[16,3584]{1,0:T(8,128)(2,1)S(1)}, u32[]{:S(2)}, u32[]{:S(2)}) collective-permute-start(bf16[16,3584]{1,0:T(8,128)(2,1)S(1)} %get-tuple-element.79), channel_id=1, source_target_pairs={{0,24},{1,25},{2,26},{3,27},{4,28},{5,29},{6,30},{7,31},{8,16},{9,... | collective-permute-start | bytes 344072 | tf_op jit(solution)/shard_map/ppermute | solution.py:21
  89.1 0.7 shard_map.90
  89.8 0.8 collective-permute-done.24.refs_1_
  90.6 4.8 %collective-permute-done.25.refs_2_ = bf16[16,3584]{1,0:T(8,128)(2,1)S(1)} collective-permute-done((bf16[16,3584]{1,0:T(8,128)(2,1)S(1)}, bf16[16,3584]{1,0:T(8,128)(2,1)S(1)}, u32[]{:S(2)}, u32[]{:S(2)}) %collective-permute-start.25) | collective-permute-done | bytes 114720 | tf_op jit(solution)/shard_map/ppermute | solution.py:21
  95.4 0.7 shard_map.94
  (41 shorter events, 1.0 us)
Async XLA Ops:
  0.6 14.4 %collective-permute-start.3 = (bf16[1,3584,512]{2,1,0:T(8,128)(2,1)}, bf16[1,3584,512]{2,1,0:T(8,128)(2,1)S(1)}, u32[]{:S(2)}, u32[]{:S(2)}) collective-permute-start(bf16[1,3584,512]{2,1,0:T(8,128)(2,1)} %g0.1), channel_id=1, source_target_pairs={{0,1},{1,0},{2,3},{3,2},{4,5},{5,4},{6,7},{7,6},{8,9},{9,8},{10,11... | collective-permute-start | bytes 11010056 | tf_op jit(solution)/shard_map/ppermute | solution.py:21
  1.1 20.1 %collective-permute-start.4 = (bf16[1,3584,512]{2,1,0:T(8,128)(2,1)}, bf16[1,3584,512]{2,1,0:T(8,128)(2,1)}, u32[]{:S(2)}, u32[]{:S(2)}) collective-permute-start(bf16[1,3584,512]{2,1,0:T(8,128)(2,1)} %u0.1), channel_id=1, source_target_pairs={{0,1},{1,0},{2,3},{3,2},{4,5},{5,4},{6,7},{7,6},{8,9},{9,8},{10,11... | collective-permute-start | bytes 11010056 | tf_op jit(solution)/shard_map/ppermute | solution.py:21
  1.2 27.1 %collective-permute-start.9 = (bf16[1,512,3584]{2,1,0:T(8,128)(2,1)}, bf16[1,512,3584]{2,1,0:T(8,128)(2,1)}, u32[]{:S(2)}, u32[]{:S(2)}) collective-permute-start(bf16[1,512,3584]{2,1,0:T(8,128)(2,1)} %d0.1), channel_id=1, source_target_pairs={{0,1},{1,0},{2,3},{3,2},{4,5},{5,4},{6,7},{7,6},{8,9},{9,8},{10,11... | collective-permute-start | bytes 11010056 | tf_op jit(solution)/shard_map/ppermute | solution.py:21
  1.7 0.9 copy-start.10
  2.6 0.7 copy-start.11
  3.2 0.7 copy-start.12
  4.1 10.2 %collective-permute-start.1 = (bf16[16,3712]{1,0:T(8,128)(2,1)S(1)}, bf16[16,3712]{1,0:T(8,128)(2,1)S(1)}, u32[]{:S(2)}, u32[]{:S(2)}) collective-permute-start(bf16[16,3712]{1,0:T(8,128)(2,1)S(1)} %shard_map.86.refs_0_), channel_id=1, source_target_pairs={{0,16},{1,17},{2,18},{3,19},{4,20},{5,21},{6,22},{7,23},{8,24},{9,... | collective-permute-start | bytes 356360 | tf_op jit(solution)/shard_map/ppermute | solution.py:21
  7.9 12.4 %collective-permute-start = (bf16[16,3712]{1,0:T(8,128)(2,1)S(1)}, bf16[16,3712]{1,0:T(8,128)(2,1)S(1)}, u32[]{:S(2)}, u32[]{:S(2)}) collective-permute-start(bf16[16,3712]{1,0:T(8,128)(2,1)S(1)} %shard_map.86.refs_0_), channel_id=1, source_target_pairs={{0,8},{1,9},{2,10},{3,11},{4,12},{5,13},{6,14},{7,15},{8,0},{9,1},... | collective-permute-start | bytes 356360 | tf_op jit(solution)/shard_map/ppermute | solution.py:21
  14.3 5.9 %collective-permute-start.2 = (bf16[16,3712]{1,0:T(8,128)(2,1)S(1)}, bf16[16,3712]{1,0:T(8,128)(2,1)S(1)}, u32[]{:S(2)}, u32[]{:S(2)}) collective-permute-start(bf16[16,3712]{1,0:T(8,128)(2,1)S(1)} %collective-permute-done.1.refs_2_), channel_id=1, source_target_pairs={{0,8},{1,9},{2,10},{3,11},{4,12},{5,13},{6,14},{7,15},{8,0},{9,1},... | collective-permute-start | bytes 356360 | tf_op jit(solution)/shard_map/ppermute | solution.py:21
  15.0 1.9 %copy-start.6 = (bf16[1,3584,512]{2,1,0:T(8,128)(2,1)}, bf16[1,3584,512]{2,1,0:T(8,128)(2,1)S(1)}, u32[]{:S(2)}) copy-start(bf16[1,3584,512]{2,1,0:T(8,128)(2,1)S(1)} %collective-permute-done.3.g1) | copy-start | bytes 11010052
  16.9 9.0 %collective-permute-start.7 = (bf16[16,3584]{1,0:T(8,128)(2,1)}, bf16[16,3584]{1,0:T(8,128)(2,1)S(1)}, u32[]{:S(2)}, u32[]{:S(2)}) collective-permute-start(bf16[16,3584]{1,0:T(8,128)(2,1)} %refs_0_.1), channel_id=1, source_target_pairs={{0,16},{1,17},{2,18},{3,19},{4,20},{5,21},{6,22},{7,23},{8,24},{9,... | collective-permute-start | bytes 344072 | tf_op jit(solution)/shard_map/ppermute | solution.py:21
  21.3 16.9 %collective-permute-start.5 = (bf16[40,3584]{1,0:T(8,128)(2,1)S(1)}, bf16[40,3584]{1,0:T(8,128)(2,1)S(1)}, u32[]{:S(2)}, u32[]{:S(2)}) collective-permute-start(bf16[40,3584]{1,0:T(8,128)(2,1)S(1)} %get-tuple-element.45), channel_id=1, source_target_pairs={{0,2},{1,3},{2,0},{3,1},{4,6},{5,7},{6,4},{7,5},{8,10},{9,11},{10,... | collective-permute-start | bytes 860168 | tf_op jit(solution)/shard_map/ppermute | solution.py:21
  22.9 17.8 %collective-permute-start.6 = (bf16[40,3584]{1,0:T(8,128)(2,1)S(1)}, bf16[40,3584]{1,0:T(8,128)(2,1)S(1)}, u32[]{:S(2)}, u32[]{:S(2)}) collective-permute-start(bf16[40,3584]{1,0:T(8,128)(2,1)S(1)} %get-tuple-element.47), channel_id=1, source_target_pairs={{0,4},{1,5},{2,6},{3,7},{4,0},{5,1},{6,2},{7,3},{8,12},{9,13},{10,... | collective-permute-start | bytes 860168 | tf_op jit(solution)/shard_map/ppermute | solution.py:21
  25.9 14.7 %collective-permute-start.8 = (bf16[40,3584]{1,0:T(8,128)(2,1)S(1)}, bf16[40,3584]{1,0:T(8,128)(2,1)S(1)}, u32[]{:S(2)}, u32[]{:S(2)}) collective-permute-start(bf16[40,3584]{1,0:T(8,128)(2,1)S(1)} %get-tuple-element.51), channel_id=1, source_target_pairs={{0,6},{1,7},{2,4},{3,5},{4,2},{5,3},{6,0},{7,1},{8,14},{9,15},{10,... | collective-permute-start | bytes 860168 | tf_op jit(solution)/shard_map/ppermute | solution.py:21
  28.4 6.0 %collective-permute-start.16 = (bf16[16,3584]{1,0:T(8,128)(2,1)}, bf16[16,3584]{1,0:T(8,128)(2,1)S(1)}, u32[]{:S(2)}, u32[]{:S(2)}) collective-permute-start(bf16[16,3584]{1,0:T(8,128)(2,1)} %refs_0_.1), channel_id=1, source_target_pairs={{0,8},{1,9},{2,10},{3,11},{4,12},{5,13},{6,14},{7,15},{8,0},{9,1},... | collective-permute-start | bytes 344072 | tf_op jit(solution)/shard_map/ppermute | solution.py:21
  28.4 7.2 %collective-permute-start.17 = (bf16[16,3584]{1,0:T(8,128)(2,1)S(1)}, bf16[16,3584]{1,0:T(8,128)(2,1)S(1)}, u32[]{:S(2)}, u32[]{:S(2)}) collective-permute-start(bf16[16,3584]{1,0:T(8,128)(2,1)S(1)} %collective-permute-done.7.refs_2_), channel_id=1, source_target_pairs={{0,8},{1,9},{2,10},{3,11},{4,12},{5,13},{6,14},{7,15},{8,0},{9,1},... | collective-permute-start | bytes 344072 | tf_op jit(solution)/shard_map/ppermute | solution.py:21
  35.6 0.9 copy-start.9
  37.1 21.2 %collective-permute-start.18 = (bf16[40,3584]{1,0:T(8,128)(2,1)S(1)}, bf16[40,3584]{1,0:T(8,128)(2,1)S(1)}, u32[]{:S(2)}, u32[]{:S(2)}) collective-permute-start(bf16[40,3584]{1,0:T(8,128)(2,1)S(1)} %get-tuple-element.67), channel_id=1, source_target_pairs={{0,2},{1,3},{2,0},{3,1},{4,6},{5,7},{6,4},{7,5},{8,10},{9,11},{10,... | collective-permute-start | bytes 860168 | tf_op jit(solution)/shard_map/ppermute | solution.py:21
  37.7 23.0 %collective-permute-start.19 = (bf16[40,3584]{1,0:T(8,128)(2,1)S(1)}, bf16[40,3584]{1,0:T(8,128)(2,1)S(1)}, u32[]{:S(2)}, u32[]{:S(2)}) collective-permute-start(bf16[40,3584]{1,0:T(8,128)(2,1)S(1)} %get-tuple-element.68), channel_id=1, source_target_pairs={{0,4},{1,5},{2,6},{3,7},{4,0},{5,1},{6,2},{7,3},{8,12},{9,13},{10,... | collective-permute-start | bytes 860168 | tf_op jit(solution)/shard_map/ppermute | solution.py:21
  38.2 22.5 %collective-permute-start.20 = (bf16[40,3584]{1,0:T(8,128)(2,1)S(1)}, bf16[40,3584]{1,0:T(8,128)(2,1)S(1)}, u32[]{:S(2)}, u32[]{:S(2)}) collective-permute-start(bf16[40,3584]{1,0:T(8,128)(2,1)S(1)} %get-tuple-element.69), channel_id=1, source_target_pairs={{0,6},{1,7},{2,4},{3,5},{4,2},{5,3},{6,0},{7,1},{8,14},{9,15},{10,... | collective-permute-start | bytes 860168 | tf_op jit(solution)/shard_map/ppermute | solution.py:21
  40.6 2.0 %copy-start = (bf16[1,3584,512]{2,1,0:T(8,128)(2,1)S(1)}, bf16[1,3584,512]{2,1,0:T(8,128)(2,1)}, u32[]{:S(2)}) copy-start(bf16[1,3584,512]{2,1,0:T(8,128)(2,1)} %g0.1) | copy-start | bytes 11010052
  42.7 2.0 %copy-start.2 = (bf16[1,3584,512]{2,1,0:T(8,128)(2,1)S(1)}, bf16[1,3584,512]{2,1,0:T(8,128)(2,1)}, u32[]{:S(2)}) copy-start(bf16[1,3584,512]{2,1,0:T(8,128)(2,1)} %u0.1) | copy-start | bytes 11010052
  44.7 2.0 %copy-start.4 = (bf16[1,512,3584]{2,1,0:T(8,128)(2,1)S(1)}, bf16[1,512,3584]{2,1,0:T(8,128)(2,1)}, u32[]{:S(2)}) copy-start(bf16[1,512,3584]{2,1,0:T(8,128)(2,1)} %d0.1) | copy-start | bytes 11010052
  46.8 2.0 %copy-start.7 = (bf16[1,3584,512]{2,1,0:T(8,128)(2,1)S(1)}, bf16[1,3584,512]{2,1,0:T(8,128)(2,1)}, u32[]{:S(2)}) copy-start(bf16[1,3584,512]{2,1,0:T(8,128)(2,1)} %copy-done.6) | copy-start | bytes 11010052
  48.8 11.9 %copy-start.1 = (bf16[1,3584,512]{2,1,0:T(8,128)(2,1)S(1)}, bf16[1,3584,512]{2,1,0:T(8,128)(2,1)}, u32[]{:S(2)}) copy-start(bf16[1,3584,512]{2,1,0:T(8,128)(2,1)} %g0.1) | copy-start | bytes 11010052
  48.8 11.9 %copy-start.3 = (bf16[1,3584,512]{2,1,0:T(8,128)(2,1)S(1)}, bf16[1,3584,512]{2,1,0:T(8,128)(2,1)}, u32[]{:S(2)}) copy-start(bf16[1,3584,512]{2,1,0:T(8,128)(2,1)} %u0.1) | copy-start | bytes 11010052
  48.8 11.9 %copy-start.5 = (bf16[1,512,3584]{2,1,0:T(8,128)(2,1)S(1)}, bf16[1,512,3584]{2,1,0:T(8,128)(2,1)}, u32[]{:S(2)}) copy-start(bf16[1,512,3584]{2,1,0:T(8,128)(2,1)} %d0.1) | copy-start | bytes 11010052
  48.8 11.9 %copy-start.8 = (bf16[1,3584,512]{2,1,0:T(8,128)(2,1)S(1)}, bf16[1,3584,512]{2,1,0:T(8,128)(2,1)}, u32[]{:S(2)}) copy-start(bf16[1,3584,512]{2,1,0:T(8,128)(2,1)} %copy-done.6) | copy-start | bytes 11010052
  57.1 16.2 %collective-permute-start.10 = (bf16[40,3584]{1,0:T(8,128)(2,1)S(1)}, bf16[40,3584]{1,0:T(8,128)(2,1)S(1)}, u32[]{:S(2)}, u32[]{:S(2)}) collective-permute-start(bf16[40,3584]{1,0:T(8,128)(2,1)S(1)} %get-tuple-element.56), channel_id=1, source_target_pairs={{0,2},{1,3},{2,0},{3,1},{4,6},{5,7},{6,4},{7,5},{8,10},{9,11},{10,... | collective-permute-start | bytes 860168 | tf_op jit(solution)/shard_map/ppermute | solution.py:21
  57.7 18.0 %collective-permute-start.11 = (bf16[40,3584]{1,0:T(8,128)(2,1)S(1)}, bf16[40,3584]{1,0:T(8,128)(2,1)S(1)}, u32[]{:S(2)}, u32[]{:S(2)}) collective-permute-start(bf16[40,3584]{1,0:T(8,128)(2,1)S(1)} %get-tuple-element.57), channel_id=1, source_target_pairs={{0,4},{1,5},{2,6},{3,7},{4,0},{5,1},{6,2},{7,3},{8,12},{9,13},{10,... | collective-permute-start | bytes 860168 | tf_op jit(solution)/shard_map/ppermute | solution.py:21
  58.3 17.5 %collective-permute-start.12 = (bf16[40,3584]{1,0:T(8,128)(2,1)S(1)}, bf16[40,3584]{1,0:T(8,128)(2,1)S(1)}, u32[]{:S(2)}, u32[]{:S(2)}) collective-permute-start(bf16[40,3584]{1,0:T(8,128)(2,1)S(1)} %get-tuple-element.58), channel_id=1, source_target_pairs={{0,6},{1,7},{2,4},{3,5},{4,2},{5,3},{6,0},{7,1},{8,14},{9,15},{10,... | collective-permute-start | bytes 860168 | tf_op jit(solution)/shard_map/ppermute | solution.py:21
  72.2 8.8 %collective-permute-start.21 = (bf16[40,3584]{1,0:T(8,128)(2,1)S(1)}, bf16[40,3584]{1,0:T(8,128)(2,1)S(1)}, u32[]{:S(2)}, u32[]{:S(2)}) collective-permute-start(bf16[40,3584]{1,0:T(8,128)(2,1)S(1)} %get-tuple-element.73), channel_id=1, source_target_pairs={{0,2},{1,3},{2,0},{3,1},{4,6},{5,7},{6,4},{7,5},{8,10},{9,11},{10,... | collective-permute-start | bytes 860168 | tf_op jit(solution)/shard_map/ppermute | solution.py:21
  72.8 11.5 %collective-permute-start.22 = (bf16[40,3584]{1,0:T(8,128)(2,1)S(1)}, bf16[40,3584]{1,0:T(8,128)(2,1)S(1)}, u32[]{:S(2)}, u32[]{:S(2)}) collective-permute-start(bf16[40,3584]{1,0:T(8,128)(2,1)S(1)} %get-tuple-element.74), channel_id=1, source_target_pairs={{0,4},{1,5},{2,6},{3,7},{4,0},{5,1},{6,2},{7,3},{8,12},{9,13},{10,... | collective-permute-start | bytes 860168 | tf_op jit(solution)/shard_map/ppermute | solution.py:21
  73.3 10.9 %collective-permute-start.23 = (bf16[40,3584]{1,0:T(8,128)(2,1)S(1)}, bf16[40,3584]{1,0:T(8,128)(2,1)S(1)}, u32[]{:S(2)}, u32[]{:S(2)}) collective-permute-start(bf16[40,3584]{1,0:T(8,128)(2,1)S(1)} %get-tuple-element.75), channel_id=1, source_target_pairs={{0,6},{1,7},{2,4},{3,5},{4,2},{5,3},{6,0},{7,1},{8,14},{9,15},{10,... | collective-permute-start | bytes 860168 | tf_op jit(solution)/shard_map/ppermute | solution.py:21
  76.4 10.3 %collective-permute-start.13 = (bf16[16,3584]{1,0:T(8,128)(2,1)S(1)}, bf16[16,3584]{1,0:T(8,128)(2,1)S(1)}, u32[]{:S(2)}, u32[]{:S(2)}) collective-permute-start(bf16[16,3584]{1,0:T(8,128)(2,1)S(1)} %get-tuple-element.60), channel_id=1, source_target_pairs={{0,8},{1,9},{2,10},{3,11},{4,12},{5,13},{6,14},{7,15},{8,0},{9,1},... | collective-permute-start | bytes 344072 | tf_op jit(solution)/shard_map/ppermute | solution.py:21
  76.7 12.4 %collective-permute-start.14 = (bf16[16,3584]{1,0:T(8,128)(2,1)S(1)}, bf16[16,3584]{1,0:T(8,128)(2,1)S(1)}, u32[]{:S(2)}, u32[]{:S(2)}) collective-permute-start(bf16[16,3584]{1,0:T(8,128)(2,1)S(1)} %get-tuple-element.61), channel_id=1, source_target_pairs={{0,16},{1,17},{2,18},{3,19},{4,20},{5,21},{6,22},{7,23},{8,24},{9,... | collective-permute-start | bytes 344072 | tf_op jit(solution)/shard_map/ppermute | solution.py:21
  81.0 8.1 %collective-permute-start.15 = (bf16[16,3584]{1,0:T(8,128)(2,1)S(1)}, bf16[16,3584]{1,0:T(8,128)(2,1)S(1)}, u32[]{:S(2)}, u32[]{:S(2)}) collective-permute-start(bf16[16,3584]{1,0:T(8,128)(2,1)S(1)} %get-tuple-element.62), channel_id=1, source_target_pairs={{0,24},{1,25},{2,26},{3,27},{4,28},{5,29},{6,30},{7,31},{8,16},{9,... | collective-permute-start | bytes 344072 | tf_op jit(solution)/shard_map/ppermute | solution.py:21
  84.6 6.0 %collective-permute-start.24 = (bf16[16,3584]{1,0:T(8,128)(2,1)S(1)}, bf16[16,3584]{1,0:T(8,128)(2,1)S(1)}, u32[]{:S(2)}, u32[]{:S(2)}) collective-permute-start(bf16[16,3584]{1,0:T(8,128)(2,1)S(1)} %get-tuple-element.77), channel_id=1, source_target_pairs={{0,8},{1,9},{2,10},{3,11},{4,12},{5,13},{6,14},{7,15},{8,0},{9,1},... | collective-permute-start | bytes 344072 | tf_op jit(solution)/shard_map/ppermute | solution.py:21
  85.3 10.1 %collective-permute-start.25 = (bf16[16,3584]{1,0:T(8,128)(2,1)S(1)}, bf16[16,3584]{1,0:T(8,128)(2,1)S(1)}, u32[]{:S(2)}, u32[]{:S(2)}) collective-permute-start(bf16[16,3584]{1,0:T(8,128)(2,1)S(1)} %get-tuple-element.78), channel_id=1, source_target_pairs={{0,16},{1,17},{2,18},{3,19},{4,20},{5,21},{6,22},{7,23},{8,24},{9,... | collective-permute-start | bytes 344072 | tf_op jit(solution)/shard_map/ppermute | solution.py:21
  86.6 8.8 %collective-permute-start.26 = (bf16[16,3584]{1,0:T(8,128)(2,1)S(1)}, bf16[16,3584]{1,0:T(8,128)(2,1)S(1)}, u32[]{:S(2)}, u32[]{:S(2)}) collective-permute-start(bf16[16,3584]{1,0:T(8,128)(2,1)S(1)} %get-tuple-element.79), channel_id=1, source_target_pairs={{0,24},{1,25},{2,26},{3,27},{4,28},{5,29},{6,30},{7,31},{8,16},{9,... | collective-permute-start | bytes 344072 | tf_op jit(solution)/shard_map/ppermute | solution.py:21

commit v10 on v8

--- a/solution.py
+++ b/solution.py
@@ -32,6 +32,10 @@
 
 def chunk_of(width):
     return 512 if width % 512 == 0 else LANES
+
+
+def back_chunk(width):
+    return width // 2 if width % (2 * LANES) == 0 else LANES
 
 
 def column_chunks(width):
@@ -177,7 +181,7 @@
     *slabs, o0, o1, o2, o3, for_up, for_gate, x, hidden, into, back, sems = refs
     rows, width = x.shape
     units = back.shape[0] // 2
-    chunk, tiles, chunks = chunk_of(width), 2 * units // tile, width // chunk_of(width)
+    chunk, tiles, chunks = back_chunk(width), 2 * units // tile, width // back_chunk(width)
     triples = []
     for number in range(tiles):
         slab, at = divmod(number * tile, units)
@@ -225,7 +229,7 @@
     *slabs, o0, o1, o2, o3, x, grads, into, back, sems = refs
     rows, width = x.shape
     units = back.shape[0] // 2
-    chunk, chunks = chunk_of(width), width // chunk_of(width)
+    chunk, chunks = back_chunk(width), width // back_chunk(width)
     triples = []
     for slab in range(2):
         place = back.at[pl.ds(slab * units, units)]
@@ -297,7 +301,8 @@
         flops=2 * rows * slots * width,
     )
     far_cots = swap(after(cotangent, held[blocks // 2], other[0]), devices // 2)
-    packed = [after(value, far_cots, *other[:2]) for value in packed]
+    packed = [after(value, *other[:2]) for value in packed]
+    packed[-1] = after(packed[-1], far_cots)
     x = [packed[0]] + [swap(value, offset) for value, offset in zip(packed[1:], PLANE[1:])]
 
     cots, offset = {0: cotangent, blocks // 2: far_cots}, devices // 4
@@ -317,8 +322,8 @@
     grads = [packed[0]] + [swap(value, offset) for value, offset in zip(packed[1:], PLANE[1:])]
 
     all_taken = len(PLANE) * taken
-    tile = 256 if hidden % 256 == 0 else LANES
-    tiles, chunks = 2 * hidden // tile, width // chunk_of(width)
+    tile = hidden
+    tiles, chunks = 2 * hidden // tile, width // back_chunk(width)
     slab_room = [pltpu.VMEM((width, 4 * hidden), bf16), pltpu.VMEM((2 * hidden, width), bf16)]
     flops = 2 * 3 * all_taken * width * 2 * hidden
     *outs, for_up, for_gate = call(

time: 87.9 us -> 86.4 us (0.983)
  waiting for transfers between devices: 20.5 us -> 16.8 us
  starting transfers between devices: 39.8 us -> 42.9 us
    ppermute x27, waiting for transfers between devices: 20.5 us -> 16.8 us  [swap(): lax.ppermute(value, 'expert', [(i, i ^ offset) for i in range(devices)])]
    ppermute x27, starting transfers between devices: 39.8 us -> 42.9 us  [swap(): lax.ppermute(value, 'expert', [(i, i ^ offset) for i in range(devices)])]
where the time goes in v10:
time: 86.4 us; the launch traced here: 86.2 us
  starting transfers between devices  42.9 us (50%)
  Pallas kernels  22.7 us (26%)
  waiting for transfers between devices  16.8 us (19%)
  local copies, waits for them, and re-layouts  3.17 us (4%)
    ppermute x27, starting transfers between devices, swap(): lax.ppermute(value, 'expert', [(i, i ^ offset) for i in range(devices)])  42.9 us
    pallas_call x9, Pallas kernels, call(): pl.pallas_call(body, out_shape=outs, in_specs=[whole] * len(args) if in_s...  22.7 us
    ppermute x27, waiting for transfers between devices, swap(): lax.ppermute(value, 'expert', [(i, i ^ offset) for i in range(devices)])  16.8 us
    unnamed x8, local copies, waits for them, and re-layouts  3.17 us
  transfers between devices with their start and end apart: 27, of which 8 were waited for; matrix products, arithmetic and copies ran while one was open for 0% of the time, Pallas kernels for 26%

profile of v10, /device:TPU:0, one launch (start us, length us, event | category | flops | bytes accessed | tf_op | source)
XLA Modules:
  0.0 86.2 jit_solution(9773232091169503439)
XLA Ops:
  0.6 0.5 collective-permute-start.3
  1.1 0.1 collective-permute-start.4
  1.2 0.4 collective-permute-start.9
  1.7 0.9 %copy-done.1 = bf16[16,3584]{1,0:T(8,128)(2,1)S(1)} copy-done((bf16[16,3584]{1,0:T(8,128)(2,1)S(1)}, bf16[16,3584]{1,0:T(8,128)(2,1)}, u32[]{:S(2)}) %copy-start.1) | copy-done | bytes 114712
  2.6 0.7 copy-done.2
  3.2 0.7 copy-done.3
  3.9 0.2 shard_map.86.refs_0_
  4.1 3.7 %collective-permute-start.1 = (bf16[16,3712]{1,0:T(8,128)(2,1)S(1)}, bf16[16,3712]{1,0:T(8,128)(2,1)S(1)}, u32[]{:S(2)}, u32[]{:S(2)}) collective-permute-start(bf16[16,3712]{1,0:T(8,128)(2,1)S(1)} %shard_map.86.refs_0_), channel_id=1, source_target_pairs={{0,16},{1,17},{2,18},{3,19},{4,20},{5,21},{6,22},{7,23},{8,24},{9,... | collective-permute-start | bytes 356360 | tf_op jit(solution)/shard_map/ppermute | solution.py:22
  7.9 1.6 %collective-permute-start = (bf16[16,3712]{1,0:T(8,128)(2,1)S(1)}, bf16[16,3712]{1,0:T(8,128)(2,1)S(1)}, u32[]{:S(2)}, u32[]{:S(2)}) collective-permute-start(bf16[16,3712]{1,0:T(8,128)(2,1)S(1)} %shard_map.86.refs_0_), channel_id=1, source_target_pairs={{0,8},{1,9},{2,10},{3,11},{4,12},{5,13},{6,14},{7,15},{8,0},{9,1},... | collective-permute-start | bytes 356360 | tf_op jit(solution)/shard_map/ppermute | solution.py:22
  9.4 4.9 %collective-permute-done.1.refs_2_ = bf16[16,3712]{1,0:T(8,128)(2,1)S(1)} collective-permute-done((bf16[16,3712]{1,0:T(8,128)(2,1)S(1)}, bf16[16,3712]{1,0:T(8,128)(2,1)S(1)}, u32[]{:S(2)}, u32[]{:S(2)}) %collective-permute-start.1) | collective-permute-done | bytes 118816 | tf_op jit(solution)/shard_map/ppermute | solution.py:22
  14.3 0.6 collective-permute-start.2
  15.0 3.4 %collective-permute-start.7 = (bf16[16,3584]{1,0:T(8,128)(2,1)}, bf16[16,3584]{1,0:T(8,128)(2,1)S(1)}, u32[]{:S(2)}, u32[]{:S(2)}) collective-permute-start(bf16[16,3584]{1,0:T(8,128)(2,1)} %refs_0_.4), channel_id=1, source_target_pairs={{0,16},{1,17},{2,18},{3,19},{4,20},{5,21},{6,22},{7,23},{8,24},{9,... | collective-permute-start | bytes 344072 | tf_op jit(solution)/shard_map/ppermute | solution.py:22
  18.4 0.0 collective-permute-done.refs_1_
  18.4 0.9 %collective-permute-done.2.refs_3_ = bf16[16,3712]{1,0:T(8,128)(2,1)S(1)} collective-permute-done((bf16[16,3712]{1,0:T(8,128)(2,1)S(1)}, bf16[16,3712]{1,0:T(8,128)(2,1)S(1)}, u32[]{:S(2)}, u32[]{:S(2)}) %collective-permute-start.2) | collective-permute-done | bytes 118816 | tf_op jit(solution)/shard_map/ppermute | solution.py:22
  19.2 1.0 %shard_map.87 = (bf16[40,3584]{1,0:T(8,128)(2,1)S(1)}, bf16[40,3584]{1,0:T(8,128)(2,1)S(1)}, bf16[40,3584]{1,0:T(8,128)(2,1)S(1)}, bf16[40,3584]{1,0:T(8,128)(2,...) custom-call(s32[1]{0:T(128)} %bitcast.chip, bf16[16,3712]{1,0:T(8,128)(2,1)S(1)} %shard_map.86.refs_0_, ...), custom_call_target="tpu_custom_call" | custom-call | flops 117440512 | bytes 1753092 | tf_op jit(solution)/shard_map/pallas_call | solution.py:48
  20.3 1.6 %collective-permute-start.5 = (bf16[40,3584]{1,0:T(8,128)(2,1)S(1)}, bf16[40,3584]{1,0:T(8,128)(2,1)S(1)}, u32[]{:S(2)}, u32[]{:S(2)}) collective-permute-start(bf16[40,3584]{1,0:T(8,128)(2,1)S(1)} %get-tuple-element.42), channel_id=1, source_target_pairs={{0,2},{1,3},{2,0},{3,1},{4,6},{5,7},{6,4},{7,5},{8,10},{9,11},{10,... | collective-permute-start | bytes 860168 | tf_op jit(solution)/shard_map/ppermute | solution.py:22
  21.8 1.5 %collective-permute-start.6 = (bf16[40,3584]{1,0:T(8,128)(2,1)S(1)}, bf16[40,3584]{1,0:T(8,128)(2,1)S(1)}, u32[]{:S(2)}, u32[]{:S(2)}) collective-permute-start(bf16[40,3584]{1,0:T(8,128)(2,1)S(1)} %get-tuple-element.44), channel_id=1, source_target_pairs={{0,4},{1,5},{2,6},{3,7},{4,0},{5,1},{6,2},{7,3},{8,12},{9,13},{10,... | collective-permute-start | bytes 860168 | tf_op jit(solution)/shard_map/ppermute | solution.py:22
  23.4 0.7 collective-permute-done.7.refs_2_
  24.1 2.4 %collective-permute-start.8 = (bf16[40,3584]{1,0:T(8,128)(2,1)S(1)}, bf16[40,3584]{1,0:T(8,128)(2,1)S(1)}, u32[]{:S(2)}, u32[]{:S(2)}) collective-permute-start(bf16[40,3584]{1,0:T(8,128)(2,1)S(1)} %get-tuple-element.48), channel_id=1, source_target_pairs={{0,6},{1,7},{2,4},{3,5},{4,2},{5,3},{6,0},{7,1},{8,14},{9,15},{10,... | collective-permute-start | bytes 860168 | tf_op jit(solution)/shard_map/ppermute | solution.py:22
  26.6 0.3 collective-permute-start.16
  26.8 1.8 %collective-permute-start.17 = (bf16[16,3584]{1,0:T(8,128)(2,1)S(1)}, bf16[16,3584]{1,0:T(8,128)(2,1)S(1)}, u32[]{:S(2)}, u32[]{:S(2)}) collective-permute-start(bf16[16,3584]{1,0:T(8,128)(2,1)S(1)} %collective-permute-done.7.refs_2_), channel_id=1, source_target_pairs={{0,8},{1,9},{2,10},{3,11},{4,12},{5,13},{6,14},{7,15},{8,0},{9,1},... | collective-permute-start | bytes 344072 | tf_op jit(solution)/shard_map/ppermute | solution.py:22
  28.6 3.0 %collective-permute-done.16.refs_1_ = bf16[16,3584]{1,0:T(8,128)(2,1)S(1)} collective-permute-done((bf16[16,3584]{1,0:T(8,128)(2,1)}, bf16[16,3584]{1,0:T(8,128)(2,1)S(1)}, u32[]{:S(2)}, u32[]{:S(2)}) %collective-permute-start.16) | collective-permute-done | bytes 114720 | tf_op jit(solution)/shard_map/ppermute | solution.py:22
  31.6 1.2 %collective-permute-done.17.refs_3_ = bf16[16,3584]{1,0:T(8,128)(2,1)S(1)} collective-permute-done((bf16[16,3584]{1,0:T(8,128)(2,1)S(1)}, bf16[16,3584]{1,0:T(8,128)(2,1)S(1)}, u32[]{:S(2)}, u32[]{:S(2)}) %collective-permute-start.17) | collective-permute-done | bytes 114720 | tf_op jit(solution)/shard_map/ppermute | solution.py:22
  32.8 0.9 %copy-done = bf16[16,3584]{1,0:T(8,128)(2,1)S(1)} copy-done((bf16[16,3584]{1,0:T(8,128)(2,1)S(1)}, bf16[16,3584]{1,0:T(8,128)(2,1)}, u32[]{:S(2)}) %copy-start) | copy-done | bytes 114712
  33.7 0.6 shard_map.91
  34.3 0.6 collective-permute-start.18
  34.9 0.5 collective-permute-start.19
  35.4 2.4 %collective-permute-start.20 = (bf16[40,3584]{1,0:T(8,128)(2,1)S(1)}, bf16[40,3584]{1,0:T(8,128)(2,1)S(1)}, u32[]{:S(2)}, u32[]{:S(2)}) collective-permute-start(bf16[40,3584]{1,0:T(8,128)(2,1)S(1)} %get-tuple-element.63), channel_id=1, source_target_pairs={{0,6},{1,7},{2,4},{3,5},{4,2},{5,3},{6,0},{7,1},{8,14},{9,15},{10,... | collective-permute-start | bytes 860168 | tf_op jit(solution)/shard_map/ppermute | solution.py:22
  37.9 8.2 %shard_map.88 = (bf16[40,3584]{1,0:T(8,128)(2,1)S(1)}, bf16[40,3584]{1,0:T(8,128)(2,1)S(1)}, bf16[40,3584]{1,0:T(8,128)(2,1)S(1)}, bf16[40,3584]{1,0:T(8,128)(2,...) custom-call(bf16[40,3584]{1,0:T(8,128)(2,1)S(1)} %get-tuple-element.40.x0, ...), custom_call_target="tpu_custom_call" | custom-call | flops 3523215360 | bytes 25624576 | tf_op jit(solution)/shard_map/pallas_call | solution.py:48
  46.1 0.6 collective-permute-start.10
  46.7 0.5 collective-permute-start.11
  47.2 2.4 %collective-permute-start.12 = (bf16[40,3584]{1,0:T(8,128)(2,1)S(1)}, bf16[40,3584]{1,0:T(8,128)(2,1)S(1)}, u32[]{:S(2)}, u32[]{:S(2)}) collective-permute-start(bf16[40,3584]{1,0:T(8,128)(2,1)S(1)} %get-tuple-element.52), channel_id=1, source_target_pairs={{0,6},{1,7},{2,4},{3,5},{4,2},{5,3},{6,0},{7,1},{8,14},{9,15},{10,... | collective-permute-start | bytes 860168 | tf_op jit(solution)/shard_map/ppermute | solution.py:22
  49.7 10.4 %shard_map.92 = (bf16[40,3584]{1,0:T(8,128)(2,1)S(1)}, bf16[40,3584]{1,0:T(8,128)(2,1)S(1)}, bf16[40,3584]{1,0:T(8,128)(2,1)S(1)}, bf16[40,3584]{1,0:T(8,128)(2,1)S(1)}) custom-call(bf16[40,3584]{1,0:T(8,128)(2,1)S(1)} %get-tuple-element.60.x0, bf16[40,3584]{1,0:T(8,128)(2,1)S(1)} %collective-permute-done.18.x1, ...), custom_call_target="tpu_custom_call" | custom-call | flops 3523215360 | bytes 25624576 | tf_op jit(solution)/shard_map/pallas_call | solution.py:48
  60.0 1.2 %collective-permute-start.21 = (bf16[40,3584]{1,0:T(8,128)(2,1)S(1)}, bf16[40,3584]{1,0:T(8,128)(2,1)S(1)}, u32[]{:S(2)}, u32[]{:S(2)}) collective-permute-start(bf16[40,3584]{1,0:T(8,128)(2,1)S(1)} %get-tuple-element.67), channel_id=1, source_target_pairs={{0,2},{1,3},{2,0},{3,1},{4,6},{5,7},{6,4},{7,5},{8,10},{9,11},{10,... | collective-permute-start | bytes 860168 | tf_op jit(solution)/shard_map/ppermute | solution.py:22
  61.3 0.6 collective-permute-start.22
  61.8 1.8 %collective-permute-start.23 = (bf16[40,3584]{1,0:T(8,128)(2,1)S(1)}, bf16[40,3584]{1,0:T(8,128)(2,1)S(1)}, u32[]{:S(2)}, u32[]{:S(2)}) collective-permute-start(bf16[40,3584]{1,0:T(8,128)(2,1)S(1)} %get-tuple-element.69), channel_id=1, source_target_pairs={{0,6},{1,7},{2,4},{3,5},{4,2},{5,3},{6,0},{7,1},{8,14},{9,15},{10,... | collective-permute-start | bytes 860168 | tf_op jit(solution)/shard_map/ppermute | solution.py:22
  63.6 0.6 shard_map.89
  64.2 1.0 %collective-permute-start.13 = (bf16[16,3584]{1,0:T(8,128)(2,1)S(1)}, bf16[16,3584]{1,0:T(8,128)(2,1)S(1)}, u32[]{:S(2)}, u32[]{:S(2)}) collective-permute-start(bf16[16,3584]{1,0:T(8,128)(2,1)S(1)} %get-tuple-element.54), channel_id=1, source_target_pairs={{0,8},{1,9},{2,10},{3,11},{4,12},{5,13},{6,14},{7,15},{8,0},{9,1},... | collective-permute-start | bytes 344072 | tf_op jit(solution)/shard_map/ppermute | solution.py:22
  65.2 4.5 %collective-permute-start.14 = (bf16[16,3584]{1,0:T(8,128)(2,1)S(1)}, bf16[16,3584]{1,0:T(8,128)(2,1)S(1)}, u32[]{:S(2)}, u32[]{:S(2)}) collective-permute-start(bf16[16,3584]{1,0:T(8,128)(2,1)S(1)} %get-tuple-element.55), channel_id=1, source_target_pairs={{0,16},{1,17},{2,18},{3,19},{4,20},{5,21},{6,22},{7,23},{8,24},{9,... | collective-permute-start | bytes 344072 | tf_op jit(solution)/shard_map/ppermute | solution.py:22
  69.7 3.7 %collective-permute-start.15 = (bf16[16,3584]{1,0:T(8,128)(2,1)S(1)}, bf16[16,3584]{1,0:T(8,128)(2,1)S(1)}, u32[]{:S(2)}, u32[]{:S(2)}) collective-permute-start(bf16[16,3584]{1,0:T(8,128)(2,1)S(1)} %get-tuple-element.56), channel_id=1, source_target_pairs={{0,24},{1,25},{2,26},{3,27},{4,28},{5,29},{6,30},{7,31},{8,16},{9,... | collective-permute-start | bytes 344072 | tf_op jit(solution)/shard_map/ppermute | solution.py:22
  73.4 0.3 shard_map.93
  73.7 0.5 collective-permute-start.24
  74.3 4.6 %collective-permute-start.25 = (bf16[16,3584]{1,0:T(8,128)(2,1)S(1)}, bf16[16,3584]{1,0:T(8,128)(2,1)S(1)}, u32[]{:S(2)}, u32[]{:S(2)}) collective-permute-start(bf16[16,3584]{1,0:T(8,128)(2,1)S(1)} %get-tuple-element.72), channel_id=1, source_target_pairs={{0,16},{1,17},{2,18},{3,19},{4,20},{5,21},{6,22},{7,23},{8,24},{9,... | collective-permute-start | bytes 344072 | tf_op jit(solution)/shard_map/ppermute | solution.py:22
  78.8 0.7 shard_map.90
  79.5 0.8 collective-permute-done.24.refs_1_
  80.4 3.3 %collective-permute-done.25.refs_2_ = bf16[16,3584]{1,0:T(8,128)(2,1)S(1)} collective-permute-done((bf16[16,3584]{1,0:T(8,128)(2,1)S(1)}, bf16[16,3584]{1,0:T(8,128)(2,1)S(1)}, u32[]{:S(2)}, u32[]{:S(2)}) %collective-permute-start.25) | collective-permute-done | bytes 114720 | tf_op jit(solution)/shard_map/ppermute | solution.py:22
  83.6 1.9 %collective-permute-done.26.refs_3_ = bf16[16,3584]{1,0:T(8,128)(2,1)S(1)} collective-permute-done((bf16[16,3584]{1,0:T(8,128)(2,1)S(1)}, bf16[16,3584]{1,0:T(8,128)(2,1)S(1)}, u32[]{:S(2)}, u32[]{:S(2)}) %collective-permute-start.26) | collective-permute-done | bytes 114720 | tf_op jit(solution)/shard_map/ppermute | solution.py:22
  85.5 0.7 shard_map.94
  (23 shorter events, 0.1 us)
Async XLA Ops:
  0.6 14.4 %collective-permute-start.3 = (bf16[1,3584,512]{2,1,0:T(8,128)(2,1)}, bf16[1,3584,512]{2,1,0:T(8,128)(2,1)}, u32[]{:S(2)}, u32[]{:S(2)}) collective-permute-start(bf16[1,3584,512]{2,1,0:T(8,128)(2,1)} %refs_0_.5), channel_id=1, source_target_pairs={{0,1},{1,0},{2,3},{3,2},{4,5},{5,4},{6,7},{7,6},{8,9},{9,8},{10,11... | collective-permute-start | bytes 11010056 | tf_op jit(solution)/shard_map/ppermute | solution.py:22
  1.1 19.1 %collective-permute-start.4 = (bf16[1,3584,512]{2,1,0:T(8,128)(2,1)}, bf16[1,3584,512]{2,1,0:T(8,128)(2,1)}, u32[]{:S(2)}, u32[]{:S(2)}) collective-permute-start(bf16[1,3584,512]{2,1,0:T(8,128)(2,1)} %refs_1_.3), channel_id=1, source_target_pairs={{0,1},{1,0},{2,3},{3,2},{4,5},{5,4},{6,7},{7,6},{8,9},{9,8},{10,11... | collective-permute-start | bytes 11010056 | tf_op jit(solution)/shard_map/ppermute | solution.py:22
  1.2 25.3 %collective-permute-start.9 = (bf16[1,512,3584]{2,1,0:T(8,128)(2,1)}, bf16[1,512,3584]{2,1,0:T(8,128)(2,1)}, u32[]{:S(2)}, u32[]{:S(2)}) collective-permute-start(bf16[1,512,3584]{2,1,0:T(8,128)(2,1)} %refs_2_.3), channel_id=1, source_target_pairs={{0,1},{1,0},{2,3},{3,2},{4,5},{5,4},{6,7},{7,6},{8,9},{9,8},{10,11... | collective-permute-start | bytes 11010056 | tf_op jit(solution)/shard_map/ppermute | solution.py:22
  1.7 0.9 %copy-start.1 = (bf16[16,3584]{1,0:T(8,128)(2,1)S(1)}, bf16[16,3584]{1,0:T(8,128)(2,1)}, u32[]{:S(2)}) copy-start(bf16[16,3584]{1,0:T(8,128)(2,1)} %tokens.1) | copy-start | bytes 344068
  2.6 0.7 copy-start.2
  3.2 0.7 copy-start.3
  4.1 10.2 %collective-permute-start.1 = (bf16[16,3712]{1,0:T(8,128)(2,1)S(1)}, bf16[16,3712]{1,0:T(8,128)(2,1)S(1)}, u32[]{:S(2)}, u32[]{:S(2)}) collective-permute-start(bf16[16,3712]{1,0:T(8,128)(2,1)S(1)} %shard_map.86.refs_0_), channel_id=1, source_target_pairs={{0,16},{1,17},{2,18},{3,19},{4,20},{5,21},{6,22},{7,23},{8,24},{9,... | collective-permute-start | bytes 356360 | tf_op jit(solution)/shard_map/ppermute | solution.py:22
  7.9 10.5 %collective-permute-start = (bf16[16,3712]{1,0:T(8,128)(2,1)S(1)}, bf16[16,3712]{1,0:T(8,128)(2,1)S(1)}, u32[]{:S(2)}, u32[]{:S(2)}) collective-permute-start(bf16[16,3712]{1,0:T(8,128)(2,1)S(1)} %shard_map.86.refs_0_), channel_id=1, source_target_pairs={{0,8},{1,9},{2,10},{3,11},{4,12},{5,13},{6,14},{7,15},{8,0},{9,1},... | collective-permute-start | bytes 356360 | tf_op jit(solution)/shard_map/ppermute | solution.py:22
  14.3 4.9 %collective-permute-start.2 = (bf16[16,3712]{1,0:T(8,128)(2,1)S(1)}, bf16[16,3712]{1,0:T(8,128)(2,1)S(1)}, u32[]{:S(2)}, u32[]{:S(2)}) collective-permute-start(bf16[16,3712]{1,0:T(8,128)(2,1)S(1)} %collective-permute-done.1.refs_2_), channel_id=1, source_target_pairs={{0,8},{1,9},{2,10},{3,11},{4,12},{5,13},{6,14},{7,15},{8,0},{9,1},... | collective-permute-start | bytes 356360 | tf_op jit(solution)/shard_map/ppermute | solution.py:22
  15.0 9.1 %collective-permute-start.7 = (bf16[16,3584]{1,0:T(8,128)(2,1)}, bf16[16,3584]{1,0:T(8,128)(2,1)S(1)}, u32[]{:S(2)}, u32[]{:S(2)}) collective-permute-start(bf16[16,3584]{1,0:T(8,128)(2,1)} %refs_0_.4), channel_id=1, source_target_pairs={{0,16},{1,17},{2,18},{3,19},{4,20},{5,21},{6,22},{7,23},{8,24},{9,... | collective-permute-start | bytes 344072 | tf_op jit(solution)/shard_map/ppermute | solution.py:22
  20.3 15.1 %collective-permute-start.5 = (bf16[40,3584]{1,0:T(8,128)(2,1)S(1)}, bf16[40,3584]{1,0:T(8,128)(2,1)S(1)}, u32[]{:S(2)}, u32[]{:S(2)}) collective-permute-start(bf16[40,3584]{1,0:T(8,128)(2,1)S(1)} %get-tuple-element.42), channel_id=1, source_target_pairs={{0,2},{1,3},{2,0},{3,1},{4,6},{5,7},{6,4},{7,5},{8,10},{9,11},{10,... | collective-permute-start | bytes 860168 | tf_op jit(solution)/shard_map/ppermute | solution.py:22
  21.8 16.0 %collective-permute-start.6 = (bf16[40,3584]{1,0:T(8,128)(2,1)S(1)}, bf16[40,3584]{1,0:T(8,128)(2,1)S(1)}, u32[]{:S(2)}, u32[]{:S(2)}) collective-permute-start(bf16[40,3584]{1,0:T(8,128)(2,1)S(1)} %get-tuple-element.44), channel_id=1, source_target_pairs={{0,4},{1,5},{2,6},{3,7},{4,0},{5,1},{6,2},{7,3},{8,12},{9,13},{10,... | collective-permute-start | bytes 860168 | tf_op jit(solution)/shard_map/ppermute | solution.py:22
  24.1 13.8 %collective-permute-start.8 = (bf16[40,3584]{1,0:T(8,128)(2,1)S(1)}, bf16[40,3584]{1,0:T(8,128)(2,1)S(1)}, u32[]{:S(2)}, u32[]{:S(2)}) collective-permute-start(bf16[40,3584]{1,0:T(8,128)(2,1)S(1)} %get-tuple-element.48), channel_id=1, source_target_pairs={{0,6},{1,7},{2,4},{3,5},{4,2},{5,3},{6,0},{7,1},{8,14},{9,15},{10,... | collective-permute-start | bytes 860168 | tf_op jit(solution)/shard_map/ppermute | solution.py:22
  26.6 5.0 %collective-permute-start.16 = (bf16[16,3584]{1,0:T(8,128)(2,1)}, bf16[16,3584]{1,0:T(8,128)(2,1)S(1)}, u32[]{:S(2)}, u32[]{:S(2)}) collective-permute-start(bf16[16,3584]{1,0:T(8,128)(2,1)} %refs_0_.4), channel_id=1, source_target_pairs={{0,8},{1,9},{2,10},{3,11},{4,12},{5,13},{6,14},{7,15},{8,0},{9,1},... | collective-permute-start | bytes 344072 | tf_op jit(solution)/shard_map/ppermute | solution.py:22
  26.8 6.0 %collective-permute-start.17 = (bf16[16,3584]{1,0:T(8,128)(2,1)S(1)}, bf16[16,3584]{1,0:T(8,128)(2,1)S(1)}, u32[]{:S(2)}, u32[]{:S(2)}) collective-permute-start(bf16[16,3584]{1,0:T(8,128)(2,1)S(1)} %collective-permute-done.7.refs_2_), channel_id=1, source_target_pairs={{0,8},{1,9},{2,10},{3,11},{4,12},{5,13},{6,14},{7,15},{8,0},{9,1},... | collective-permute-start | bytes 344072 | tf_op jit(solution)/shard_map/ppermute | solution.py:22
  32.8 0.9 %copy-start = (bf16[16,3584]{1,0:T(8,128)(2,1)S(1)}, bf16[16,3584]{1,0:T(8,128)(2,1)}, u32[]{:S(2)}) copy-start(bf16[16,3584]{1,0:T(8,128)(2,1)} %refs_0_.4) | copy-start | bytes 344068
  34.3 12.9 %collective-permute-start.18 = (bf16[40,3584]{1,0:T(8,128)(2,1)S(1)}, bf16[40,3584]{1,0:T(8,128)(2,1)S(1)}, u32[]{:S(2)}, u32[]{:S(2)}) collective-permute-start(bf16[40,3584]{1,0:T(8,128)(2,1)S(1)} %get-tuple-element.61), channel_id=1, source_target_pairs={{0,2},{1,3},{2,0},{3,1},{4,6},{5,7},{6,4},{7,5},{8,10},{9,11},{10,... | collective-permute-start | bytes 860168 | tf_op jit(solution)/shard_map/ppermute | solution.py:22
  34.9 14.8 %collective-permute-start.19 = (bf16[40,3584]{1,0:T(8,128)(2,1)S(1)}, bf16[40,3584]{1,0:T(8,128)(2,1)S(1)}, u32[]{:S(2)}, u32[]{:S(2)}) collective-permute-start(bf16[40,3584]{1,0:T(8,128)(2,1)S(1)} %get-tuple-element.62), channel_id=1, source_target_pairs={{0,4},{1,5},{2,6},{3,7},{4,0},{5,1},{6,2},{7,3},{8,12},{9,13},{10,... | collective-permute-start | bytes 860168 | tf_op jit(solution)/shard_map/ppermute | solution.py:22
  35.4 14.2 %collective-permute-start.20 = (bf16[40,3584]{1,0:T(8,128)(2,1)S(1)}, bf16[40,3584]{1,0:T(8,128)(2,1)S(1)}, u32[]{:S(2)}, u32[]{:S(2)}) collective-permute-start(bf16[40,3584]{1,0:T(8,128)(2,1)S(1)} %get-tuple-element.63), channel_id=1, source_target_pairs={{0,6},{1,7},{2,4},{3,5},{4,2},{5,3},{6,0},{7,1},{8,14},{9,15},{10,... | collective-permute-start | bytes 860168 | tf_op jit(solution)/shard_map/ppermute | solution.py:22
  46.1 15.7 %collective-permute-start.10 = (bf16[40,3584]{1,0:T(8,128)(2,1)S(1)}, bf16[40,3584]{1,0:T(8,128)(2,1)S(1)}, u32[]{:S(2)}, u32[]{:S(2)}) collective-permute-start(bf16[40,3584]{1,0:T(8,128)(2,1)S(1)} %get-tuple-element.50), channel_id=1, source_target_pairs={{0,2},{1,3},{2,0},{3,1},{4,6},{5,7},{6,4},{7,5},{8,10},{9,11},{10,... | collective-permute-start | bytes 860168 | tf_op jit(solution)/shard_map/ppermute | solution.py:22
  46.7 16.9 %collective-permute-start.11 = (bf16[40,3584]{1,0:T(8,128)(2,1)S(1)}, bf16[40,3584]{1,0:T(8,128)(2,1)S(1)}, u32[]{:S(2)}, u32[]{:S(2)}) collective-permute-start(bf16[40,3584]{1,0:T(8,128)(2,1)S(1)} %get-tuple-element.51), channel_id=1, source_target_pairs={{0,4},{1,5},{2,6},{3,7},{4,0},{5,1},{6,2},{7,3},{8,12},{9,13},{10,... | collective-permute-start | bytes 860168 | tf_op jit(solution)/shard_map/ppermute | solution.py:22
  47.2 16.4 %collective-permute-start.12 = (bf16[40,3584]{1,0:T(8,128)(2,1)S(1)}, bf16[40,3584]{1,0:T(8,128)(2,1)S(1)}, u32[]{:S(2)}, u32[]{:S(2)}) collective-permute-start(bf16[40,3584]{1,0:T(8,128)(2,1)S(1)} %get-tuple-element.52), channel_id=1, source_target_pairs={{0,6},{1,7},{2,4},{3,5},{4,2},{5,3},{6,0},{7,1},{8,14},{9,15},{10,... | collective-permute-start | bytes 860168 | tf_op jit(solution)/shard_map/ppermute | solution.py:22
  60.0 9.7 %collective-permute-start.21 = (bf16[40,3584]{1,0:T(8,128)(2,1)S(1)}, bf16[40,3584]{1,0:T(8,128)(2,1)S(1)}, u32[]{:S(2)}, u32[]{:S(2)}) collective-permute-start(bf16[40,3584]{1,0:T(8,128)(2,1)S(1)} %get-tuple-element.67), channel_id=1, source_target_pairs={{0,2},{1,3},{2,0},{3,1},{4,6},{5,7},{6,4},{7,5},{8,10},{9,11},{10,... | collective-permute-start | bytes 860168 | tf_op jit(solution)/shard_map/ppermute | solution.py:22
  61.3 12.2 %collective-permute-start.22 = (bf16[40,3584]{1,0:T(8,128)(2,1)S(1)}, bf16[40,3584]{1,0:T(8,128)(2,1)S(1)}, u32[]{:S(2)}, u32[]{:S(2)}) collective-permute-start(bf16[40,3584]{1,0:T(8,128)(2,1)S(1)} %get-tuple-element.68), channel_id=1, source_target_pairs={{0,4},{1,5},{2,6},{3,7},{4,0},{5,1},{6,2},{7,3},{8,12},{9,13},{10,... | collective-permute-start | bytes 860168 | tf_op jit(solution)/shard_map/ppermute | solution.py:22
  61.8 11.6 %collective-permute-start.23 = (bf16[40,3584]{1,0:T(8,128)(2,1)S(1)}, bf16[40,3584]{1,0:T(8,128)(2,1)S(1)}, u32[]{:S(2)}, u32[]{:S(2)}) collective-permute-start(bf16[40,3584]{1,0:T(8,128)(2,1)S(1)} %get-tuple-element.69), channel_id=1, source_target_pairs={{0,6},{1,7},{2,4},{3,5},{4,2},{5,3},{6,0},{7,1},{8,14},{9,15},{10,... | collective-permute-start | bytes 860168 | tf_op jit(solution)/shard_map/ppermute | solution.py:22
  64.2 14.6 %collective-permute-start.13 = (bf16[16,3584]{1,0:T(8,128)(2,1)S(1)}, bf16[16,3584]{1,0:T(8,128)(2,1)S(1)}, u32[]{:S(2)}, u32[]{:S(2)}) collective-permute-start(bf16[16,3584]{1,0:T(8,128)(2,1)S(1)} %get-tuple-element.54), channel_id=1, source_target_pairs={{0,8},{1,9},{2,10},{3,11},{4,12},{5,13},{6,14},{7,15},{8,0},{9,1},... | collective-permute-start | bytes 344072 | tf_op jit(solution)/shard_map/ppermute | solution.py:22
  65.2 13.6 %collective-permute-start.14 = (bf16[16,3584]{1,0:T(8,128)(2,1)S(1)}, bf16[16,3584]{1,0:T(8,128)(2,1)S(1)}, u32[]{:S(2)}, u32[]{:S(2)}) collective-permute-start(bf16[16,3584]{1,0:T(8,128)(2,1)S(1)} %get-tuple-element.55), channel_id=1, source_target_pairs={{0,16},{1,17},{2,18},{3,19},{4,20},{5,21},{6,22},{7,23},{8,24},{9,... | collective-permute-start | bytes 344072 | tf_op jit(solution)/shard_map/ppermute | solution.py:22
  69.7 9.1 %collective-permute-start.15 = (bf16[16,3584]{1,0:T(8,128)(2,1)S(1)}, bf16[16,3584]{1,0:T(8,128)(2,1)S(1)}, u32[]{:S(2)}, u32[]{:S(2)}) collective-permute-start(bf16[16,3584]{1,0:T(8,128)(2,1)S(1)} %get-tuple-element.56), channel_id=1, source_target_pairs={{0,24},{1,25},{2,26},{3,27},{4,28},{5,29},{6,30},{7,31},{8,16},{9,... | collective-permute-start | bytes 344072 | tf_op jit(solution)/shard_map/ppermute | solution.py:22
  73.7 6.6 %collective-permute-start.24 = (bf16[16,3584]{1,0:T(8,128)(2,1)S(1)}, bf16[16,3584]{1,0:T(8,128)(2,1)S(1)}, u32[]{:S(2)}, u32[]{:S(2)}) collective-permute-start(bf16[16,3584]{1,0:T(8,128)(2,1)S(1)} %get-tuple-element.71), channel_id=1, source_target_pairs={{0,8},{1,9},{2,10},{3,11},{4,12},{5,13},{6,14},{7,15},{8,0},{9,1},... | collective-permute-start | bytes 344072 | tf_op jit(solution)/shard_map/ppermute | solution.py:22
  74.3 9.4 %collective-permute-start.25 = (bf16[16,3584]{1,0:T(8,128)(2,1)S(1)}, bf16[16,3584]{1,0:T(8,128)(2,1)S(1)}, u32[]{:S(2)}, u32[]{:S(2)}) collective-permute-start(bf16[16,3584]{1,0:T(8,128)(2,1)S(1)} %get-tuple-element.72), channel_id=1, source_target_pairs={{0,16},{1,17},{2,18},{3,19},{4,20},{5,21},{6,22},{7,23},{8,24},{9,... | collective-permute-start | bytes 344072 | tf_op jit(solution)/shard_map/ppermute | solution.py:22
  78.8 6.7 %collective-permute-start.26 = (bf16[16,3584]{1,0:T(8,128)(2,1)S(1)}, bf16[16,3584]{1,0:T(8,128)(2,1)S(1)}, u32[]{:S(2)}, u32[]{:S(2)}) collective-permute-start(bf16[16,3584]{1,0:T(8,128)(2,1)S(1)} %get-tuple-element.73), channel_id=1, source_target_pairs={{0,24},{1,25},{2,26},{3,27},{4,28},{5,29},{6,30},{7,31},{8,16},{9,... | collective-permute-start | bytes 344072 | tf_op jit(solution)/shard_map/ppermute | solution.py:22

commit v11 on v9

--- a/solution.py
+++ b/solution.py
@@ -33,11 +33,15 @@
     return 512 if width % 512 == 0 else LANES
 
 
+def back_chunk(width):
+    return width // 2 if width % (2 * LANES) == 0 else LANES
+
+
 def column_chunks(width):
     return [slice(at, at + chunk_of(width)) for at in range(0, width, chunk_of(width))]
 
 
-def call(body, outs, args, flops=0, scratch=(), in_specs=None):
+def call(body, outs, args, flops=0, scratch=(), in_specs=None, limit=VMEM_LIMIT):
     size = sum(math.prod(a.shape) * a.dtype.itemsize for a in (*args, *outs))
     whole = pl.BlockSpec(memory_space=pltpu.VMEM)
     return pl.pallas_call(
@@ -46,7 +50,7 @@
         in_specs=[whole] * len(args) if in_specs is None else in_specs,
         out_specs=[whole] * len(outs),
         scratch_shapes=scratch,
-        compiler_params=pltpu.CompilerParams(vmem_limit_bytes=VMEM_LIMIT),
+        compiler_params=pltpu.CompilerParams(vmem_limit_bytes=limit),
         cost_estimate=pl.CostEstimate(flops=flops, bytes_accessed=size, transcendentals=0),
     )(*args)
 
@@ -161,61 +165,33 @@
         out[:, part] = total.astype(bf16)
 
 
-def forward_kernel(x0, x1, x2, x3, g0, u0, d0, g1, u1, d1, *refs):
-    o0, o1, o2, o3, for_up, for_gate, x, hidden = refs
-    rows, width = x.shape
-    units = g0.shape[2]
-    for part in column_chunks(width):
-        x[:, part] = joined((x0, x1, x2, x3), part, rows)
-
-    for slab, (gate_w, up_w) in enumerate(((g0, u0), (g1, u1))):
-        at = slice(slab * units, (slab + 1) * units)
-        pre_gate = jnp.dot(x[...], gate_w[0], preferred_element_type=f32)
-        pre_up = jnp.dot(x[...], up_w[0], preferred_element_type=f32)
+def join_kernel(x0, x1, x2, x3, out):
+    for part in column_chunks(out.shape[1]):
+        out[:, part] = joined((x0, x1, x2, x3), part, out.shape[0])
+
+
+def forward(x, slabs):
+    kept, total = [], 0.0
+    for gate_w, up_w, down_w in slabs:
+        pre_gate = jnp.dot(x, gate_w[0], preferred_element_type=f32)
+        pre_up = jnp.dot(x, up_w[0], preferred_element_type=f32)
         sigma = jax.nn.sigmoid(pre_gate)
         activated = pre_gate * sigma
-        hidden[:, at] = (activated * pre_up).astype(bf16)
-        for_up[:, at] = activated
-        for_gate[:, at] = pre_up * sigma * (1.0 + pre_gate * (1.0 - sigma))
-
-    @pl.loop(0, width // chunk_of(width))
-    def _(number):
-        part = pl.ds(pl.multiple_of(number * chunk_of(width), LANES), chunk_of(width))
-        total = jnp.dot(hidden[:, :units], d0[0, :, part], preferred_element_type=f32)
-        total = total + jnp.dot(hidden[:, units:], d1[0, :, part], preferred_element_type=f32)
-        store_packed(total, (o0, o1, o2, o3), part)
-
-
-def store_packed(total, outs, at):
-    taken = outs[0].shape[0]
-    for number, out in enumerate(outs):
-        out[:, at] = total[number * taken : (number + 1) * taken].astype(bf16)
-
-
-def backward_kernel(x0, x1, x2, x3, for_up, for_gate, g0, u0, d0, g1, u1, d1, *refs):
-    o0, o1, o2, o3, x, gate_grad, up_grad = refs
-    rows, width = x.shape
-    units = g0.shape[2]
-    for part in column_chunks(width):
-        x[:, part] = joined((x0, x1, x2, x3), part, rows)
-
-    def transposed(left, right):
-        return lax.dot_general(left, right, CONTRACT_COLS, preferred_element_type=f32)
-
-    for slab, down_w in enumerate((d0, d1)):
-        at = slice(slab * units, (slab + 1) * units)
-        hidden_grad = transposed(x[...], down_w[0])
-        gate_grad[:, at] = (hidden_grad * for_gate[:, at]).astype(bf16)
-        up_grad[:, at] = (hidden_grad * for_up[:, at]).astype(bf16)
-
-    @pl.loop(0, width // chunk_of(width))
-    def _(number):
-        part = pl.ds(pl.multiple_of(number * chunk_of(width), LANES), chunk_of(width))
-        total = transposed(gate_grad[:, :units], g0[0, part])
-        total = total + transposed(up_grad[:, :units], u0[0, part])
-        total = total + transposed(gate_grad[:, units:], g1[0, part])
-        total = total + transposed(up_grad[:, units:], u1[0, part])
-        store_packed(total, (o0, o1, o2, o3), part)
+        kept.append((activated, pre_up * sigma * (1.0 + pre_gate * (1.0 - sigma))))
+        hidden = (activated * pre_up).astype(bf16)
+        total = total + jnp.dot(hidden, down_w[0], preferred_element_type=f32)
+    return total.astype(bf16), kept
+
+
+def backward(cots, kept, slabs):
+    total = 0.0
+    for (for_up, for_gate), (gate_w, up_w, down_w) in zip(kept, slabs):
+        hidden_grad = lax.dot_general(cots, down_w[0], CONTRACT_COLS, preferred_element_type=f32)
+        for grad, weight in ((hidden_grad * for_gate, gate_w), (hidden_grad * for_up, up_w)):
+            total = total + lax.dot_general(
+                grad.astype(bf16), weight[0], CONTRACT_COLS, preferred_element_type=f32
+            )
+    return total.astype(bf16)
 
 
 def on_device(tokens, expert_ids, gate_values, cotangent, gate_weight, up_weight, down_weight):
@@ -255,7 +231,7 @@
         flops=2 * rows * slots * width,
     )
     far_cots = swap(after(cotangent, held[blocks // 2], other[0]), devices // 2)
-    packed = packed_tokens = [after(value, *other[:2]) for value in packed]
+    packed = [after(value, *other[:2]) for value in packed]
     packed[-1] = after(packed[-1], far_cots)
     x = [packed[0]] + [swap(value, offset) for value, offset in zip(packed[1:], PLANE[1:])]
 
@@ -275,19 +251,14 @@
     )
     grads = [packed[0]] + [swap(value, offset) for value, offset in zip(packed[1:], PLANE[1:])]
 
-    all_taken = len(PLANE) * taken
-    flops = 2 * 3 * all_taken * width * 2 * hidden
-    own = [after(slab, packed_tokens[0]) for slab in own]
-    *outs, for_up, for_gate = call(
-        forward_kernel,
-        packed_shapes + [shape((all_taken, 2 * hidden), f32)] * 2,
-        (*x, *own, *other),
-        flops=flops,
-        scratch=[
-            pltpu.VMEM((all_taken, width), bf16),
-            pltpu.VMEM((all_taken, 2 * hidden), bf16),
-        ],
-    )
+    def join(parts):
+        return call(join_kernel, [shape((len(PLANE) * taken, width), bf16)], parts)[0]
+
+    def split(total):
+        return [total[at : at + taken] for at in range(0, len(PLANE) * taken, taken)]
+
+    out, kept = forward(join(x), (other, own))
+    outs = split(out)
 
     def go_home(values, weighted):
         back = [values[0]] + [swap(value, offset) for value, offset in zip(values[1:], PLANE[1:])]
@@ -302,17 +273,7 @@
         return result
 
     layer_out = go_home(outs, True)
-    backs = call(
-        backward_kernel,
-        packed_shapes,
-        (*grads, for_up, for_gate, *own, *other),
-        flops=flops,
-        scratch=[
-            pltpu.VMEM((all_taken, width), bf16),
-            pltpu.VMEM((all_taken, 2 * hidden), bf16),
-            pltpu.VMEM((all_taken, 2 * hidden), bf16),
-        ],
-    )
+    backs = split(backward(join(grads), kept, (other, own)))
     token_grad = go_home(backs, False)
     return layer_out, token_grad
 

time: 96.5 us -> 96.9 us (level)
  matrix products: 0 us -> 27.1 us
  Pallas kernels: 23.9 us -> 4.28 us
  local copies, waits for them, and re-layouts: 13.2 us -> 5.5 us
  starting transfers between devices: 36.9 us -> 41.8 us
  waiting for transfers between devices: 21.4 us -> 16.9 us
    dot_general x0 -> x12, matrix products: none -> 27.1 us  [the longest x4 9.44 us: backward(): lax.dot_general(grad.astype(bf16), weight[0], CONTRACT_COLS, preferred_el...]
    pallas_call x9, Pallas kernels: 23.9 us -> 4.28 us  [call(): pl.pallas_call(body, out_shape=outs, in_specs=[whole] * len(args) if in_s...]
    unnamed x26 -> x14, local copies, waits for them, and re-layouts: 13.2 us -> 5.33 us
    ppermute x27, starting transfers between devices: 36.9 us -> 41.8 us  [swap(): lax.ppermute(value, 'expert', [(i, i ^ offset) for i in range(devices)])]
    ppermute x27, waiting for transfers between devices: 21.4 us -> 16.9 us  [swap(): lax.ppermute(value, 'expert', [(i, i ^ offset) for i in range(devices)])]
  transfers between devices with their start and end apart: 27 -> 27, of which waited for: 8 -> 7; matrix products, arithmetic and copies ran while one was open for 0% -> 28% of each run, Pallas kernels for 24% -> 4%
where the time goes in v11:
time: 96.9 us; the launch traced here: 96.3 us
  starting transfers between devices  41.8 us (43%)
  matrix products  27.1 us (28%)
  waiting for transfers between devices  16.9 us (17%)
  local copies, waits for them, and re-layouts  5.5 us (6%)
  Pallas kernels  4.28 us (4%)
    ppermute x27, starting transfers between devices, swap(): lax.ppermute(value, 'expert', [(i, i ^ offset) for i in range(devices)])  41.8 us
    ppermute x27, waiting for transfers between devices, swap(): lax.ppermute(value, 'expert', [(i, i ^ offset) for i in range(devices)])  16.9 us
    dot_general x4, matrix products, backward(): lax.dot_general(grad.astype(bf16), weight[0], CONTRACT_COLS, preferred_el...  9.44 us
    dot_general x2, matrix products, forward(): pre_gate = jnp.dot(x, gate_w[0], preferred_element_type=f32)  5.74 us
    unnamed x14, local copies, waits for them, and re-layouts  5.33 us
    dot_general x2, matrix products, backward(): lax.dot_general(cots, down_w[0], CONTRACT_COLS, preferred_element_type=f32)  4.71 us
    pallas_call x9, Pallas kernels, call(): pl.pallas_call(body, out_shape=outs, in_specs=[whole] * len(args) if in_s...  4.28 us
    dot_general x2, matrix products, forward(): total = total + jnp.dot(hidden, down_w[0], preferred_element_type=f32)  3.63 us
  transfers between devices with their start and end apart: 27, of which 7 were waited for; matrix products, arithmetic and copies ran while one was open for 28% of the time, Pallas kernels for 4%

profile of v11, /device:TPU:0, one launch (start us, length us, event | category | flops | bytes accessed | tf_op | source)
XLA Modules:
  0.0 96.3 jit_solution(6156830414757539546)
XLA Ops:
  1.7 0.9 copy-done.1
  2.6 0.7 copy-done.2
  3.2 0.7 copy-done.3
  4.1 3.7 %collective-permute-start.1 = (bf16[16,3712]{1,0:T(8,128)(2,1)S(1)}, bf16[16,3712]{1,0:T(8,128)(2,1)S(1)}, u32[]{:S(2)}, u32[]{:S(2)}) collective-permute-start(bf16[16,3712]{1,0:T(8,128)(2,1)S(1)} %shard_map.86.refs_0_), channel_id=1, source_target_pairs={{0,16},{1,17},{2,18},{3,19},{4,20},{5,21},{6,22},{7,23},{8,24},{9,... | collective-permute-start | bytes 356360 | tf_op jit(solution)/shard_map/ppermute | solution.py:21
  7.9 1.6 %collective-permute-start = (bf16[16,3712]{1,0:T(8,128)(2,1)S(1)}, bf16[16,3712]{1,0:T(8,128)(2,1)S(1)}, u32[]{:S(2)}, u32[]{:S(2)}) collective-permute-start(bf16[16,3712]{1,0:T(8,128)(2,1)S(1)} %shard_map.86.refs_0_), channel_id=1, source_target_pairs={{0,8},{1,9},{2,10},{3,11},{4,12},{5,13},{6,14},{7,15},{8,0},{9,1},... | collective-permute-start | bytes 356360 | tf_op jit(solution)/shard_map/ppermute | solution.py:21
  9.4 4.9 %collective-permute-done.1.refs_2_ = bf16[16,3712]{1,0:T(8,128)(2,1)S(1)} collective-permute-done((bf16[16,3712]{1,0:T(8,128)(2,1)S(1)}, bf16[16,3712]{1,0:T(8,128)(2,1)S(1)}, u32[]{:S(2)}, u32[]{:S(2)}) %collective-permute-start.1) | collective-permute-done | bytes 118816 | tf_op jit(solution)/shard_map/ppermute | solution.py:21
  14.3 0.6 collective-permute-start.2
  15.0 3.4 %collective-permute-start.7 = (bf16[16,3584]{1,0:T(8,128)(2,1)}, bf16[16,3584]{1,0:T(8,128)(2,1)S(1)}, u32[]{:S(2)}, u32[]{:S(2)}) collective-permute-start(bf16[16,3584]{1,0:T(8,128)(2,1)} %refs_0_.1), channel_id=1, source_target_pairs={{0,16},{1,17},{2,18},{3,19},{4,20},{5,21},{6,22},{7,23},{8,24},{9,... | collective-permute-start | bytes 344072 | tf_op jit(solution)/shard_map/ppermute | solution.py:21
  18.4 0.9 collective-permute-done.2.refs_3_
  19.2 1.0 %shard_map.87 = (bf16[40,3584]{1,0:T(8,128)(2,1)S(1)}, bf16[40,3584]{1,0:T(8,128)(2,1)S(1)}, bf16[40,3584]{1,0:T(8,128)(2,1)S(1)}, bf16[40,3584]{1,0:T(8,128)(2,...) custom-call(s32[1]{0:T(128)} %bitcast.chip, bf16[16,3712]{1,0:T(8,128)(2,1)S(1)} %shard_map.86.refs_0_, ...), custom_call_target="tpu_custom_call" | custom-call | flops 117440512 | bytes 1753092 | tf_op jit(solution)/shard_map/pallas_call | solution.py:47
  20.3 1.6 %collective-permute-start.5 = (bf16[40,3584]{1,0:T(8,128)(2,1)S(1)}, bf16[40,3584]{1,0:T(8,128)(2,1)S(1)}, u32[]{:S(2)}, u32[]{:S(2)}) collective-permute-start(bf16[40,3584]{1,0:T(8,128)(2,1)S(1)} %get-tuple-element.32), channel_id=1, source_target_pairs={{0,2},{1,3},{2,0},{3,1},{4,6},{5,7},{6,4},{7,5},{8,10},{9,11},{10,... | collective-permute-start | bytes 860168 | tf_op jit(solution)/shard_map/ppermute | solution.py:21
  21.8 1.5 %collective-permute-start.6 = (bf16[40,3584]{1,0:T(8,128)(2,1)S(1)}, bf16[40,3584]{1,0:T(8,128)(2,1)S(1)}, u32[]{:S(2)}, u32[]{:S(2)}) collective-permute-start(bf16[40,3584]{1,0:T(8,128)(2,1)S(1)} %get-tuple-element.34), channel_id=1, source_target_pairs={{0,4},{1,5},{2,6},{3,7},{4,0},{5,1},{6,2},{7,3},{8,12},{9,13},{10,... | collective-permute-start | bytes 860168 | tf_op jit(solution)/shard_map/ppermute | solution.py:21
  23.4 0.7 collective-permute-done.7.refs_2_
  24.1 2.4 %collective-permute-start.8 = (bf16[40,3584]{1,0:T(8,128)(2,1)S(1)}, bf16[40,3584]{1,0:T(8,128)(2,1)S(1)}, u32[]{:S(2)}, u32[]{:S(2)}) collective-permute-start(bf16[40,3584]{1,0:T(8,128)(2,1)S(1)} %get-tuple-element.38), channel_id=1, source_target_pairs={{0,6},{1,7},{2,4},{3,5},{4,2},{5,3},{6,0},{7,1},{8,14},{9,15},{10,... | collective-permute-start | bytes 860168 | tf_op jit(solution)/shard_map/ppermute | solution.py:21
  26.8 1.8 %collective-permute-start.17 = (bf16[16,3584]{1,0:T(8,128)(2,1)S(1)}, bf16[16,3584]{1,0:T(8,128)(2,1)S(1)}, u32[]{:S(2)}, u32[]{:S(2)}) collective-permute-start(bf16[16,3584]{1,0:T(8,128)(2,1)S(1)} %collective-permute-done.7.refs_2_), channel_id=1, source_target_pairs={{0,8},{1,9},{2,10},{3,11},{4,12},{5,13},{6,14},{7,15},{8,0},{9,1},... | collective-permute-start | bytes 344072 | tf_op jit(solution)/shard_map/ppermute | solution.py:21
  28.6 3.0 %collective-permute-done.16.refs_1_ = bf16[16,3584]{1,0:T(8,128)(2,1)S(1)} collective-permute-done((bf16[16,3584]{1,0:T(8,128)(2,1)}, bf16[16,3584]{1,0:T(8,128)(2,1)S(1)}, u32[]{:S(2)}, u32[]{:S(2)}) %collective-permute-start.16) | collective-permute-done | bytes 114720 | tf_op jit(solution)/shard_map/ppermute | solution.py:21
  31.6 1.2 %collective-permute-done.17.refs_3_ = bf16[16,3584]{1,0:T(8,128)(2,1)S(1)} collective-permute-done((bf16[16,3584]{1,0:T(8,128)(2,1)S(1)}, bf16[16,3584]{1,0:T(8,128)(2,1)S(1)}, u32[]{:S(2)}, u32[]{:S(2)}) %collective-permute-start.17) | collective-permute-done | bytes 114720 | tf_op jit(solution)/shard_map/ppermute | solution.py:21
  32.8 0.9 copy-done
  33.7 0.6 shard_map.91
  34.3 0.6 collective-permute-start.18
  35.4 2.4 %collective-permute-start.20 = (bf16[40,3584]{1,0:T(8,128)(2,1)S(1)}, bf16[40,3584]{1,0:T(8,128)(2,1)S(1)}, u32[]{:S(2)}, u32[]{:S(2)}) collective-permute-start(bf16[40,3584]{1,0:T(8,128)(2,1)S(1)} %get-tuple-element.49), channel_id=1, source_target_pairs={{0,6},{1,7},{2,4},{3,5},{4,2},{5,3},{6,0},{7,1},{8,14},{9,15},{10,... | collective-permute-start | bytes 860168 | tf_op jit(solution)/shard_map/ppermute | solution.py:21
  38.0 2.9 %fusion.12 = f32[160,512]{1,0:T(8,128)S(1)} fusion(bf16[160,3584]{1,0:T(8,128)(2,1)S(1)} %shard_map.88, bf16[1,3584,512]{2,1,0:T(8,128)(2,1)} %param.11), kind=kOutput, calls=%fused_computation.15 | convolution fusion | flops 587202560 | bytes 5144576 | tf_op jit(solution)/shard_map/dot_general | solution.py:176
  41.1 0.8 fusion.8
  41.9 1.3 %copy-done.4 = bf16[1,512,3584]{2,1,0:T(8,128)(2,1)S(1)} copy-done((bf16[1,512,3584]{2,1,0:T(8,128)(2,1)S(1)}, bf16[1,512,3584]{2,1,0:T(8,128)(2,1)}, u32[]{:S(2)}) %copy-start.4) | copy-done | bytes 3670040
  43.1 0.8 fusion.5
  43.9 2.8 %fusion.22 = f32[160,512]{1,0:T(8,128)S(1)} fusion(bf16[160,3584]{1,0:T(8,128)(2,1)S(1)} %shard_map.88, bf16[1,3584,512]{2,1,0:T(8,128)(2,1)} %collective-permute-done.3), kind=kOutput, calls=%fused_computation.25 | convolution fusion | flops 587202560 | bytes 5144576 | tf_op jit(solution)/shard_map/dot_general | solution.py:176
  46.7 2.8 %fusion.19 = f32[160,512]{1,0:T(8,128)S(1)} fusion(bf16[160,3584]{1,0:T(8,128)(2,1)S(1)} %shard_map.88, bf16[1,3584,512]{2,1,0:T(8,128)(2,1)} %collective-permute-done.4), kind=kOutput, calls=%fused_computation.22 | convolution fusion | flops 587202560 | bytes 5144576 | tf_op jit(solution)/shard_map/dot_general | solution.py:177
  49.5 2.8 %fusion.1 = bf16[160,3584]{1,0:T(8,128)(2,1)S(1)} fusion(f32[160,3584]{1,0:T(8,128)S(1)} %fusion.5, bf16[1,512,3584]{2,1,0:T(8,128)(2,1)} %collective-permute-done.9, f32[160,512]{1,0:T(8,128)S(1)} %fusion.19, f32[160,512]{1,0:T(8,128)S(1)} %fusion.22), kind=kOutput, calls=%fused_computation.4 | convolution fusion | flops 588840960 | bytes 7766016 | tf_op jit(solution)/shard_map/dot_general | solution.py:182
  53.0 1.5 %collective-permute-start.11 = (bf16[40,3584]{1,0:T(8,128)(2,1)S(1)}, bf16[40,3584]{1,0:T(8,128)(2,1)S(1)}, u32[]{:S(2)}, u32[]{:S(2)}) collective-permute-start(bf16[40,3584]{1,0:T(8,128)(2,1)S(1)} %get-tuple-element.59), channel_id=1, source_target_pairs={{0,4},{1,5},{2,6},{3,7},{4,0},{5,1},{6,2},{7,3},{8,12},{9,13},{10,... | collective-permute-start | bytes 860168 | tf_op jit(solution)/shard_map/ppermute | solution.py:21
  54.5 1.5 %collective-permute-start.10 = (bf16[40,3584]{1,0:T(8,128)(2,1)S(1)}, bf16[40,3584]{1,0:T(8,128)(2,1)S(1)}, u32[]{:S(2)}, u32[]{:S(2)}) collective-permute-start(bf16[40,3584]{1,0:T(8,128)(2,1)S(1)} %get-tuple-element.60), channel_id=1, source_target_pairs={{0,2},{1,3},{2,0},{3,1},{4,6},{5,7},{6,4},{7,5},{8,10},{9,11},{10,... | collective-permute-start | bytes 860168 | tf_op jit(solution)/shard_map/ppermute | solution.py:21
  56.1 1.3 %fusion.3 = f32[160,512]{1,0:T(8,128)S(1)} fusion(bf16[160,3584]{1,0:T(8,128)(2,1)S(1)} %shard_map.92, bf16[1,512,3584]{2,1,0:T(8,128)(2,1)S(1)} %copy-done.4), kind=kOutput, calls=%fused_computation.6 | convolution fusion | flops 587202560 | bytes 5144576 | tf_op jit(solution)/shard_map/dot_general | solution.py:189
  57.5 0.7 copy-done.5
  58.2 1.3 %fusion.10 = f32[160,3584]{1,0:T(8,128)S(1)} fusion(bf16[1,3584,512]{2,1,0:T(8,128)(2,1)S(1)} %copy-done.5, f32[160,512]{1,0:T(8,128)S(1)} %fusion.3, f32[160,512]{1,0:T(8,128)S(1)} %fusion.12, f32[160,512]{1,0:T(8,128)S(1)} %fusion.8), kind=kOutput, calls=%fused_computation.13 | convolution fusion | flops 588021760 | bytes 6946816 | tf_op jit(solution)/shard_map/dot_general | solution.py:191
  59.5 3.4 %fusion.14 = f32[160,512]{1,0:T(8,128)S(1)} fusion(bf16[160,3584]{1,0:T(8,128)(2,1)S(1)} %shard_map.92, bf16[1,512,3584]{2,1,0:T(8,128)(2,1)} %collective-permute-done.9), kind=kOutput, calls=%fused_computation.17 | convolution fusion | flops 587202560 | bytes 5144576 | tf_op jit(solution)/shard_map/dot_general | solution.py:189
  62.9 3.4 %fusion.17 = f32[160,3584]{1,0:T(8,128)S(1)} fusion(bf16[1,3584,512]{2,1,0:T(8,128)(2,1)} %collective-permute-done.4, f32[160,512]{1,0:T(8,128)S(1)} %fusion.14, f32[160,512]{1,0:T(8,128)S(1)} %fusion.22), kind=kOutput, calls=%fused_computation.20 | convolution fusion | flops 587694080 | bytes 6619136 | tf_op jit(solution)/shard_map/dot_general | solution.py:191
  66.2 3.4 %fusion = f32[160,3584]{1,0:T(8,128)S(1)} fusion(f32[160,3584]{1,0:T(8,128)S(1)} %fusion.10, f32[160,3584]{1,0:T(8,128)S(1)} %fusion.17, bf16[1,3584,512]{2,1,0:T(8,128)(2,1)} %collective-permute-done.3, f32[160,512]{1,0:T(8,128)S(1)} %fusion.14, f32[160,512]{1,0:T(8,128)S(1)} %fusion.22, f32[160,512]{1,0:T(8,128)S(1)} %fusion.19), kind=kOutput, calls=%fused_computation.3 | convolution fusion | flops 589168640 | bytes 11534336 | tf_op jit(solution)/shard_map/dot_general | solution.py:191
  69.6 1.4 %fusion.2 = bf16[160,3584]{1,0:T(8,128)(2,1)S(1)} fusion(f32[160,3584]{1,0:T(8,128)S(1)} %fusion, bf16[1,3584,512]{2,1,0:T(8,128)(2,1)S(1)} %copy-done.6, f32[160,512]{1,0:T(8,128)S(1)} %fusion.3, f32[160,512]{1,0:T(8,128)S(1)} %fusion.12), kind=kOutput, calls=%fused_computation.5 | convolution fusion | flops 588840960 | bytes 7766016 | tf_op jit(solution)/shard_map/dot_general | solution.py:191
  71.6 1.5 %collective-permute-start.22 = (bf16[40,3584]{1,0:T(8,128)(2,1)S(1)}, bf16[40,3584]{1,0:T(8,128)(2,1)S(1)}, u32[]{:S(2)}, u32[]{:S(2)}) collective-permute-start(bf16[40,3584]{1,0:T(8,128)(2,1)S(1)} %get-tuple-element.55), channel_id=1, source_target_pairs={{0,4},{1,5},{2,6},{3,7},{4,0},{5,1},{6,2},{7,3},{8,12},{9,13},{10,... | collective-permute-start | bytes 860168 | tf_op jit(solution)/shard_map/ppermute | solution.py:21
  73.1 1.5 %collective-permute-start.21 = (bf16[40,3584]{1,0:T(8,128)(2,1)S(1)}, bf16[40,3584]{1,0:T(8,128)(2,1)S(1)}, u32[]{:S(2)}, u32[]{:S(2)}) collective-permute-start(bf16[40,3584]{1,0:T(8,128)(2,1)S(1)} %get-tuple-element.56), channel_id=1, source_target_pairs={{0,2},{1,3},{2,0},{3,1},{4,6},{5,7},{6,4},{7,5},{8,10},{9,11},{10,... | collective-permute-start | bytes 860168 | tf_op jit(solution)/shard_map/ppermute | solution.py:21
  74.6 0.6 shard_map.89
  75.3 1.0 %collective-permute-start.13 = (bf16[16,3584]{1,0:T(8,128)(2,1)S(1)}, bf16[16,3584]{1,0:T(8,128)(2,1)S(1)}, u32[]{:S(2)}, u32[]{:S(2)}) collective-permute-start(bf16[16,3584]{1,0:T(8,128)(2,1)S(1)} %get-tuple-element.40), channel_id=1, source_target_pairs={{0,8},{1,9},{2,10},{3,11},{4,12},{5,13},{6,14},{7,15},{8,0},{9,1},... | collective-permute-start | bytes 344072 | tf_op jit(solution)/shard_map/ppermute | solution.py:21
  76.3 4.0 %collective-permute-start.14 = (bf16[16,3584]{1,0:T(8,128)(2,1)S(1)}, bf16[16,3584]{1,0:T(8,128)(2,1)S(1)}, u32[]{:S(2)}, u32[]{:S(2)}) collective-permute-start(bf16[16,3584]{1,0:T(8,128)(2,1)S(1)} %get-tuple-element.41), channel_id=1, source_target_pairs={{0,16},{1,17},{2,18},{3,19},{4,20},{5,21},{6,22},{7,23},{8,24},{9,... | collective-permute-start | bytes 344072 | tf_op jit(solution)/shard_map/ppermute | solution.py:21
  80.3 3.8 %collective-permute-start.15 = (bf16[16,3584]{1,0:T(8,128)(2,1)S(1)}, bf16[16,3584]{1,0:T(8,128)(2,1)S(1)}, u32[]{:S(2)}, u32[]{:S(2)}) collective-permute-start(bf16[16,3584]{1,0:T(8,128)(2,1)S(1)} %get-tuple-element.42), channel_id=1, source_target_pairs={{0,24},{1,25},{2,26},{3,27},{4,28},{5,29},{6,30},{7,31},{8,16},{9,... | collective-permute-start | bytes 344072 | tf_op jit(solution)/shard_map/ppermute | solution.py:21
  84.5 3.5 %collective-permute-start.25 = (bf16[16,3584]{1,0:T(8,128)(2,1)S(1)}, bf16[16,3584]{1,0:T(8,128)(2,1)S(1)}, u32[]{:S(2)}, u32[]{:S(2)}) collective-permute-start(bf16[16,3584]{1,0:T(8,128)(2,1)S(1)} %get-tuple-element.52), channel_id=1, source_target_pairs={{0,16},{1,17},{2,18},{3,19},{4,20},{5,21},{6,22},{7,23},{8,24},{9,... | collective-permute-start | bytes 344072 | tf_op jit(solution)/shard_map/ppermute | solution.py:21
  87.9 0.9 collective-permute-start.26
  88.8 0.7 shard_map.90
  90.0 5.6 %collective-permute-done.25.refs_2_ = bf16[16,3584]{1,0:T(8,128)(2,1)S(1)} collective-permute-done((bf16[16,3584]{1,0:T(8,128)(2,1)S(1)}, bf16[16,3584]{1,0:T(8,128)(2,1)S(1)}, u32[]{:S(2)}, u32[]{:S(2)}) %collective-permute-start.25) | collective-permute-done | bytes 114720 | tf_op jit(solution)/shard_map/ppermute | solution.py:21
  95.6 0.7 shard_map.94
  (43 shorter events, 4.5 us)
Async XLA Ops:
  0.6 14.4 %collective-permute-start.3 = (bf16[1,3584,512]{2,1,0:T(8,128)(2,1)}, bf16[1,3584,512]{2,1,0:T(8,128)(2,1)}, u32[]{:S(2)}, u32[]{:S(2)}) collective-permute-start(bf16[1,3584,512]{2,1,0:T(8,128)(2,1)} %param.11), channel_id=1, source_target_pairs={{0,1},{1,0},{2,3},{3,2},{4,5},{5,4},{6,7},{7,6},{8,9},{9,8},{10,11... | collective-permute-start | bytes 11010056 | tf_op jit(solution)/shard_map/ppermute | solution.py:21
  1.1 19.1 %collective-permute-start.4 = (bf16[1,3584,512]{2,1,0:T(8,128)(2,1)}, bf16[1,3584,512]{2,1,0:T(8,128)(2,1)}, u32[]{:S(2)}, u32[]{:S(2)}) collective-permute-start(bf16[1,3584,512]{2,1,0:T(8,128)(2,1)} %param.12), channel_id=1, source_target_pairs={{0,1},{1,0},{2,3},{3,2},{4,5},{5,4},{6,7},{7,6},{8,9},{9,8},{10,11... | collective-permute-start | bytes 11010056 | tf_op jit(solution)/shard_map/ppermute | solution.py:21
  1.2 25.3 %collective-permute-start.9 = (bf16[1,512,3584]{2,1,0:T(8,128)(2,1)}, bf16[1,512,3584]{2,1,0:T(8,128)(2,1)}, u32[]{:S(2)}, u32[]{:S(2)}) collective-permute-start(bf16[1,512,3584]{2,1,0:T(8,128)(2,1)} %param.13), channel_id=1, source_target_pairs={{0,1},{1,0},{2,3},{3,2},{4,5},{5,4},{6,7},{7,6},{8,9},{9,8},{10,11... | collective-permute-start | bytes 11010056 | tf_op jit(solution)/shard_map/ppermute | solution.py:21
  1.7 0.9 copy-start.1
  2.6 0.7 copy-start.2
  3.2 0.7 copy-start.3
  4.1 10.2 %collective-permute-start.1 = (bf16[16,3712]{1,0:T(8,128)(2,1)S(1)}, bf16[16,3712]{1,0:T(8,128)(2,1)S(1)}, u32[]{:S(2)}, u32[]{:S(2)}) collective-permute-start(bf16[16,3712]{1,0:T(8,128)(2,1)S(1)} %shard_map.86.refs_0_), channel_id=1, source_target_pairs={{0,16},{1,17},{2,18},{3,19},{4,20},{5,21},{6,22},{7,23},{8,24},{9,... | collective-permute-start | bytes 356360 | tf_op jit(solution)/shard_map/ppermute | solution.py:21
  7.9 10.5 %collective-permute-start = (bf16[16,3712]{1,0:T(8,128)(2,1)S(1)}, bf16[16,3712]{1,0:T(8,128)(2,1)S(1)}, u32[]{:S(2)}, u32[]{:S(2)}) collective-permute-start(bf16[16,3712]{1,0:T(8,128)(2,1)S(1)} %shard_map.86.refs_0_), channel_id=1, source_target_pairs={{0,8},{1,9},{2,10},{3,11},{4,12},{5,13},{6,14},{7,15},{8,0},{9,1},... | collective-permute-start | bytes 356360 | tf_op jit(solution)/shard_map/ppermute | solution.py:21
  14.3 4.9 %collective-permute-start.2 = (bf16[16,3712]{1,0:T(8,128)(2,1)S(1)}, bf16[16,3712]{1,0:T(8,128)(2,1)S(1)}, u32[]{:S(2)}, u32[]{:S(2)}) collective-permute-start(bf16[16,3712]{1,0:T(8,128)(2,1)S(1)} %collective-permute-done.1.refs_2_), channel_id=1, source_target_pairs={{0,8},{1,9},{2,10},{3,11},{4,12},{5,13},{6,14},{7,15},{8,0},{9,1},... | collective-permute-start | bytes 356360 | tf_op jit(solution)/shard_map/ppermute | solution.py:21
  15.0 9.1 %collective-permute-start.7 = (bf16[16,3584]{1,0:T(8,128)(2,1)}, bf16[16,3584]{1,0:T(8,128)(2,1)S(1)}, u32[]{:S(2)}, u32[]{:S(2)}) collective-permute-start(bf16[16,3584]{1,0:T(8,128)(2,1)} %refs_0_.1), channel_id=1, source_target_pairs={{0,16},{1,17},{2,18},{3,19},{4,20},{5,21},{6,22},{7,23},{8,24},{9,... | collective-permute-start | bytes 344072 | tf_op jit(solution)/shard_map/ppermute | solution.py:21
  20.3 15.1 %collective-permute-start.5 = (bf16[40,3584]{1,0:T(8,128)(2,1)S(1)}, bf16[40,3584]{1,0:T(8,128)(2,1)S(1)}, u32[]{:S(2)}, u32[]{:S(2)}) collective-permute-start(bf16[40,3584]{1,0:T(8,128)(2,1)S(1)} %get-tuple-element.32), channel_id=1, source_target_pairs={{0,2},{1,3},{2,0},{3,1},{4,6},{5,7},{6,4},{7,5},{8,10},{9,11},{10,... | collective-permute-start | bytes 860168 | tf_op jit(solution)/shard_map/ppermute | solution.py:21
  21.8 16.0 %collective-permute-start.6 = (bf16[40,3584]{1,0:T(8,128)(2,1)S(1)}, bf16[40,3584]{1,0:T(8,128)(2,1)S(1)}, u32[]{:S(2)}, u32[]{:S(2)}) collective-permute-start(bf16[40,3584]{1,0:T(8,128)(2,1)S(1)} %get-tuple-element.34), channel_id=1, source_target_pairs={{0,4},{1,5},{2,6},{3,7},{4,0},{5,1},{6,2},{7,3},{8,12},{9,13},{10,... | collective-permute-start | bytes 860168 | tf_op jit(solution)/shard_map/ppermute | solution.py:21
  24.1 13.8 %collective-permute-start.8 = (bf16[40,3584]{1,0:T(8,128)(2,1)S(1)}, bf16[40,3584]{1,0:T(8,128)(2,1)S(1)}, u32[]{:S(2)}, u32[]{:S(2)}) collective-permute-start(bf16[40,3584]{1,0:T(8,128)(2,1)S(1)} %get-tuple-element.38), channel_id=1, source_target_pairs={{0,6},{1,7},{2,4},{3,5},{4,2},{5,3},{6,0},{7,1},{8,14},{9,15},{10,... | collective-permute-start | bytes 860168 | tf_op jit(solution)/shard_map/ppermute | solution.py:21
  26.6 5.0 %collective-permute-start.16 = (bf16[16,3584]{1,0:T(8,128)(2,1)}, bf16[16,3584]{1,0:T(8,128)(2,1)S(1)}, u32[]{:S(2)}, u32[]{:S(2)}) collective-permute-start(bf16[16,3584]{1,0:T(8,128)(2,1)} %refs_0_.1), channel_id=1, source_target_pairs={{0,8},{1,9},{2,10},{3,11},{4,12},{5,13},{6,14},{7,15},{8,0},{9,1},... | collective-permute-start | bytes 344072 | tf_op jit(solution)/shard_map/ppermute | solution.py:21
  26.8 6.0 %collective-permute-start.17 = (bf16[16,3584]{1,0:T(8,128)(2,1)S(1)}, bf16[16,3584]{1,0:T(8,128)(2,1)S(1)}, u32[]{:S(2)}, u32[]{:S(2)}) collective-permute-start(bf16[16,3584]{1,0:T(8,128)(2,1)S(1)} %collective-permute-done.7.refs_2_), channel_id=1, source_target_pairs={{0,8},{1,9},{2,10},{3,11},{4,12},{5,13},{6,14},{7,15},{8,0},{9,1},... | collective-permute-start | bytes 344072 | tf_op jit(solution)/shard_map/ppermute | solution.py:21
  32.8 0.9 copy-start
  34.3 20.2 %collective-permute-start.18 = (bf16[40,3584]{1,0:T(8,128)(2,1)S(1)}, bf16[40,3584]{1,0:T(8,128)(2,1)S(1)}, u32[]{:S(2)}, u32[]{:S(2)}) collective-permute-start(bf16[40,3584]{1,0:T(8,128)(2,1)S(1)} %get-tuple-element.47), channel_id=1, source_target_pairs={{0,2},{1,3},{2,0},{3,1},{4,6},{5,7},{6,4},{7,5},{8,10},{9,11},{10,... | collective-permute-start | bytes 860168 | tf_op jit(solution)/shard_map/ppermute | solution.py:21
  34.9 21.1 %collective-permute-start.19 = (bf16[40,3584]{1,0:T(8,128)(2,1)S(1)}, bf16[40,3584]{1,0:T(8,128)(2,1)S(1)}, u32[]{:S(2)}, u32[]{:S(2)}) collective-permute-start(bf16[40,3584]{1,0:T(8,128)(2,1)S(1)} %get-tuple-element.48), channel_id=1, source_target_pairs={{0,4},{1,5},{2,6},{3,7},{4,0},{5,1},{6,2},{7,3},{8,12},{9,13},{10,... | collective-permute-start | bytes 860168 | tf_op jit(solution)/shard_map/ppermute | solution.py:21
  35.4 20.6 %collective-permute-start.20 = (bf16[40,3584]{1,0:T(8,128)(2,1)S(1)}, bf16[40,3584]{1,0:T(8,128)(2,1)S(1)}, u32[]{:S(2)}, u32[]{:S(2)}) collective-permute-start(bf16[40,3584]{1,0:T(8,128)(2,1)S(1)} %get-tuple-element.49), channel_id=1, source_target_pairs={{0,6},{1,7},{2,4},{3,5},{4,2},{5,3},{6,0},{7,1},{8,14},{9,15},{10,... | collective-permute-start | bytes 860168 | tf_op jit(solution)/shard_map/ppermute | solution.py:21
  37.9 3.1 %copy-start.6 = (bf16[1,3584,512]{2,1,0:T(8,128)(2,1)S(1)}, bf16[1,3584,512]{2,1,0:T(8,128)(2,1)}, u32[]{:S(2)}) copy-start(bf16[1,3584,512]{2,1,0:T(8,128)(2,1)} %param.12) | copy-start | bytes 11010052
  41.1 2.0 %copy-start.4 = (bf16[1,512,3584]{2,1,0:T(8,128)(2,1)S(1)}, bf16[1,512,3584]{2,1,0:T(8,128)(2,1)}, u32[]{:S(2)}) copy-start(bf16[1,512,3584]{2,1,0:T(8,128)(2,1)} %param.13) | copy-start | bytes 11010052
  52.5 20.7 %collective-permute-start.12 = (bf16[40,3584]{1,0:T(8,128)(2,1)S(1)}, bf16[40,3584]{1,0:T(8,128)(2,1)S(1)}, u32[]{:S(2)}, u32[]{:S(2)}) collective-permute-start(bf16[40,3584]{1,0:T(8,128)(2,1)S(1)} %get-tuple-element.58), channel_id=1, source_target_pairs={{0,6},{1,7},{2,4},{3,5},{4,2},{5,3},{6,0},{7,1},{8,14},{9,15},{10,... | collective-permute-start | bytes 860168 | tf_op jit(solution)/shard_map/ppermute | solution.py:21
  53.0 21.6 %collective-permute-start.11 = (bf16[40,3584]{1,0:T(8,128)(2,1)S(1)}, bf16[40,3584]{1,0:T(8,128)(2,1)S(1)}, u32[]{:S(2)}, u32[]{:S(2)}) collective-permute-start(bf16[40,3584]{1,0:T(8,128)(2,1)S(1)} %get-tuple-element.59), channel_id=1, source_target_pairs={{0,4},{1,5},{2,6},{3,7},{4,0},{5,1},{6,2},{7,3},{8,12},{9,13},{10,... | collective-permute-start | bytes 860168 | tf_op jit(solution)/shard_map/ppermute | solution.py:21
  54.5 20.1 %collective-permute-start.10 = (bf16[40,3584]{1,0:T(8,128)(2,1)S(1)}, bf16[40,3584]{1,0:T(8,128)(2,1)S(1)}, u32[]{:S(2)}, u32[]{:S(2)}) collective-permute-start(bf16[40,3584]{1,0:T(8,128)(2,1)S(1)} %get-tuple-element.60), channel_id=1, source_target_pairs={{0,2},{1,3},{2,0},{3,1},{4,6},{5,7},{6,4},{7,5},{8,10},{9,11},{10,... | collective-permute-start | bytes 860168 | tf_op jit(solution)/shard_map/ppermute | solution.py:21
  56.1 2.0 %copy-start.5 = (bf16[1,3584,512]{2,1,0:T(8,128)(2,1)S(1)}, bf16[1,3584,512]{2,1,0:T(8,128)(2,1)}, u32[]{:S(2)}) copy-start(bf16[1,3584,512]{2,1,0:T(8,128)(2,1)} %param.11) | copy-start | bytes 11010052
  71.1 9.2 %collective-permute-start.23 = (bf16[40,3584]{1,0:T(8,128)(2,1)S(1)}, bf16[40,3584]{1,0:T(8,128)(2,1)S(1)}, u32[]{:S(2)}, u32[]{:S(2)}) collective-permute-start(bf16[40,3584]{1,0:T(8,128)(2,1)S(1)} %get-tuple-element.54), channel_id=1, source_target_pairs={{0,6},{1,7},{2,4},{3,5},{4,2},{5,3},{6,0},{7,1},{8,14},{9,15},{10,... | collective-permute-start | bytes 860168 | tf_op jit(solution)/shard_map/ppermute | solution.py:21
  71.6 12.4 %collective-permute-start.22 = (bf16[40,3584]{1,0:T(8,128)(2,1)S(1)}, bf16[40,3584]{1,0:T(8,128)(2,1)S(1)}, u32[]{:S(2)}, u32[]{:S(2)}) collective-permute-start(bf16[40,3584]{1,0:T(8,128)(2,1)S(1)} %get-tuple-element.55), channel_id=1, source_target_pairs={{0,4},{1,5},{2,6},{3,7},{4,0},{5,1},{6,2},{7,3},{8,12},{9,13},{10,... | collective-permute-start | bytes 860168 | tf_op jit(solution)/shard_map/ppermute | solution.py:21
  73.1 10.9 %collective-permute-start.21 = (bf16[40,3584]{1,0:T(8,128)(2,1)S(1)}, bf16[40,3584]{1,0:T(8,128)(2,1)S(1)}, u32[]{:S(2)}, u32[]{:S(2)}) collective-permute-start(bf16[40,3584]{1,0:T(8,128)(2,1)S(1)} %get-tuple-element.56), channel_id=1, source_target_pairs={{0,2},{1,3},{2,0},{3,1},{4,6},{5,7},{6,4},{7,5},{8,10},{9,11},{10,... | collective-permute-start | bytes 860168 | tf_op jit(solution)/shard_map/ppermute | solution.py:21
  75.3 12.7 %collective-permute-start.13 = (bf16[16,3584]{1,0:T(8,128)(2,1)S(1)}, bf16[16,3584]{1,0:T(8,128)(2,1)S(1)}, u32[]{:S(2)}, u32[]{:S(2)}) collective-permute-start(bf16[16,3584]{1,0:T(8,128)(2,1)S(1)} %get-tuple-element.40), channel_id=1, source_target_pairs={{0,8},{1,9},{2,10},{3,11},{4,12},{5,13},{6,14},{7,15},{8,0},{9,1},... | collective-permute-start | bytes 344072 | tf_op jit(solution)/shard_map/ppermute | solution.py:21
  76.3 12.6 %collective-permute-start.14 = (bf16[16,3584]{1,0:T(8,128)(2,1)S(1)}, bf16[16,3584]{1,0:T(8,128)(2,1)S(1)}, u32[]{:S(2)}, u32[]{:S(2)}) collective-permute-start(bf16[16,3584]{1,0:T(8,128)(2,1)S(1)} %get-tuple-element.41), channel_id=1, source_target_pairs={{0,16},{1,17},{2,18},{3,19},{4,20},{5,21},{6,22},{7,23},{8,24},{9,... | collective-permute-start | bytes 344072 | tf_op jit(solution)/shard_map/ppermute | solution.py:21
  80.3 8.6 %collective-permute-start.15 = (bf16[16,3584]{1,0:T(8,128)(2,1)S(1)}, bf16[16,3584]{1,0:T(8,128)(2,1)S(1)}, u32[]{:S(2)}, u32[]{:S(2)}) collective-permute-start(bf16[16,3584]{1,0:T(8,128)(2,1)S(1)} %get-tuple-element.42), channel_id=1, source_target_pairs={{0,24},{1,25},{2,26},{3,27},{4,28},{5,29},{6,30},{7,31},{8,16},{9,... | collective-permute-start | bytes 344072 | tf_op jit(solution)/shard_map/ppermute | solution.py:21
  84.4 5.6 %collective-permute-start.24 = (bf16[16,3584]{1,0:T(8,128)(2,1)S(1)}, bf16[16,3584]{1,0:T(8,128)(2,1)S(1)}, u32[]{:S(2)}, u32[]{:S(2)}) collective-permute-start(bf16[16,3584]{1,0:T(8,128)(2,1)S(1)} %get-tuple-element.51), channel_id=1, source_target_pairs={{0,8},{1,9},{2,10},{3,11},{4,12},{5,13},{6,14},{7,15},{8,0},{9,1},... | collective-permute-start | bytes 344072 | tf_op jit(solution)/shard_map/ppermute | solution.py:21
  84.5 11.2 %collective-permute-start.25 = (bf16[16,3584]{1,0:T(8,128)(2,1)S(1)}, bf16[16,3584]{1,0:T(8,128)(2,1)S(1)}, u32[]{:S(2)}, u32[]{:S(2)}) collective-permute-start(bf16[16,3584]{1,0:T(8,128)(2,1)S(1)} %get-tuple-element.52), channel_id=1, source_target_pairs={{0,16},{1,17},{2,18},{3,19},{4,20},{5,21},{6,22},{7,23},{8,24},{9,... | collective-permute-start | bytes 344072 | tf_op jit(solution)/shard_map/ppermute | solution.py:21
  87.9 7.7 %collective-permute-start.26 = (bf16[16,3584]{1,0:T(8,128)(2,1)S(1)}, bf16[16,3584]{1,0:T(8,128)(2,1)S(1)}, u32[]{:S(2)}, u32[]{:S(2)}) collective-permute-start(bf16[16,3584]{1,0:T(8,128)(2,1)S(1)} %get-tuple-element.53), channel_id=1, source_target_pairs={{0,24},{1,25},{2,26},{3,27},{4,28},{5,29},{6,30},{7,31},{8,16},{9,... | collective-permute-start | bytes 344072 | tf_op jit(solution)/shard_map/ppermute | solution.py:21

commit v12 on v10

--- a/solution.py
+++ b/solution.py
@@ -300,16 +300,19 @@
         in_specs=[pl.BlockSpec(memory_space=pltpu.SMEM)] + [whole] * blocks,
         flops=2 * rows * slots * width,
     )
-    far_cots = swap(after(cotangent, held[blocks // 2], other[0]), devices // 2)
-    packed = [after(value, *other[:2]) for value in packed]
-    packed[-1] = after(packed[-1], far_cots)
+    ready = after(cotangent, held[blocks // 2], *other[:2])
+    far_cots, near_cots = swap(ready, devices // 2), swap(ready, FAR)
+    packed[2] = after(packed[2], near_cots)
+    packed[3] = after(packed[3], far_cots)
     x = [packed[0]] + [swap(value, offset) for value, offset in zip(packed[1:], PLANE[1:])]
 
     cots, offset = {0: cotangent, blocks // 2: far_cots}, devices // 4
     while offset >= FAR:
+        near = {0: near_cots} if offset == FAR else {}
         wait = other[2] if offset == FAR else cotangent
-        ready = {at: after(value, wait) for at, value in cots.items()}
-        cots.update({at ^ offset // FAR: swap(value, offset) for at, value in ready.items()})
+        ready = {at: after(value, wait) for at, value in cots.items() if at not in near}
+        near.update({at: swap(value, offset) for at, value in ready.items()})
+        cots.update({at ^ offset // FAR: value for at, value in near.items()})
         offset //= 2
     cots = [cots[at] for at in sorted(cots)]
 

time: 86.4 us -> 90.6 us (1.049)
  waiting for transfers between devices: 16.8 us -> 22.4 us
  starting transfers between devices: 42.9 us -> 41.4 us
    ppermute x27, waiting for transfers between devices: 16.8 us -> 22.4 us  [swap(): lax.ppermute(value, 'expert', [(i, i ^ offset) for i in range(devices)])]
    ppermute x27, starting transfers between devices: 42.9 us -> 41.4 us  [swap(): lax.ppermute(value, 'expert', [(i, i ^ offset) for i in range(devices)])]
    unnamed x8 -> x12, local copies, waits for them, and re-layouts: 3.17 us -> 3.18 us
  transfers between devices with their start and end apart: 27 -> 27, of which waited for: 8 -> 9; matrix products, arithmetic and copies ran while one was open for 0% -> 0% of each run, Pallas kernels for 26% -> 24%
where the time goes in v12:
time: 90.6 us; the launch traced here: 90.4 us
  starting transfers between devices  41.4 us (46%)
  Pallas kernels  22.7 us (25%)
  waiting for transfers between devices  22.4 us (25%)
  local copies, waits for them, and re-layouts  3.18 us (4%)
    ppermute x27, starting transfers between devices, swap(): lax.ppermute(value, 'expert', [(i, i ^ offset) for i in range(devices)])  41.4 us
    pallas_call x9, Pallas kernels, call(): pl.pallas_call(body, out_shape=outs, in_specs=[whole] * len(args) if in_s...  22.7 us
    ppermute x27, waiting for transfers between devices, swap(): lax.ppermute(value, 'expert', [(i, i ^ offset) for i in range(devices)])  22.4 us
    unnamed x12, local copies, waits for them, and re-layouts  3.18 us
  transfers between devices with their start and end apart: 27, of which 9 were waited for; matrix products, arithmetic and copies ran while one was open for 0% of the time, Pallas kernels for 24%

profile of v12, /device:TPU:0, one launch (start us, length us, event | category | flops | bytes accessed | tf_op | source)
XLA Modules:
  0.0 90.4 jit_solution(1194426359623792660)
XLA Ops:
  0.6 0.5 collective-permute-start.4
  1.2 0.4 collective-permute-start.10
  1.7 0.9 copy-done.1
  2.6 0.7 copy-done.2
  3.2 0.7 copy-done.3
  3.9 0.2 shard_map.86.refs_0_
  4.1 3.7 %collective-permute-start.1 = (bf16[16,3712]{1,0:T(8,128)(2,1)S(1)}, bf16[16,3712]{1,0:T(8,128)(2,1)S(1)}, u32[]{:S(2)}, u32[]{:S(2)}) collective-permute-start(bf16[16,3712]{1,0:T(8,128)(2,1)S(1)} %shard_map.86.refs_0_), channel_id=1, source_target_pairs={{0,16},{1,17},{2,18},{3,19},{4,20},{5,21},{6,22},{7,23},{8,24},{9,... | collective-permute-start | bytes 356360 | tf_op jit(solution)/shard_map/ppermute | solution.py:22
  7.9 1.6 %collective-permute-start = (bf16[16,3712]{1,0:T(8,128)(2,1)S(1)}, bf16[16,3712]{1,0:T(8,128)(2,1)S(1)}, u32[]{:S(2)}, u32[]{:S(2)}) collective-permute-start(bf16[16,3712]{1,0:T(8,128)(2,1)S(1)} %shard_map.86.refs_0_), channel_id=1, source_target_pairs={{0,8},{1,9},{2,10},{3,11},{4,12},{5,13},{6,14},{7,15},{8,0},{9,1},... | collective-permute-start | bytes 356360 | tf_op jit(solution)/shard_map/ppermute | solution.py:22
  9.4 4.9 %collective-permute-done.1.refs_2_ = bf16[16,3712]{1,0:T(8,128)(2,1)S(1)} collective-permute-done((bf16[16,3712]{1,0:T(8,128)(2,1)S(1)}, bf16[16,3712]{1,0:T(8,128)(2,1)S(1)}, u32[]{:S(2)}, u32[]{:S(2)}) %collective-permute-start.1) | collective-permute-done | bytes 118816 | tf_op jit(solution)/shard_map/ppermute | solution.py:22
  14.3 0.6 collective-permute-start.2
  15.0 2.9 %collective-permute-done.5.refs_4_ = bf16[1,3584,512]{2,1,0:T(8,128)(2,1)S(1)} collective-permute-done((bf16[1,3584,512]{2,1,0:T(8,128)(2,1)}, bf16[1,3584,512]{2,1,0:T(8,128)(2,1)S(1)}, u32[]{:S(2)}, u32[]{:S(2)}) %collective-permute-start.5) | collective-permute-done | bytes 3670048 | tf_op jit(solution)/shard_map/ppermute | solution.py:22
  17.9 2.9 %collective-permute-start.6 = (bf16[16,3584]{1,0:T(8,128)(2,1)}, bf16[16,3584]{1,0:T(8,128)(2,1)S(1)}, u32[]{:S(2)}, u32[]{:S(2)}) collective-permute-start(bf16[16,3584]{1,0:T(8,128)(2,1)} %refs_0_.4), channel_id=1, source_target_pairs={{0,8},{1,9},{2,10},{3,11},{4,12},{5,13},{6,14},{7,15},{8,0},{9,1},... | collective-permute-start | bytes 344072 | tf_op jit(solution)/shard_map/ppermute | solution.py:22
  20.8 2.8 %collective-permute-start.8 = (bf16[16,3584]{1,0:T(8,128)(2,1)}, bf16[16,3584]{1,0:T(8,128)(2,1)S(1)}, u32[]{:S(2)}, u32[]{:S(2)}) collective-permute-start(bf16[16,3584]{1,0:T(8,128)(2,1)} %refs_0_.4), channel_id=1, source_target_pairs={{0,16},{1,17},{2,18},{3,19},{4,20},{5,21},{6,22},{7,23},{8,24},{9,... | collective-permute-start | bytes 344072 | tf_op jit(solution)/shard_map/ppermute | solution.py:22
  23.7 1.0 %shard_map.87 = (bf16[40,3584]{1,0:T(8,128)(2,1)S(1)}, bf16[40,3584]{1,0:T(8,128)(2,1)S(1)}, bf16[40,3584]{1,0:T(8,128)(2,1)S(1)}, bf16[40,3584]{1,0:T(8,128)(2,...) custom-call(s32[1]{0:T(128)} %bitcast.chip, bf16[16,3712]{1,0:T(8,128)(2,1)S(1)} %shard_map.86.refs_0_, ...), custom_call_target="tpu_custom_call" | custom-call | flops 117440512 | bytes 1753092 | tf_op jit(solution)/shard_map/pallas_call | solution.py:48
  24.7 1.6 %collective-permute-start.3 = (bf16[40,3584]{1,0:T(8,128)(2,1)S(1)}, bf16[40,3584]{1,0:T(8,128)(2,1)S(1)}, u32[]{:S(2)}, u32[]{:S(2)}) collective-permute-start(bf16[40,3584]{1,0:T(8,128)(2,1)S(1)} %get-tuple-element.36), channel_id=1, source_target_pairs={{0,2},{1,3},{2,0},{3,1},{4,6},{5,7},{6,4},{7,5},{8,10},{9,11},{10,... | collective-permute-start | bytes 860168 | tf_op jit(solution)/shard_map/ppermute | solution.py:22
  26.3 1.5 %collective-permute-start.7 = (bf16[40,3584]{1,0:T(8,128)(2,1)S(1)}, bf16[40,3584]{1,0:T(8,128)(2,1)S(1)}, u32[]{:S(2)}, u32[]{:S(2)}) collective-permute-start(bf16[40,3584]{1,0:T(8,128)(2,1)S(1)} %get-tuple-element.39), channel_id=1, source_target_pairs={{0,4},{1,5},{2,6},{3,7},{4,0},{5,1},{6,2},{7,3},{8,12},{9,13},{10,... | collective-permute-start | bytes 860168 | tf_op jit(solution)/shard_map/ppermute | solution.py:22
  27.8 2.0 %collective-permute-done.8.refs_2_ = bf16[16,3584]{1,0:T(8,128)(2,1)S(1)} collective-permute-done((bf16[16,3584]{1,0:T(8,128)(2,1)}, bf16[16,3584]{1,0:T(8,128)(2,1)S(1)}, u32[]{:S(2)}, u32[]{:S(2)}) %collective-permute-start.8) | collective-permute-done | bytes 114720 | tf_op jit(solution)/shard_map/ppermute | solution.py:22
  29.8 2.5 %collective-permute-start.9 = (bf16[40,3584]{1,0:T(8,128)(2,1)S(1)}, bf16[40,3584]{1,0:T(8,128)(2,1)S(1)}, u32[]{:S(2)}, u32[]{:S(2)}) collective-permute-start(bf16[40,3584]{1,0:T(8,128)(2,1)S(1)} %get-tuple-element.41), channel_id=1, source_target_pairs={{0,6},{1,7},{2,4},{3,5},{4,2},{5,3},{6,0},{7,1},{8,14},{9,15},{10,... | collective-permute-start | bytes 860168 | tf_op jit(solution)/shard_map/ppermute | solution.py:22
  32.3 0.8 collective-permute-start.17
  33.1 4.0 %collective-permute-done.17.refs_3_ = bf16[16,3584]{1,0:T(8,128)(2,1)S(1)} collective-permute-done((bf16[16,3584]{1,0:T(8,128)(2,1)S(1)}, bf16[16,3584]{1,0:T(8,128)(2,1)S(1)}, u32[]{:S(2)}, u32[]{:S(2)}) %collective-permute-start.17) | collective-permute-done | bytes 114720 | tf_op jit(solution)/shard_map/ppermute | solution.py:22
  37.1 0.9 copy-done
  38.0 0.6 shard_map.91
  38.6 0.6 collective-permute-start.18
  39.2 0.5 collective-permute-start.19
  39.6 2.5 %collective-permute-start.20 = (bf16[40,3584]{1,0:T(8,128)(2,1)S(1)}, bf16[40,3584]{1,0:T(8,128)(2,1)S(1)}, u32[]{:S(2)}, u32[]{:S(2)}) collective-permute-start(bf16[40,3584]{1,0:T(8,128)(2,1)S(1)} %get-tuple-element.55), channel_id=1, source_target_pairs={{0,6},{1,7},{2,4},{3,5},{4,2},{5,3},{6,0},{7,1},{8,14},{9,15},{10,... | collective-permute-start | bytes 860168 | tf_op jit(solution)/shard_map/ppermute | solution.py:22
  42.1 8.2 %shard_map.88 = (bf16[40,3584]{1,0:T(8,128)(2,1)S(1)}, bf16[40,3584]{1,0:T(8,128)(2,1)S(1)}, bf16[40,3584]{1,0:T(8,128)(2,1)S(1)}, bf16[40,3584]{1,0:T(8,128)(2,...) custom-call(bf16[40,3584]{1,0:T(8,128)(2,1)S(1)} %get-tuple-element.35.x0, ...), custom_call_target="tpu_custom_call" | custom-call | flops 3523215360 | bytes 25624576 | tf_op jit(solution)/shard_map/pallas_call | solution.py:48
  50.4 1.0 %collective-permute-start.11 = (bf16[40,3584]{1,0:T(8,128)(2,1)S(1)}, bf16[40,3584]{1,0:T(8,128)(2,1)S(1)}, u32[]{:S(2)}, u32[]{:S(2)}) collective-permute-start(bf16[40,3584]{1,0:T(8,128)(2,1)S(1)} %get-tuple-element.43), channel_id=1, source_target_pairs={{0,2},{1,3},{2,0},{3,1},{4,6},{5,7},{6,4},{7,5},{8,10},{9,11},{10,... | collective-permute-start | bytes 860168 | tf_op jit(solution)/shard_map/ppermute | solution.py:22
  51.4 0.5 collective-permute-start.12
  51.9 2.0 %collective-permute-start.13 = (bf16[40,3584]{1,0:T(8,128)(2,1)S(1)}, bf16[40,3584]{1,0:T(8,128)(2,1)S(1)}, u32[]{:S(2)}, u32[]{:S(2)}) collective-permute-start(bf16[40,3584]{1,0:T(8,128)(2,1)S(1)} %get-tuple-element.45), channel_id=1, source_target_pairs={{0,6},{1,7},{2,4},{3,5},{4,2},{5,3},{6,0},{7,1},{8,14},{9,15},{10,... | collective-permute-start | bytes 860168 | tf_op jit(solution)/shard_map/ppermute | solution.py:22
  54.0 0.6 collective-permute-done.20.x3
  54.5 10.4 %shard_map.92 = (bf16[40,3584]{1,0:T(8,128)(2,1)S(1)}, bf16[40,3584]{1,0:T(8,128)(2,1)S(1)}, bf16[40,3584]{1,0:T(8,128)(2,1)S(1)}, bf16[40,3584]{1,0:T(8,128)(2,1)S(1)}) custom-call(bf16[40,3584]{1,0:T(8,128)(2,1)S(1)} %get-tuple-element.52.x0, bf16[40,3584]{1,0:T(8,128)(2,1)S(1)} %collective-permute-done.18.x1, ...), custom_call_target="tpu_custom_call" | custom-call | flops 3523215360 | bytes 25624576 | tf_op jit(solution)/shard_map/pallas_call | solution.py:48
  64.9 0.9 collective-permute-start.21
  65.8 0.9 %collective-permute-start.22 = (bf16[40,3584]{1,0:T(8,128)(2,1)S(1)}, bf16[40,3584]{1,0:T(8,128)(2,1)S(1)}, u32[]{:S(2)}, u32[]{:S(2)}) collective-permute-start(bf16[40,3584]{1,0:T(8,128)(2,1)S(1)} %get-tuple-element.60), channel_id=1, source_target_pairs={{0,4},{1,5},{2,6},{3,7},{4,0},{5,1},{6,2},{7,3},{8,12},{9,13},{10,... | collective-permute-start | bytes 860168 | tf_op jit(solution)/shard_map/ppermute | solution.py:22
  66.7 1.7 %collective-permute-start.23 = (bf16[40,3584]{1,0:T(8,128)(2,1)S(1)}, bf16[40,3584]{1,0:T(8,128)(2,1)S(1)}, u32[]{:S(2)}, u32[]{:S(2)}) collective-permute-start(bf16[40,3584]{1,0:T(8,128)(2,1)S(1)} %get-tuple-element.61), channel_id=1, source_target_pairs={{0,6},{1,7},{2,4},{3,5},{4,2},{5,3},{6,0},{7,1},{8,14},{9,15},{10,... | collective-permute-start | bytes 860168 | tf_op jit(solution)/shard_map/ppermute | solution.py:22
  68.5 0.6 shard_map.89
  69.1 1.1 %collective-permute-start.14 = (bf16[16,3584]{1,0:T(8,128)(2,1)S(1)}, bf16[16,3584]{1,0:T(8,128)(2,1)S(1)}, u32[]{:S(2)}, u32[]{:S(2)}) collective-permute-start(bf16[16,3584]{1,0:T(8,128)(2,1)S(1)} %get-tuple-element.47), channel_id=1, source_target_pairs={{0,8},{1,9},{2,10},{3,11},{4,12},{5,13},{6,14},{7,15},{8,0},{9,1},... | collective-permute-start | bytes 344072 | tf_op jit(solution)/shard_map/ppermute | solution.py:22
  70.2 2.5 %collective-permute-start.15 = (bf16[16,3584]{1,0:T(8,128)(2,1)S(1)}, bf16[16,3584]{1,0:T(8,128)(2,1)S(1)}, u32[]{:S(2)}, u32[]{:S(2)}) collective-permute-start(bf16[16,3584]{1,0:T(8,128)(2,1)S(1)} %get-tuple-element.48), channel_id=1, source_target_pairs={{0,16},{1,17},{2,18},{3,19},{4,20},{5,21},{6,22},{7,23},{8,24},{9,... | collective-permute-start | bytes 344072 | tf_op jit(solution)/shard_map/ppermute | solution.py:22
  72.6 1.2 %collective-permute-done.21.second = bf16[40,3584]{1,0:T(8,128)(2,1)S(1)} collective-permute-done((bf16[40,3584]{1,0:T(8,128)(2,1)S(1)}, bf16[40,3584]{1,0:T(8,128)(2,1)S(1)}, u32[]{:S(2)}, u32[]{:S(2)}) %collective-permute-start.21) | collective-permute-done | bytes 286752 | tf_op jit(solution)/shard_map/ppermute | solution.py:22
  73.8 3.6 %collective-permute-start.16 = (bf16[16,3584]{1,0:T(8,128)(2,1)S(1)}, bf16[16,3584]{1,0:T(8,128)(2,1)S(1)}, u32[]{:S(2)}, u32[]{:S(2)}) collective-permute-start(bf16[16,3584]{1,0:T(8,128)(2,1)S(1)} %get-tuple-element.49), channel_id=1, source_target_pairs={{0,24},{1,25},{2,26},{3,27},{4,28},{5,29},{6,30},{7,31},{8,16},{9,... | collective-permute-start | bytes 344072 | tf_op jit(solution)/shard_map/ppermute | solution.py:22
  77.4 0.9 collective-permute-done.22.third
  78.3 0.3 shard_map.93
  78.6 1.7 %collective-permute-start.24 = (bf16[16,3584]{1,0:T(8,128)(2,1)S(1)}, bf16[16,3584]{1,0:T(8,128)(2,1)S(1)}, u32[]{:S(2)}, u32[]{:S(2)}) collective-permute-start(bf16[16,3584]{1,0:T(8,128)(2,1)S(1)} %get-tuple-element.63), channel_id=1, source_target_pairs={{0,8},{1,9},{2,10},{3,11},{4,12},{5,13},{6,14},{7,15},{8,0},{9,1},... | collective-permute-start | bytes 344072 | tf_op jit(solution)/shard_map/ppermute | solution.py:22
  80.3 1.4 %collective-permute-start.25 = (bf16[16,3584]{1,0:T(8,128)(2,1)S(1)}, bf16[16,3584]{1,0:T(8,128)(2,1)S(1)}, u32[]{:S(2)}, u32[]{:S(2)}) collective-permute-start(bf16[16,3584]{1,0:T(8,128)(2,1)S(1)} %get-tuple-element.64), channel_id=1, source_target_pairs={{0,16},{1,17},{2,18},{3,19},{4,20},{5,21},{6,22},{7,23},{8,24},{9,... | collective-permute-start | bytes 344072 | tf_op jit(solution)/shard_map/ppermute | solution.py:22
  81.7 1.4 %collective-permute-start.26 = (bf16[16,3584]{1,0:T(8,128)(2,1)S(1)}, bf16[16,3584]{1,0:T(8,128)(2,1)S(1)}, u32[]{:S(2)}, u32[]{:S(2)}) collective-permute-start(bf16[16,3584]{1,0:T(8,128)(2,1)S(1)} %get-tuple-element.65), channel_id=1, source_target_pairs={{0,24},{1,25},{2,26},{3,27},{4,28},{5,29},{6,30},{7,31},{8,16},{9,... | collective-permute-start | bytes 344072 | tf_op jit(solution)/shard_map/ppermute | solution.py:22
  83.1 0.7 shard_map.90
  83.8 1.3 %collective-permute-done.24.refs_1_ = bf16[16,3584]{1,0:T(8,128)(2,1)S(1)} collective-permute-done((bf16[16,3584]{1,0:T(8,128)(2,1)S(1)}, bf16[16,3584]{1,0:T(8,128)(2,1)S(1)}, u32[]{:S(2)}, u32[]{:S(2)}) %collective-permute-start.24) | collective-permute-done | bytes 114720 | tf_op jit(solution)/shard_map/ppermute | solution.py:22
  85.1 4.6 %collective-permute-done.25.refs_2_ = bf16[16,3584]{1,0:T(8,128)(2,1)S(1)} collective-permute-done((bf16[16,3584]{1,0:T(8,128)(2,1)S(1)}, bf16[16,3584]{1,0:T(8,128)(2,1)S(1)}, u32[]{:S(2)}, u32[]{:S(2)}) %collective-permute-start.25) | collective-permute-done | bytes 114720 | tf_op jit(solution)/shard_map/ppermute | solution.py:22
  89.7 0.7 shard_map.94
  (27 shorter events, 0.1 us)
Async XLA Ops:
  0.6 14.4 %collective-permute-start.4 = (bf16[1,3584,512]{2,1,0:T(8,128)(2,1)}, bf16[1,3584,512]{2,1,0:T(8,128)(2,1)S(1)}, u32[]{:S(2)}, u32[]{:S(2)}) collective-permute-start(bf16[1,3584,512]{2,1,0:T(8,128)(2,1)} %refs_0_.5), channel_id=1, source_target_pairs={{0,1},{1,0},{2,3},{3,2},{4,5},{5,4},{6,7},{7,6},{8,9},{9,8},{10,11... | collective-permute-start | bytes 11010056 | tf_op jit(solution)/shard_map/ppermute | solution.py:22
  1.1 16.7 %collective-permute-start.5 = (bf16[1,3584,512]{2,1,0:T(8,128)(2,1)}, bf16[1,3584,512]{2,1,0:T(8,128)(2,1)S(1)}, u32[]{:S(2)}, u32[]{:S(2)}) collective-permute-start(bf16[1,3584,512]{2,1,0:T(8,128)(2,1)} %refs_1_.3), channel_id=1, source_target_pairs={{0,1},{1,0},{2,3},{3,2},{4,5},{5,4},{6,7},{7,6},{8,9},{9,8},{10,11... | collective-permute-start | bytes 11010056 | tf_op jit(solution)/shard_map/ppermute | solution.py:22
  1.2 31.0 %collective-permute-start.10 = (bf16[1,512,3584]{2,1,0:T(8,128)(2,1)}, bf16[1,512,3584]{2,1,0:T(8,128)(2,1)}, u32[]{:S(2)}, u32[]{:S(2)}) collective-permute-start(bf16[1,512,3584]{2,1,0:T(8,128)(2,1)} %refs_2_.3), channel_id=1, source_target_pairs={{0,1},{1,0},{2,3},{3,2},{4,5},{5,4},{6,7},{7,6},{8,9},{9,8},{10,11... | collective-permute-start | bytes 11010056 | tf_op jit(solution)/shard_map/ppermute | solution.py:22
  1.7 0.9 copy-start.1
  2.6 0.7 copy-start.2
  3.2 0.7 copy-start.3
  4.1 10.2 %collective-permute-start.1 = (bf16[16,3712]{1,0:T(8,128)(2,1)S(1)}, bf16[16,3712]{1,0:T(8,128)(2,1)S(1)}, u32[]{:S(2)}, u32[]{:S(2)}) collective-permute-start(bf16[16,3712]{1,0:T(8,128)(2,1)S(1)} %shard_map.86.refs_0_), channel_id=1, source_target_pairs={{0,16},{1,17},{2,18},{3,19},{4,20},{5,21},{6,22},{7,23},{8,24},{9,... | collective-permute-start | bytes 356360 | tf_op jit(solution)/shard_map/ppermute | solution.py:22
  7.9 15.8 %collective-permute-start = (bf16[16,3712]{1,0:T(8,128)(2,1)S(1)}, bf16[16,3712]{1,0:T(8,128)(2,1)S(1)}, u32[]{:S(2)}, u32[]{:S(2)}) collective-permute-start(bf16[16,3712]{1,0:T(8,128)(2,1)S(1)} %shard_map.86.refs_0_), channel_id=1, source_target_pairs={{0,8},{1,9},{2,10},{3,11},{4,12},{5,13},{6,14},{7,15},{8,0},{9,1},... | collective-permute-start | bytes 356360 | tf_op jit(solution)/shard_map/ppermute | solution.py:22
  14.3 9.3 %collective-permute-start.2 = (bf16[16,3712]{1,0:T(8,128)(2,1)S(1)}, bf16[16,3712]{1,0:T(8,128)(2,1)S(1)}, u32[]{:S(2)}, u32[]{:S(2)}) collective-permute-start(bf16[16,3712]{1,0:T(8,128)(2,1)S(1)} %collective-permute-done.1.refs_2_), channel_id=1, source_target_pairs={{0,8},{1,9},{2,10},{3,11},{4,12},{5,13},{6,14},{7,15},{8,0},{9,1},... | collective-permute-start | bytes 356360 | tf_op jit(solution)/shard_map/ppermute | solution.py:22
  15.0 2.9 %copy-start.4 = (bf16[1,3584,512]{2,1,0:T(8,128)(2,1)}, bf16[1,3584,512]{2,1,0:T(8,128)(2,1)S(1)}, u32[]{:S(2)}) copy-start(bf16[1,3584,512]{2,1,0:T(8,128)(2,1)S(1)} %collective-permute-done.4.refs_3_) | copy-start | bytes 11010052
  17.9 2.9 %copy-start.5 = (bf16[1,3584,512]{2,1,0:T(8,128)(2,1)}, bf16[1,3584,512]{2,1,0:T(8,128)(2,1)S(1)}, u32[]{:S(2)}) copy-start(bf16[1,3584,512]{2,1,0:T(8,128)(2,1)S(1)} %collective-permute-done.5.refs_4_) | copy-start | bytes 11010052
  17.9 8.4 %collective-permute-start.6 = (bf16[16,3584]{1,0:T(8,128)(2,1)}, bf16[16,3584]{1,0:T(8,128)(2,1)S(1)}, u32[]{:S(2)}, u32[]{:S(2)}) collective-permute-start(bf16[16,3584]{1,0:T(8,128)(2,1)} %refs_0_.4), channel_id=1, source_target_pairs={{0,8},{1,9},{2,10},{3,11},{4,12},{5,13},{6,14},{7,15},{8,0},{9,1},... | collective-permute-start | bytes 344072 | tf_op jit(solution)/shard_map/ppermute | solution.py:22
  20.8 8.9 %collective-permute-start.8 = (bf16[16,3584]{1,0:T(8,128)(2,1)}, bf16[16,3584]{1,0:T(8,128)(2,1)S(1)}, u32[]{:S(2)}, u32[]{:S(2)}) collective-permute-start(bf16[16,3584]{1,0:T(8,128)(2,1)} %refs_0_.4), channel_id=1, source_target_pairs={{0,16},{1,17},{2,18},{3,19},{4,20},{5,21},{6,22},{7,23},{8,24},{9,... | collective-permute-start | bytes 344072 | tf_op jit(solution)/shard_map/ppermute | solution.py:22
  24.7 14.9 %collective-permute-start.3 = (bf16[40,3584]{1,0:T(8,128)(2,1)S(1)}, bf16[40,3584]{1,0:T(8,128)(2,1)S(1)}, u32[]{:S(2)}, u32[]{:S(2)}) collective-permute-start(bf16[40,3584]{1,0:T(8,128)(2,1)S(1)} %get-tuple-element.36), channel_id=1, source_target_pairs={{0,2},{1,3},{2,0},{3,1},{4,6},{5,7},{6,4},{7,5},{8,10},{9,11},{10,... | collective-permute-start | bytes 860168 | tf_op jit(solution)/shard_map/ppermute | solution.py:22
  26.3 15.9 %collective-permute-start.7 = (bf16[40,3584]{1,0:T(8,128)(2,1)S(1)}, bf16[40,3584]{1,0:T(8,128)(2,1)S(1)}, u32[]{:S(2)}, u32[]{:S(2)}) collective-permute-start(bf16[40,3584]{1,0:T(8,128)(2,1)S(1)} %get-tuple-element.39), channel_id=1, source_target_pairs={{0,4},{1,5},{2,6},{3,7},{4,0},{5,1},{6,2},{7,3},{8,12},{9,13},{10,... | collective-permute-start | bytes 860168 | tf_op jit(solution)/shard_map/ppermute | solution.py:22
  29.8 12.4 %collective-permute-start.9 = (bf16[40,3584]{1,0:T(8,128)(2,1)S(1)}, bf16[40,3584]{1,0:T(8,128)(2,1)S(1)}, u32[]{:S(2)}, u32[]{:S(2)}) collective-permute-start(bf16[40,3584]{1,0:T(8,128)(2,1)S(1)} %get-tuple-element.41), channel_id=1, source_target_pairs={{0,6},{1,7},{2,4},{3,5},{4,2},{5,3},{6,0},{7,1},{8,14},{9,15},{10,... | collective-permute-start | bytes 860168 | tf_op jit(solution)/shard_map/ppermute | solution.py:22
  32.3 4.8 %collective-permute-start.17 = (bf16[16,3584]{1,0:T(8,128)(2,1)S(1)}, bf16[16,3584]{1,0:T(8,128)(2,1)S(1)}, u32[]{:S(2)}, u32[]{:S(2)}) collective-permute-start(bf16[16,3584]{1,0:T(8,128)(2,1)S(1)} %collective-permute-done.8.refs_2_), channel_id=1, source_target_pairs={{0,8},{1,9},{2,10},{3,11},{4,12},{5,13},{6,14},{7,15},{8,0},{9,1},... | collective-permute-start | bytes 344072 | tf_op jit(solution)/shard_map/ppermute | solution.py:22
  37.1 0.9 copy-start
  38.6 13.3 %collective-permute-start.18 = (bf16[40,3584]{1,0:T(8,128)(2,1)S(1)}, bf16[40,3584]{1,0:T(8,128)(2,1)S(1)}, u32[]{:S(2)}, u32[]{:S(2)}) collective-permute-start(bf16[40,3584]{1,0:T(8,128)(2,1)S(1)} %get-tuple-element.53), channel_id=1, source_target_pairs={{0,2},{1,3},{2,0},{3,1},{4,6},{5,7},{6,4},{7,5},{8,10},{9,11},{10,... | collective-permute-start | bytes 860168 | tf_op jit(solution)/shard_map/ppermute | solution.py:22
  39.2 14.8 %collective-permute-start.19 = (bf16[40,3584]{1,0:T(8,128)(2,1)S(1)}, bf16[40,3584]{1,0:T(8,128)(2,1)S(1)}, u32[]{:S(2)}, u32[]{:S(2)}) collective-permute-start(bf16[40,3584]{1,0:T(8,128)(2,1)S(1)} %get-tuple-element.54), channel_id=1, source_target_pairs={{0,4},{1,5},{2,6},{3,7},{4,0},{5,1},{6,2},{7,3},{8,12},{9,13},{10,... | collective-permute-start | bytes 860168 | tf_op jit(solution)/shard_map/ppermute | solution.py:22
  39.6 14.9 %collective-permute-start.20 = (bf16[40,3584]{1,0:T(8,128)(2,1)S(1)}, bf16[40,3584]{1,0:T(8,128)(2,1)S(1)}, u32[]{:S(2)}, u32[]{:S(2)}) collective-permute-start(bf16[40,3584]{1,0:T(8,128)(2,1)S(1)} %get-tuple-element.55), channel_id=1, source_target_pairs={{0,6},{1,7},{2,4},{3,5},{4,2},{5,3},{6,0},{7,1},{8,14},{9,15},{10,... | collective-permute-start | bytes 860168 | tf_op jit(solution)/shard_map/ppermute | solution.py:22
  50.4 16.4 %collective-permute-start.11 = (bf16[40,3584]{1,0:T(8,128)(2,1)S(1)}, bf16[40,3584]{1,0:T(8,128)(2,1)S(1)}, u32[]{:S(2)}, u32[]{:S(2)}) collective-permute-start(bf16[40,3584]{1,0:T(8,128)(2,1)S(1)} %get-tuple-element.43), channel_id=1, source_target_pairs={{0,2},{1,3},{2,0},{3,1},{4,6},{5,7},{6,4},{7,5},{8,10},{9,11},{10,... | collective-permute-start | bytes 860168 | tf_op jit(solution)/shard_map/ppermute | solution.py:22
  51.4 17.1 %collective-permute-start.12 = (bf16[40,3584]{1,0:T(8,128)(2,1)S(1)}, bf16[40,3584]{1,0:T(8,128)(2,1)S(1)}, u32[]{:S(2)}, u32[]{:S(2)}) collective-permute-start(bf16[40,3584]{1,0:T(8,128)(2,1)S(1)} %get-tuple-element.44), channel_id=1, source_target_pairs={{0,4},{1,5},{2,6},{3,7},{4,0},{5,1},{6,2},{7,3},{8,12},{9,13},{10,... | collective-permute-start | bytes 860168 | tf_op jit(solution)/shard_map/ppermute | solution.py:22
  51.9 16.6 %collective-permute-start.13 = (bf16[40,3584]{1,0:T(8,128)(2,1)S(1)}, bf16[40,3584]{1,0:T(8,128)(2,1)S(1)}, u32[]{:S(2)}, u32[]{:S(2)}) collective-permute-start(bf16[40,3584]{1,0:T(8,128)(2,1)S(1)} %get-tuple-element.45), channel_id=1, source_target_pairs={{0,6},{1,7},{2,4},{3,5},{4,2},{5,3},{6,0},{7,1},{8,14},{9,15},{10,... | collective-permute-start | bytes 860168 | tf_op jit(solution)/shard_map/ppermute | solution.py:22
  64.9 8.9 %collective-permute-start.21 = (bf16[40,3584]{1,0:T(8,128)(2,1)S(1)}, bf16[40,3584]{1,0:T(8,128)(2,1)S(1)}, u32[]{:S(2)}, u32[]{:S(2)}) collective-permute-start(bf16[40,3584]{1,0:T(8,128)(2,1)S(1)} %get-tuple-element.59), channel_id=1, source_target_pairs={{0,2},{1,3},{2,0},{3,1},{4,6},{5,7},{6,4},{7,5},{8,10},{9,11},{10,... | collective-permute-start | bytes 860168 | tf_op jit(solution)/shard_map/ppermute | solution.py:22
  65.8 12.5 %collective-permute-start.22 = (bf16[40,3584]{1,0:T(8,128)(2,1)S(1)}, bf16[40,3584]{1,0:T(8,128)(2,1)S(1)}, u32[]{:S(2)}, u32[]{:S(2)}) collective-permute-start(bf16[40,3584]{1,0:T(8,128)(2,1)S(1)} %get-tuple-element.60), channel_id=1, source_target_pairs={{0,4},{1,5},{2,6},{3,7},{4,0},{5,1},{6,2},{7,3},{8,12},{9,13},{10,... | collective-permute-start | bytes 860168 | tf_op jit(solution)/shard_map/ppermute | solution.py:22
  66.7 11.5 %collective-permute-start.23 = (bf16[40,3584]{1,0:T(8,128)(2,1)S(1)}, bf16[40,3584]{1,0:T(8,128)(2,1)S(1)}, u32[]{:S(2)}, u32[]{:S(2)}) collective-permute-start(bf16[40,3584]{1,0:T(8,128)(2,1)S(1)} %get-tuple-element.61), channel_id=1, source_target_pairs={{0,6},{1,7},{2,4},{3,5},{4,2},{5,3},{6,0},{7,1},{8,14},{9,15},{10,... | collective-permute-start | bytes 860168 | tf_op jit(solution)/shard_map/ppermute | solution.py:22
  69.1 12.6 %collective-permute-start.14 = (bf16[16,3584]{1,0:T(8,128)(2,1)S(1)}, bf16[16,3584]{1,0:T(8,128)(2,1)S(1)}, u32[]{:S(2)}, u32[]{:S(2)}) collective-permute-start(bf16[16,3584]{1,0:T(8,128)(2,1)S(1)} %get-tuple-element.47), channel_id=1, source_target_pairs={{0,8},{1,9},{2,10},{3,11},{4,12},{5,13},{6,14},{7,15},{8,0},{9,1},... | collective-permute-start | bytes 344072 | tf_op jit(solution)/shard_map/ppermute | solution.py:22
  70.2 12.9 %collective-permute-start.15 = (bf16[16,3584]{1,0:T(8,128)(2,1)S(1)}, bf16[16,3584]{1,0:T(8,128)(2,1)S(1)}, u32[]{:S(2)}, u32[]{:S(2)}) collective-permute-start(bf16[16,3584]{1,0:T(8,128)(2,1)S(1)} %get-tuple-element.48), channel_id=1, source_target_pairs={{0,16},{1,17},{2,18},{3,19},{4,20},{5,21},{6,22},{7,23},{8,24},{9,... | collective-permute-start | bytes 344072 | tf_op jit(solution)/shard_map/ppermute | solution.py:22
  73.8 9.3 %collective-permute-start.16 = (bf16[16,3584]{1,0:T(8,128)(2,1)S(1)}, bf16[16,3584]{1,0:T(8,128)(2,1)S(1)}, u32[]{:S(2)}, u32[]{:S(2)}) collective-permute-start(bf16[16,3584]{1,0:T(8,128)(2,1)S(1)} %get-tuple-element.49), channel_id=1, source_target_pairs={{0,24},{1,25},{2,26},{3,27},{4,28},{5,29},{6,30},{7,31},{8,16},{9,... | collective-permute-start | bytes 344072 | tf_op jit(solution)/shard_map/ppermute | solution.py:22
  78.6 6.5 %collective-permute-start.24 = (bf16[16,3584]{1,0:T(8,128)(2,1)S(1)}, bf16[16,3584]{1,0:T(8,128)(2,1)S(1)}, u32[]{:S(2)}, u32[]{:S(2)}) collective-permute-start(bf16[16,3584]{1,0:T(8,128)(2,1)S(1)} %get-tuple-element.63), channel_id=1, source_target_pairs={{0,8},{1,9},{2,10},{3,11},{4,12},{5,13},{6,14},{7,15},{8,0},{9,1},... | collective-permute-start | bytes 344072 | tf_op jit(solution)/shard_map/ppermute | solution.py:22
  80.3 9.4 %collective-permute-start.25 = (bf16[16,3584]{1,0:T(8,128)(2,1)S(1)}, bf16[16,3584]{1,0:T(8,128)(2,1)S(1)}, u32[]{:S(2)}, u32[]{:S(2)}) collective-permute-start(bf16[16,3584]{1,0:T(8,128)(2,1)S(1)} %get-tuple-element.64), channel_id=1, source_target_pairs={{0,16},{1,17},{2,18},{3,19},{4,20},{5,21},{6,22},{7,23},{8,24},{9,... | collective-permute-start | bytes 344072 | tf_op jit(solution)/shard_map/ppermute | solution.py:22
  81.7 8.0 %collective-permute-start.26 = (bf16[16,3584]{1,0:T(8,128)(2,1)S(1)}, bf16[16,3584]{1,0:T(8,128)(2,1)S(1)}, u32[]{:S(2)}, u32[]{:S(2)}) collective-permute-start(bf16[16,3584]{1,0:T(8,128)(2,1)S(1)} %get-tuple-element.65), channel_id=1, source_target_pairs={{0,24},{1,25},{2,26},{3,27},{4,28},{5,29},{6,30},{7,31},{8,16},{9,... | collective-permute-start | bytes 344072 | tf_op jit(solution)/shard_map/ppermute | solution.py:22

commit v13 on v9

--- a/solution.py
+++ b/solution.py
@@ -14,6 +14,7 @@
 LANES = 128
 PIECES = 3
 VMEM_LIMIT = 16 * 1024 * 1024
+VMEM_LIMIT_EXPERT = 38 * 1024 * 1024
 
 
 def swap(value, offset):
@@ -33,11 +34,15 @@
     return 512 if width % 512 == 0 else LANES
 
 
+def back_chunk(width):
+    return width // 2 if width % (2 * LANES) == 0 else LANES
+
+
 def column_chunks(width):
     return [slice(at, at + chunk_of(width)) for at in range(0, width, chunk_of(width))]
 
 
-def call(body, outs, args, flops=0, scratch=(), in_specs=None):
+def call(body, outs, args, flops=0, scratch=(), in_specs=None, limit=VMEM_LIMIT):
     size = sum(math.prod(a.shape) * a.dtype.itemsize for a in (*args, *outs))
     whole = pl.BlockSpec(memory_space=pltpu.VMEM)
     return pl.pallas_call(
@@ -46,9 +51,20 @@
         in_specs=[whole] * len(args) if in_specs is None else in_specs,
         out_specs=[whole] * len(outs),
         scratch_shapes=scratch,
-        compiler_params=pltpu.CompilerParams(vmem_limit_bytes=VMEM_LIMIT),
+        compiler_params=pltpu.CompilerParams(vmem_limit_bytes=limit),
         cost_estimate=pl.CostEstimate(flops=flops, bytes_accessed=size, transcendentals=0),
     )(*args)
+
+
+def streams(triples):
+    copies = [pltpu.make_async_copy(*triple) for triple in triples]
+    for copy in copies:
+        copy.start()
+    return copies
+
+
+def await_place(place, sem):
+    pltpu.make_async_copy(place, place, sem).wait()
 
 
 def code_kernel(experts, tokens, ids, gates, out):
@@ -161,29 +177,42 @@
         out[:, part] = total.astype(bf16)
 
 
-def forward_kernel(x0, x1, x2, x3, g0, u0, d0, g1, u1, d1, *refs):
-    o0, o1, o2, o3, for_up, for_gate, x, hidden = refs
+def forward_kernel(x0, x1, x2, x3, g1, u1, d1, g0, u0, d0, *refs):
+    o0, o1, o2, o3, for_up, for_gate, x, hidden, into, back, sems = refs
     rows, width = x.shape
-    units = g0.shape[2]
+    units = back.shape[0]
+    chunk = back_chunk(width)
+    streams(own_slab(g0, u0, into, sems.at[0]) + [(d0.at[0], back, sems.at[1])])
     for part in column_chunks(width):
         x[:, part] = joined((x0, x1, x2, x3), part, rows)
 
-    for slab, (gate_w, up_w) in enumerate(((g0, u0), (g1, u1))):
-        at = slice(slab * units, (slab + 1) * units)
-        pre_gate = jnp.dot(x[...], gate_w[0], preferred_element_type=f32)
-        pre_up = jnp.dot(x[...], up_w[0], preferred_element_type=f32)
+    def activate(pre_gate, pre_up, at):
         sigma = jax.nn.sigmoid(pre_gate)
         activated = pre_gate * sigma
         hidden[:, at] = (activated * pre_up).astype(bf16)
         for_up[:, at] = activated
         for_gate[:, at] = pre_up * sigma * (1.0 + pre_gate * (1.0 - sigma))
 
-    @pl.loop(0, width // chunk_of(width))
+    pre_gate = jnp.dot(x[...], g1[0], preferred_element_type=f32)
+    pre_up = jnp.dot(x[...], u1[0], preferred_element_type=f32)
+    activate(pre_gate, pre_up, slice(units, 2 * units))
+    await_place(into, sems.at[0])
+    pre = jnp.dot(x[...], into[...], preferred_element_type=f32)
+    activate(pre[:, :units], pre[:, units:], slice(0, units))
+    await_place(back, sems.at[1])
+
+    @pl.loop(0, width // chunk)
     def _(number):
-        part = pl.ds(pl.multiple_of(number * chunk_of(width), LANES), chunk_of(width))
-        total = jnp.dot(hidden[:, :units], d0[0, :, part], preferred_element_type=f32)
-        total = total + jnp.dot(hidden[:, units:], d1[0, :, part], preferred_element_type=f32)
+        part = pl.ds(pl.multiple_of(number * chunk, chunk), chunk)
+        total = jnp.dot(hidden[:, units:], d1[0, :, part], preferred_element_type=f32)
+        total = total + jnp.dot(hidden[:, :units], back[:, part], preferred_element_type=f32)
         store_packed(total, (o0, o1, o2, o3), part)
+
+
+def own_slab(gate_w, up_w, into, sem):
+    units = gate_w.shape[2]
+    places = (into.at[:, pl.ds(0, units)], into.at[:, pl.ds(units, units)])
+    return [(source.at[0], place, sem) for source, place in zip((gate_w, up_w), places)]
 
 
 def store_packed(total, outs, at):
@@ -192,29 +221,35 @@
         out[:, at] = total[number * taken : (number + 1) * taken].astype(bf16)
 
 
-def backward_kernel(x0, x1, x2, x3, for_up, for_gate, g0, u0, d0, g1, u1, d1, *refs):
-    o0, o1, o2, o3, x, gate_grad, up_grad = refs
+def backward_kernel(x0, x1, x2, x3, for_up, for_gate, g1, u1, d1, g0, u0, d0, *refs):
+    o0, o1, o2, o3, x, grads, into, back, sems = refs
     rows, width = x.shape
-    units = g0.shape[2]
+    units = back.shape[0]
+    chunk = back_chunk(width)
+    streams([(d0.at[0], back, sems.at[1])] + own_slab(g0, u0, into, sems.at[0]))
     for part in column_chunks(width):
         x[:, part] = joined((x0, x1, x2, x3), part, rows)
 
     def transposed(left, right):
         return lax.dot_general(left, right, CONTRACT_COLS, preferred_element_type=f32)
 
-    for slab, down_w in enumerate((d0, d1)):
-        at = slice(slab * units, (slab + 1) * units)
-        hidden_grad = transposed(x[...], down_w[0])
-        gate_grad[:, at] = (hidden_grad * for_gate[:, at]).astype(bf16)
-        up_grad[:, at] = (hidden_grad * for_up[:, at]).astype(bf16)
-
-    @pl.loop(0, width // chunk_of(width))
+    def differentiate(down_w, slab):
+        at, start = slice(slab * units, (slab + 1) * units), 2 * slab * units
+        hidden_grad = transposed(x[...], down_w)
+        grads[:, start : start + units] = (hidden_grad * for_gate[:, at]).astype(bf16)
+        grads[:, start + units : start + 2 * units] = (hidden_grad * for_up[:, at]).astype(bf16)
+
+    differentiate(d1[0], 1)
+    await_place(back, sems.at[1])
+    differentiate(back[...], 0)
+    await_place(into, sems.at[0])
+
+    @pl.loop(0, width // chunk)
     def _(number):
-        part = pl.ds(pl.multiple_of(number * chunk_of(width), LANES), chunk_of(width))
-        total = transposed(gate_grad[:, :units], g0[0, part])
-        total = total + transposed(up_grad[:, :units], u0[0, part])
-        total = total + transposed(gate_grad[:, units:], g1[0, part])
-        total = total + transposed(up_grad[:, units:], u1[0, part])
+        part = pl.ds(pl.multiple_of(number * chunk, chunk), chunk)
+        total = transposed(grads[:, : 2 * units], into[part])
+        total = total + transposed(grads[:, 2 * units : 3 * units], g1[0, part])
+        total = total + transposed(grads[:, 3 * units :], u1[0, part])
         store_packed(total, (o0, o1, o2, o3), part)
 
 
@@ -235,6 +270,7 @@
     own = (gate_weight, up_weight, down_weight)
     other = tuple(swap(slab, CORE) for slab in own)
 
+    in_place = pl.BlockSpec(memory_space=pltpu.HBM)
     (coded,) = call(
         functools.partial(code_kernel, experts),
         [shape((tok_dev, width + padded(PIECES * experts)), bf16)],
@@ -255,7 +291,7 @@
         flops=2 * rows * slots * width,
     )
     far_cots = swap(after(cotangent, held[blocks // 2], other[0]), devices // 2)
-    packed = packed_tokens = [after(value, *other[:2]) for value in packed]
+    packed = [after(value, *other[:2]) for value in packed]
     packed[-1] = after(packed[-1], far_cots)
     x = [packed[0]] + [swap(value, offset) for value, offset in zip(packed[1:], PLANE[1:])]
 
@@ -276,16 +312,23 @@
     grads = [packed[0]] + [swap(value, offset) for value, offset in zip(packed[1:], PLANE[1:])]
 
     all_taken = len(PLANE) * taken
+    slab_room = [
+        pltpu.VMEM((width, 2 * hidden), bf16),
+        pltpu.VMEM((hidden, width), bf16),
+        pltpu.SemaphoreType.DMA((2,)),
+    ]
     flops = 2 * 3 * all_taken * width * 2 * hidden
-    own = [after(slab, packed_tokens[0]) for slab in own]
     *outs, for_up, for_gate = call(
         forward_kernel,
         packed_shapes + [shape((all_taken, 2 * hidden), f32)] * 2,
-        (*x, *own, *other),
+        (*x, *other, *own),
         flops=flops,
+        in_specs=[whole] * 7 + [in_place] * 3,
+        limit=VMEM_LIMIT_EXPERT,
         scratch=[
             pltpu.VMEM((all_taken, width), bf16),
             pltpu.VMEM((all_taken, 2 * hidden), bf16),
+            *slab_room,
         ],
     )
 
@@ -305,12 +348,14 @@
     backs = call(
         backward_kernel,
         packed_shapes,
-        (*grads, for_up, for_gate, *own, *other),
+        (*grads, for_up, for_gate, *other, *own),
         flops=flops,
+        in_specs=[whole] * 9 + [in_place] * 3,
+        limit=VMEM_LIMIT_EXPERT,
         scratch=[
             pltpu.VMEM((all_taken, width), bf16),
-            pltpu.VMEM((all_taken, 2 * hidden), bf16),
-            pltpu.VMEM((all_taken, 2 * hidden), bf16),
+            pltpu.VMEM((all_taken, 4 * hidden), bf16),
+            *slab_room,
         ],
     )
     token_grad = go_home(backs, False)

time: 96.5 us -> 93.8 us (0.972)
  local copies, waits for them, and re-layouts: 13.2 us -> 7.14 us
  Pallas kernels: 23.9 us -> 27.5 us
    unnamed x26 -> x14, local copies, waits for them, and re-layouts: 13.2 us -> 7.14 us
    pallas_call x9, Pallas kernels: 23.9 us -> 27.5 us  [call(): pl.pallas_call(body, out_shape=outs, in_specs=[whole] * len(args) if in_s...]
  transfers between devices with their start and end apart: 27 -> 27, of which waited for: 8 -> 8; matrix products, arithmetic and copies ran while one was open for 0% -> 0% of each run, Pallas kernels for 24% -> 29%
where the time goes in v13:
time: 93.8 us; the launch traced here: 93.6 us
  starting transfers between devices  36.9 us (39%)
  Pallas kernels  27.5 us (29%)
  waiting for transfers between devices  21.4 us (23%)
  local copies, waits for them, and re-layouts  7.14 us (8%)
    ppermute x27, starting transfers between devices, swap(): lax.ppermute(value, 'expert', [(i, i ^ offset) for i in range(devices)])  36.9 us
    pallas_call x9, Pallas kernels, call(): pl.pallas_call(body, out_shape=outs, in_specs=[whole] * len(args) if in_s...  27.5 us
    ppermute x27, waiting for transfers between devices, swap(): lax.ppermute(value, 'expert', [(i, i ^ offset) for i in range(devices)])  21.4 us
    unnamed x14, local copies, waits for them, and re-layouts  7.14 us
  transfers between devices with their start and end apart: 27, of which 8 were waited for; matrix products, arithmetic and copies ran while one was open for 0% of the time, Pallas kernels for 29%

profile of v13, /device:TPU:0, one launch (start us, length us, event | category | flops | bytes accessed | tf_op | source)
XLA Modules:
  0.0 93.6 jit_solution(4606246317407734237)
XLA Ops:
  0.6 0.5 collective-permute-start.3
  1.2 0.4 collective-permute-start.9
  1.7 0.9 copy-done.4
  2.6 0.7 copy-done.5
  3.2 0.7 copy-done.6
  3.9 0.2 shard_map.86.refs_0_
  4.1 3.7 %collective-permute-start.1 = (bf16[16,3712]{1,0:T(8,128)(2,1)S(1)}, bf16[16,3712]{1,0:T(8,128)(2,1)S(1)}, u32[]{:S(2)}, u32[]{:S(2)}) collective-permute-start(bf16[16,3712]{1,0:T(8,128)(2,1)S(1)} %shard_map.86.refs_0_), channel_id=1, source_target_pairs={{0,16},{1,17},{2,18},{3,19},{4,20},{5,21},{6,22},{7,23},{8,24},{9,... | collective-permute-start | bytes 356360 | tf_op jit(solution)/shard_map/ppermute | solution.py:22
  7.9 1.6 %collective-permute-start = (bf16[16,3712]{1,0:T(8,128)(2,1)S(1)}, bf16[16,3712]{1,0:T(8,128)(2,1)S(1)}, u32[]{:S(2)}, u32[]{:S(2)}) collective-permute-start(bf16[16,3712]{1,0:T(8,128)(2,1)S(1)} %shard_map.86.refs_0_), channel_id=1, source_target_pairs={{0,8},{1,9},{2,10},{3,11},{4,12},{5,13},{6,14},{7,15},{8,0},{9,1},... | collective-permute-start | bytes 356360 | tf_op jit(solution)/shard_map/ppermute | solution.py:22
  9.4 4.9 %collective-permute-done.1.refs_2_ = bf16[16,3712]{1,0:T(8,128)(2,1)S(1)} collective-permute-done((bf16[16,3712]{1,0:T(8,128)(2,1)S(1)}, bf16[16,3712]{1,0:T(8,128)(2,1)S(1)}, u32[]{:S(2)}, u32[]{:S(2)}) %collective-permute-start.1) | collective-permute-done | bytes 118816 | tf_op jit(solution)/shard_map/ppermute | solution.py:22
  14.3 0.6 collective-permute-start.2
  15.0 1.9 %copy-done = bf16[1,3584,512]{2,1,0:T(8,128)(2,1)} copy-done((bf16[1,3584,512]{2,1,0:T(8,128)(2,1)}, bf16[1,3584,512]{2,1,0:T(8,128)(2,1)S(1)}, u32[]{:S(2)}) %copy-start) | copy-done | bytes 3670040
  16.9 3.4 %collective-permute-start.7 = (bf16[16,3584]{1,0:T(8,128)(2,1)}, bf16[16,3584]{1,0:T(8,128)(2,1)S(1)}, u32[]{:S(2)}, u32[]{:S(2)}) collective-permute-start(bf16[16,3584]{1,0:T(8,128)(2,1)} %refs_0_.1), channel_id=1, source_target_pairs={{0,16},{1,17},{2,18},{3,19},{4,20},{5,21},{6,22},{7,23},{8,24},{9,... | collective-permute-start | bytes 344072 | tf_op jit(solution)/shard_map/ppermute | solution.py:22
  20.3 1.0 %shard_map.87 = (bf16[40,3584]{1,0:T(8,128)(2,1)S(1)}, bf16[40,3584]{1,0:T(8,128)(2,1)S(1)}, bf16[40,3584]{1,0:T(8,128)(2,1)S(1)}, bf16[40,3584]{1,0:T(8,128)(2,...) custom-call(s32[1]{0:T(128)} %bitcast.chip, bf16[16,3712]{1,0:T(8,128)(2,1)S(1)} %shard_map.86.refs_0_, ...), custom_call_target="tpu_custom_call" | custom-call | flops 117440512 | bytes 1753092 | tf_op jit(solution)/shard_map/pallas_call | solution.py:48
  21.3 1.6 %collective-permute-start.5 = (bf16[40,3584]{1,0:T(8,128)(2,1)S(1)}, bf16[40,3584]{1,0:T(8,128)(2,1)S(1)}, u32[]{:S(2)}, u32[]{:S(2)}) collective-permute-start(bf16[40,3584]{1,0:T(8,128)(2,1)S(1)} %get-tuple-element.42), channel_id=1, source_target_pairs={{0,2},{1,3},{2,0},{3,1},{4,6},{5,7},{6,4},{7,5},{8,10},{9,11},{10,... | collective-permute-start | bytes 860168 | tf_op jit(solution)/shard_map/ppermute | solution.py:22
  22.9 1.5 %collective-permute-start.6 = (bf16[40,3584]{1,0:T(8,128)(2,1)S(1)}, bf16[40,3584]{1,0:T(8,128)(2,1)S(1)}, u32[]{:S(2)}, u32[]{:S(2)}) collective-permute-start(bf16[40,3584]{1,0:T(8,128)(2,1)S(1)} %get-tuple-element.44), channel_id=1, source_target_pairs={{0,4},{1,5},{2,6},{3,7},{4,0},{5,1},{6,2},{7,3},{8,12},{9,13},{10,... | collective-permute-start | bytes 860168 | tf_op jit(solution)/shard_map/ppermute | solution.py:22
  24.4 1.6 %collective-permute-done.7.refs_2_ = bf16[16,3584]{1,0:T(8,128)(2,1)S(1)} collective-permute-done((bf16[16,3584]{1,0:T(8,128)(2,1)}, bf16[16,3584]{1,0:T(8,128)(2,1)S(1)}, u32[]{:S(2)}, u32[]{:S(2)}) %collective-permute-start.7) | collective-permute-done | bytes 114720 | tf_op jit(solution)/shard_map/ppermute | solution.py:22
  26.0 2.4 %collective-permute-start.8 = (bf16[40,3584]{1,0:T(8,128)(2,1)S(1)}, bf16[40,3584]{1,0:T(8,128)(2,1)S(1)}, u32[]{:S(2)}, u32[]{:S(2)}) collective-permute-start(bf16[40,3584]{1,0:T(8,128)(2,1)S(1)} %get-tuple-element.48), channel_id=1, source_target_pairs={{0,6},{1,7},{2,4},{3,5},{4,2},{5,3},{6,0},{7,1},{8,14},{9,15},{10,... | collective-permute-start | bytes 860168 | tf_op jit(solution)/shard_map/ppermute | solution.py:22
  28.4 2.0 %collective-permute-start.17 = (bf16[16,3584]{1,0:T(8,128)(2,1)S(1)}, bf16[16,3584]{1,0:T(8,128)(2,1)S(1)}, u32[]{:S(2)}, u32[]{:S(2)}) collective-permute-start(bf16[16,3584]{1,0:T(8,128)(2,1)S(1)} %collective-permute-done.7.refs_2_), channel_id=1, source_target_pairs={{0,8},{1,9},{2,10},{3,11},{4,12},{5,13},{6,14},{7,15},{8,0},{9,1},... | collective-permute-start | bytes 344072 | tf_op jit(solution)/shard_map/ppermute | solution.py:22
  30.4 4.0 %collective-permute-done.16.refs_1_ = bf16[16,3584]{1,0:T(8,128)(2,1)S(1)} collective-permute-done((bf16[16,3584]{1,0:T(8,128)(2,1)}, bf16[16,3584]{1,0:T(8,128)(2,1)S(1)}, u32[]{:S(2)}, u32[]{:S(2)}) %collective-permute-start.16) | collective-permute-done | bytes 114720 | tf_op jit(solution)/shard_map/ppermute | solution.py:22
  34.4 1.2 %collective-permute-done.17.refs_3_ = bf16[16,3584]{1,0:T(8,128)(2,1)S(1)} collective-permute-done((bf16[16,3584]{1,0:T(8,128)(2,1)S(1)}, bf16[16,3584]{1,0:T(8,128)(2,1)S(1)}, u32[]{:S(2)}, u32[]{:S(2)}) %collective-permute-start.17) | collective-permute-done | bytes 114720 | tf_op jit(solution)/shard_map/ppermute | solution.py:22
  35.6 0.9 copy-done.3
  36.5 0.6 shard_map.91
  37.1 0.6 collective-permute-start.18
  37.7 0.6 collective-permute-start.19
  38.3 2.4 %collective-permute-start.20 = (bf16[40,3584]{1,0:T(8,128)(2,1)S(1)}, bf16[40,3584]{1,0:T(8,128)(2,1)S(1)}, u32[]{:S(2)}, u32[]{:S(2)}) collective-permute-start(bf16[40,3584]{1,0:T(8,128)(2,1)S(1)} %get-tuple-element.63), channel_id=1, source_target_pairs={{0,6},{1,7},{2,4},{3,5},{4,2},{5,3},{6,0},{7,1},{8,14},{9,15},{10,... | collective-permute-start | bytes 860168 | tf_op jit(solution)/shard_map/ppermute | solution.py:22
  40.7 2.0 %copy-done.1 = bf16[1,3584,512]{2,1,0:T(8,128)(2,1)S(1)} copy-done((bf16[1,3584,512]{2,1,0:T(8,128)(2,1)S(1)}, bf16[1,3584,512]{2,1,0:T(8,128)(2,1)}, u32[]{:S(2)}) %copy-start.1) | copy-done | bytes 3670040
  42.7 10.6 %shard_map.88 = (bf16[40,3584]{1,0:T(8,128)(2,1)S(1)}, bf16[40,3584]{1,0:T(8,128)(2,1)S(1)}, bf16[40,3584]{1,0:T(8,128)(2,1)S(1)}, bf16[40,3584]{1,0:T(8,128)(2,...) custom-call(bf16[40,3584]{1,0:T(8,128)(2,1)S(1)} %get-tuple-element.40.x0, ...), custom_call_target="tpu_custom_call" | custom-call | flops 3523215360 | bytes 25624576 | tf_op jit(solution)/shard_map/pallas_call | solution.py:48
  53.4 0.6 collective-permute-start.10
  54.0 0.6 collective-permute-start.11
  54.5 2.4 %collective-permute-start.12 = (bf16[40,3584]{1,0:T(8,128)(2,1)S(1)}, bf16[40,3584]{1,0:T(8,128)(2,1)S(1)}, u32[]{:S(2)}, u32[]{:S(2)}) collective-permute-start(bf16[40,3584]{1,0:T(8,128)(2,1)S(1)} %get-tuple-element.52), channel_id=1, source_target_pairs={{0,6},{1,7},{2,4},{3,5},{4,2},{5,3},{6,0},{7,1},{8,14},{9,15},{10,... | collective-permute-start | bytes 860168 | tf_op jit(solution)/shard_map/ppermute | solution.py:22
  56.9 12.7 %shard_map.92 = (bf16[40,3584]{1,0:T(8,128)(2,1)S(1)}, bf16[40,3584]{1,0:T(8,128)(2,1)S(1)}, bf16[40,3584]{1,0:T(8,128)(2,1)S(1)}, bf16[40,3584]{1,0:T(8,128)(2,1)S(1)}) custom-call(bf16[40,3584]{1,0:T(8,128)(2,1)S(1)} %get-tuple-element.60.x0, bf16[40,3584]{1,0:T(8,128)(2,1)S(1)} %collective-permute-done.18.x1, ...), custom_call_target="tpu_custom_call" | custom-call | flops 3523215360 | bytes 25624576 | tf_op jit(solution)/shard_map/pallas_call | solution.py:48
  69.6 0.6 collective-permute-start.21
  70.3 0.6 collective-permute-start.22
  70.8 2.4 %collective-permute-start.23 = (bf16[40,3584]{1,0:T(8,128)(2,1)S(1)}, bf16[40,3584]{1,0:T(8,128)(2,1)S(1)}, u32[]{:S(2)}, u32[]{:S(2)}) collective-permute-start(bf16[40,3584]{1,0:T(8,128)(2,1)S(1)} %get-tuple-element.69), channel_id=1, source_target_pairs={{0,6},{1,7},{2,4},{3,5},{4,2},{5,3},{6,0},{7,1},{8,14},{9,15},{10,... | collective-permute-start | bytes 860168 | tf_op jit(solution)/shard_map/ppermute | solution.py:22
  73.2 0.6 shard_map.89
  73.8 0.3 collective-permute-start.13
  74.2 2.2 %collective-permute-start.14 = (bf16[16,3584]{1,0:T(8,128)(2,1)S(1)}, bf16[16,3584]{1,0:T(8,128)(2,1)S(1)}, u32[]{:S(2)}, u32[]{:S(2)}) collective-permute-start(bf16[16,3584]{1,0:T(8,128)(2,1)S(1)} %get-tuple-element.55), channel_id=1, source_target_pairs={{0,16},{1,17},{2,18},{3,19},{4,20},{5,21},{6,22},{7,23},{8,24},{9,... | collective-permute-start | bytes 344072 | tf_op jit(solution)/shard_map/ppermute | solution.py:22
  76.4 2.1 %collective-permute-done.21.second = bf16[40,3584]{1,0:T(8,128)(2,1)S(1)} collective-permute-done((bf16[40,3584]{1,0:T(8,128)(2,1)S(1)}, bf16[40,3584]{1,0:T(8,128)(2,1)S(1)}, u32[]{:S(2)}, u32[]{:S(2)}) %collective-permute-start.21) | collective-permute-done | bytes 286752 | tf_op jit(solution)/shard_map/ppermute | solution.py:22
  78.4 1.3 %collective-permute-start.15 = (bf16[16,3584]{1,0:T(8,128)(2,1)S(1)}, bf16[16,3584]{1,0:T(8,128)(2,1)S(1)}, u32[]{:S(2)}, u32[]{:S(2)}) collective-permute-start(bf16[16,3584]{1,0:T(8,128)(2,1)S(1)} %get-tuple-element.56), channel_id=1, source_target_pairs={{0,24},{1,25},{2,26},{3,27},{4,28},{5,29},{6,30},{7,31},{8,16},{9,... | collective-permute-start | bytes 344072 | tf_op jit(solution)/shard_map/ppermute | solution.py:22
  79.8 2.0 %collective-permute-done.22.third = bf16[40,3584]{1,0:T(8,128)(2,1)S(1)} collective-permute-done((bf16[40,3584]{1,0:T(8,128)(2,1)S(1)}, bf16[40,3584]{1,0:T(8,128)(2,1)S(1)}, u32[]{:S(2)}, u32[]{:S(2)}) %collective-permute-start.22) | collective-permute-done | bytes 286752 | tf_op jit(solution)/shard_map/ppermute | solution.py:22
  81.8 0.3 shard_map.93
  82.1 0.7 collective-permute-start.24
  82.7 1.3 %collective-permute-start.25 = (bf16[16,3584]{1,0:T(8,128)(2,1)S(1)}, bf16[16,3584]{1,0:T(8,128)(2,1)S(1)}, u32[]{:S(2)}, u32[]{:S(2)}) collective-permute-start(bf16[16,3584]{1,0:T(8,128)(2,1)S(1)} %get-tuple-element.72), channel_id=1, source_target_pairs={{0,16},{1,17},{2,18},{3,19},{4,20},{5,21},{6,22},{7,23},{8,24},{9,... | collective-permute-start | bytes 344072 | tf_op jit(solution)/shard_map/ppermute | solution.py:22
  84.1 2.5 %collective-permute-start.26 = (bf16[16,3584]{1,0:T(8,128)(2,1)S(1)}, bf16[16,3584]{1,0:T(8,128)(2,1)S(1)}, u32[]{:S(2)}, u32[]{:S(2)}) collective-permute-start(bf16[16,3584]{1,0:T(8,128)(2,1)S(1)} %get-tuple-element.73), channel_id=1, source_target_pairs={{0,24},{1,25},{2,26},{3,27},{4,28},{5,29},{6,30},{7,31},{8,16},{9,... | collective-permute-start | bytes 344072 | tf_op jit(solution)/shard_map/ppermute | solution.py:22
  86.5 0.7 shard_map.90
  87.2 0.8 collective-permute-done.24.refs_1_
  88.1 4.8 %collective-permute-done.25.refs_2_ = bf16[16,3584]{1,0:T(8,128)(2,1)S(1)} collective-permute-done((bf16[16,3584]{1,0:T(8,128)(2,1)S(1)}, bf16[16,3584]{1,0:T(8,128)(2,1)S(1)}, u32[]{:S(2)}, u32[]{:S(2)}) %collective-permute-start.25) | collective-permute-done | bytes 114720 | tf_op jit(solution)/shard_map/ppermute | solution.py:22
  92.9 0.7 shard_map.94
  (29 shorter events, 0.1 us)
Async XLA Ops:
  0.6 14.4 %collective-permute-start.3 = (bf16[1,3584,512]{2,1,0:T(8,128)(2,1)}, bf16[1,3584,512]{2,1,0:T(8,128)(2,1)S(1)}, u32[]{:S(2)}, u32[]{:S(2)}) collective-permute-start(bf16[1,3584,512]{2,1,0:T(8,128)(2,1)} %g0.3), channel_id=1, source_target_pairs={{0,1},{1,0},{2,3},{3,2},{4,5},{5,4},{6,7},{7,6},{8,9},{9,8},{10,11... | collective-permute-start | bytes 11010056 | tf_op jit(solution)/shard_map/ppermute | solution.py:22
  1.1 20.2 %collective-permute-start.4 = (bf16[1,3584,512]{2,1,0:T(8,128)(2,1)}, bf16[1,3584,512]{2,1,0:T(8,128)(2,1)}, u32[]{:S(2)}, u32[]{:S(2)}) collective-permute-start(bf16[1,3584,512]{2,1,0:T(8,128)(2,1)} %u0.3), channel_id=1, source_target_pairs={{0,1},{1,0},{2,3},{3,2},{4,5},{5,4},{6,7},{7,6},{8,9},{9,8},{10,11... | collective-permute-start | bytes 11010056 | tf_op jit(solution)/shard_map/ppermute | solution.py:22
  1.2 27.2 %collective-permute-start.9 = (bf16[1,512,3584]{2,1,0:T(8,128)(2,1)}, bf16[1,512,3584]{2,1,0:T(8,128)(2,1)}, u32[]{:S(2)}, u32[]{:S(2)}) collective-permute-start(bf16[1,512,3584]{2,1,0:T(8,128)(2,1)} %d0.3), channel_id=1, source_target_pairs={{0,1},{1,0},{2,3},{3,2},{4,5},{5,4},{6,7},{7,6},{8,9},{9,8},{10,11... | collective-permute-start | bytes 11010056 | tf_op jit(solution)/shard_map/ppermute | solution.py:22
  1.7 0.9 copy-start.4
  2.6 0.7 copy-start.5
  3.2 0.7 copy-start.6
  4.1 10.2 %collective-permute-start.1 = (bf16[16,3712]{1,0:T(8,128)(2,1)S(1)}, bf16[16,3712]{1,0:T(8,128)(2,1)S(1)}, u32[]{:S(2)}, u32[]{:S(2)}) collective-permute-start(bf16[16,3712]{1,0:T(8,128)(2,1)S(1)} %shard_map.86.refs_0_), channel_id=1, source_target_pairs={{0,16},{1,17},{2,18},{3,19},{4,20},{5,21},{6,22},{7,23},{8,24},{9,... | collective-permute-start | bytes 356360 | tf_op jit(solution)/shard_map/ppermute | solution.py:22
  7.9 12.4 %collective-permute-start = (bf16[16,3712]{1,0:T(8,128)(2,1)S(1)}, bf16[16,3712]{1,0:T(8,128)(2,1)S(1)}, u32[]{:S(2)}, u32[]{:S(2)}) collective-permute-start(bf16[16,3712]{1,0:T(8,128)(2,1)S(1)} %shard_map.86.refs_0_), channel_id=1, source_target_pairs={{0,8},{1,9},{2,10},{3,11},{4,12},{5,13},{6,14},{7,15},{8,0},{9,1},... | collective-permute-start | bytes 356360 | tf_op jit(solution)/shard_map/ppermute | solution.py:22
  14.3 5.9 %collective-permute-start.2 = (bf16[16,3712]{1,0:T(8,128)(2,1)S(1)}, bf16[16,3712]{1,0:T(8,128)(2,1)S(1)}, u32[]{:S(2)}, u32[]{:S(2)}) collective-permute-start(bf16[16,3712]{1,0:T(8,128)(2,1)S(1)} %collective-permute-done.1.refs_2_), channel_id=1, source_target_pairs={{0,8},{1,9},{2,10},{3,11},{4,12},{5,13},{6,14},{7,15},{8,0},{9,1},... | collective-permute-start | bytes 356360 | tf_op jit(solution)/shard_map/ppermute | solution.py:22
  15.0 1.9 %copy-start = (bf16[1,3584,512]{2,1,0:T(8,128)(2,1)}, bf16[1,3584,512]{2,1,0:T(8,128)(2,1)S(1)}, u32[]{:S(2)}) copy-start(bf16[1,3584,512]{2,1,0:T(8,128)(2,1)S(1)} %collective-permute-done.3.g1) | copy-start | bytes 11010052
  16.9 9.0 %collective-permute-start.7 = (bf16[16,3584]{1,0:T(8,128)(2,1)}, bf16[16,3584]{1,0:T(8,128)(2,1)S(1)}, u32[]{:S(2)}, u32[]{:S(2)}) collective-permute-start(bf16[16,3584]{1,0:T(8,128)(2,1)} %refs_0_.1), channel_id=1, source_target_pairs={{0,16},{1,17},{2,18},{3,19},{4,20},{5,21},{6,22},{7,23},{8,24},{9,... | collective-permute-start | bytes 344072 | tf_op jit(solution)/shard_map/ppermute | solution.py:22
  21.3 17.0 %collective-permute-start.5 = (bf16[40,3584]{1,0:T(8,128)(2,1)S(1)}, bf16[40,3584]{1,0:T(8,128)(2,1)S(1)}, u32[]{:S(2)}, u32[]{:S(2)}) collective-permute-start(bf16[40,3584]{1,0:T(8,128)(2,1)S(1)} %get-tuple-element.42), channel_id=1, source_target_pairs={{0,2},{1,3},{2,0},{3,1},{4,6},{5,7},{6,4},{7,5},{8,10},{9,11},{10,... | collective-permute-start | bytes 860168 | tf_op jit(solution)/shard_map/ppermute | solution.py:22
  22.9 17.8 %collective-permute-start.6 = (bf16[40,3584]{1,0:T(8,128)(2,1)S(1)}, bf16[40,3584]{1,0:T(8,128)(2,1)S(1)}, u32[]{:S(2)}, u32[]{:S(2)}) collective-permute-start(bf16[40,3584]{1,0:T(8,128)(2,1)S(1)} %get-tuple-element.44), channel_id=1, source_target_pairs={{0,4},{1,5},{2,6},{3,7},{4,0},{5,1},{6,2},{7,3},{8,12},{9,13},{10,... | collective-permute-start | bytes 860168 | tf_op jit(solution)/shard_map/ppermute | solution.py:22
  26.0 14.7 %collective-permute-start.8 = (bf16[40,3584]{1,0:T(8,128)(2,1)S(1)}, bf16[40,3584]{1,0:T(8,128)(2,1)S(1)}, u32[]{:S(2)}, u32[]{:S(2)}) collective-permute-start(bf16[40,3584]{1,0:T(8,128)(2,1)S(1)} %get-tuple-element.48), channel_id=1, source_target_pairs={{0,6},{1,7},{2,4},{3,5},{4,2},{5,3},{6,0},{7,1},{8,14},{9,15},{10,... | collective-permute-start | bytes 860168 | tf_op jit(solution)/shard_map/ppermute | solution.py:22
  28.4 6.0 %collective-permute-start.16 = (bf16[16,3584]{1,0:T(8,128)(2,1)}, bf16[16,3584]{1,0:T(8,128)(2,1)S(1)}, u32[]{:S(2)}, u32[]{:S(2)}) collective-permute-start(bf16[16,3584]{1,0:T(8,128)(2,1)} %refs_0_.1), channel_id=1, source_target_pairs={{0,8},{1,9},{2,10},{3,11},{4,12},{5,13},{6,14},{7,15},{8,0},{9,1},... | collective-permute-start | bytes 344072 | tf_op jit(solution)/shard_map/ppermute | solution.py:22
  28.4 7.2 %collective-permute-start.17 = (bf16[16,3584]{1,0:T(8,128)(2,1)S(1)}, bf16[16,3584]{1,0:T(8,128)(2,1)S(1)}, u32[]{:S(2)}, u32[]{:S(2)}) collective-permute-start(bf16[16,3584]{1,0:T(8,128)(2,1)S(1)} %collective-permute-done.7.refs_2_), channel_id=1, source_target_pairs={{0,8},{1,9},{2,10},{3,11},{4,12},{5,13},{6,14},{7,15},{8,0},{9,1},... | collective-permute-start | bytes 344072 | tf_op jit(solution)/shard_map/ppermute | solution.py:22
  35.6 0.9 copy-start.3
  37.1 17.4 %collective-permute-start.18 = (bf16[40,3584]{1,0:T(8,128)(2,1)S(1)}, bf16[40,3584]{1,0:T(8,128)(2,1)S(1)}, u32[]{:S(2)}, u32[]{:S(2)}) collective-permute-start(bf16[40,3584]{1,0:T(8,128)(2,1)S(1)} %get-tuple-element.61), channel_id=1, source_target_pairs={{0,2},{1,3},{2,0},{3,1},{4,6},{5,7},{6,4},{7,5},{8,10},{9,11},{10,... | collective-permute-start | bytes 860168 | tf_op jit(solution)/shard_map/ppermute | solution.py:22
  37.7 19.2 %collective-permute-start.19 = (bf16[40,3584]{1,0:T(8,128)(2,1)S(1)}, bf16[40,3584]{1,0:T(8,128)(2,1)S(1)}, u32[]{:S(2)}, u32[]{:S(2)}) collective-permute-start(bf16[40,3584]{1,0:T(8,128)(2,1)S(1)} %get-tuple-element.62), channel_id=1, source_target_pairs={{0,4},{1,5},{2,6},{3,7},{4,0},{5,1},{6,2},{7,3},{8,12},{9,13},{10,... | collective-permute-start | bytes 860168 | tf_op jit(solution)/shard_map/ppermute | solution.py:22
  38.3 18.6 %collective-permute-start.20 = (bf16[40,3584]{1,0:T(8,128)(2,1)S(1)}, bf16[40,3584]{1,0:T(8,128)(2,1)S(1)}, u32[]{:S(2)}, u32[]{:S(2)}) collective-permute-start(bf16[40,3584]{1,0:T(8,128)(2,1)S(1)} %get-tuple-element.63), channel_id=1, source_target_pairs={{0,6},{1,7},{2,4},{3,5},{4,2},{5,3},{6,0},{7,1},{8,14},{9,15},{10,... | collective-permute-start | bytes 860168 | tf_op jit(solution)/shard_map/ppermute | solution.py:22
  40.7 2.0 %copy-start.1 = (bf16[1,3584,512]{2,1,0:T(8,128)(2,1)S(1)}, bf16[1,3584,512]{2,1,0:T(8,128)(2,1)}, u32[]{:S(2)}) copy-start(bf16[1,3584,512]{2,1,0:T(8,128)(2,1)} %copy-done) | copy-start | bytes 11010052
  42.7 14.2 %copy-start.2 = (bf16[1,3584,512]{2,1,0:T(8,128)(2,1)S(1)}, bf16[1,3584,512]{2,1,0:T(8,128)(2,1)}, u32[]{:S(2)}) copy-start(bf16[1,3584,512]{2,1,0:T(8,128)(2,1)} %copy-done) | copy-start | bytes 11010052
  53.4 17.5 %collective-permute-start.10 = (bf16[40,3584]{1,0:T(8,128)(2,1)S(1)}, bf16[40,3584]{1,0:T(8,128)(2,1)S(1)}, u32[]{:S(2)}, u32[]{:S(2)}) collective-permute-start(bf16[40,3584]{1,0:T(8,128)(2,1)S(1)} %get-tuple-element.50), channel_id=1, source_target_pairs={{0,2},{1,3},{2,0},{3,1},{4,6},{5,7},{6,4},{7,5},{8,10},{9,11},{10,... | collective-permute-start | bytes 860168 | tf_op jit(solution)/shard_map/ppermute | solution.py:22
  54.0 19.2 %collective-permute-start.11 = (bf16[40,3584]{1,0:T(8,128)(2,1)S(1)}, bf16[40,3584]{1,0:T(8,128)(2,1)S(1)}, u32[]{:S(2)}, u32[]{:S(2)}) collective-permute-start(bf16[40,3584]{1,0:T(8,128)(2,1)S(1)} %get-tuple-element.51), channel_id=1, source_target_pairs={{0,4},{1,5},{2,6},{3,7},{4,0},{5,1},{6,2},{7,3},{8,12},{9,13},{10,... | collective-permute-start | bytes 860168 | tf_op jit(solution)/shard_map/ppermute | solution.py:22
  54.5 18.7 %collective-permute-start.12 = (bf16[40,3584]{1,0:T(8,128)(2,1)S(1)}, bf16[40,3584]{1,0:T(8,128)(2,1)S(1)}, u32[]{:S(2)}, u32[]{:S(2)}) collective-permute-start(bf16[40,3584]{1,0:T(8,128)(2,1)S(1)} %get-tuple-element.52), channel_id=1, source_target_pairs={{0,6},{1,7},{2,4},{3,5},{4,2},{5,3},{6,0},{7,1},{8,14},{9,15},{10,... | collective-permute-start | bytes 860168 | tf_op jit(solution)/shard_map/ppermute | solution.py:22
  69.6 8.8 %collective-permute-start.21 = (bf16[40,3584]{1,0:T(8,128)(2,1)S(1)}, bf16[40,3584]{1,0:T(8,128)(2,1)S(1)}, u32[]{:S(2)}, u32[]{:S(2)}) collective-permute-start(bf16[40,3584]{1,0:T(8,128)(2,1)S(1)} %get-tuple-element.67), channel_id=1, source_target_pairs={{0,2},{1,3},{2,0},{3,1},{4,6},{5,7},{6,4},{7,5},{8,10},{9,11},{10,... | collective-permute-start | bytes 860168 | tf_op jit(solution)/shard_map/ppermute | solution.py:22
  70.3 11.5 %collective-permute-start.22 = (bf16[40,3584]{1,0:T(8,128)(2,1)S(1)}, bf16[40,3584]{1,0:T(8,128)(2,1)S(1)}, u32[]{:S(2)}, u32[]{:S(2)}) collective-permute-start(bf16[40,3584]{1,0:T(8,128)(2,1)S(1)} %get-tuple-element.68), channel_id=1, source_target_pairs={{0,4},{1,5},{2,6},{3,7},{4,0},{5,1},{6,2},{7,3},{8,12},{9,13},{10,... | collective-permute-start | bytes 860168 | tf_op jit(solution)/shard_map/ppermute | solution.py:22
  70.8 10.9 %collective-permute-start.23 = (bf16[40,3584]{1,0:T(8,128)(2,1)S(1)}, bf16[40,3584]{1,0:T(8,128)(2,1)S(1)}, u32[]{:S(2)}, u32[]{:S(2)}) collective-permute-start(bf16[40,3584]{1,0:T(8,128)(2,1)S(1)} %get-tuple-element.69), channel_id=1, source_target_pairs={{0,6},{1,7},{2,4},{3,5},{4,2},{5,3},{6,0},{7,1},{8,14},{9,15},{10,... | collective-permute-start | bytes 860168 | tf_op jit(solution)/shard_map/ppermute | solution.py:22
  73.8 10.2 %collective-permute-start.13 = (bf16[16,3584]{1,0:T(8,128)(2,1)S(1)}, bf16[16,3584]{1,0:T(8,128)(2,1)S(1)}, u32[]{:S(2)}, u32[]{:S(2)}) collective-permute-start(bf16[16,3584]{1,0:T(8,128)(2,1)S(1)} %get-tuple-element.54), channel_id=1, source_target_pairs={{0,8},{1,9},{2,10},{3,11},{4,12},{5,13},{6,14},{7,15},{8,0},{9,1},... | collective-permute-start | bytes 344072 | tf_op jit(solution)/shard_map/ppermute | solution.py:22
  74.2 12.4 %collective-permute-start.14 = (bf16[16,3584]{1,0:T(8,128)(2,1)S(1)}, bf16[16,3584]{1,0:T(8,128)(2,1)S(1)}, u32[]{:S(2)}, u32[]{:S(2)}) collective-permute-start(bf16[16,3584]{1,0:T(8,128)(2,1)S(1)} %get-tuple-element.55), channel_id=1, source_target_pairs={{0,16},{1,17},{2,18},{3,19},{4,20},{5,21},{6,22},{7,23},{8,24},{9,... | collective-permute-start | bytes 344072 | tf_op jit(solution)/shard_map/ppermute | solution.py:22
  78.4 8.1 %collective-permute-start.15 = (bf16[16,3584]{1,0:T(8,128)(2,1)S(1)}, bf16[16,3584]{1,0:T(8,128)(2,1)S(1)}, u32[]{:S(2)}, u32[]{:S(2)}) collective-permute-start(bf16[16,3584]{1,0:T(8,128)(2,1)S(1)} %get-tuple-element.56), channel_id=1, source_target_pairs={{0,24},{1,25},{2,26},{3,27},{4,28},{5,29},{6,30},{7,31},{8,16},{9,... | collective-permute-start | bytes 344072 | tf_op jit(solution)/shard_map/ppermute | solution.py:22
  82.1 6.0 %collective-permute-start.24 = (bf16[16,3584]{1,0:T(8,128)(2,1)S(1)}, bf16[16,3584]{1,0:T(8,128)(2,1)S(1)}, u32[]{:S(2)}, u32[]{:S(2)}) collective-permute-start(bf16[16,3584]{1,0:T(8,128)(2,1)S(1)} %get-tuple-element.71), channel_id=1, source_target_pairs={{0,8},{1,9},{2,10},{3,11},{4,12},{5,13},{6,14},{7,15},{8,0},{9,1},... | collective-permute-start | bytes 344072 | tf_op jit(solution)/shard_map/ppermute | solution.py:22
  82.7 10.1 %collective-permute-start.25 = (bf16[16,3584]{1,0:T(8,128)(2,1)S(1)}, bf16[16,3584]{1,0:T(8,128)(2,1)S(1)}, u32[]{:S(2)}, u32[]{:S(2)}) collective-permute-start(bf16[16,3584]{1,0:T(8,128)(2,1)S(1)} %get-tuple-element.72), channel_id=1, source_target_pairs={{0,16},{1,17},{2,18},{3,19},{4,20},{5,21},{6,22},{7,23},{8,24},{9,... | collective-permute-start | bytes 344072 | tf_op jit(solution)/shard_map/ppermute | solution.py:22
  84.1 8.8 %collective-permute-start.26 = (bf16[16,3584]{1,0:T(8,128)(2,1)S(1)}, bf16[16,3584]{1,0:T(8,128)(2,1)S(1)}, u32[]{:S(2)}, u32[]{:S(2)}) collective-permute-start(bf16[16,3584]{1,0:T(8,128)(2,1)S(1)} %get-tuple-element.73), channel_id=1, source_target_pairs={{0,24},{1,25},{2,26},{3,27},{4,28},{5,29},{6,30},{7,31},{8,16},{9,... | collective-permute-start | bytes 344072 | tf_op jit(solution)/shard_map/ppermute | solution.py:22

commit v14 on v13

--- a/solution.py
+++ b/solution.py
@@ -32,10 +32,6 @@
 
 def chunk_of(width):
     return 512 if width % 512 == 0 else LANES
-
-
-def back_chunk(width):
-    return width // 2 if width % (2 * LANES) == 0 else LANES
 
 
 def column_chunks(width):
@@ -178,27 +174,46 @@
 
 
 def forward_kernel(x0, x1, x2, x3, g1, u1, d1, g0, u0, d0, *refs):
-    o0, o1, o2, o3, for_up, for_gate, x, hidden, into, back, sems = refs
+    o0, o1, o2, o3, for_up, for_gate, x, hidden, pre, into, back, sems = refs
     rows, width = x.shape
     units = back.shape[0]
-    chunk = back_chunk(width)
+    chunk = chunk_of(width)
     streams(own_slab(g0, u0, into, sems.at[0]) + [(d0.at[0], back, sems.at[1])])
     for part in column_chunks(width):
         x[:, part] = joined((x0, x1, x2, x3), part, rows)
 
-    def activate(pre_gate, pre_up, at):
+    def activate(at):
+        pre_gate, pre_up = pre[:, :units], pre[:, units:]
         sigma = jax.nn.sigmoid(pre_gate)
         activated = pre_gate * sigma
         hidden[:, at] = (activated * pre_up).astype(bf16)
         for_up[:, at] = activated
         for_gate[:, at] = pre_up * sigma * (1.0 + pre_gate * (1.0 - sigma))
 
-    pre_gate = jnp.dot(x[...], g1[0], preferred_element_type=f32)
-    pre_up = jnp.dot(x[...], u1[0], preferred_element_type=f32)
-    activate(pre_gate, pre_up, slice(units, 2 * units))
+    def contract(left, right):
+        return jnp.dot(left, right, preferred_element_type=f32)
+
+    def project(dots):
+        pre[...] = jnp.zeros_like(pre)
+
+        @pl.loop(0, width // chunk)
+        def _(number):
+            part = pl.ds(pl.multiple_of(number * chunk, chunk), chunk)
+            dots(x[:, part], part)
+
+    def other_slab(rows_part, part):
+        pre[:, :units] += contract(rows_part, g1[0, part])
+        pre[:, units:] += contract(rows_part, u1[0, part])
+
+    def this_slab(rows_part, part):
+        pre[:, :units] += contract(rows_part, into[part, :units])
+        pre[:, units:] += contract(rows_part, into[part, units:])
+
+    project(other_slab)
+    activate(slice(units, 2 * units))
     await_place(into, sems.at[0])
-    pre = jnp.dot(x[...], into[...], preferred_element_type=f32)
-    activate(pre[:, :units], pre[:, units:], slice(0, units))
+    project(this_slab)
+    activate(slice(0, units))
     await_place(back, sems.at[1])
 
     @pl.loop(0, width // chunk)
@@ -222,10 +237,10 @@
 
 
 def backward_kernel(x0, x1, x2, x3, for_up, for_gate, g1, u1, d1, g0, u0, d0, *refs):
-    o0, o1, o2, o3, x, grads, into, back, sems = refs
+    o0, o1, o2, o3, x, grads, hidden_grad, into, back, sems = refs
     rows, width = x.shape
     units = back.shape[0]
-    chunk = back_chunk(width)
+    chunk = chunk_of(width)
     streams([(d0.at[0], back, sems.at[1])] + own_slab(g0, u0, into, sems.at[0]))
     for part in column_chunks(width):
         x[:, part] = joined((x0, x1, x2, x3), part, rows)
@@ -233,15 +248,22 @@
     def transposed(left, right):
         return lax.dot_general(left, right, CONTRACT_COLS, preferred_element_type=f32)
 
-    def differentiate(down_w, slab):
+    def differentiate(down_at, slab):
         at, start = slice(slab * units, (slab + 1) * units), 2 * slab * units
-        hidden_grad = transposed(x[...], down_w)
-        grads[:, start : start + units] = (hidden_grad * for_gate[:, at]).astype(bf16)
-        grads[:, start + units : start + 2 * units] = (hidden_grad * for_up[:, at]).astype(bf16)
-
-    differentiate(d1[0], 1)
+        hidden_grad[...] = jnp.zeros_like(hidden_grad)
+
+        @pl.loop(0, width // chunk)
+        def _(number):
+            part = pl.ds(pl.multiple_of(number * chunk, chunk), chunk)
+            hidden_grad[...] += transposed(x[:, part], down_at(part))
+
+        wide = hidden_grad[...]
+        grads[:, start : start + units] = (wide * for_gate[:, at]).astype(bf16)
+        grads[:, start + units : start + 2 * units] = (wide * for_up[:, at]).astype(bf16)
+
+    differentiate(lambda part: d1[0, :, part], 1)
     await_place(back, sems.at[1])
-    differentiate(back[...], 0)
+    differentiate(lambda part: back[:, part], 0)
     await_place(into, sems.at[0])
 
     @pl.loop(0, width // chunk)
@@ -328,6 +350,7 @@
         scratch=[
             pltpu.VMEM((all_taken, width), bf16),
             pltpu.VMEM((all_taken, 2 * hidden), bf16),
+            pltpu.VMEM((all_taken, 2 * hidden), f32),
             *slab_room,
         ],
     )
@@ -355,6 +378,7 @@
         scratch=[
             pltpu.VMEM((all_taken, width), bf16),
             pltpu.VMEM((all_taken, 4 * hidden), bf16),
+            pltpu.VMEM((all_taken, hidden), f32),
             *slab_room,
         ],
     )

time: 93.8 us -> 95.7 us (1.020)
  Pallas kernels: 27.5 us -> 29.4 us
    pallas_call x9, Pallas kernels: 27.5 us -> 29.4 us  [call(): pl.pallas_call(body, out_shape=outs, in_specs=[whole] * len(args) if in_s...]
  transfers between devices with their start and end apart: 27 -> 27, of which waited for: 8 -> 8; matrix products, arithmetic and copies ran while one was open for 0% -> 0% of each run, Pallas kernels for 29% -> 30%
where the time goes in v14:
time: 95.7 us; the launch traced here: 95.5 us
  starting transfers between devices  36.9 us (39%)
  Pallas kernels  29.4 us (31%)
  waiting for transfers between devices  21.4 us (22%)
  local copies, waits for them, and re-layouts  7.14 us (7%)
    ppermute x27, starting transfers between devices, swap(): lax.ppermute(value, 'expert', [(i, i ^ offset) for i in range(devices)])  36.9 us
    pallas_call x9, Pallas kernels, call(): pl.pallas_call(body, out_shape=outs, in_specs=[whole] * len(args) if in_s...  29.4 us
    ppermute x27, waiting for transfers between devices, swap(): lax.ppermute(value, 'expert', [(i, i ^ offset) for i in range(devices)])  21.4 us
    unnamed x14, local copies, waits for them, and re-layouts  7.14 us
  transfers between devices with their start and end apart: 27, of which 8 were waited for; matrix products, arithmetic and copies ran while one was open for 0% of the time, Pallas kernels for 30%

profile of v14, /device:TPU:0, one launch (start us, length us, event | category | flops | bytes accessed | tf_op | source)
XLA Modules:
  0.0 95.5 jit_solution(18244254847296249194)
XLA Ops:
  0.6 0.5 collective-permute-start.3
  1.2 0.4 collective-permute-start.9
  1.7 0.9 copy-done.4
  2.6 0.7 copy-done.5
  3.2 0.7 copy-done.6
  3.9 0.2 shard_map.86.refs_0_
  4.1 3.7 %collective-permute-start.1 = (bf16[16,3712]{1,0:T(8,128)(2,1)S(1)}, bf16[16,3712]{1,0:T(8,128)(2,1)S(1)}, u32[]{:S(2)}, u32[]{:S(2)}) collective-permute-start(bf16[16,3712]{1,0:T(8,128)(2,1)S(1)} %shard_map.86.refs_0_), channel_id=1, source_target_pairs={{0,16},{1,17},{2,18},{3,19},{4,20},{5,21},{6,22},{7,23},{8,24},{9,... | collective-permute-start | bytes 356360 | tf_op jit(solution)/shard_map/ppermute | solution.py:22
  7.9 1.6 %collective-permute-start = (bf16[16,3712]{1,0:T(8,128)(2,1)S(1)}, bf16[16,3712]{1,0:T(8,128)(2,1)S(1)}, u32[]{:S(2)}, u32[]{:S(2)}) collective-permute-start(bf16[16,3712]{1,0:T(8,128)(2,1)S(1)} %shard_map.86.refs_0_), channel_id=1, source_target_pairs={{0,8},{1,9},{2,10},{3,11},{4,12},{5,13},{6,14},{7,15},{8,0},{9,1},... | collective-permute-start | bytes 356360 | tf_op jit(solution)/shard_map/ppermute | solution.py:22
  9.4 4.9 %collective-permute-done.1.refs_2_ = bf16[16,3712]{1,0:T(8,128)(2,1)S(1)} collective-permute-done((bf16[16,3712]{1,0:T(8,128)(2,1)S(1)}, bf16[16,3712]{1,0:T(8,128)(2,1)S(1)}, u32[]{:S(2)}, u32[]{:S(2)}) %collective-permute-start.1) | collective-permute-done | bytes 118816 | tf_op jit(solution)/shard_map/ppermute | solution.py:22
  14.3 0.6 collective-permute-start.2
  15.0 1.9 %copy-done = bf16[1,3584,512]{2,1,0:T(8,128)(2,1)} copy-done((bf16[1,3584,512]{2,1,0:T(8,128)(2,1)}, bf16[1,3584,512]{2,1,0:T(8,128)(2,1)S(1)}, u32[]{:S(2)}) %copy-start) | copy-done | bytes 3670040
  16.9 3.4 %collective-permute-start.7 = (bf16[16,3584]{1,0:T(8,128)(2,1)}, bf16[16,3584]{1,0:T(8,128)(2,1)S(1)}, u32[]{:S(2)}, u32[]{:S(2)}) collective-permute-start(bf16[16,3584]{1,0:T(8,128)(2,1)} %refs_0_.1), channel_id=1, source_target_pairs={{0,16},{1,17},{2,18},{3,19},{4,20},{5,21},{6,22},{7,23},{8,24},{9,... | collective-permute-start | bytes 344072 | tf_op jit(solution)/shard_map/ppermute | solution.py:22
  20.3 1.0 %shard_map.87 = (bf16[40,3584]{1,0:T(8,128)(2,1)S(1)}, bf16[40,3584]{1,0:T(8,128)(2,1)S(1)}, bf16[40,3584]{1,0:T(8,128)(2,1)S(1)}, bf16[40,3584]{1,0:T(8,128)(2,...) custom-call(s32[1]{0:T(128)} %bitcast.chip, bf16[16,3712]{1,0:T(8,128)(2,1)S(1)} %shard_map.86.refs_0_, ...), custom_call_target="tpu_custom_call" | custom-call | flops 117440512 | bytes 1753092 | tf_op jit(solution)/shard_map/pallas_call | solution.py:44
  21.3 1.6 %collective-permute-start.5 = (bf16[40,3584]{1,0:T(8,128)(2,1)S(1)}, bf16[40,3584]{1,0:T(8,128)(2,1)S(1)}, u32[]{:S(2)}, u32[]{:S(2)}) collective-permute-start(bf16[40,3584]{1,0:T(8,128)(2,1)S(1)} %get-tuple-element.42), channel_id=1, source_target_pairs={{0,2},{1,3},{2,0},{3,1},{4,6},{5,7},{6,4},{7,5},{8,10},{9,11},{10,... | collective-permute-start | bytes 860168 | tf_op jit(solution)/shard_map/ppermute | solution.py:22
  22.9 1.5 %collective-permute-start.6 = (bf16[40,3584]{1,0:T(8,128)(2,1)S(1)}, bf16[40,3584]{1,0:T(8,128)(2,1)S(1)}, u32[]{:S(2)}, u32[]{:S(2)}) collective-permute-start(bf16[40,3584]{1,0:T(8,128)(2,1)S(1)} %get-tuple-element.44), channel_id=1, source_target_pairs={{0,4},{1,5},{2,6},{3,7},{4,0},{5,1},{6,2},{7,3},{8,12},{9,13},{10,... | collective-permute-start | bytes 860168 | tf_op jit(solution)/shard_map/ppermute | solution.py:22
  24.4 1.6 %collective-permute-done.7.refs_2_ = bf16[16,3584]{1,0:T(8,128)(2,1)S(1)} collective-permute-done((bf16[16,3584]{1,0:T(8,128)(2,1)}, bf16[16,3584]{1,0:T(8,128)(2,1)S(1)}, u32[]{:S(2)}, u32[]{:S(2)}) %collective-permute-start.7) | collective-permute-done | bytes 114720 | tf_op jit(solution)/shard_map/ppermute | solution.py:22
  26.0 2.4 %collective-permute-start.8 = (bf16[40,3584]{1,0:T(8,128)(2,1)S(1)}, bf16[40,3584]{1,0:T(8,128)(2,1)S(1)}, u32[]{:S(2)}, u32[]{:S(2)}) collective-permute-start(bf16[40,3584]{1,0:T(8,128)(2,1)S(1)} %get-tuple-element.48), channel_id=1, source_target_pairs={{0,6},{1,7},{2,4},{3,5},{4,2},{5,3},{6,0},{7,1},{8,14},{9,15},{10,... | collective-permute-start | bytes 860168 | tf_op jit(solution)/shard_map/ppermute | solution.py:22
  28.4 2.0 %collective-permute-start.17 = (bf16[16,3584]{1,0:T(8,128)(2,1)S(1)}, bf16[16,3584]{1,0:T(8,128)(2,1)S(1)}, u32[]{:S(2)}, u32[]{:S(2)}) collective-permute-start(bf16[16,3584]{1,0:T(8,128)(2,1)S(1)} %collective-permute-done.7.refs_2_), channel_id=1, source_target_pairs={{0,8},{1,9},{2,10},{3,11},{4,12},{5,13},{6,14},{7,15},{8,0},{9,1},... | collective-permute-start | bytes 344072 | tf_op jit(solution)/shard_map/ppermute | solution.py:22
  30.4 4.0 %collective-permute-done.16.refs_1_ = bf16[16,3584]{1,0:T(8,128)(2,1)S(1)} collective-permute-done((bf16[16,3584]{1,0:T(8,128)(2,1)}, bf16[16,3584]{1,0:T(8,128)(2,1)S(1)}, u32[]{:S(2)}, u32[]{:S(2)}) %collective-permute-start.16) | collective-permute-done | bytes 114720 | tf_op jit(solution)/shard_map/ppermute | solution.py:22
  34.4 1.2 %collective-permute-done.17.refs_3_ = bf16[16,3584]{1,0:T(8,128)(2,1)S(1)} collective-permute-done((bf16[16,3584]{1,0:T(8,128)(2,1)S(1)}, bf16[16,3584]{1,0:T(8,128)(2,1)S(1)}, u32[]{:S(2)}, u32[]{:S(2)}) %collective-permute-start.17) | collective-permute-done | bytes 114720 | tf_op jit(solution)/shard_map/ppermute | solution.py:22
  35.6 0.9 copy-done.3
  36.5 0.6 shard_map.91
  37.1 0.6 collective-permute-start.18
  37.7 0.6 collective-permute-start.19
  38.3 2.4 %collective-permute-start.20 = (bf16[40,3584]{1,0:T(8,128)(2,1)S(1)}, bf16[40,3584]{1,0:T(8,128)(2,1)S(1)}, u32[]{:S(2)}, u32[]{:S(2)}) collective-permute-start(bf16[40,3584]{1,0:T(8,128)(2,1)S(1)} %get-tuple-element.63), channel_id=1, source_target_pairs={{0,6},{1,7},{2,4},{3,5},{4,2},{5,3},{6,0},{7,1},{8,14},{9,15},{10,... | collective-permute-start | bytes 860168 | tf_op jit(solution)/shard_map/ppermute | solution.py:22
  40.7 2.0 %copy-done.1 = bf16[1,3584,512]{2,1,0:T(8,128)(2,1)S(1)} copy-done((bf16[1,3584,512]{2,1,0:T(8,128)(2,1)S(1)}, bf16[1,3584,512]{2,1,0:T(8,128)(2,1)}, u32[]{:S(2)}) %copy-start.1) | copy-done | bytes 3670040
  42.7 11.5 %shard_map.88 = (bf16[40,3584]{1,0:T(8,128)(2,1)S(1)}, bf16[40,3584]{1,0:T(8,128)(2,1)S(1)}, bf16[40,3584]{1,0:T(8,128)(2,1)S(1)}, bf16[40,3584]{1,0:T(8,128)(2,...) custom-call(bf16[40,3584]{1,0:T(8,128)(2,1)S(1)} %get-tuple-element.40.x0, ...), custom_call_target="tpu_custom_call" | custom-call | flops 3523215360 | bytes 25624576 | tf_op jit(solution)/shard_map/pallas_call | solution.py:44
  54.2 0.6 collective-permute-start.10
  54.8 0.6 collective-permute-start.11
  55.4 2.4 %collective-permute-start.12 = (bf16[40,3584]{1,0:T(8,128)(2,1)S(1)}, bf16[40,3584]{1,0:T(8,128)(2,1)S(1)}, u32[]{:S(2)}, u32[]{:S(2)}) collective-permute-start(bf16[40,3584]{1,0:T(8,128)(2,1)S(1)} %get-tuple-element.52), channel_id=1, source_target_pairs={{0,6},{1,7},{2,4},{3,5},{4,2},{5,3},{6,0},{7,1},{8,14},{9,15},{10,... | collective-permute-start | bytes 860168 | tf_op jit(solution)/shard_map/ppermute | solution.py:22
  57.8 13.8 %shard_map.92 = (bf16[40,3584]{1,0:T(8,128)(2,1)S(1)}, bf16[40,3584]{1,0:T(8,128)(2,1)S(1)}, bf16[40,3584]{1,0:T(8,128)(2,1)S(1)}, bf16[40,3584]{1,0:T(8,128)(2,1)S(1)}) custom-call(bf16[40,3584]{1,0:T(8,128)(2,1)S(1)} %get-tuple-element.60.x0, bf16[40,3584]{1,0:T(8,128)(2,1)S(1)} %collective-permute-done.18.x1, ...), custom_call_target="tpu_custom_call" | custom-call | flops 3523215360 | bytes 25624576 | tf_op jit(solution)/shard_map/pallas_call | solution.py:44
  71.6 0.6 collective-permute-start.21
  72.2 0.6 collective-permute-start.22
  72.7 2.4 %collective-permute-start.23 = (bf16[40,3584]{1,0:T(8,128)(2,1)S(1)}, bf16[40,3584]{1,0:T(8,128)(2,1)S(1)}, u32[]{:S(2)}, u32[]{:S(2)}) collective-permute-start(bf16[40,3584]{1,0:T(8,128)(2,1)S(1)} %get-tuple-element.69), channel_id=1, source_target_pairs={{0,6},{1,7},{2,4},{3,5},{4,2},{5,3},{6,0},{7,1},{8,14},{9,15},{10,... | collective-permute-start | bytes 860168 | tf_op jit(solution)/shard_map/ppermute | solution.py:22
  75.1 0.6 shard_map.89
  75.7 0.3 collective-permute-start.13
  76.1 2.2 %collective-permute-start.14 = (bf16[16,3584]{1,0:T(8,128)(2,1)S(1)}, bf16[16,3584]{1,0:T(8,128)(2,1)S(1)}, u32[]{:S(2)}, u32[]{:S(2)}) collective-permute-start(bf16[16,3584]{1,0:T(8,128)(2,1)S(1)} %get-tuple-element.55), channel_id=1, source_target_pairs={{0,16},{1,17},{2,18},{3,19},{4,20},{5,21},{6,22},{7,23},{8,24},{9,... | collective-permute-start | bytes 344072 | tf_op jit(solution)/shard_map/ppermute | solution.py:22
  78.3 2.1 %collective-permute-done.21.second = bf16[40,3584]{1,0:T(8,128)(2,1)S(1)} collective-permute-done((bf16[40,3584]{1,0:T(8,128)(2,1)S(1)}, bf16[40,3584]{1,0:T(8,128)(2,1)S(1)}, u32[]{:S(2)}, u32[]{:S(2)}) %collective-permute-start.21) | collective-permute-done | bytes 286752 | tf_op jit(solution)/shard_map/ppermute | solution.py:22
  80.3 1.3 %collective-permute-start.15 = (bf16[16,3584]{1,0:T(8,128)(2,1)S(1)}, bf16[16,3584]{1,0:T(8,128)(2,1)S(1)}, u32[]{:S(2)}, u32[]{:S(2)}) collective-permute-start(bf16[16,3584]{1,0:T(8,128)(2,1)S(1)} %get-tuple-element.56), channel_id=1, source_target_pairs={{0,24},{1,25},{2,26},{3,27},{4,28},{5,29},{6,30},{7,31},{8,16},{9,... | collective-permute-start | bytes 344072 | tf_op jit(solution)/shard_map/ppermute | solution.py:22
  81.7 2.0 %collective-permute-done.22.third = bf16[40,3584]{1,0:T(8,128)(2,1)S(1)} collective-permute-done((bf16[40,3584]{1,0:T(8,128)(2,1)S(1)}, bf16[40,3584]{1,0:T(8,128)(2,1)S(1)}, u32[]{:S(2)}, u32[]{:S(2)}) %collective-permute-start.22) | collective-permute-done | bytes 286752 | tf_op jit(solution)/shard_map/ppermute | solution.py:22
  83.7 0.3 shard_map.93
  84.0 0.7 collective-permute-start.24
  84.6 1.3 %collective-permute-start.25 = (bf16[16,3584]{1,0:T(8,128)(2,1)S(1)}, bf16[16,3584]{1,0:T(8,128)(2,1)S(1)}, u32[]{:S(2)}, u32[]{:S(2)}) collective-permute-start(bf16[16,3584]{1,0:T(8,128)(2,1)S(1)} %get-tuple-element.72), channel_id=1, source_target_pairs={{0,16},{1,17},{2,18},{3,19},{4,20},{5,21},{6,22},{7,23},{8,24},{9,... | collective-permute-start | bytes 344072 | tf_op jit(solution)/shard_map/ppermute | solution.py:22
  86.0 2.5 %collective-permute-start.26 = (bf16[16,3584]{1,0:T(8,128)(2,1)S(1)}, bf16[16,3584]{1,0:T(8,128)(2,1)S(1)}, u32[]{:S(2)}, u32[]{:S(2)}) collective-permute-start(bf16[16,3584]{1,0:T(8,128)(2,1)S(1)} %get-tuple-element.73), channel_id=1, source_target_pairs={{0,24},{1,25},{2,26},{3,27},{4,28},{5,29},{6,30},{7,31},{8,16},{9,... | collective-permute-start | bytes 344072 | tf_op jit(solution)/shard_map/ppermute | solution.py:22
  88.4 0.7 shard_map.90
  89.1 0.8 collective-permute-done.24.refs_1_
  90.0 4.8 %collective-permute-done.25.refs_2_ = bf16[16,3584]{1,0:T(8,128)(2,1)S(1)} collective-permute-done((bf16[16,3584]{1,0:T(8,128)(2,1)S(1)}, bf16[16,3584]{1,0:T(8,128)(2,1)S(1)}, u32[]{:S(2)}, u32[]{:S(2)}) %collective-permute-start.25) | collective-permute-done | bytes 114720 | tf_op jit(solution)/shard_map/ppermute | solution.py:22
  94.8 0.7 shard_map.94
  (29 shorter events, 0.1 us)
Async XLA Ops:
  0.6 14.4 %collective-permute-start.3 = (bf16[1,3584,512]{2,1,0:T(8,128)(2,1)}, bf16[1,3584,512]{2,1,0:T(8,128)(2,1)S(1)}, u32[]{:S(2)}, u32[]{:S(2)}) collective-permute-start(bf16[1,3584,512]{2,1,0:T(8,128)(2,1)} %g0.3), channel_id=1, source_target_pairs={{0,1},{1,0},{2,3},{3,2},{4,5},{5,4},{6,7},{7,6},{8,9},{9,8},{10,11... | collective-permute-start | bytes 11010056 | tf_op jit(solution)/shard_map/ppermute | solution.py:22
  1.1 20.2 %collective-permute-start.4 = (bf16[1,3584,512]{2,1,0:T(8,128)(2,1)}, bf16[1,3584,512]{2,1,0:T(8,128)(2,1)}, u32[]{:S(2)}, u32[]{:S(2)}) collective-permute-start(bf16[1,3584,512]{2,1,0:T(8,128)(2,1)} %u0.3), channel_id=1, source_target_pairs={{0,1},{1,0},{2,3},{3,2},{4,5},{5,4},{6,7},{7,6},{8,9},{9,8},{10,11... | collective-permute-start | bytes 11010056 | tf_op jit(solution)/shard_map/ppermute | solution.py:22
  1.2 27.2 %collective-permute-start.9 = (bf16[1,512,3584]{2,1,0:T(8,128)(2,1)}, bf16[1,512,3584]{2,1,0:T(8,128)(2,1)}, u32[]{:S(2)}, u32[]{:S(2)}) collective-permute-start(bf16[1,512,3584]{2,1,0:T(8,128)(2,1)} %d0.3), channel_id=1, source_target_pairs={{0,1},{1,0},{2,3},{3,2},{4,5},{5,4},{6,7},{7,6},{8,9},{9,8},{10,11... | collective-permute-start | bytes 11010056 | tf_op jit(solution)/shard_map/ppermute | solution.py:22
  1.7 0.9 copy-start.4
  2.6 0.7 copy-start.5
  3.2 0.7 copy-start.6
  4.1 10.2 %collective-permute-start.1 = (bf16[16,3712]{1,0:T(8,128)(2,1)S(1)}, bf16[16,3712]{1,0:T(8,128)(2,1)S(1)}, u32[]{:S(2)}, u32[]{:S(2)}) collective-permute-start(bf16[16,3712]{1,0:T(8,128)(2,1)S(1)} %shard_map.86.refs_0_), channel_id=1, source_target_pairs={{0,16},{1,17},{2,18},{3,19},{4,20},{5,21},{6,22},{7,23},{8,24},{9,... | collective-permute-start | bytes 356360 | tf_op jit(solution)/shard_map/ppermute | solution.py:22
  7.9 12.4 %collective-permute-start = (bf16[16,3712]{1,0:T(8,128)(2,1)S(1)}, bf16[16,3712]{1,0:T(8,128)(2,1)S(1)}, u32[]{:S(2)}, u32[]{:S(2)}) collective-permute-start(bf16[16,3712]{1,0:T(8,128)(2,1)S(1)} %shard_map.86.refs_0_), channel_id=1, source_target_pairs={{0,8},{1,9},{2,10},{3,11},{4,12},{5,13},{6,14},{7,15},{8,0},{9,1},... | collective-permute-start | bytes 356360 | tf_op jit(solution)/shard_map/ppermute | solution.py:22
  14.3 5.9 %collective-permute-start.2 = (bf16[16,3712]{1,0:T(8,128)(2,1)S(1)}, bf16[16,3712]{1,0:T(8,128)(2,1)S(1)}, u32[]{:S(2)}, u32[]{:S(2)}) collective-permute-start(bf16[16,3712]{1,0:T(8,128)(2,1)S(1)} %collective-permute-done.1.refs_2_), channel_id=1, source_target_pairs={{0,8},{1,9},{2,10},{3,11},{4,12},{5,13},{6,14},{7,15},{8,0},{9,1},... | collective-permute-start | bytes 356360 | tf_op jit(solution)/shard_map/ppermute | solution.py:22
  15.0 1.9 %copy-start = (bf16[1,3584,512]{2,1,0:T(8,128)(2,1)}, bf16[1,3584,512]{2,1,0:T(8,128)(2,1)S(1)}, u32[]{:S(2)}) copy-start(bf16[1,3584,512]{2,1,0:T(8,128)(2,1)S(1)} %collective-permute-done.3.g1) | copy-start | bytes 11010052
  16.9 9.0 %collective-permute-start.7 = (bf16[16,3584]{1,0:T(8,128)(2,1)}, bf16[16,3584]{1,0:T(8,128)(2,1)S(1)}, u32[]{:S(2)}, u32[]{:S(2)}) collective-permute-start(bf16[16,3584]{1,0:T(8,128)(2,1)} %refs_0_.1), channel_id=1, source_target_pairs={{0,16},{1,17},{2,18},{3,19},{4,20},{5,21},{6,22},{7,23},{8,24},{9,... | collective-permute-start | bytes 344072 | tf_op jit(solution)/shard_map/ppermute | solution.py:22
  21.3 17.0 %collective-permute-start.5 = (bf16[40,3584]{1,0:T(8,128)(2,1)S(1)}, bf16[40,3584]{1,0:T(8,128)(2,1)S(1)}, u32[]{:S(2)}, u32[]{:S(2)}) collective-permute-start(bf16[40,3584]{1,0:T(8,128)(2,1)S(1)} %get-tuple-element.42), channel_id=1, source_target_pairs={{0,2},{1,3},{2,0},{3,1},{4,6},{5,7},{6,4},{7,5},{8,10},{9,11},{10,... | collective-permute-start | bytes 860168 | tf_op jit(solution)/shard_map/ppermute | solution.py:22
  22.9 17.8 %collective-permute-start.6 = (bf16[40,3584]{1,0:T(8,128)(2,1)S(1)}, bf16[40,3584]{1,0:T(8,128)(2,1)S(1)}, u32[]{:S(2)}, u32[]{:S(2)}) collective-permute-start(bf16[40,3584]{1,0:T(8,128)(2,1)S(1)} %get-tuple-element.44), channel_id=1, source_target_pairs={{0,4},{1,5},{2,6},{3,7},{4,0},{5,1},{6,2},{7,3},{8,12},{9,13},{10,... | collective-permute-start | bytes 860168 | tf_op jit(solution)/shard_map/ppermute | solution.py:22
  26.0 14.7 %collective-permute-start.8 = (bf16[40,3584]{1,0:T(8,128)(2,1)S(1)}, bf16[40,3584]{1,0:T(8,128)(2,1)S(1)}, u32[]{:S(2)}, u32[]{:S(2)}) collective-permute-start(bf16[40,3584]{1,0:T(8,128)(2,1)S(1)} %get-tuple-element.48), channel_id=1, source_target_pairs={{0,6},{1,7},{2,4},{3,5},{4,2},{5,3},{6,0},{7,1},{8,14},{9,15},{10,... | collective-permute-start | bytes 860168 | tf_op jit(solution)/shard_map/ppermute | solution.py:22
  28.4 6.0 %collective-permute-start.16 = (bf16[16,3584]{1,0:T(8,128)(2,1)}, bf16[16,3584]{1,0:T(8,128)(2,1)S(1)}, u32[]{:S(2)}, u32[]{:S(2)}) collective-permute-start(bf16[16,3584]{1,0:T(8,128)(2,1)} %refs_0_.1), channel_id=1, source_target_pairs={{0,8},{1,9},{2,10},{3,11},{4,12},{5,13},{6,14},{7,15},{8,0},{9,1},... | collective-permute-start | bytes 344072 | tf_op jit(solution)/shard_map/ppermute | solution.py:22
  28.4 7.2 %collective-permute-start.17 = (bf16[16,3584]{1,0:T(8,128)(2,1)S(1)}, bf16[16,3584]{1,0:T(8,128)(2,1)S(1)}, u32[]{:S(2)}, u32[]{:S(2)}) collective-permute-start(bf16[16,3584]{1,0:T(8,128)(2,1)S(1)} %collective-permute-done.7.refs_2_), channel_id=1, source_target_pairs={{0,8},{1,9},{2,10},{3,11},{4,12},{5,13},{6,14},{7,15},{8,0},{9,1},... | collective-permute-start | bytes 344072 | tf_op jit(solution)/shard_map/ppermute | solution.py:22
  35.6 0.9 copy-start.3
  37.1 18.3 %collective-permute-start.18 = (bf16[40,3584]{1,0:T(8,128)(2,1)S(1)}, bf16[40,3584]{1,0:T(8,128)(2,1)S(1)}, u32[]{:S(2)}, u32[]{:S(2)}) collective-permute-start(bf16[40,3584]{1,0:T(8,128)(2,1)S(1)} %get-tuple-element.61), channel_id=1, source_target_pairs={{0,2},{1,3},{2,0},{3,1},{4,6},{5,7},{6,4},{7,5},{8,10},{9,11},{10,... | collective-permute-start | bytes 860168 | tf_op jit(solution)/shard_map/ppermute | solution.py:22
  37.7 20.1 %collective-permute-start.19 = (bf16[40,3584]{1,0:T(8,128)(2,1)S(1)}, bf16[40,3584]{1,0:T(8,128)(2,1)S(1)}, u32[]{:S(2)}, u32[]{:S(2)}) collective-permute-start(bf16[40,3584]{1,0:T(8,128)(2,1)S(1)} %get-tuple-element.62), channel_id=1, source_target_pairs={{0,4},{1,5},{2,6},{3,7},{4,0},{5,1},{6,2},{7,3},{8,12},{9,13},{10,... | collective-permute-start | bytes 860168 | tf_op jit(solution)/shard_map/ppermute | solution.py:22
  38.3 19.5 %collective-permute-start.20 = (bf16[40,3584]{1,0:T(8,128)(2,1)S(1)}, bf16[40,3584]{1,0:T(8,128)(2,1)S(1)}, u32[]{:S(2)}, u32[]{:S(2)}) collective-permute-start(bf16[40,3584]{1,0:T(8,128)(2,1)S(1)} %get-tuple-element.63), channel_id=1, source_target_pairs={{0,6},{1,7},{2,4},{3,5},{4,2},{5,3},{6,0},{7,1},{8,14},{9,15},{10,... | collective-permute-start | bytes 860168 | tf_op jit(solution)/shard_map/ppermute | solution.py:22
  40.7 2.0 %copy-start.1 = (bf16[1,3584,512]{2,1,0:T(8,128)(2,1)S(1)}, bf16[1,3584,512]{2,1,0:T(8,128)(2,1)}, u32[]{:S(2)}) copy-start(bf16[1,3584,512]{2,1,0:T(8,128)(2,1)} %copy-done) | copy-start | bytes 11010052
  42.7 15.1 %copy-start.2 = (bf16[1,3584,512]{2,1,0:T(8,128)(2,1)S(1)}, bf16[1,3584,512]{2,1,0:T(8,128)(2,1)}, u32[]{:S(2)}) copy-start(bf16[1,3584,512]{2,1,0:T(8,128)(2,1)} %copy-done) | copy-start | bytes 11010052
  54.2 18.5 %collective-permute-start.10 = (bf16[40,3584]{1,0:T(8,128)(2,1)S(1)}, bf16[40,3584]{1,0:T(8,128)(2,1)S(1)}, u32[]{:S(2)}, u32[]{:S(2)}) collective-permute-start(bf16[40,3584]{1,0:T(8,128)(2,1)S(1)} %get-tuple-element.50), channel_id=1, source_target_pairs={{0,2},{1,3},{2,0},{3,1},{4,6},{5,7},{6,4},{7,5},{8,10},{9,11},{10,... | collective-permute-start | bytes 860168 | tf_op jit(solution)/shard_map/ppermute | solution.py:22
  54.8 20.3 %collective-permute-start.11 = (bf16[40,3584]{1,0:T(8,128)(2,1)S(1)}, bf16[40,3584]{1,0:T(8,128)(2,1)S(1)}, u32[]{:S(2)}, u32[]{:S(2)}) collective-permute-start(bf16[40,3584]{1,0:T(8,128)(2,1)S(1)} %get-tuple-element.51), channel_id=1, source_target_pairs={{0,4},{1,5},{2,6},{3,7},{4,0},{5,1},{6,2},{7,3},{8,12},{9,13},{10,... | collective-permute-start | bytes 860168 | tf_op jit(solution)/shard_map/ppermute | solution.py:22
  55.4 19.7 %collective-permute-start.12 = (bf16[40,3584]{1,0:T(8,128)(2,1)S(1)}, bf16[40,3584]{1,0:T(8,128)(2,1)S(1)}, u32[]{:S(2)}, u32[]{:S(2)}) collective-permute-start(bf16[40,3584]{1,0:T(8,128)(2,1)S(1)} %get-tuple-element.52), channel_id=1, source_target_pairs={{0,6},{1,7},{2,4},{3,5},{4,2},{5,3},{6,0},{7,1},{8,14},{9,15},{10,... | collective-permute-start | bytes 860168 | tf_op jit(solution)/shard_map/ppermute | solution.py:22
  71.6 8.8 %collective-permute-start.21 = (bf16[40,3584]{1,0:T(8,128)(2,1)S(1)}, bf16[40,3584]{1,0:T(8,128)(2,1)S(1)}, u32[]{:S(2)}, u32[]{:S(2)}) collective-permute-start(bf16[40,3584]{1,0:T(8,128)(2,1)S(1)} %get-tuple-element.67), channel_id=1, source_target_pairs={{0,2},{1,3},{2,0},{3,1},{4,6},{5,7},{6,4},{7,5},{8,10},{9,11},{10,... | collective-permute-start | bytes 860168 | tf_op jit(solution)/shard_map/ppermute | solution.py:22
  72.2 11.5 %collective-permute-start.22 = (bf16[40,3584]{1,0:T(8,128)(2,1)S(1)}, bf16[40,3584]{1,0:T(8,128)(2,1)S(1)}, u32[]{:S(2)}, u32[]{:S(2)}) collective-permute-start(bf16[40,3584]{1,0:T(8,128)(2,1)S(1)} %get-tuple-element.68), channel_id=1, source_target_pairs={{0,4},{1,5},{2,6},{3,7},{4,0},{5,1},{6,2},{7,3},{8,12},{9,13},{10,... | collective-permute-start | bytes 860168 | tf_op jit(solution)/shard_map/ppermute | solution.py:22
  72.7 10.9 %collective-permute-start.23 = (bf16[40,3584]{1,0:T(8,128)(2,1)S(1)}, bf16[40,3584]{1,0:T(8,128)(2,1)S(1)}, u32[]{:S(2)}, u32[]{:S(2)}) collective-permute-start(bf16[40,3584]{1,0:T(8,128)(2,1)S(1)} %get-tuple-element.69), channel_id=1, source_target_pairs={{0,6},{1,7},{2,4},{3,5},{4,2},{5,3},{6,0},{7,1},{8,14},{9,15},{10,... | collective-permute-start | bytes 860168 | tf_op jit(solution)/shard_map/ppermute | solution.py:22
  75.7 10.2 %collective-permute-start.13 = (bf16[16,3584]{1,0:T(8,128)(2,1)S(1)}, bf16[16,3584]{1,0:T(8,128)(2,1)S(1)}, u32[]{:S(2)}, u32[]{:S(2)}) collective-permute-start(bf16[16,3584]{1,0:T(8,128)(2,1)S(1)} %get-tuple-element.54), channel_id=1, source_target_pairs={{0,8},{1,9},{2,10},{3,11},{4,12},{5,13},{6,14},{7,15},{8,0},{9,1},... | collective-permute-start | bytes 344072 | tf_op jit(solution)/shard_map/ppermute | solution.py:22
  76.1 12.4 %collective-permute-start.14 = (bf16[16,3584]{1,0:T(8,128)(2,1)S(1)}, bf16[16,3584]{1,0:T(8,128)(2,1)S(1)}, u32[]{:S(2)}, u32[]{:S(2)}) collective-permute-start(bf16[16,3584]{1,0:T(8,128)(2,1)S(1)} %get-tuple-element.55), channel_id=1, source_target_pairs={{0,16},{1,17},{2,18},{3,19},{4,20},{5,21},{6,22},{7,23},{8,24},{9,... | collective-permute-start | bytes 344072 | tf_op jit(solution)/shard_map/ppermute | solution.py:22
  80.3 8.1 %collective-permute-start.15 = (bf16[16,3584]{1,0:T(8,128)(2,1)S(1)}, bf16[16,3584]{1,0:T(8,128)(2,1)S(1)}, u32[]{:S(2)}, u32[]{:S(2)}) collective-permute-start(bf16[16,3584]{1,0:T(8,128)(2,1)S(1)} %get-tuple-element.56), channel_id=1, source_target_pairs={{0,24},{1,25},{2,26},{3,27},{4,28},{5,29},{6,30},{7,31},{8,16},{9,... | collective-permute-start | bytes 344072 | tf_op jit(solution)/shard_map/ppermute | solution.py:22
  84.0 6.0 %collective-permute-start.24 = (bf16[16,3584]{1,0:T(8,128)(2,1)S(1)}, bf16[16,3584]{1,0:T(8,128)(2,1)S(1)}, u32[]{:S(2)}, u32[]{:S(2)}) collective-permute-start(bf16[16,3584]{1,0:T(8,128)(2,1)S(1)} %get-tuple-element.71), channel_id=1, source_target_pairs={{0,8},{1,9},{2,10},{3,11},{4,12},{5,13},{6,14},{7,15},{8,0},{9,1},... | collective-permute-start | bytes 344072 | tf_op jit(solution)/shard_map/ppermute | solution.py:22
  84.6 10.1 %collective-permute-start.25 = (bf16[16,3584]{1,0:T(8,128)(2,1)S(1)}, bf16[16,3584]{1,0:T(8,128)(2,1)S(1)}, u32[]{:S(2)}, u32[]{:S(2)}) collective-permute-start(bf16[16,3584]{1,0:T(8,128)(2,1)S(1)} %get-tuple-element.72), channel_id=1, source_target_pairs={{0,16},{1,17},{2,18},{3,19},{4,20},{5,21},{6,22},{7,23},{8,24},{9,... | collective-permute-start | bytes 344072 | tf_op jit(solution)/shard_map/ppermute | solution.py:22
  86.0 8.8 %collective-permute-start.26 = (bf16[16,3584]{1,0:T(8,128)(2,1)S(1)}, bf16[16,3584]{1,0:T(8,128)(2,1)S(1)}, u32[]{:S(2)}, u32[]{:S(2)}) collective-permute-start(bf16[16,3584]{1,0:T(8,128)(2,1)S(1)} %get-tuple-element.73), channel_id=1, source_target_pairs={{0,24},{1,25},{2,26},{3,27},{4,28},{5,29},{6,30},{7,31},{8,16},{9,... | collective-permute-start | bytes 344072 | tf_op jit(solution)/shard_map/ppermute | solution.py:22

commit v15 on v10

--- a/solution.py
+++ b/solution.py
@@ -233,30 +233,29 @@
     triples = []
     for slab in range(2):
         place = back.at[pl.ds(slab * units, units)]
-        triples.append((slabs[3 * slab + 2].at[0], place, sems.at[slab]))
+        triples.append((slabs[3 * slab + 2].at[0], place, sems.at[0]))
     for number in range(chunks):
         lines = pl.ds(number * chunk, chunk)
         for column, matrix in enumerate((0, 1, 3, 4)):
             place = into.at[lines, pl.ds(column * units, units)]
-            triples.append((slabs[matrix].at[0, lines], place, sems.at[2 + number]))
+            triples.append((slabs[matrix].at[0, lines], place, sems.at[1 + number]))
     streams(triples)
     for part in column_chunks(width):
         x[:, part] = joined((x0, x1, x2, x3), part, rows)
 
-    @pl.loop(0, 2)
-    def _(slab):
-        at = pl.ds(pl.multiple_of(slab * units, units), units)
-        await_place(back.at[at], sems.at[slab])
-        hidden_grad = lax.dot_general(x[...], back[at], CONTRACT_COLS, preferred_element_type=f32)
-        start = pl.multiple_of(2 * slab * units, 2 * units)
-        gate_at, up_at = pl.ds(start, units), pl.ds(start + units, units)
-        grads[:, gate_at] = (hidden_grad * for_gate[:, at]).astype(bf16)
-        grads[:, up_at] = (hidden_grad * for_up[:, at]).astype(bf16)
+    await_place(back, sems.at[0])
+    hidden_grad = lax.dot_general(x[...], back[...], CONTRACT_COLS, preferred_element_type=f32)
+    for slab in range(2):
+        at = slice(slab * units, (slab + 1) * units)
+        start = 2 * slab * units
+        grads[:, start : start + units] = (hidden_grad[:, at] * for_gate[:, at]).astype(bf16)
+        up_at = slice(start + units, start + 2 * units)
+        grads[:, up_at] = (hidden_grad[:, at] * for_up[:, at]).astype(bf16)
 
     @pl.loop(0, chunks)
     def _(number):
         part = pl.ds(pl.multiple_of(number * chunk, chunk), chunk)
-        await_place(into.at[part], sems.at[2 + number])
+        await_place(into.at[part], sems.at[1 + number])
         total = lax.dot_general(
             grads[...], into[part], CONTRACT_COLS, preferred_element_type=f32
         )
@@ -365,7 +364,7 @@
             pltpu.VMEM((all_taken, width), bf16),
             pltpu.VMEM((all_taken, 4 * hidden), bf16),
             *slab_room,
-            pltpu.SemaphoreType.DMA((2 + chunks,)),
+            pltpu.SemaphoreType.DMA((1 + chunks,)),
         ],
     )
     token_grad = go_home(backs, False)

time: 86.4 us -> 86.6 us (level)
  no operation moved by 1% of the time
where the time goes in v15:
time: 86.6 us; the launch traced here: 86.3 us
  starting transfers between devices  42.5 us (49%)
  Pallas kernels  23.2 us (27%)
  waiting for transfers between devices  16.7 us (19%)
  local copies, waits for them, and re-layouts  3.17 us (4%)
    ppermute x27, starting transfers between devices, swap(): lax.ppermute(value, 'expert', [(i, i ^ offset) for i in range(devices)])  42.5 us
    pallas_call x9, Pallas kernels, call(): pl.pallas_call(body, out_shape=outs, in_specs=[whole] * len(args) if in_s...  23.2 us
    ppermute x27, waiting for transfers between devices, swap(): lax.ppermute(value, 'expert', [(i, i ^ offset) for i in range(devices)])  16.7 us
    unnamed x8, local copies, waits for them, and re-layouts  3.17 us
  transfers between devices with their start and end apart: 27, of which 8 were waited for; matrix products, arithmetic and copies ran while one was open for 0% of the time, Pallas kernels for 26%

profile of v15, /device:TPU:0, one launch (start us, length us, event | category | flops | bytes accessed | tf_op | source)
XLA Modules:
  0.0 86.3 jit_solution(14074631750326720476)
XLA Ops:
  0.6 0.5 collective-permute-start.3
  1.1 0.1 collective-permute-start.4
  1.2 0.4 collective-permute-start.9
  1.7 0.9 %copy-done.1 = bf16[16,3584]{1,0:T(8,128)(2,1)S(1)} copy-done((bf16[16,3584]{1,0:T(8,128)(2,1)S(1)}, bf16[16,3584]{1,0:T(8,128)(2,1)}, u32[]{:S(2)}) %copy-start.1) | copy-done | bytes 114712
  2.6 0.7 copy-done.2
  3.2 0.7 copy-done.3
  3.9 0.2 shard_map.86.refs_0_
  4.1 3.7 %collective-permute-start.1 = (bf16[16,3712]{1,0:T(8,128)(2,1)S(1)}, bf16[16,3712]{1,0:T(8,128)(2,1)S(1)}, u32[]{:S(2)}, u32[]{:S(2)}) collective-permute-start(bf16[16,3712]{1,0:T(8,128)(2,1)S(1)} %shard_map.86.refs_0_), channel_id=1, source_target_pairs={{0,16},{1,17},{2,18},{3,19},{4,20},{5,21},{6,22},{7,23},{8,24},{9,... | collective-permute-start | bytes 356360 | tf_op jit(solution)/shard_map/ppermute | solution.py:22
  7.9 1.6 %collective-permute-start = (bf16[16,3712]{1,0:T(8,128)(2,1)S(1)}, bf16[16,3712]{1,0:T(8,128)(2,1)S(1)}, u32[]{:S(2)}, u32[]{:S(2)}) collective-permute-start(bf16[16,3712]{1,0:T(8,128)(2,1)S(1)} %shard_map.86.refs_0_), channel_id=1, source_target_pairs={{0,8},{1,9},{2,10},{3,11},{4,12},{5,13},{6,14},{7,15},{8,0},{9,1},... | collective-permute-start | bytes 356360 | tf_op jit(solution)/shard_map/ppermute | solution.py:22
  9.4 4.9 %collective-permute-done.1.refs_2_ = bf16[16,3712]{1,0:T(8,128)(2,1)S(1)} collective-permute-done((bf16[16,3712]{1,0:T(8,128)(2,1)S(1)}, bf16[16,3712]{1,0:T(8,128)(2,1)S(1)}, u32[]{:S(2)}, u32[]{:S(2)}) %collective-permute-start.1) | collective-permute-done | bytes 118816 | tf_op jit(solution)/shard_map/ppermute | solution.py:22
  14.3 0.6 collective-permute-start.2
  15.0 0.0 collective-permute-done.3.refs_3_
  15.0 3.4 %collective-permute-start.7 = (bf16[16,3584]{1,0:T(8,128)(2,1)}, bf16[16,3584]{1,0:T(8,128)(2,1)S(1)}, u32[]{:S(2)}, u32[]{:S(2)}) collective-permute-start(bf16[16,3584]{1,0:T(8,128)(2,1)} %refs_0_.4), channel_id=1, source_target_pairs={{0,16},{1,17},{2,18},{3,19},{4,20},{5,21},{6,22},{7,23},{8,24},{9,... | collective-permute-start | bytes 344072 | tf_op jit(solution)/shard_map/ppermute | solution.py:22
  18.4 0.9 %collective-permute-done.2.refs_3_ = bf16[16,3712]{1,0:T(8,128)(2,1)S(1)} collective-permute-done((bf16[16,3712]{1,0:T(8,128)(2,1)S(1)}, bf16[16,3712]{1,0:T(8,128)(2,1)S(1)}, u32[]{:S(2)}, u32[]{:S(2)}) %collective-permute-start.2) | collective-permute-done | bytes 118816 | tf_op jit(solution)/shard_map/ppermute | solution.py:22
  19.2 1.0 %shard_map.87 = (bf16[40,3584]{1,0:T(8,128)(2,1)S(1)}, bf16[40,3584]{1,0:T(8,128)(2,1)S(1)}, bf16[40,3584]{1,0:T(8,128)(2,1)S(1)}, bf16[40,3584]{1,0:T(8,128)(2,...) custom-call(s32[1]{0:T(128)} %bitcast.chip, bf16[16,3712]{1,0:T(8,128)(2,1)S(1)} %shard_map.86.refs_0_, ...), custom_call_target="tpu_custom_call" | custom-call | flops 117440512 | bytes 1753092 | tf_op jit(solution)/shard_map/pallas_call | solution.py:48
  20.3 1.6 %collective-permute-start.5 = (bf16[40,3584]{1,0:T(8,128)(2,1)S(1)}, bf16[40,3584]{1,0:T(8,128)(2,1)S(1)}, u32[]{:S(2)}, u32[]{:S(2)}) collective-permute-start(bf16[40,3584]{1,0:T(8,128)(2,1)S(1)} %get-tuple-element.42), channel_id=1, source_target_pairs={{0,2},{1,3},{2,0},{3,1},{4,6},{5,7},{6,4},{7,5},{8,10},{9,11},{10,... | collective-permute-start | bytes 860168 | tf_op jit(solution)/shard_map/ppermute | solution.py:22
  21.8 1.5 %collective-permute-start.6 = (bf16[40,3584]{1,0:T(8,128)(2,1)S(1)}, bf16[40,3584]{1,0:T(8,128)(2,1)S(1)}, u32[]{:S(2)}, u32[]{:S(2)}) collective-permute-start(bf16[40,3584]{1,0:T(8,128)(2,1)S(1)} %get-tuple-element.44), channel_id=1, source_target_pairs={{0,4},{1,5},{2,6},{3,7},{4,0},{5,1},{6,2},{7,3},{8,12},{9,13},{10,... | collective-permute-start | bytes 860168 | tf_op jit(solution)/shard_map/ppermute | solution.py:22
  23.4 0.7 collective-permute-done.7.refs_2_
  24.1 2.4 %collective-permute-start.8 = (bf16[40,3584]{1,0:T(8,128)(2,1)S(1)}, bf16[40,3584]{1,0:T(8,128)(2,1)S(1)}, u32[]{:S(2)}, u32[]{:S(2)}) collective-permute-start(bf16[40,3584]{1,0:T(8,128)(2,1)S(1)} %get-tuple-element.48), channel_id=1, source_target_pairs={{0,6},{1,7},{2,4},{3,5},{4,2},{5,3},{6,0},{7,1},{8,14},{9,15},{10,... | collective-permute-start | bytes 860168 | tf_op jit(solution)/shard_map/ppermute | solution.py:22
  26.6 0.3 collective-permute-start.16
  26.8 1.8 %collective-permute-start.17 = (bf16[16,3584]{1,0:T(8,128)(2,1)S(1)}, bf16[16,3584]{1,0:T(8,128)(2,1)S(1)}, u32[]{:S(2)}, u32[]{:S(2)}) collective-permute-start(bf16[16,3584]{1,0:T(8,128)(2,1)S(1)} %collective-permute-done.7.refs_2_), channel_id=1, source_target_pairs={{0,8},{1,9},{2,10},{3,11},{4,12},{5,13},{6,14},{7,15},{8,0},{9,1},... | collective-permute-start | bytes 344072 | tf_op jit(solution)/shard_map/ppermute | solution.py:22
  28.6 3.0 %collective-permute-done.16.refs_1_ = bf16[16,3584]{1,0:T(8,128)(2,1)S(1)} collective-permute-done((bf16[16,3584]{1,0:T(8,128)(2,1)}, bf16[16,3584]{1,0:T(8,128)(2,1)S(1)}, u32[]{:S(2)}, u32[]{:S(2)}) %collective-permute-start.16) | collective-permute-done | bytes 114720 | tf_op jit(solution)/shard_map/ppermute | solution.py:22
  31.6 1.2 %collective-permute-done.17.refs_3_ = bf16[16,3584]{1,0:T(8,128)(2,1)S(1)} collective-permute-done((bf16[16,3584]{1,0:T(8,128)(2,1)S(1)}, bf16[16,3584]{1,0:T(8,128)(2,1)S(1)}, u32[]{:S(2)}, u32[]{:S(2)}) %collective-permute-start.17) | collective-permute-done | bytes 114720 | tf_op jit(solution)/shard_map/ppermute | solution.py:22
  32.8 0.9 %copy-done = bf16[16,3584]{1,0:T(8,128)(2,1)S(1)} copy-done((bf16[16,3584]{1,0:T(8,128)(2,1)S(1)}, bf16[16,3584]{1,0:T(8,128)(2,1)}, u32[]{:S(2)}) %copy-start) | copy-done | bytes 114712
  33.7 0.6 shard_map.91
  34.3 0.6 collective-permute-start.18
  34.9 0.5 collective-permute-start.19
  35.4 2.4 %collective-permute-start.20 = (bf16[40,3584]{1,0:T(8,128)(2,1)S(1)}, bf16[40,3584]{1,0:T(8,128)(2,1)S(1)}, u32[]{:S(2)}, u32[]{:S(2)}) collective-permute-start(bf16[40,3584]{1,0:T(8,128)(2,1)S(1)} %get-tuple-element.63), channel_id=1, source_target_pairs={{0,6},{1,7},{2,4},{3,5},{4,2},{5,3},{6,0},{7,1},{8,14},{9,15},{10,... | collective-permute-start | bytes 860168 | tf_op jit(solution)/shard_map/ppermute | solution.py:22
  37.9 8.2 %shard_map.88 = (bf16[40,3584]{1,0:T(8,128)(2,1)S(1)}, bf16[40,3584]{1,0:T(8,128)(2,1)S(1)}, bf16[40,3584]{1,0:T(8,128)(2,1)S(1)}, bf16[40,3584]{1,0:T(8,128)(2,...) custom-call(bf16[40,3584]{1,0:T(8,128)(2,1)S(1)} %get-tuple-element.40.x0, ...), custom_call_target="tpu_custom_call" | custom-call | flops 3523215360 | bytes 25624576 | tf_op jit(solution)/shard_map/pallas_call | solution.py:48
  46.1 0.6 collective-permute-start.10
  46.7 0.5 collective-permute-start.11
  47.2 2.4 %collective-permute-start.12 = (bf16[40,3584]{1,0:T(8,128)(2,1)S(1)}, bf16[40,3584]{1,0:T(8,128)(2,1)S(1)}, u32[]{:S(2)}, u32[]{:S(2)}) collective-permute-start(bf16[40,3584]{1,0:T(8,128)(2,1)S(1)} %get-tuple-element.52), channel_id=1, source_target_pairs={{0,6},{1,7},{2,4},{3,5},{4,2},{5,3},{6,0},{7,1},{8,14},{9,15},{10,... | collective-permute-start | bytes 860168 | tf_op jit(solution)/shard_map/ppermute | solution.py:22
  49.7 10.8 %shard_map.92 = (bf16[40,3584]{1,0:T(8,128)(2,1)S(1)}, bf16[40,3584]{1,0:T(8,128)(2,1)S(1)}, bf16[40,3584]{1,0:T(8,128)(2,1)S(1)}, bf16[40,3584]{1,0:T(8,128)(2,1)S(1)}) custom-call(bf16[40,3584]{1,0:T(8,128)(2,1)S(1)} %get-tuple-element.60.x0, bf16[40,3584]{1,0:T(8,128)(2,1)S(1)} %collective-permute-done.18.x1, ...), custom_call_target="tpu_custom_call" | custom-call | flops 3523215360 | bytes 25624576 | tf_op jit(solution)/shard_map/pallas_call | solution.py:48
  60.5 1.2 %collective-permute-start.21 = (bf16[40,3584]{1,0:T(8,128)(2,1)S(1)}, bf16[40,3584]{1,0:T(8,128)(2,1)S(1)}, u32[]{:S(2)}, u32[]{:S(2)}) collective-permute-start(bf16[40,3584]{1,0:T(8,128)(2,1)S(1)} %get-tuple-element.67), channel_id=1, source_target_pairs={{0,2},{1,3},{2,0},{3,1},{4,6},{5,7},{6,4},{7,5},{8,10},{9,11},{10,... | collective-permute-start | bytes 860168 | tf_op jit(solution)/shard_map/ppermute | solution.py:22
  61.7 0.6 collective-permute-start.22
  62.3 1.8 %collective-permute-start.23 = (bf16[40,3584]{1,0:T(8,128)(2,1)S(1)}, bf16[40,3584]{1,0:T(8,128)(2,1)S(1)}, u32[]{:S(2)}, u32[]{:S(2)}) collective-permute-start(bf16[40,3584]{1,0:T(8,128)(2,1)S(1)} %get-tuple-element.69), channel_id=1, source_target_pairs={{0,6},{1,7},{2,4},{3,5},{4,2},{5,3},{6,0},{7,1},{8,14},{9,15},{10,... | collective-permute-start | bytes 860168 | tf_op jit(solution)/shard_map/ppermute | solution.py:22
  64.1 0.6 shard_map.89
  64.7 1.0 %collective-permute-start.13 = (bf16[16,3584]{1,0:T(8,128)(2,1)S(1)}, bf16[16,3584]{1,0:T(8,128)(2,1)S(1)}, u32[]{:S(2)}, u32[]{:S(2)}) collective-permute-start(bf16[16,3584]{1,0:T(8,128)(2,1)S(1)} %get-tuple-element.54), channel_id=1, source_target_pairs={{0,8},{1,9},{2,10},{3,11},{4,12},{5,13},{6,14},{7,15},{8,0},{9,1},... | collective-permute-start | bytes 344072 | tf_op jit(solution)/shard_map/ppermute | solution.py:22
  65.7 4.5 %collective-permute-start.14 = (bf16[16,3584]{1,0:T(8,128)(2,1)S(1)}, bf16[16,3584]{1,0:T(8,128)(2,1)S(1)}, u32[]{:S(2)}, u32[]{:S(2)}) collective-permute-start(bf16[16,3584]{1,0:T(8,128)(2,1)S(1)} %get-tuple-element.55), channel_id=1, source_target_pairs={{0,16},{1,17},{2,18},{3,19},{4,20},{5,21},{6,22},{7,23},{8,24},{9,... | collective-permute-start | bytes 344072 | tf_op jit(solution)/shard_map/ppermute | solution.py:22
  70.2 3.6 %collective-permute-start.15 = (bf16[16,3584]{1,0:T(8,128)(2,1)S(1)}, bf16[16,3584]{1,0:T(8,128)(2,1)S(1)}, u32[]{:S(2)}, u32[]{:S(2)}) collective-permute-start(bf16[16,3584]{1,0:T(8,128)(2,1)S(1)} %get-tuple-element.56), channel_id=1, source_target_pairs={{0,24},{1,25},{2,26},{3,27},{4,28},{5,29},{6,30},{7,31},{8,16},{9,... | collective-permute-start | bytes 344072 | tf_op jit(solution)/shard_map/ppermute | solution.py:22
  73.9 0.3 shard_map.93
  74.2 0.4 collective-permute-start.24
  74.5 4.4 %collective-permute-start.25 = (bf16[16,3584]{1,0:T(8,128)(2,1)S(1)}, bf16[16,3584]{1,0:T(8,128)(2,1)S(1)}, u32[]{:S(2)}, u32[]{:S(2)}) collective-permute-start(bf16[16,3584]{1,0:T(8,128)(2,1)S(1)} %get-tuple-element.72), channel_id=1, source_target_pairs={{0,16},{1,17},{2,18},{3,19},{4,20},{5,21},{6,22},{7,23},{8,24},{9,... | collective-permute-start | bytes 344072 | tf_op jit(solution)/shard_map/ppermute | solution.py:22
  79.0 0.7 shard_map.90
  79.7 1.8 %collective-permute-done.24.refs_1_ = bf16[16,3584]{1,0:T(8,128)(2,1)S(1)} collective-permute-done((bf16[16,3584]{1,0:T(8,128)(2,1)S(1)}, bf16[16,3584]{1,0:T(8,128)(2,1)S(1)}, u32[]{:S(2)}, u32[]{:S(2)}) %collective-permute-start.24) | collective-permute-done | bytes 114720 | tf_op jit(solution)/shard_map/ppermute | solution.py:22
  81.5 2.6 %collective-permute-done.25.refs_2_ = bf16[16,3584]{1,0:T(8,128)(2,1)S(1)} collective-permute-done((bf16[16,3584]{1,0:T(8,128)(2,1)S(1)}, bf16[16,3584]{1,0:T(8,128)(2,1)S(1)}, u32[]{:S(2)}, u32[]{:S(2)}) %collective-permute-start.25) | collective-permute-done | bytes 114720 | tf_op jit(solution)/shard_map/ppermute | solution.py:22
  84.0 1.6 %collective-permute-done.26.refs_3_ = bf16[16,3584]{1,0:T(8,128)(2,1)S(1)} collective-permute-done((bf16[16,3584]{1,0:T(8,128)(2,1)S(1)}, bf16[16,3584]{1,0:T(8,128)(2,1)S(1)}, u32[]{:S(2)}, u32[]{:S(2)}) %collective-permute-start.26) | collective-permute-done | bytes 114720 | tf_op jit(solution)/shard_map/ppermute | solution.py:22
  85.6 0.7 shard_map.94
  (23 shorter events, 0.1 us)
Async XLA Ops:
  0.6 14.4 %collective-permute-start.3 = (bf16[1,3584,512]{2,1,0:T(8,128)(2,1)}, bf16[1,3584,512]{2,1,0:T(8,128)(2,1)}, u32[]{:S(2)}, u32[]{:S(2)}) collective-permute-start(bf16[1,3584,512]{2,1,0:T(8,128)(2,1)} %refs_0_.5), channel_id=1, source_target_pairs={{0,1},{1,0},{2,3},{3,2},{4,5},{5,4},{6,7},{7,6},{8,9},{9,8},{10,11... | collective-permute-start | bytes 11010056 | tf_op jit(solution)/shard_map/ppermute | solution.py:22
  1.1 19.1 %collective-permute-start.4 = (bf16[1,3584,512]{2,1,0:T(8,128)(2,1)}, bf16[1,3584,512]{2,1,0:T(8,128)(2,1)}, u32[]{:S(2)}, u32[]{:S(2)}) collective-permute-start(bf16[1,3584,512]{2,1,0:T(8,128)(2,1)} %refs_1_.3), channel_id=1, source_target_pairs={{0,1},{1,0},{2,3},{3,2},{4,5},{5,4},{6,7},{7,6},{8,9},{9,8},{10,11... | collective-permute-start | bytes 11010056 | tf_op jit(solution)/shard_map/ppermute | solution.py:22
  1.2 25.3 %collective-permute-start.9 = (bf16[1,512,3584]{2,1,0:T(8,128)(2,1)}, bf16[1,512,3584]{2,1,0:T(8,128)(2,1)}, u32[]{:S(2)}, u32[]{:S(2)}) collective-permute-start(bf16[1,512,3584]{2,1,0:T(8,128)(2,1)} %refs_2_.3), channel_id=1, source_target_pairs={{0,1},{1,0},{2,3},{3,2},{4,5},{5,4},{6,7},{7,6},{8,9},{9,8},{10,11... | collective-permute-start | bytes 11010056 | tf_op jit(solution)/shard_map/ppermute | solution.py:22
  1.7 0.9 %copy-start.1 = (bf16[16,3584]{1,0:T(8,128)(2,1)S(1)}, bf16[16,3584]{1,0:T(8,128)(2,1)}, u32[]{:S(2)}) copy-start(bf16[16,3584]{1,0:T(8,128)(2,1)} %tokens.1) | copy-start | bytes 344068
  2.6 0.7 copy-start.2
  3.2 0.7 copy-start.3
  4.1 10.2 %collective-permute-start.1 = (bf16[16,3712]{1,0:T(8,128)(2,1)S(1)}, bf16[16,3712]{1,0:T(8,128)(2,1)S(1)}, u32[]{:S(2)}, u32[]{:S(2)}) collective-permute-start(bf16[16,3712]{1,0:T(8,128)(2,1)S(1)} %shard_map.86.refs_0_), channel_id=1, source_target_pairs={{0,16},{1,17},{2,18},{3,19},{4,20},{5,21},{6,22},{7,23},{8,24},{9,... | collective-permute-start | bytes 356360 | tf_op jit(solution)/shard_map/ppermute | solution.py:22
  7.9 10.5 %collective-permute-start = (bf16[16,3712]{1,0:T(8,128)(2,1)S(1)}, bf16[16,3712]{1,0:T(8,128)(2,1)S(1)}, u32[]{:S(2)}, u32[]{:S(2)}) collective-permute-start(bf16[16,3712]{1,0:T(8,128)(2,1)S(1)} %shard_map.86.refs_0_), channel_id=1, source_target_pairs={{0,8},{1,9},{2,10},{3,11},{4,12},{5,13},{6,14},{7,15},{8,0},{9,1},... | collective-permute-start | bytes 356360 | tf_op jit(solution)/shard_map/ppermute | solution.py:22
  14.3 4.9 %collective-permute-start.2 = (bf16[16,3712]{1,0:T(8,128)(2,1)S(1)}, bf16[16,3712]{1,0:T(8,128)(2,1)S(1)}, u32[]{:S(2)}, u32[]{:S(2)}) collective-permute-start(bf16[16,3712]{1,0:T(8,128)(2,1)S(1)} %collective-permute-done.1.refs_2_), channel_id=1, source_target_pairs={{0,8},{1,9},{2,10},{3,11},{4,12},{5,13},{6,14},{7,15},{8,0},{9,1},... | collective-permute-start | bytes 356360 | tf_op jit(solution)/shard_map/ppermute | solution.py:22
  15.0 9.1 %collective-permute-start.7 = (bf16[16,3584]{1,0:T(8,128)(2,1)}, bf16[16,3584]{1,0:T(8,128)(2,1)S(1)}, u32[]{:S(2)}, u32[]{:S(2)}) collective-permute-start(bf16[16,3584]{1,0:T(8,128)(2,1)} %refs_0_.4), channel_id=1, source_target_pairs={{0,16},{1,17},{2,18},{3,19},{4,20},{5,21},{6,22},{7,23},{8,24},{9,... | collective-permute-start | bytes 344072 | tf_op jit(solution)/shard_map/ppermute | solution.py:22
  20.3 15.1 %collective-permute-start.5 = (bf16[40,3584]{1,0:T(8,128)(2,1)S(1)}, bf16[40,3584]{1,0:T(8,128)(2,1)S(1)}, u32[]{:S(2)}, u32[]{:S(2)}) collective-permute-start(bf16[40,3584]{1,0:T(8,128)(2,1)S(1)} %get-tuple-element.42), channel_id=1, source_target_pairs={{0,2},{1,3},{2,0},{3,1},{4,6},{5,7},{6,4},{7,5},{8,10},{9,11},{10,... | collective-permute-start | bytes 860168 | tf_op jit(solution)/shard_map/ppermute | solution.py:22
  21.8 16.0 %collective-permute-start.6 = (bf16[40,3584]{1,0:T(8,128)(2,1)S(1)}, bf16[40,3584]{1,0:T(8,128)(2,1)S(1)}, u32[]{:S(2)}, u32[]{:S(2)}) collective-permute-start(bf16[40,3584]{1,0:T(8,128)(2,1)S(1)} %get-tuple-element.44), channel_id=1, source_target_pairs={{0,4},{1,5},{2,6},{3,7},{4,0},{5,1},{6,2},{7,3},{8,12},{9,13},{10,... | collective-permute-start | bytes 860168 | tf_op jit(solution)/shard_map/ppermute | solution.py:22
  24.1 13.8 %collective-permute-start.8 = (bf16[40,3584]{1,0:T(8,128)(2,1)S(1)}, bf16[40,3584]{1,0:T(8,128)(2,1)S(1)}, u32[]{:S(2)}, u32[]{:S(2)}) collective-permute-start(bf16[40,3584]{1,0:T(8,128)(2,1)S(1)} %get-tuple-element.48), channel_id=1, source_target_pairs={{0,6},{1,7},{2,4},{3,5},{4,2},{5,3},{6,0},{7,1},{8,14},{9,15},{10,... | collective-permute-start | bytes 860168 | tf_op jit(solution)/shard_map/ppermute | solution.py:22
  26.6 5.0 %collective-permute-start.16 = (bf16[16,3584]{1,0:T(8,128)(2,1)}, bf16[16,3584]{1,0:T(8,128)(2,1)S(1)}, u32[]{:S(2)}, u32[]{:S(2)}) collective-permute-start(bf16[16,3584]{1,0:T(8,128)(2,1)} %refs_0_.4), channel_id=1, source_target_pairs={{0,8},{1,9},{2,10},{3,11},{4,12},{5,13},{6,14},{7,15},{8,0},{9,1},... | collective-permute-start | bytes 344072 | tf_op jit(solution)/shard_map/ppermute | solution.py:22
  26.8 6.0 %collective-permute-start.17 = (bf16[16,3584]{1,0:T(8,128)(2,1)S(1)}, bf16[16,3584]{1,0:T(8,128)(2,1)S(1)}, u32[]{:S(2)}, u32[]{:S(2)}) collective-permute-start(bf16[16,3584]{1,0:T(8,128)(2,1)S(1)} %collective-permute-done.7.refs_2_), channel_id=1, source_target_pairs={{0,8},{1,9},{2,10},{3,11},{4,12},{5,13},{6,14},{7,15},{8,0},{9,1},... | collective-permute-start | bytes 344072 | tf_op jit(solution)/shard_map/ppermute | solution.py:22
  32.8 0.9 %copy-start = (bf16[16,3584]{1,0:T(8,128)(2,1)S(1)}, bf16[16,3584]{1,0:T(8,128)(2,1)}, u32[]{:S(2)}) copy-start(bf16[16,3584]{1,0:T(8,128)(2,1)} %refs_0_.4) | copy-start | bytes 344068
  34.3 12.9 %collective-permute-start.18 = (bf16[40,3584]{1,0:T(8,128)(2,1)S(1)}, bf16[40,3584]{1,0:T(8,128)(2,1)S(1)}, u32[]{:S(2)}, u32[]{:S(2)}) collective-permute-start(bf16[40,3584]{1,0:T(8,128)(2,1)S(1)} %get-tuple-element.61), channel_id=1, source_target_pairs={{0,2},{1,3},{2,0},{3,1},{4,6},{5,7},{6,4},{7,5},{8,10},{9,11},{10,... | collective-permute-start | bytes 860168 | tf_op jit(solution)/shard_map/ppermute | solution.py:22
  34.9 14.8 %collective-permute-start.19 = (bf16[40,3584]{1,0:T(8,128)(2,1)S(1)}, bf16[40,3584]{1,0:T(8,128)(2,1)S(1)}, u32[]{:S(2)}, u32[]{:S(2)}) collective-permute-start(bf16[40,3584]{1,0:T(8,128)(2,1)S(1)} %get-tuple-element.62), channel_id=1, source_target_pairs={{0,4},{1,5},{2,6},{3,7},{4,0},{5,1},{6,2},{7,3},{8,12},{9,13},{10,... | collective-permute-start | bytes 860168 | tf_op jit(solution)/shard_map/ppermute | solution.py:22
  35.4 14.2 %collective-permute-start.20 = (bf16[40,3584]{1,0:T(8,128)(2,1)S(1)}, bf16[40,3584]{1,0:T(8,128)(2,1)S(1)}, u32[]{:S(2)}, u32[]{:S(2)}) collective-permute-start(bf16[40,3584]{1,0:T(8,128)(2,1)S(1)} %get-tuple-element.63), channel_id=1, source_target_pairs={{0,6},{1,7},{2,4},{3,5},{4,2},{5,3},{6,0},{7,1},{8,14},{9,15},{10,... | collective-permute-start | bytes 860168 | tf_op jit(solution)/shard_map/ppermute | solution.py:22
  46.1 16.2 %collective-permute-start.10 = (bf16[40,3584]{1,0:T(8,128)(2,1)S(1)}, bf16[40,3584]{1,0:T(8,128)(2,1)S(1)}, u32[]{:S(2)}, u32[]{:S(2)}) collective-permute-start(bf16[40,3584]{1,0:T(8,128)(2,1)S(1)} %get-tuple-element.50), channel_id=1, source_target_pairs={{0,2},{1,3},{2,0},{3,1},{4,6},{5,7},{6,4},{7,5},{8,10},{9,11},{10,... | collective-permute-start | bytes 860168 | tf_op jit(solution)/shard_map/ppermute | solution.py:22
  46.7 17.4 %collective-permute-start.11 = (bf16[40,3584]{1,0:T(8,128)(2,1)S(1)}, bf16[40,3584]{1,0:T(8,128)(2,1)S(1)}, u32[]{:S(2)}, u32[]{:S(2)}) collective-permute-start(bf16[40,3584]{1,0:T(8,128)(2,1)S(1)} %get-tuple-element.51), channel_id=1, source_target_pairs={{0,4},{1,5},{2,6},{3,7},{4,0},{5,1},{6,2},{7,3},{8,12},{9,13},{10,... | collective-permute-start | bytes 860168 | tf_op jit(solution)/shard_map/ppermute | solution.py:22
  47.2 16.8 %collective-permute-start.12 = (bf16[40,3584]{1,0:T(8,128)(2,1)S(1)}, bf16[40,3584]{1,0:T(8,128)(2,1)S(1)}, u32[]{:S(2)}, u32[]{:S(2)}) collective-permute-start(bf16[40,3584]{1,0:T(8,128)(2,1)S(1)} %get-tuple-element.52), channel_id=1, source_target_pairs={{0,6},{1,7},{2,4},{3,5},{4,2},{5,3},{6,0},{7,1},{8,14},{9,15},{10,... | collective-permute-start | bytes 860168 | tf_op jit(solution)/shard_map/ppermute | solution.py:22
  60.5 9.7 %collective-permute-start.21 = (bf16[40,3584]{1,0:T(8,128)(2,1)S(1)}, bf16[40,3584]{1,0:T(8,128)(2,1)S(1)}, u32[]{:S(2)}, u32[]{:S(2)}) collective-permute-start(bf16[40,3584]{1,0:T(8,128)(2,1)S(1)} %get-tuple-element.67), channel_id=1, source_target_pairs={{0,2},{1,3},{2,0},{3,1},{4,6},{5,7},{6,4},{7,5},{8,10},{9,11},{10,... | collective-permute-start | bytes 860168 | tf_op jit(solution)/shard_map/ppermute | solution.py:22
  61.7 12.1 %collective-permute-start.22 = (bf16[40,3584]{1,0:T(8,128)(2,1)S(1)}, bf16[40,3584]{1,0:T(8,128)(2,1)S(1)}, u32[]{:S(2)}, u32[]{:S(2)}) collective-permute-start(bf16[40,3584]{1,0:T(8,128)(2,1)S(1)} %get-tuple-element.68), channel_id=1, source_target_pairs={{0,4},{1,5},{2,6},{3,7},{4,0},{5,1},{6,2},{7,3},{8,12},{9,13},{10,... | collective-permute-start | bytes 860168 | tf_op jit(solution)/shard_map/ppermute | solution.py:22
  62.3 11.6 %collective-permute-start.23 = (bf16[40,3584]{1,0:T(8,128)(2,1)S(1)}, bf16[40,3584]{1,0:T(8,128)(2,1)S(1)}, u32[]{:S(2)}, u32[]{:S(2)}) collective-permute-start(bf16[40,3584]{1,0:T(8,128)(2,1)S(1)} %get-tuple-element.69), channel_id=1, source_target_pairs={{0,6},{1,7},{2,4},{3,5},{4,2},{5,3},{6,0},{7,1},{8,14},{9,15},{10,... | collective-permute-start | bytes 860168 | tf_op jit(solution)/shard_map/ppermute | solution.py:22
  64.7 14.3 %collective-permute-start.13 = (bf16[16,3584]{1,0:T(8,128)(2,1)S(1)}, bf16[16,3584]{1,0:T(8,128)(2,1)S(1)}, u32[]{:S(2)}, u32[]{:S(2)}) collective-permute-start(bf16[16,3584]{1,0:T(8,128)(2,1)S(1)} %get-tuple-element.54), channel_id=1, source_target_pairs={{0,8},{1,9},{2,10},{3,11},{4,12},{5,13},{6,14},{7,15},{8,0},{9,1},... | collective-permute-start | bytes 344072 | tf_op jit(solution)/shard_map/ppermute | solution.py:22
  65.7 13.3 %collective-permute-start.14 = (bf16[16,3584]{1,0:T(8,128)(2,1)S(1)}, bf16[16,3584]{1,0:T(8,128)(2,1)S(1)}, u32[]{:S(2)}, u32[]{:S(2)}) collective-permute-start(bf16[16,3584]{1,0:T(8,128)(2,1)S(1)} %get-tuple-element.55), channel_id=1, source_target_pairs={{0,16},{1,17},{2,18},{3,19},{4,20},{5,21},{6,22},{7,23},{8,24},{9,... | collective-permute-start | bytes 344072 | tf_op jit(solution)/shard_map/ppermute | solution.py:22
  70.2 8.7 %collective-permute-start.15 = (bf16[16,3584]{1,0:T(8,128)(2,1)S(1)}, bf16[16,3584]{1,0:T(8,128)(2,1)S(1)}, u32[]{:S(2)}, u32[]{:S(2)}) collective-permute-start(bf16[16,3584]{1,0:T(8,128)(2,1)S(1)} %get-tuple-element.56), channel_id=1, source_target_pairs={{0,24},{1,25},{2,26},{3,27},{4,28},{5,29},{6,30},{7,31},{8,16},{9,... | collective-permute-start | bytes 344072 | tf_op jit(solution)/shard_map/ppermute | solution.py:22
  74.2 7.3 %collective-permute-start.24 = (bf16[16,3584]{1,0:T(8,128)(2,1)S(1)}, bf16[16,3584]{1,0:T(8,128)(2,1)S(1)}, u32[]{:S(2)}, u32[]{:S(2)}) collective-permute-start(bf16[16,3584]{1,0:T(8,128)(2,1)S(1)} %get-tuple-element.71), channel_id=1, source_target_pairs={{0,8},{1,9},{2,10},{3,11},{4,12},{5,13},{6,14},{7,15},{8,0},{9,1},... | collective-permute-start | bytes 344072 | tf_op jit(solution)/shard_map/ppermute | solution.py:22
  74.5 9.5 %collective-permute-start.25 = (bf16[16,3584]{1,0:T(8,128)(2,1)S(1)}, bf16[16,3584]{1,0:T(8,128)(2,1)S(1)}, u32[]{:S(2)}, u32[]{:S(2)}) collective-permute-start(bf16[16,3584]{1,0:T(8,128)(2,1)S(1)} %get-tuple-element.72), channel_id=1, source_target_pairs={{0,16},{1,17},{2,18},{3,19},{4,20},{5,21},{6,22},{7,23},{8,24},{9,... | collective-permute-start | bytes 344072 | tf_op jit(solution)/shard_map/ppermute | solution.py:22
  78.9 6.7 %collective-permute-start.26 = (bf16[16,3584]{1,0:T(8,128)(2,1)S(1)}, bf16[16,3584]{1,0:T(8,128)(2,1)S(1)}, u32[]{:S(2)}, u32[]{:S(2)}) collective-permute-start(bf16[16,3584]{1,0:T(8,128)(2,1)S(1)} %get-tuple-element.73), channel_id=1, source_target_pairs={{0,24},{1,25},{2,26},{3,27},{4,28},{5,29},{6,30},{7,31},{8,16},{9,... | collective-permute-start | bytes 344072 | tf_op jit(solution)/shard_map/ppermute | solution.py:22

commit v16 on v10

--- a/solution.py
+++ b/solution.py
@@ -57,10 +57,8 @@
 
 
 def streams(triples):
-    copies = [pltpu.make_async_copy(*triple) for triple in triples]
-    for copy in copies:
-        copy.start()
-    return copies
+    for triple in triples:
+        pltpu.make_async_copy(*triple).start()
 
 
 def await_place(place, sem):
@@ -182,7 +180,7 @@
     rows, width = x.shape
     units = back.shape[0] // 2
     chunk, tiles, chunks = back_chunk(width), 2 * units // tile, width // back_chunk(width)
-    triples = []
+    triples, later = [], []
     for number in range(tiles):
         slab, at = divmod(number * tile, units)
         for half, source in enumerate(slabs[3 * slab : 3 * slab + 2]):
@@ -193,15 +191,21 @@
         for slab in range(2):
             place = back.at[pl.ds(slab * units, units), columns]
             source = slabs[3 * slab + 2].at[0, :, columns]
-            triples.append((source, place, sems.at[tiles + number]))
-    streams(triples)
+            later.append((source, place, sems.at[tiles + number]))
+    streams(triples[:2])
     for part in column_chunks(width):
         x[:, part] = joined((x0, x1, x2, x3), part, rows)
+    streams(triples[2:])
 
     @pl.loop(0, tiles)
     def _(number):
         columns = pl.ds(pl.multiple_of(number * 2 * tile, 2 * tile), 2 * tile)
         await_place(into.at[:, columns], sems.at[number])
+
+        @pl.when(number == 0)
+        def _():
+            streams(later)
+
         pre = jnp.dot(x[...], into[:, columns], preferred_element_type=f32)
         pre_gate, pre_up = pre[:, :tile], pre[:, tile:]
         sigma = jax.nn.sigmoid(pre_gate)
@@ -230,7 +234,7 @@
     rows, width = x.shape
     units = back.shape[0] // 2
     chunk, chunks = back_chunk(width), width // back_chunk(width)
-    triples = []
+    triples, later = [], []
     for slab in range(2):
         place = back.at[pl.ds(slab * units, units)]
         triples.append((slabs[3 * slab + 2].at[0], place, sems.at[slab]))
@@ -238,7 +242,7 @@
         lines = pl.ds(number * chunk, chunk)
         for column, matrix in enumerate((0, 1, 3, 4)):
             place = into.at[lines, pl.ds(column * units, units)]
-            triples.append((slabs[matrix].at[0, lines], place, sems.at[2 + number]))
+            later.append((slabs[matrix].at[0, lines], place, sems.at[2 + number]))
     streams(triples)
     for part in column_chunks(width):
         x[:, part] = joined((x0, x1, x2, x3), part, rows)
@@ -247,6 +251,9 @@
     def _(slab):
         at = pl.ds(pl.multiple_of(slab * units, units), units)
         await_place(back.at[at], sems.at[slab])
+        half = len(later) // 2 // 4 * 4 or len(later)
+        pl.when(slab == 0)(functools.partial(streams, later[:half]))
+        pl.when(slab == 1)(functools.partial(streams, later[half:]))
         hidden_grad = lax.dot_general(x[...], back[at], CONTRACT_COLS, preferred_element_type=f32)
         start = pl.multiple_of(2 * slab * units, 2 * units)
         gate_at, up_at = pl.ds(start, units), pl.ds(start + units, units)

time: 86.4 us -> 86.5 us (level)
  no operation moved by 1% of the time
where the time goes in v16:
time: 86.5 us; the launch traced here: 86.3 us
  starting transfers between devices  42.5 us (49%)
  Pallas kernels  23.1 us (27%)
  waiting for transfers between devices  16.7 us (19%)
  local copies, waits for them, and re-layouts  3.17 us (4%)
    ppermute x27, starting transfers between devices, swap(): lax.ppermute(value, 'expert', [(i, i ^ offset) for i in range(devices)])  42.5 us
    pallas_call x9, Pallas kernels, call(): pl.pallas_call(body, out_shape=outs, in_specs=[whole] * len(args) if in_s...  23.1 us
    ppermute x27, waiting for transfers between devices, swap(): lax.ppermute(value, 'expert', [(i, i ^ offset) for i in range(devices)])  16.7 us
    unnamed x8, local copies, waits for them, and re-layouts  3.17 us
  transfers between devices with their start and end apart: 27, of which 8 were waited for; matrix products, arithmetic and copies ran while one was open for 0% of the time, Pallas kernels for 26%

profile of v16, /device:TPU:0, one launch (start us, length us, event | category | flops | bytes accessed | tf_op | source)
XLA Modules:
  0.0 86.3 jit_solution(7715968963044164652)
XLA Ops:
  0.6 0.5 collective-permute-start.3
  1.1 0.1 collective-permute-start.4
  1.2 0.4 collective-permute-start.9
  1.7 0.9 %copy-done.1 = bf16[16,3584]{1,0:T(8,128)(2,1)S(1)} copy-done((bf16[16,3584]{1,0:T(8,128)(2,1)S(1)}, bf16[16,3584]{1,0:T(8,128)(2,1)}, u32[]{:S(2)}) %copy-start.1) | copy-done | bytes 114712
  2.6 0.7 copy-done.2
  3.2 0.7 copy-done.3
  3.9 0.2 shard_map.86.refs_0_
  4.1 3.7 %collective-permute-start.1 = (bf16[16,3712]{1,0:T(8,128)(2,1)S(1)}, bf16[16,3712]{1,0:T(8,128)(2,1)S(1)}, u32[]{:S(2)}, u32[]{:S(2)}) collective-permute-start(bf16[16,3712]{1,0:T(8,128)(2,1)S(1)} %shard_map.86.refs_0_), channel_id=1, source_target_pairs={{0,16},{1,17},{2,18},{3,19},{4,20},{5,21},{6,22},{7,23},{8,24},{9,... | collective-permute-start | bytes 356360 | tf_op jit(solution)/shard_map/ppermute | solution.py:22
  7.9 1.6 %collective-permute-start = (bf16[16,3712]{1,0:T(8,128)(2,1)S(1)}, bf16[16,3712]{1,0:T(8,128)(2,1)S(1)}, u32[]{:S(2)}, u32[]{:S(2)}) collective-permute-start(bf16[16,3712]{1,0:T(8,128)(2,1)S(1)} %shard_map.86.refs_0_), channel_id=1, source_target_pairs={{0,8},{1,9},{2,10},{3,11},{4,12},{5,13},{6,14},{7,15},{8,0},{9,1},... | collective-permute-start | bytes 356360 | tf_op jit(solution)/shard_map/ppermute | solution.py:22
  9.4 4.9 %collective-permute-done.1.refs_2_ = bf16[16,3712]{1,0:T(8,128)(2,1)S(1)} collective-permute-done((bf16[16,3712]{1,0:T(8,128)(2,1)S(1)}, bf16[16,3712]{1,0:T(8,128)(2,1)S(1)}, u32[]{:S(2)}, u32[]{:S(2)}) %collective-permute-start.1) | collective-permute-done | bytes 118816 | tf_op jit(solution)/shard_map/ppermute | solution.py:22
  14.3 0.6 collective-permute-start.2
  15.0 3.4 %collective-permute-start.7 = (bf16[16,3584]{1,0:T(8,128)(2,1)}, bf16[16,3584]{1,0:T(8,128)(2,1)S(1)}, u32[]{:S(2)}, u32[]{:S(2)}) collective-permute-start(bf16[16,3584]{1,0:T(8,128)(2,1)} %refs_0_.4), channel_id=1, source_target_pairs={{0,16},{1,17},{2,18},{3,19},{4,20},{5,21},{6,22},{7,23},{8,24},{9,... | collective-permute-start | bytes 344072 | tf_op jit(solution)/shard_map/ppermute | solution.py:22
  18.4 0.0 collective-permute-done.refs_1_
  18.4 0.9 %collective-permute-done.2.refs_3_ = bf16[16,3712]{1,0:T(8,128)(2,1)S(1)} collective-permute-done((bf16[16,3712]{1,0:T(8,128)(2,1)S(1)}, bf16[16,3712]{1,0:T(8,128)(2,1)S(1)}, u32[]{:S(2)}, u32[]{:S(2)}) %collective-permute-start.2) | collective-permute-done | bytes 118816 | tf_op jit(solution)/shard_map/ppermute | solution.py:22
  19.2 1.0 %shard_map.87 = (bf16[40,3584]{1,0:T(8,128)(2,1)S(1)}, bf16[40,3584]{1,0:T(8,128)(2,1)S(1)}, bf16[40,3584]{1,0:T(8,128)(2,1)S(1)}, bf16[40,3584]{1,0:T(8,128)(2,...) custom-call(s32[1]{0:T(128)} %bitcast.chip, bf16[16,3712]{1,0:T(8,128)(2,1)S(1)} %shard_map.86.refs_0_, ...), custom_call_target="tpu_custom_call" | custom-call | flops 117440512 | bytes 1753092 | tf_op jit(solution)/shard_map/pallas_call | solution.py:48
  20.3 1.6 %collective-permute-start.5 = (bf16[40,3584]{1,0:T(8,128)(2,1)S(1)}, bf16[40,3584]{1,0:T(8,128)(2,1)S(1)}, u32[]{:S(2)}, u32[]{:S(2)}) collective-permute-start(bf16[40,3584]{1,0:T(8,128)(2,1)S(1)} %get-tuple-element.42), channel_id=1, source_target_pairs={{0,2},{1,3},{2,0},{3,1},{4,6},{5,7},{6,4},{7,5},{8,10},{9,11},{10,... | collective-permute-start | bytes 860168 | tf_op jit(solution)/shard_map/ppermute | solution.py:22
  21.8 1.5 %collective-permute-start.6 = (bf16[40,3584]{1,0:T(8,128)(2,1)S(1)}, bf16[40,3584]{1,0:T(8,128)(2,1)S(1)}, u32[]{:S(2)}, u32[]{:S(2)}) collective-permute-start(bf16[40,3584]{1,0:T(8,128)(2,1)S(1)} %get-tuple-element.44), channel_id=1, source_target_pairs={{0,4},{1,5},{2,6},{3,7},{4,0},{5,1},{6,2},{7,3},{8,12},{9,13},{10,... | collective-permute-start | bytes 860168 | tf_op jit(solution)/shard_map/ppermute | solution.py:22
  23.4 0.7 collective-permute-done.7.refs_2_
  24.1 2.4 %collective-permute-start.8 = (bf16[40,3584]{1,0:T(8,128)(2,1)S(1)}, bf16[40,3584]{1,0:T(8,128)(2,1)S(1)}, u32[]{:S(2)}, u32[]{:S(2)}) collective-permute-start(bf16[40,3584]{1,0:T(8,128)(2,1)S(1)} %get-tuple-element.48), channel_id=1, source_target_pairs={{0,6},{1,7},{2,4},{3,5},{4,2},{5,3},{6,0},{7,1},{8,14},{9,15},{10,... | collective-permute-start | bytes 860168 | tf_op jit(solution)/shard_map/ppermute | solution.py:22
  26.6 0.3 collective-permute-start.16
  26.8 1.8 %collective-permute-start.17 = (bf16[16,3584]{1,0:T(8,128)(2,1)S(1)}, bf16[16,3584]{1,0:T(8,128)(2,1)S(1)}, u32[]{:S(2)}, u32[]{:S(2)}) collective-permute-start(bf16[16,3584]{1,0:T(8,128)(2,1)S(1)} %collective-permute-done.7.refs_2_), channel_id=1, source_target_pairs={{0,8},{1,9},{2,10},{3,11},{4,12},{5,13},{6,14},{7,15},{8,0},{9,1},... | collective-permute-start | bytes 344072 | tf_op jit(solution)/shard_map/ppermute | solution.py:22
  28.6 3.0 %collective-permute-done.16.refs_1_ = bf16[16,3584]{1,0:T(8,128)(2,1)S(1)} collective-permute-done((bf16[16,3584]{1,0:T(8,128)(2,1)}, bf16[16,3584]{1,0:T(8,128)(2,1)S(1)}, u32[]{:S(2)}, u32[]{:S(2)}) %collective-permute-start.16) | collective-permute-done | bytes 114720 | tf_op jit(solution)/shard_map/ppermute | solution.py:22
  31.6 1.2 %collective-permute-done.17.refs_3_ = bf16[16,3584]{1,0:T(8,128)(2,1)S(1)} collective-permute-done((bf16[16,3584]{1,0:T(8,128)(2,1)S(1)}, bf16[16,3584]{1,0:T(8,128)(2,1)S(1)}, u32[]{:S(2)}, u32[]{:S(2)}) %collective-permute-start.17) | collective-permute-done | bytes 114720 | tf_op jit(solution)/shard_map/ppermute | solution.py:22
  32.8 0.9 %copy-done = bf16[16,3584]{1,0:T(8,128)(2,1)S(1)} copy-done((bf16[16,3584]{1,0:T(8,128)(2,1)S(1)}, bf16[16,3584]{1,0:T(8,128)(2,1)}, u32[]{:S(2)}) %copy-start) | copy-done | bytes 114712
  33.7 0.6 shard_map.91
  34.3 0.6 collective-permute-start.18
  34.9 0.5 collective-permute-start.19
  35.4 2.4 %collective-permute-start.20 = (bf16[40,3584]{1,0:T(8,128)(2,1)S(1)}, bf16[40,3584]{1,0:T(8,128)(2,1)S(1)}, u32[]{:S(2)}, u32[]{:S(2)}) collective-permute-start(bf16[40,3584]{1,0:T(8,128)(2,1)S(1)} %get-tuple-element.63), channel_id=1, source_target_pairs={{0,6},{1,7},{2,4},{3,5},{4,2},{5,3},{6,0},{7,1},{8,14},{9,15},{10,... | collective-permute-start | bytes 860168 | tf_op jit(solution)/shard_map/ppermute | solution.py:22
  37.9 8.4 %shard_map.88 = (bf16[40,3584]{1,0:T(8,128)(2,1)S(1)}, bf16[40,3584]{1,0:T(8,128)(2,1)S(1)}, bf16[40,3584]{1,0:T(8,128)(2,1)S(1)}, bf16[40,3584]{1,0:T(8,128)(2,...) custom-call(bf16[40,3584]{1,0:T(8,128)(2,1)S(1)} %get-tuple-element.40.x0, ...), custom_call_target="tpu_custom_call" | custom-call | flops 3523215360 | bytes 25624576 | tf_op jit(solution)/shard_map/pallas_call | solution.py:48
  46.2 0.6 collective-permute-start.10
  46.8 0.5 collective-permute-start.11
  47.4 2.4 %collective-permute-start.12 = (bf16[40,3584]{1,0:T(8,128)(2,1)S(1)}, bf16[40,3584]{1,0:T(8,128)(2,1)S(1)}, u32[]{:S(2)}, u32[]{:S(2)}) collective-permute-start(bf16[40,3584]{1,0:T(8,128)(2,1)S(1)} %get-tuple-element.52), channel_id=1, source_target_pairs={{0,6},{1,7},{2,4},{3,5},{4,2},{5,3},{6,0},{7,1},{8,14},{9,15},{10,... | collective-permute-start | bytes 860168 | tf_op jit(solution)/shard_map/ppermute | solution.py:22
  49.8 10.6 %shard_map.92 = (bf16[40,3584]{1,0:T(8,128)(2,1)S(1)}, bf16[40,3584]{1,0:T(8,128)(2,1)S(1)}, bf16[40,3584]{1,0:T(8,128)(2,1)S(1)}, bf16[40,3584]{1,0:T(8,128)(2,1)S(1)}) custom-call(bf16[40,3584]{1,0:T(8,128)(2,1)S(1)} %get-tuple-element.60.x0, bf16[40,3584]{1,0:T(8,128)(2,1)S(1)} %collective-permute-done.18.x1, ...), custom_call_target="tpu_custom_call" | custom-call | flops 3523215360 | bytes 25624576 | tf_op jit(solution)/shard_map/pallas_call | solution.py:48
  60.4 1.1 %collective-permute-start.21 = (bf16[40,3584]{1,0:T(8,128)(2,1)S(1)}, bf16[40,3584]{1,0:T(8,128)(2,1)S(1)}, u32[]{:S(2)}, u32[]{:S(2)}) collective-permute-start(bf16[40,3584]{1,0:T(8,128)(2,1)S(1)} %get-tuple-element.67), channel_id=1, source_target_pairs={{0,2},{1,3},{2,0},{3,1},{4,6},{5,7},{6,4},{7,5},{8,10},{9,11},{10,... | collective-permute-start | bytes 860168 | tf_op jit(solution)/shard_map/ppermute | solution.py:22
  61.5 0.5 collective-permute-start.22
  62.0 2.0 %collective-permute-start.23 = (bf16[40,3584]{1,0:T(8,128)(2,1)S(1)}, bf16[40,3584]{1,0:T(8,128)(2,1)S(1)}, u32[]{:S(2)}, u32[]{:S(2)}) collective-permute-start(bf16[40,3584]{1,0:T(8,128)(2,1)S(1)} %get-tuple-element.69), channel_id=1, source_target_pairs={{0,6},{1,7},{2,4},{3,5},{4,2},{5,3},{6,0},{7,1},{8,14},{9,15},{10,... | collective-permute-start | bytes 860168 | tf_op jit(solution)/shard_map/ppermute | solution.py:22
  64.0 0.6 shard_map.89
  64.6 1.0 %collective-permute-start.13 = (bf16[16,3584]{1,0:T(8,128)(2,1)S(1)}, bf16[16,3584]{1,0:T(8,128)(2,1)S(1)}, u32[]{:S(2)}, u32[]{:S(2)}) collective-permute-start(bf16[16,3584]{1,0:T(8,128)(2,1)S(1)} %get-tuple-element.54), channel_id=1, source_target_pairs={{0,8},{1,9},{2,10},{3,11},{4,12},{5,13},{6,14},{7,15},{8,0},{9,1},... | collective-permute-start | bytes 344072 | tf_op jit(solution)/shard_map/ppermute | solution.py:22
  65.6 4.4 %collective-permute-start.14 = (bf16[16,3584]{1,0:T(8,128)(2,1)S(1)}, bf16[16,3584]{1,0:T(8,128)(2,1)S(1)}, u32[]{:S(2)}, u32[]{:S(2)}) collective-permute-start(bf16[16,3584]{1,0:T(8,128)(2,1)S(1)} %get-tuple-element.55), channel_id=1, source_target_pairs={{0,16},{1,17},{2,18},{3,19},{4,20},{5,21},{6,22},{7,23},{8,24},{9,... | collective-permute-start | bytes 344072 | tf_op jit(solution)/shard_map/ppermute | solution.py:22
  70.0 3.6 %collective-permute-start.15 = (bf16[16,3584]{1,0:T(8,128)(2,1)S(1)}, bf16[16,3584]{1,0:T(8,128)(2,1)S(1)}, u32[]{:S(2)}, u32[]{:S(2)}) collective-permute-start(bf16[16,3584]{1,0:T(8,128)(2,1)S(1)} %get-tuple-element.56), channel_id=1, source_target_pairs={{0,24},{1,25},{2,26},{3,27},{4,28},{5,29},{6,30},{7,31},{8,16},{9,... | collective-permute-start | bytes 344072 | tf_op jit(solution)/shard_map/ppermute | solution.py:22
  73.6 0.3 shard_map.93
  73.9 0.3 collective-permute-start.24
  74.3 4.6 %collective-permute-start.25 = (bf16[16,3584]{1,0:T(8,128)(2,1)S(1)}, bf16[16,3584]{1,0:T(8,128)(2,1)S(1)}, u32[]{:S(2)}, u32[]{:S(2)}) collective-permute-start(bf16[16,3584]{1,0:T(8,128)(2,1)S(1)} %get-tuple-element.72), channel_id=1, source_target_pairs={{0,16},{1,17},{2,18},{3,19},{4,20},{5,21},{6,22},{7,23},{8,24},{9,... | collective-permute-start | bytes 344072 | tf_op jit(solution)/shard_map/ppermute | solution.py:22
  78.9 0.7 shard_map.90
  79.6 1.7 %collective-permute-done.24.refs_1_ = bf16[16,3584]{1,0:T(8,128)(2,1)S(1)} collective-permute-done((bf16[16,3584]{1,0:T(8,128)(2,1)S(1)}, bf16[16,3584]{1,0:T(8,128)(2,1)S(1)}, u32[]{:S(2)}, u32[]{:S(2)}) %collective-permute-start.24) | collective-permute-done | bytes 114720 | tf_op jit(solution)/shard_map/ppermute | solution.py:22
  81.3 2.6 %collective-permute-done.25.refs_2_ = bf16[16,3584]{1,0:T(8,128)(2,1)S(1)} collective-permute-done((bf16[16,3584]{1,0:T(8,128)(2,1)S(1)}, bf16[16,3584]{1,0:T(8,128)(2,1)S(1)}, u32[]{:S(2)}, u32[]{:S(2)}) %collective-permute-start.25) | collective-permute-done | bytes 114720 | tf_op jit(solution)/shard_map/ppermute | solution.py:22
  83.9 1.7 %collective-permute-done.26.refs_3_ = bf16[16,3584]{1,0:T(8,128)(2,1)S(1)} collective-permute-done((bf16[16,3584]{1,0:T(8,128)(2,1)S(1)}, bf16[16,3584]{1,0:T(8,128)(2,1)S(1)}, u32[]{:S(2)}, u32[]{:S(2)}) %collective-permute-start.26) | collective-permute-done | bytes 114720 | tf_op jit(solution)/shard_map/ppermute | solution.py:22
  85.5 0.7 shard_map.94
  (23 shorter events, 0.1 us)
Async XLA Ops:
  0.6 14.4 %collective-permute-start.3 = (bf16[1,3584,512]{2,1,0:T(8,128)(2,1)}, bf16[1,3584,512]{2,1,0:T(8,128)(2,1)}, u32[]{:S(2)}, u32[]{:S(2)}) collective-permute-start(bf16[1,3584,512]{2,1,0:T(8,128)(2,1)} %refs_0_.5), channel_id=1, source_target_pairs={{0,1},{1,0},{2,3},{3,2},{4,5},{5,4},{6,7},{7,6},{8,9},{9,8},{10,11... | collective-permute-start | bytes 11010056 | tf_op jit(solution)/shard_map/ppermute | solution.py:22
  1.1 19.1 %collective-permute-start.4 = (bf16[1,3584,512]{2,1,0:T(8,128)(2,1)}, bf16[1,3584,512]{2,1,0:T(8,128)(2,1)}, u32[]{:S(2)}, u32[]{:S(2)}) collective-permute-start(bf16[1,3584,512]{2,1,0:T(8,128)(2,1)} %refs_1_.3), channel_id=1, source_target_pairs={{0,1},{1,0},{2,3},{3,2},{4,5},{5,4},{6,7},{7,6},{8,9},{9,8},{10,11... | collective-permute-start | bytes 11010056 | tf_op jit(solution)/shard_map/ppermute | solution.py:22
  1.2 25.3 %collective-permute-start.9 = (bf16[1,512,3584]{2,1,0:T(8,128)(2,1)}, bf16[1,512,3584]{2,1,0:T(8,128)(2,1)}, u32[]{:S(2)}, u32[]{:S(2)}) collective-permute-start(bf16[1,512,3584]{2,1,0:T(8,128)(2,1)} %refs_2_.3), channel_id=1, source_target_pairs={{0,1},{1,0},{2,3},{3,2},{4,5},{5,4},{6,7},{7,6},{8,9},{9,8},{10,11... | collective-permute-start | bytes 11010056 | tf_op jit(solution)/shard_map/ppermute | solution.py:22
  1.7 0.9 %copy-start.1 = (bf16[16,3584]{1,0:T(8,128)(2,1)S(1)}, bf16[16,3584]{1,0:T(8,128)(2,1)}, u32[]{:S(2)}) copy-start(bf16[16,3584]{1,0:T(8,128)(2,1)} %tokens.1) | copy-start | bytes 344068
  2.6 0.7 copy-start.2
  3.2 0.7 copy-start.3
  4.1 10.2 %collective-permute-start.1 = (bf16[16,3712]{1,0:T(8,128)(2,1)S(1)}, bf16[16,3712]{1,0:T(8,128)(2,1)S(1)}, u32[]{:S(2)}, u32[]{:S(2)}) collective-permute-start(bf16[16,3712]{1,0:T(8,128)(2,1)S(1)} %shard_map.86.refs_0_), channel_id=1, source_target_pairs={{0,16},{1,17},{2,18},{3,19},{4,20},{5,21},{6,22},{7,23},{8,24},{9,... | collective-permute-start | bytes 356360 | tf_op jit(solution)/shard_map/ppermute | solution.py:22
  7.9 10.5 %collective-permute-start = (bf16[16,3712]{1,0:T(8,128)(2,1)S(1)}, bf16[16,3712]{1,0:T(8,128)(2,1)S(1)}, u32[]{:S(2)}, u32[]{:S(2)}) collective-permute-start(bf16[16,3712]{1,0:T(8,128)(2,1)S(1)} %shard_map.86.refs_0_), channel_id=1, source_target_pairs={{0,8},{1,9},{2,10},{3,11},{4,12},{5,13},{6,14},{7,15},{8,0},{9,1},... | collective-permute-start | bytes 356360 | tf_op jit(solution)/shard_map/ppermute | solution.py:22
  14.3 4.9 %collective-permute-start.2 = (bf16[16,3712]{1,0:T(8,128)(2,1)S(1)}, bf16[16,3712]{1,0:T(8,128)(2,1)S(1)}, u32[]{:S(2)}, u32[]{:S(2)}) collective-permute-start(bf16[16,3712]{1,0:T(8,128)(2,1)S(1)} %collective-permute-done.1.refs_2_), channel_id=1, source_target_pairs={{0,8},{1,9},{2,10},{3,11},{4,12},{5,13},{6,14},{7,15},{8,0},{9,1},... | collective-permute-start | bytes 356360 | tf_op jit(solution)/shard_map/ppermute | solution.py:22
  15.0 9.1 %collective-permute-start.7 = (bf16[16,3584]{1,0:T(8,128)(2,1)}, bf16[16,3584]{1,0:T(8,128)(2,1)S(1)}, u32[]{:S(2)}, u32[]{:S(2)}) collective-permute-start(bf16[16,3584]{1,0:T(8,128)(2,1)} %refs_0_.4), channel_id=1, source_target_pairs={{0,16},{1,17},{2,18},{3,19},{4,20},{5,21},{6,22},{7,23},{8,24},{9,... | collective-permute-start | bytes 344072 | tf_op jit(solution)/shard_map/ppermute | solution.py:22
  20.3 15.1 %collective-permute-start.5 = (bf16[40,3584]{1,0:T(8,128)(2,1)S(1)}, bf16[40,3584]{1,0:T(8,128)(2,1)S(1)}, u32[]{:S(2)}, u32[]{:S(2)}) collective-permute-start(bf16[40,3584]{1,0:T(8,128)(2,1)S(1)} %get-tuple-element.42), channel_id=1, source_target_pairs={{0,2},{1,3},{2,0},{3,1},{4,6},{5,7},{6,4},{7,5},{8,10},{9,11},{10,... | collective-permute-start | bytes 860168 | tf_op jit(solution)/shard_map/ppermute | solution.py:22
  21.8 16.0 %collective-permute-start.6 = (bf16[40,3584]{1,0:T(8,128)(2,1)S(1)}, bf16[40,3584]{1,0:T(8,128)(2,1)S(1)}, u32[]{:S(2)}, u32[]{:S(2)}) collective-permute-start(bf16[40,3584]{1,0:T(8,128)(2,1)S(1)} %get-tuple-element.44), channel_id=1, source_target_pairs={{0,4},{1,5},{2,6},{3,7},{4,0},{5,1},{6,2},{7,3},{8,12},{9,13},{10,... | collective-permute-start | bytes 860168 | tf_op jit(solution)/shard_map/ppermute | solution.py:22
  24.1 13.8 %collective-permute-start.8 = (bf16[40,3584]{1,0:T(8,128)(2,1)S(1)}, bf16[40,3584]{1,0:T(8,128)(2,1)S(1)}, u32[]{:S(2)}, u32[]{:S(2)}) collective-permute-start(bf16[40,3584]{1,0:T(8,128)(2,1)S(1)} %get-tuple-element.48), channel_id=1, source_target_pairs={{0,6},{1,7},{2,4},{3,5},{4,2},{5,3},{6,0},{7,1},{8,14},{9,15},{10,... | collective-permute-start | bytes 860168 | tf_op jit(solution)/shard_map/ppermute | solution.py:22
  26.6 5.0 %collective-permute-start.16 = (bf16[16,3584]{1,0:T(8,128)(2,1)}, bf16[16,3584]{1,0:T(8,128)(2,1)S(1)}, u32[]{:S(2)}, u32[]{:S(2)}) collective-permute-start(bf16[16,3584]{1,0:T(8,128)(2,1)} %refs_0_.4), channel_id=1, source_target_pairs={{0,8},{1,9},{2,10},{3,11},{4,12},{5,13},{6,14},{7,15},{8,0},{9,1},... | collective-permute-start | bytes 344072 | tf_op jit(solution)/shard_map/ppermute | solution.py:22
  26.8 6.0 %collective-permute-start.17 = (bf16[16,3584]{1,0:T(8,128)(2,1)S(1)}, bf16[16,3584]{1,0:T(8,128)(2,1)S(1)}, u32[]{:S(2)}, u32[]{:S(2)}) collective-permute-start(bf16[16,3584]{1,0:T(8,128)(2,1)S(1)} %collective-permute-done.7.refs_2_), channel_id=1, source_target_pairs={{0,8},{1,9},{2,10},{3,11},{4,12},{5,13},{6,14},{7,15},{8,0},{9,1},... | collective-permute-start | bytes 344072 | tf_op jit(solution)/shard_map/ppermute | solution.py:22
  32.8 0.9 %copy-start = (bf16[16,3584]{1,0:T(8,128)(2,1)S(1)}, bf16[16,3584]{1,0:T(8,128)(2,1)}, u32[]{:S(2)}) copy-start(bf16[16,3584]{1,0:T(8,128)(2,1)} %refs_0_.4) | copy-start | bytes 344068
  34.3 13.0 %collective-permute-start.18 = (bf16[40,3584]{1,0:T(8,128)(2,1)S(1)}, bf16[40,3584]{1,0:T(8,128)(2,1)S(1)}, u32[]{:S(2)}, u32[]{:S(2)}) collective-permute-start(bf16[40,3584]{1,0:T(8,128)(2,1)S(1)} %get-tuple-element.61), channel_id=1, source_target_pairs={{0,2},{1,3},{2,0},{3,1},{4,6},{5,7},{6,4},{7,5},{8,10},{9,11},{10,... | collective-permute-start | bytes 860168 | tf_op jit(solution)/shard_map/ppermute | solution.py:22
  34.9 14.9 %collective-permute-start.19 = (bf16[40,3584]{1,0:T(8,128)(2,1)S(1)}, bf16[40,3584]{1,0:T(8,128)(2,1)S(1)}, u32[]{:S(2)}, u32[]{:S(2)}) collective-permute-start(bf16[40,3584]{1,0:T(8,128)(2,1)S(1)} %get-tuple-element.62), channel_id=1, source_target_pairs={{0,4},{1,5},{2,6},{3,7},{4,0},{5,1},{6,2},{7,3},{8,12},{9,13},{10,... | collective-permute-start | bytes 860168 | tf_op jit(solution)/shard_map/ppermute | solution.py:22
  35.4 14.4 %collective-permute-start.20 = (bf16[40,3584]{1,0:T(8,128)(2,1)S(1)}, bf16[40,3584]{1,0:T(8,128)(2,1)S(1)}, u32[]{:S(2)}, u32[]{:S(2)}) collective-permute-start(bf16[40,3584]{1,0:T(8,128)(2,1)S(1)} %get-tuple-element.63), channel_id=1, source_target_pairs={{0,6},{1,7},{2,4},{3,5},{4,2},{5,3},{6,0},{7,1},{8,14},{9,15},{10,... | collective-permute-start | bytes 860168 | tf_op jit(solution)/shard_map/ppermute | solution.py:22
  46.2 15.7 %collective-permute-start.10 = (bf16[40,3584]{1,0:T(8,128)(2,1)S(1)}, bf16[40,3584]{1,0:T(8,128)(2,1)S(1)}, u32[]{:S(2)}, u32[]{:S(2)}) collective-permute-start(bf16[40,3584]{1,0:T(8,128)(2,1)S(1)} %get-tuple-element.50), channel_id=1, source_target_pairs={{0,2},{1,3},{2,0},{3,1},{4,6},{5,7},{6,4},{7,5},{8,10},{9,11},{10,... | collective-permute-start | bytes 860168 | tf_op jit(solution)/shard_map/ppermute | solution.py:22
  46.8 17.1 %collective-permute-start.11 = (bf16[40,3584]{1,0:T(8,128)(2,1)S(1)}, bf16[40,3584]{1,0:T(8,128)(2,1)S(1)}, u32[]{:S(2)}, u32[]{:S(2)}) collective-permute-start(bf16[40,3584]{1,0:T(8,128)(2,1)S(1)} %get-tuple-element.51), channel_id=1, source_target_pairs={{0,4},{1,5},{2,6},{3,7},{4,0},{5,1},{6,2},{7,3},{8,12},{9,13},{10,... | collective-permute-start | bytes 860168 | tf_op jit(solution)/shard_map/ppermute | solution.py:22
  47.4 16.6 %collective-permute-start.12 = (bf16[40,3584]{1,0:T(8,128)(2,1)S(1)}, bf16[40,3584]{1,0:T(8,128)(2,1)S(1)}, u32[]{:S(2)}, u32[]{:S(2)}) collective-permute-start(bf16[40,3584]{1,0:T(8,128)(2,1)S(1)} %get-tuple-element.52), channel_id=1, source_target_pairs={{0,6},{1,7},{2,4},{3,5},{4,2},{5,3},{6,0},{7,1},{8,14},{9,15},{10,... | collective-permute-start | bytes 860168 | tf_op jit(solution)/shard_map/ppermute | solution.py:22
  60.4 9.6 %collective-permute-start.21 = (bf16[40,3584]{1,0:T(8,128)(2,1)S(1)}, bf16[40,3584]{1,0:T(8,128)(2,1)S(1)}, u32[]{:S(2)}, u32[]{:S(2)}) collective-permute-start(bf16[40,3584]{1,0:T(8,128)(2,1)S(1)} %get-tuple-element.67), channel_id=1, source_target_pairs={{0,2},{1,3},{2,0},{3,1},{4,6},{5,7},{6,4},{7,5},{8,10},{9,11},{10,... | collective-permute-start | bytes 860168 | tf_op jit(solution)/shard_map/ppermute | solution.py:22
  61.5 12.1 %collective-permute-start.22 = (bf16[40,3584]{1,0:T(8,128)(2,1)S(1)}, bf16[40,3584]{1,0:T(8,128)(2,1)S(1)}, u32[]{:S(2)}, u32[]{:S(2)}) collective-permute-start(bf16[40,3584]{1,0:T(8,128)(2,1)S(1)} %get-tuple-element.68), channel_id=1, source_target_pairs={{0,4},{1,5},{2,6},{3,7},{4,0},{5,1},{6,2},{7,3},{8,12},{9,13},{10,... | collective-permute-start | bytes 860168 | tf_op jit(solution)/shard_map/ppermute | solution.py:22
  62.0 11.7 %collective-permute-start.23 = (bf16[40,3584]{1,0:T(8,128)(2,1)S(1)}, bf16[40,3584]{1,0:T(8,128)(2,1)S(1)}, u32[]{:S(2)}, u32[]{:S(2)}) collective-permute-start(bf16[40,3584]{1,0:T(8,128)(2,1)S(1)} %get-tuple-element.69), channel_id=1, source_target_pairs={{0,6},{1,7},{2,4},{3,5},{4,2},{5,3},{6,0},{7,1},{8,14},{9,15},{10,... | collective-permute-start | bytes 860168 | tf_op jit(solution)/shard_map/ppermute | solution.py:22
  64.6 14.3 %collective-permute-start.13 = (bf16[16,3584]{1,0:T(8,128)(2,1)S(1)}, bf16[16,3584]{1,0:T(8,128)(2,1)S(1)}, u32[]{:S(2)}, u32[]{:S(2)}) collective-permute-start(bf16[16,3584]{1,0:T(8,128)(2,1)S(1)} %get-tuple-element.54), channel_id=1, source_target_pairs={{0,8},{1,9},{2,10},{3,11},{4,12},{5,13},{6,14},{7,15},{8,0},{9,1},... | collective-permute-start | bytes 344072 | tf_op jit(solution)/shard_map/ppermute | solution.py:22
  65.6 13.3 %collective-permute-start.14 = (bf16[16,3584]{1,0:T(8,128)(2,1)S(1)}, bf16[16,3584]{1,0:T(8,128)(2,1)S(1)}, u32[]{:S(2)}, u32[]{:S(2)}) collective-permute-start(bf16[16,3584]{1,0:T(8,128)(2,1)S(1)} %get-tuple-element.55), channel_id=1, source_target_pairs={{0,16},{1,17},{2,18},{3,19},{4,20},{5,21},{6,22},{7,23},{8,24},{9,... | collective-permute-start | bytes 344072 | tf_op jit(solution)/shard_map/ppermute | solution.py:22
  70.0 8.9 %collective-permute-start.15 = (bf16[16,3584]{1,0:T(8,128)(2,1)S(1)}, bf16[16,3584]{1,0:T(8,128)(2,1)S(1)}, u32[]{:S(2)}, u32[]{:S(2)}) collective-permute-start(bf16[16,3584]{1,0:T(8,128)(2,1)S(1)} %get-tuple-element.56), channel_id=1, source_target_pairs={{0,24},{1,25},{2,26},{3,27},{4,28},{5,29},{6,30},{7,31},{8,16},{9,... | collective-permute-start | bytes 344072 | tf_op jit(solution)/shard_map/ppermute | solution.py:22
  73.9 7.3 %collective-permute-start.24 = (bf16[16,3584]{1,0:T(8,128)(2,1)S(1)}, bf16[16,3584]{1,0:T(8,128)(2,1)S(1)}, u32[]{:S(2)}, u32[]{:S(2)}) collective-permute-start(bf16[16,3584]{1,0:T(8,128)(2,1)S(1)} %get-tuple-element.71), channel_id=1, source_target_pairs={{0,8},{1,9},{2,10},{3,11},{4,12},{5,13},{6,14},{7,15},{8,0},{9,1},... | collective-permute-start | bytes 344072 | tf_op jit(solution)/shard_map/ppermute | solution.py:22
  74.3 9.6 %collective-permute-start.25 = (bf16[16,3584]{1,0:T(8,128)(2,1)S(1)}, bf16[16,3584]{1,0:T(8,128)(2,1)S(1)}, u32[]{:S(2)}, u32[]{:S(2)}) collective-permute-start(bf16[16,3584]{1,0:T(8,128)(2,1)S(1)} %get-tuple-element.72), channel_id=1, source_target_pairs={{0,16},{1,17},{2,18},{3,19},{4,20},{5,21},{6,22},{7,23},{8,24},{9,... | collective-permute-start | bytes 344072 | tf_op jit(solution)/shard_map/ppermute | solution.py:22
  78.8 6.7 %collective-permute-start.26 = (bf16[16,3584]{1,0:T(8,128)(2,1)S(1)}, bf16[16,3584]{1,0:T(8,128)(2,1)S(1)}, u32[]{:S(2)}, u32[]{:S(2)}) collective-permute-start(bf16[16,3584]{1,0:T(8,128)(2,1)S(1)} %get-tuple-element.73), channel_id=1, source_target_pairs={{0,24},{1,25},{2,26},{3,27},{4,28},{5,29},{6,30},{7,31},{8,16},{9,... | collective-permute-start | bytes 344072 | tf_op jit(solution)/shard_map/ppermute | solution.py:22

commit v17 on v10

--- a/solution.py
+++ b/solution.py
@@ -67,13 +67,14 @@
     pltpu.make_async_copy(place, place, sem).wait()
 
 
-def code_kernel(experts, tokens, ids, gates, out):
+def code_kernel(experts, tokens, routes, out):
     rows, width = tokens.shape
     gate_width = out.shape[1] - width
     line = lax.broadcasted_iota(jnp.int32, (gate_width, rows), 0)
     rest = jnp.zeros(line.shape, f32)
-    for k in range(ids.shape[0]):
-        rest = jnp.where(ids[k : k + 1] == line % experts, gates[k : k + 1], rest)
+    place, top = (line % experts).astype(f32), routes.shape[0] // 2
+    for k in range(top):
+        rest = jnp.where(routes[k : k + 1] == place, routes[top + k : top + k + 1], rest)
     columns = jnp.zeros(line.shape, f32)
     for number in range(PIECES):
         piece = rest.astype(bf16).astype(f32)
@@ -284,7 +285,7 @@
     (coded,) = call(
         functools.partial(code_kernel, experts),
         [shape((tok_dev, width + padded(PIECES * experts)), bf16)],
-        (tokens, expert_ids.T, gate_values.T),
+        (tokens, jnp.concatenate([expert_ids.T.astype(f32), gate_values.T], axis=0)),
     )
     held, offset = {0: coded}, devices // 2
     while offset >= FAR:

time: 86.4 us -> 86.4 us (level)
  other arithmetic: 0 us -> 1.38 us
  local copies, waits for them, and re-layouts: 3.17 us -> 1.8 us
    unnamed x8 -> x4, local copies, waits for them, and re-layouts: 3.17 us -> 1.8 us
  transfers between devices with their start and end apart: 27 -> 27, of which waited for: 8 -> 8; matrix products, arithmetic and copies ran while one was open for 0% -> 2% of each run, Pallas kernels for 26% -> 26%
where the time goes in v17:
time: 86.4 us; the launch traced here: 86.2 us
  starting transfers between devices  42.8 us (50%)
  Pallas kernels  22.7 us (26%)
  waiting for transfers between devices  16.8 us (19%)
  local copies, waits for them, and re-layouts  1.8 us (2%)
  other arithmetic  1.38 us (2%)
    ppermute x27, starting transfers between devices, swap(): lax.ppermute(value, 'expert', [(i, i ^ offset) for i in range(devices)])  42.8 us
    pallas_call x9, Pallas kernels, call(): pl.pallas_call(body, out_shape=outs, in_specs=[whole] * len(args) if in_s...  22.7 us
    ppermute x27, waiting for transfers between devices, swap(): lax.ppermute(value, 'expert', [(i, i ^ offset) for i in range(devices)])  16.8 us
    unnamed x4, local copies, waits for them, and re-layouts  1.8 us
  transfers between devices with their start and end apart: 27, of which 8 were waited for; matrix products, arithmetic and copies ran while one was open for 2% of the time, Pallas kernels for 26%

profile of v17, /device:TPU:0, one launch (start us, length us, event | category | flops | bytes accessed | tf_op | source)
XLA Modules:
  0.0 86.2 jit_solution(8864326420478653845)
XLA Ops:
  0.6 0.5 collective-permute-start.3
  1.1 0.1 collective-permute-start.4
  1.2 0.4 collective-permute-start.9
  1.7 0.7 convert_bitcast_fusion
  2.3 0.7 pad_maximum_fusion.routes
  3.0 0.9 %copy-done.1 = bf16[16,3584]{1,0:T(8,128)(2,1)S(1)} copy-done((bf16[16,3584]{1,0:T(8,128)(2,1)S(1)}, bf16[16,3584]{1,0:T(8,128)(2,1)}, u32[]{:S(2)}) %copy-start.1) | copy-done | bytes 114712
  3.9 0.2 shard_map.86.refs_0_
  4.1 3.7 %collective-permute-start.1 = (bf16[16,3712]{1,0:T(8,128)(2,1)S(1)}, bf16[16,3712]{1,0:T(8,128)(2,1)S(1)}, u32[]{:S(2)}, u32[]{:S(2)}) collective-permute-start(bf16[16,3712]{1,0:T(8,128)(2,1)S(1)} %shard_map.86.refs_0_), channel_id=1, source_target_pairs={{0,16},{1,17},{2,18},{3,19},{4,20},{5,21},{6,22},{7,23},{8,24},{9,... | collective-permute-start | bytes 356360 | tf_op jit(solution)/shard_map/ppermute | solution.py:22
  7.9 1.6 %collective-permute-start = (bf16[16,3712]{1,0:T(8,128)(2,1)S(1)}, bf16[16,3712]{1,0:T(8,128)(2,1)S(1)}, u32[]{:S(2)}, u32[]{:S(2)}) collective-permute-start(bf16[16,3712]{1,0:T(8,128)(2,1)S(1)} %shard_map.86.refs_0_), channel_id=1, source_target_pairs={{0,8},{1,9},{2,10},{3,11},{4,12},{5,13},{6,14},{7,15},{8,0},{9,1},... | collective-permute-start | bytes 356360 | tf_op jit(solution)/shard_map/ppermute | solution.py:22
  9.4 4.9 %collective-permute-done.1.refs_2_ = bf16[16,3712]{1,0:T(8,128)(2,1)S(1)} collective-permute-done((bf16[16,3712]{1,0:T(8,128)(2,1)S(1)}, bf16[16,3712]{1,0:T(8,128)(2,1)S(1)}, u32[]{:S(2)}, u32[]{:S(2)}) %collective-permute-start.1) | collective-permute-done | bytes 118816 | tf_op jit(solution)/shard_map/ppermute | solution.py:22
  14.3 0.6 collective-permute-start.2
  15.0 0.0 collective-permute-done.3.refs_3_
  15.0 3.4 %collective-permute-start.7 = (bf16[16,3584]{1,0:T(8,128)(2,1)}, bf16[16,3584]{1,0:T(8,128)(2,1)S(1)}, u32[]{:S(2)}, u32[]{:S(2)}) collective-permute-start(bf16[16,3584]{1,0:T(8,128)(2,1)} %refs_0_.4), channel_id=1, source_target_pairs={{0,16},{1,17},{2,18},{3,19},{4,20},{5,21},{6,22},{7,23},{8,24},{9,... | collective-permute-start | bytes 344072 | tf_op jit(solution)/shard_map/ppermute | solution.py:22
  18.4 0.9 %collective-permute-done.2.refs_3_ = bf16[16,3712]{1,0:T(8,128)(2,1)S(1)} collective-permute-done((bf16[16,3712]{1,0:T(8,128)(2,1)S(1)}, bf16[16,3712]{1,0:T(8,128)(2,1)S(1)}, u32[]{:S(2)}, u32[]{:S(2)}) %collective-permute-start.2) | collective-permute-done | bytes 118816 | tf_op jit(solution)/shard_map/ppermute | solution.py:22
  19.2 1.0 %shard_map.87 = (bf16[40,3584]{1,0:T(8,128)(2,1)S(1)}, bf16[40,3584]{1,0:T(8,128)(2,1)S(1)}, bf16[40,3584]{1,0:T(8,128)(2,1)S(1)}, bf16[40,3584]{1,0:T(8,128)(2,...) custom-call(s32[1]{0:T(128)} %bitcast.chip, bf16[16,3712]{1,0:T(8,128)(2,1)S(1)} %shard_map.86.refs_0_, ...), custom_call_target="tpu_custom_call" | custom-call | flops 117440512 | bytes 1753092 | tf_op jit(solution)/shard_map/pallas_call | solution.py:48
  20.3 1.6 %collective-permute-start.5 = (bf16[40,3584]{1,0:T(8,128)(2,1)S(1)}, bf16[40,3584]{1,0:T(8,128)(2,1)S(1)}, u32[]{:S(2)}, u32[]{:S(2)}) collective-permute-start(bf16[40,3584]{1,0:T(8,128)(2,1)S(1)} %get-tuple-element.42), channel_id=1, source_target_pairs={{0,2},{1,3},{2,0},{3,1},{4,6},{5,7},{6,4},{7,5},{8,10},{9,11},{10,... | collective-permute-start | bytes 860168 | tf_op jit(solution)/shard_map/ppermute | solution.py:22
  21.8 1.5 %collective-permute-start.6 = (bf16[40,3584]{1,0:T(8,128)(2,1)S(1)}, bf16[40,3584]{1,0:T(8,128)(2,1)S(1)}, u32[]{:S(2)}, u32[]{:S(2)}) collective-permute-start(bf16[40,3584]{1,0:T(8,128)(2,1)S(1)} %get-tuple-element.44), channel_id=1, source_target_pairs={{0,4},{1,5},{2,6},{3,7},{4,0},{5,1},{6,2},{7,3},{8,12},{9,13},{10,... | collective-permute-start | bytes 860168 | tf_op jit(solution)/shard_map/ppermute | solution.py:22
  23.4 0.8 collective-permute-done.7.refs_2_
  24.1 2.4 %collective-permute-start.8 = (bf16[40,3584]{1,0:T(8,128)(2,1)S(1)}, bf16[40,3584]{1,0:T(8,128)(2,1)S(1)}, u32[]{:S(2)}, u32[]{:S(2)}) collective-permute-start(bf16[40,3584]{1,0:T(8,128)(2,1)S(1)} %get-tuple-element.48), channel_id=1, source_target_pairs={{0,6},{1,7},{2,4},{3,5},{4,2},{5,3},{6,0},{7,1},{8,14},{9,15},{10,... | collective-permute-start | bytes 860168 | tf_op jit(solution)/shard_map/ppermute | solution.py:22
  26.6 0.3 collective-permute-start.16
  26.8 1.8 %collective-permute-start.17 = (bf16[16,3584]{1,0:T(8,128)(2,1)S(1)}, bf16[16,3584]{1,0:T(8,128)(2,1)S(1)}, u32[]{:S(2)}, u32[]{:S(2)}) collective-permute-start(bf16[16,3584]{1,0:T(8,128)(2,1)S(1)} %collective-permute-done.7.refs_2_), channel_id=1, source_target_pairs={{0,8},{1,9},{2,10},{3,11},{4,12},{5,13},{6,14},{7,15},{8,0},{9,1},... | collective-permute-start | bytes 344072 | tf_op jit(solution)/shard_map/ppermute | solution.py:22
  28.6 3.0 %collective-permute-done.16.refs_1_ = bf16[16,3584]{1,0:T(8,128)(2,1)S(1)} collective-permute-done((bf16[16,3584]{1,0:T(8,128)(2,1)}, bf16[16,3584]{1,0:T(8,128)(2,1)S(1)}, u32[]{:S(2)}, u32[]{:S(2)}) %collective-permute-start.16) | collective-permute-done | bytes 114720 | tf_op jit(solution)/shard_map/ppermute | solution.py:22
  31.6 1.2 %collective-permute-done.17.refs_3_ = bf16[16,3584]{1,0:T(8,128)(2,1)S(1)} collective-permute-done((bf16[16,3584]{1,0:T(8,128)(2,1)S(1)}, bf16[16,3584]{1,0:T(8,128)(2,1)S(1)}, u32[]{:S(2)}, u32[]{:S(2)}) %collective-permute-start.17) | collective-permute-done | bytes 114720 | tf_op jit(solution)/shard_map/ppermute | solution.py:22
  32.8 0.9 %copy-done = bf16[16,3584]{1,0:T(8,128)(2,1)S(1)} copy-done((bf16[16,3584]{1,0:T(8,128)(2,1)S(1)}, bf16[16,3584]{1,0:T(8,128)(2,1)}, u32[]{:S(2)}) %copy-start) | copy-done | bytes 114712
  33.7 0.6 shard_map.91
  34.3 0.6 collective-permute-start.18
  34.9 0.5 collective-permute-start.19
  35.4 2.4 %collective-permute-start.20 = (bf16[40,3584]{1,0:T(8,128)(2,1)S(1)}, bf16[40,3584]{1,0:T(8,128)(2,1)S(1)}, u32[]{:S(2)}, u32[]{:S(2)}) collective-permute-start(bf16[40,3584]{1,0:T(8,128)(2,1)S(1)} %get-tuple-element.63), channel_id=1, source_target_pairs={{0,6},{1,7},{2,4},{3,5},{4,2},{5,3},{6,0},{7,1},{8,14},{9,15},{10,... | collective-permute-start | bytes 860168 | tf_op jit(solution)/shard_map/ppermute | solution.py:22
  37.9 8.2 %shard_map.88 = (bf16[40,3584]{1,0:T(8,128)(2,1)S(1)}, bf16[40,3584]{1,0:T(8,128)(2,1)S(1)}, bf16[40,3584]{1,0:T(8,128)(2,1)S(1)}, bf16[40,3584]{1,0:T(8,128)(2,...) custom-call(bf16[40,3584]{1,0:T(8,128)(2,1)S(1)} %get-tuple-element.40.x0, ...), custom_call_target="tpu_custom_call" | custom-call | flops 3523215360 | bytes 25624576 | tf_op jit(solution)/shard_map/pallas_call | solution.py:48
  46.1 0.6 collective-permute-start.10
  46.7 0.5 collective-permute-start.11
  47.2 2.4 %collective-permute-start.12 = (bf16[40,3584]{1,0:T(8,128)(2,1)S(1)}, bf16[40,3584]{1,0:T(8,128)(2,1)S(1)}, u32[]{:S(2)}, u32[]{:S(2)}) collective-permute-start(bf16[40,3584]{1,0:T(8,128)(2,1)S(1)} %get-tuple-element.52), channel_id=1, source_target_pairs={{0,6},{1,7},{2,4},{3,5},{4,2},{5,3},{6,0},{7,1},{8,14},{9,15},{10,... | collective-permute-start | bytes 860168 | tf_op jit(solution)/shard_map/ppermute | solution.py:22
  49.7 10.4 %shard_map.92 = (bf16[40,3584]{1,0:T(8,128)(2,1)S(1)}, bf16[40,3584]{1,0:T(8,128)(2,1)S(1)}, bf16[40,3584]{1,0:T(8,128)(2,1)S(1)}, bf16[40,3584]{1,0:T(8,128)(2,1)S(1)}) custom-call(bf16[40,3584]{1,0:T(8,128)(2,1)S(1)} %get-tuple-element.60.x0, bf16[40,3584]{1,0:T(8,128)(2,1)S(1)} %collective-permute-done.18.x1, ...), custom_call_target="tpu_custom_call" | custom-call | flops 3523215360 | bytes 25624576 | tf_op jit(solution)/shard_map/pallas_call | solution.py:48
  60.0 1.2 %collective-permute-start.21 = (bf16[40,3584]{1,0:T(8,128)(2,1)S(1)}, bf16[40,3584]{1,0:T(8,128)(2,1)S(1)}, u32[]{:S(2)}, u32[]{:S(2)}) collective-permute-start(bf16[40,3584]{1,0:T(8,128)(2,1)S(1)} %get-tuple-element.67), channel_id=1, source_target_pairs={{0,2},{1,3},{2,0},{3,1},{4,6},{5,7},{6,4},{7,5},{8,10},{9,11},{10,... | collective-permute-start | bytes 860168 | tf_op jit(solution)/shard_map/ppermute | solution.py:22
  61.3 0.6 collective-permute-start.22
  61.8 1.8 %collective-permute-start.23 = (bf16[40,3584]{1,0:T(8,128)(2,1)S(1)}, bf16[40,3584]{1,0:T(8,128)(2,1)S(1)}, u32[]{:S(2)}, u32[]{:S(2)}) collective-permute-start(bf16[40,3584]{1,0:T(8,128)(2,1)S(1)} %get-tuple-element.69), channel_id=1, source_target_pairs={{0,6},{1,7},{2,4},{3,5},{4,2},{5,3},{6,0},{7,1},{8,14},{9,15},{10,... | collective-permute-start | bytes 860168 | tf_op jit(solution)/shard_map/ppermute | solution.py:22
  63.6 0.6 shard_map.89
  64.2 1.0 %collective-permute-start.13 = (bf16[16,3584]{1,0:T(8,128)(2,1)S(1)}, bf16[16,3584]{1,0:T(8,128)(2,1)S(1)}, u32[]{:S(2)}, u32[]{:S(2)}) collective-permute-start(bf16[16,3584]{1,0:T(8,128)(2,1)S(1)} %get-tuple-element.54), channel_id=1, source_target_pairs={{0,8},{1,9},{2,10},{3,11},{4,12},{5,13},{6,14},{7,15},{8,0},{9,1},... | collective-permute-start | bytes 344072 | tf_op jit(solution)/shard_map/ppermute | solution.py:22
  65.2 4.5 %collective-permute-start.14 = (bf16[16,3584]{1,0:T(8,128)(2,1)S(1)}, bf16[16,3584]{1,0:T(8,128)(2,1)S(1)}, u32[]{:S(2)}, u32[]{:S(2)}) collective-permute-start(bf16[16,3584]{1,0:T(8,128)(2,1)S(1)} %get-tuple-element.55), channel_id=1, source_target_pairs={{0,16},{1,17},{2,18},{3,19},{4,20},{5,21},{6,22},{7,23},{8,24},{9,... | collective-permute-start | bytes 344072 | tf_op jit(solution)/shard_map/ppermute | solution.py:22
  69.8 3.7 %collective-permute-start.15 = (bf16[16,3584]{1,0:T(8,128)(2,1)S(1)}, bf16[16,3584]{1,0:T(8,128)(2,1)S(1)}, u32[]{:S(2)}, u32[]{:S(2)}) collective-permute-start(bf16[16,3584]{1,0:T(8,128)(2,1)S(1)} %get-tuple-element.56), channel_id=1, source_target_pairs={{0,24},{1,25},{2,26},{3,27},{4,28},{5,29},{6,30},{7,31},{8,16},{9,... | collective-permute-start | bytes 344072 | tf_op jit(solution)/shard_map/ppermute | solution.py:22
  73.4 0.3 shard_map.93
  73.8 0.5 collective-permute-start.24
  74.3 4.5 %collective-permute-start.25 = (bf16[16,3584]{1,0:T(8,128)(2,1)S(1)}, bf16[16,3584]{1,0:T(8,128)(2,1)S(1)}, u32[]{:S(2)}, u32[]{:S(2)}) collective-permute-start(bf16[16,3584]{1,0:T(8,128)(2,1)S(1)} %get-tuple-element.72), channel_id=1, source_target_pairs={{0,16},{1,17},{2,18},{3,19},{4,20},{5,21},{6,22},{7,23},{8,24},{9,... | collective-permute-start | bytes 344072 | tf_op jit(solution)/shard_map/ppermute | solution.py:22
  78.8 0.7 shard_map.90
  79.5 0.9 %collective-permute-done.24.refs_1_ = bf16[16,3584]{1,0:T(8,128)(2,1)S(1)} collective-permute-done((bf16[16,3584]{1,0:T(8,128)(2,1)S(1)}, bf16[16,3584]{1,0:T(8,128)(2,1)S(1)}, u32[]{:S(2)}, u32[]{:S(2)}) %collective-permute-start.24) | collective-permute-done | bytes 114720 | tf_op jit(solution)/shard_map/ppermute | solution.py:22
  80.4 3.2 %collective-permute-done.25.refs_2_ = bf16[16,3584]{1,0:T(8,128)(2,1)S(1)} collective-permute-done((bf16[16,3584]{1,0:T(8,128)(2,1)S(1)}, bf16[16,3584]{1,0:T(8,128)(2,1)S(1)}, u32[]{:S(2)}, u32[]{:S(2)}) %collective-permute-start.25) | collective-permute-done | bytes 114720 | tf_op jit(solution)/shard_map/ppermute | solution.py:22
  83.6 1.9 %collective-permute-done.26.refs_3_ = bf16[16,3584]{1,0:T(8,128)(2,1)S(1)} collective-permute-done((bf16[16,3584]{1,0:T(8,128)(2,1)S(1)}, bf16[16,3584]{1,0:T(8,128)(2,1)S(1)}, u32[]{:S(2)}, u32[]{:S(2)}) %collective-permute-start.26) | collective-permute-done | bytes 114720 | tf_op jit(solution)/shard_map/ppermute | solution.py:22
  85.5 0.7 shard_map.94
  (21 shorter events, 0.1 us)
Async XLA Ops:
  0.6 14.4 %collective-permute-start.3 = (bf16[1,3584,512]{2,1,0:T(8,128)(2,1)}, bf16[1,3584,512]{2,1,0:T(8,128)(2,1)}, u32[]{:S(2)}, u32[]{:S(2)}) collective-permute-start(bf16[1,3584,512]{2,1,0:T(8,128)(2,1)} %refs_0_.5), channel_id=1, source_target_pairs={{0,1},{1,0},{2,3},{3,2},{4,5},{5,4},{6,7},{7,6},{8,9},{9,8},{10,11... | collective-permute-start | bytes 11010056 | tf_op jit(solution)/shard_map/ppermute | solution.py:22
  1.1 19.1 %collective-permute-start.4 = (bf16[1,3584,512]{2,1,0:T(8,128)(2,1)}, bf16[1,3584,512]{2,1,0:T(8,128)(2,1)}, u32[]{:S(2)}, u32[]{:S(2)}) collective-permute-start(bf16[1,3584,512]{2,1,0:T(8,128)(2,1)} %refs_1_.3), channel_id=1, source_target_pairs={{0,1},{1,0},{2,3},{3,2},{4,5},{5,4},{6,7},{7,6},{8,9},{9,8},{10,11... | collective-permute-start | bytes 11010056 | tf_op jit(solution)/shard_map/ppermute | solution.py:22
  1.2 25.3 %collective-permute-start.9 = (bf16[1,512,3584]{2,1,0:T(8,128)(2,1)}, bf16[1,512,3584]{2,1,0:T(8,128)(2,1)}, u32[]{:S(2)}, u32[]{:S(2)}) collective-permute-start(bf16[1,512,3584]{2,1,0:T(8,128)(2,1)} %refs_2_.3), channel_id=1, source_target_pairs={{0,1},{1,0},{2,3},{3,2},{4,5},{5,4},{6,7},{7,6},{8,9},{9,8},{10,11... | collective-permute-start | bytes 11010056 | tf_op jit(solution)/shard_map/ppermute | solution.py:22
  3.0 0.9 %copy-start.1 = (bf16[16,3584]{1,0:T(8,128)(2,1)S(1)}, bf16[16,3584]{1,0:T(8,128)(2,1)}, u32[]{:S(2)}) copy-start(bf16[16,3584]{1,0:T(8,128)(2,1)} %tokens.1) | copy-start | bytes 344068
  4.1 10.2 %collective-permute-start.1 = (bf16[16,3712]{1,0:T(8,128)(2,1)S(1)}, bf16[16,3712]{1,0:T(8,128)(2,1)S(1)}, u32[]{:S(2)}, u32[]{:S(2)}) collective-permute-start(bf16[16,3712]{1,0:T(8,128)(2,1)S(1)} %shard_map.86.refs_0_), channel_id=1, source_target_pairs={{0,16},{1,17},{2,18},{3,19},{4,20},{5,21},{6,22},{7,23},{8,24},{9,... | collective-permute-start | bytes 356360 | tf_op jit(solution)/shard_map/ppermute | solution.py:22
  7.9 10.5 %collective-permute-start = (bf16[16,3712]{1,0:T(8,128)(2,1)S(1)}, bf16[16,3712]{1,0:T(8,128)(2,1)S(1)}, u32[]{:S(2)}, u32[]{:S(2)}) collective-permute-start(bf16[16,3712]{1,0:T(8,128)(2,1)S(1)} %shard_map.86.refs_0_), channel_id=1, source_target_pairs={{0,8},{1,9},{2,10},{3,11},{4,12},{5,13},{6,14},{7,15},{8,0},{9,1},... | collective-permute-start | bytes 356360 | tf_op jit(solution)/shard_map/ppermute | solution.py:22
  14.3 4.9 %collective-permute-start.2 = (bf16[16,3712]{1,0:T(8,128)(2,1)S(1)}, bf16[16,3712]{1,0:T(8,128)(2,1)S(1)}, u32[]{:S(2)}, u32[]{:S(2)}) collective-permute-start(bf16[16,3712]{1,0:T(8,128)(2,1)S(1)} %collective-permute-done.1.refs_2_), channel_id=1, source_target_pairs={{0,8},{1,9},{2,10},{3,11},{4,12},{5,13},{6,14},{7,15},{8,0},{9,1},... | collective-permute-start | bytes 356360 | tf_op jit(solution)/shard_map/ppermute | solution.py:22
  15.0 9.1 %collective-permute-start.7 = (bf16[16,3584]{1,0:T(8,128)(2,1)}, bf16[16,3584]{1,0:T(8,128)(2,1)S(1)}, u32[]{:S(2)}, u32[]{:S(2)}) collective-permute-start(bf16[16,3584]{1,0:T(8,128)(2,1)} %refs_0_.4), channel_id=1, source_target_pairs={{0,16},{1,17},{2,18},{3,19},{4,20},{5,21},{6,22},{7,23},{8,24},{9,... | collective-permute-start | bytes 344072 | tf_op jit(solution)/shard_map/ppermute | solution.py:22
  20.3 15.1 %collective-permute-start.5 = (bf16[40,3584]{1,0:T(8,128)(2,1)S(1)}, bf16[40,3584]{1,0:T(8,128)(2,1)S(1)}, u32[]{:S(2)}, u32[]{:S(2)}) collective-permute-start(bf16[40,3584]{1,0:T(8,128)(2,1)S(1)} %get-tuple-element.42), channel_id=1, source_target_pairs={{0,2},{1,3},{2,0},{3,1},{4,6},{5,7},{6,4},{7,5},{8,10},{9,11},{10,... | collective-permute-start | bytes 860168 | tf_op jit(solution)/shard_map/ppermute | solution.py:22
  21.8 16.0 %collective-permute-start.6 = (bf16[40,3584]{1,0:T(8,128)(2,1)S(1)}, bf16[40,3584]{1,0:T(8,128)(2,1)S(1)}, u32[]{:S(2)}, u32[]{:S(2)}) collective-permute-start(bf16[40,3584]{1,0:T(8,128)(2,1)S(1)} %get-tuple-element.44), channel_id=1, source_target_pairs={{0,4},{1,5},{2,6},{3,7},{4,0},{5,1},{6,2},{7,3},{8,12},{9,13},{10,... | collective-permute-start | bytes 860168 | tf_op jit(solution)/shard_map/ppermute | solution.py:22
  24.1 13.8 %collective-permute-start.8 = (bf16[40,3584]{1,0:T(8,128)(2,1)S(1)}, bf16[40,3584]{1,0:T(8,128)(2,1)S(1)}, u32[]{:S(2)}, u32[]{:S(2)}) collective-permute-start(bf16[40,3584]{1,0:T(8,128)(2,1)S(1)} %get-tuple-element.48), channel_id=1, source_target_pairs={{0,6},{1,7},{2,4},{3,5},{4,2},{5,3},{6,0},{7,1},{8,14},{9,15},{10,... | collective-permute-start | bytes 860168 | tf_op jit(solution)/shard_map/ppermute | solution.py:22
  26.6 5.0 %collective-permute-start.16 = (bf16[16,3584]{1,0:T(8,128)(2,1)}, bf16[16,3584]{1,0:T(8,128)(2,1)S(1)}, u32[]{:S(2)}, u32[]{:S(2)}) collective-permute-start(bf16[16,3584]{1,0:T(8,128)(2,1)} %refs_0_.4), channel_id=1, source_target_pairs={{0,8},{1,9},{2,10},{3,11},{4,12},{5,13},{6,14},{7,15},{8,0},{9,1},... | collective-permute-start | bytes 344072 | tf_op jit(solution)/shard_map/ppermute | solution.py:22
  26.8 6.0 %collective-permute-start.17 = (bf16[16,3584]{1,0:T(8,128)(2,1)S(1)}, bf16[16,3584]{1,0:T(8,128)(2,1)S(1)}, u32[]{:S(2)}, u32[]{:S(2)}) collective-permute-start(bf16[16,3584]{1,0:T(8,128)(2,1)S(1)} %collective-permute-done.7.refs_2_), channel_id=1, source_target_pairs={{0,8},{1,9},{2,10},{3,11},{4,12},{5,13},{6,14},{7,15},{8,0},{9,1},... | collective-permute-start | bytes 344072 | tf_op jit(solution)/shard_map/ppermute | solution.py:22
  32.8 0.9 %copy-start = (bf16[16,3584]{1,0:T(8,128)(2,1)S(1)}, bf16[16,3584]{1,0:T(8,128)(2,1)}, u32[]{:S(2)}) copy-start(bf16[16,3584]{1,0:T(8,128)(2,1)} %refs_0_.4) | copy-start | bytes 344068
  34.3 12.9 %collective-permute-start.18 = (bf16[40,3584]{1,0:T(8,128)(2,1)S(1)}, bf16[40,3584]{1,0:T(8,128)(2,1)S(1)}, u32[]{:S(2)}, u32[]{:S(2)}) collective-permute-start(bf16[40,3584]{1,0:T(8,128)(2,1)S(1)} %get-tuple-element.61), channel_id=1, source_target_pairs={{0,2},{1,3},{2,0},{3,1},{4,6},{5,7},{6,4},{7,5},{8,10},{9,11},{10,... | collective-permute-start | bytes 860168 | tf_op jit(solution)/shard_map/ppermute | solution.py:22
  34.9 14.8 %collective-permute-start.19 = (bf16[40,3584]{1,0:T(8,128)(2,1)S(1)}, bf16[40,3584]{1,0:T(8,128)(2,1)S(1)}, u32[]{:S(2)}, u32[]{:S(2)}) collective-permute-start(bf16[40,3584]{1,0:T(8,128)(2,1)S(1)} %get-tuple-element.62), channel_id=1, source_target_pairs={{0,4},{1,5},{2,6},{3,7},{4,0},{5,1},{6,2},{7,3},{8,12},{9,13},{10,... | collective-permute-start | bytes 860168 | tf_op jit(solution)/shard_map/ppermute | solution.py:22
  35.4 14.2 %collective-permute-start.20 = (bf16[40,3584]{1,0:T(8,128)(2,1)S(1)}, bf16[40,3584]{1,0:T(8,128)(2,1)S(1)}, u32[]{:S(2)}, u32[]{:S(2)}) collective-permute-start(bf16[40,3584]{1,0:T(8,128)(2,1)S(1)} %get-tuple-element.63), channel_id=1, source_target_pairs={{0,6},{1,7},{2,4},{3,5},{4,2},{5,3},{6,0},{7,1},{8,14},{9,15},{10,... | collective-permute-start | bytes 860168 | tf_op jit(solution)/shard_map/ppermute | solution.py:22
  46.1 15.7 %collective-permute-start.10 = (bf16[40,3584]{1,0:T(8,128)(2,1)S(1)}, bf16[40,3584]{1,0:T(8,128)(2,1)S(1)}, u32[]{:S(2)}, u32[]{:S(2)}) collective-permute-start(bf16[40,3584]{1,0:T(8,128)(2,1)S(1)} %get-tuple-element.50), channel_id=1, source_target_pairs={{0,2},{1,3},{2,0},{3,1},{4,6},{5,7},{6,4},{7,5},{8,10},{9,11},{10,... | collective-permute-start | bytes 860168 | tf_op jit(solution)/shard_map/ppermute | solution.py:22
  46.7 16.9 %collective-permute-start.11 = (bf16[40,3584]{1,0:T(8,128)(2,1)S(1)}, bf16[40,3584]{1,0:T(8,128)(2,1)S(1)}, u32[]{:S(2)}, u32[]{:S(2)}) collective-permute-start(bf16[40,3584]{1,0:T(8,128)(2,1)S(1)} %get-tuple-element.51), channel_id=1, source_target_pairs={{0,4},{1,5},{2,6},{3,7},{4,0},{5,1},{6,2},{7,3},{8,12},{9,13},{10,... | collective-permute-start | bytes 860168 | tf_op jit(solution)/shard_map/ppermute | solution.py:22
  47.2 16.4 %collective-permute-start.12 = (bf16[40,3584]{1,0:T(8,128)(2,1)S(1)}, bf16[40,3584]{1,0:T(8,128)(2,1)S(1)}, u32[]{:S(2)}, u32[]{:S(2)}) collective-permute-start(bf16[40,3584]{1,0:T(8,128)(2,1)S(1)} %get-tuple-element.52), channel_id=1, source_target_pairs={{0,6},{1,7},{2,4},{3,5},{4,2},{5,3},{6,0},{7,1},{8,14},{9,15},{10,... | collective-permute-start | bytes 860168 | tf_op jit(solution)/shard_map/ppermute | solution.py:22
  60.0 9.7 %collective-permute-start.21 = (bf16[40,3584]{1,0:T(8,128)(2,1)S(1)}, bf16[40,3584]{1,0:T(8,128)(2,1)S(1)}, u32[]{:S(2)}, u32[]{:S(2)}) collective-permute-start(bf16[40,3584]{1,0:T(8,128)(2,1)S(1)} %get-tuple-element.67), channel_id=1, source_target_pairs={{0,2},{1,3},{2,0},{3,1},{4,6},{5,7},{6,4},{7,5},{8,10},{9,11},{10,... | collective-permute-start | bytes 860168 | tf_op jit(solution)/shard_map/ppermute | solution.py:22
  61.3 12.2 %collective-permute-start.22 = (bf16[40,3584]{1,0:T(8,128)(2,1)S(1)}, bf16[40,3584]{1,0:T(8,128)(2,1)S(1)}, u32[]{:S(2)}, u32[]{:S(2)}) collective-permute-start(bf16[40,3584]{1,0:T(8,128)(2,1)S(1)} %get-tuple-element.68), channel_id=1, source_target_pairs={{0,4},{1,5},{2,6},{3,7},{4,0},{5,1},{6,2},{7,3},{8,12},{9,13},{10,... | collective-permute-start | bytes 860168 | tf_op jit(solution)/shard_map/ppermute | solution.py:22
  61.8 11.6 %collective-permute-start.23 = (bf16[40,3584]{1,0:T(8,128)(2,1)S(1)}, bf16[40,3584]{1,0:T(8,128)(2,1)S(1)}, u32[]{:S(2)}, u32[]{:S(2)}) collective-permute-start(bf16[40,3584]{1,0:T(8,128)(2,1)S(1)} %get-tuple-element.69), channel_id=1, source_target_pairs={{0,6},{1,7},{2,4},{3,5},{4,2},{5,3},{6,0},{7,1},{8,14},{9,15},{10,... | collective-permute-start | bytes 860168 | tf_op jit(solution)/shard_map/ppermute | solution.py:22
  64.2 14.6 %collective-permute-start.13 = (bf16[16,3584]{1,0:T(8,128)(2,1)S(1)}, bf16[16,3584]{1,0:T(8,128)(2,1)S(1)}, u32[]{:S(2)}, u32[]{:S(2)}) collective-permute-start(bf16[16,3584]{1,0:T(8,128)(2,1)S(1)} %get-tuple-element.54), channel_id=1, source_target_pairs={{0,8},{1,9},{2,10},{3,11},{4,12},{5,13},{6,14},{7,15},{8,0},{9,1},... | collective-permute-start | bytes 344072 | tf_op jit(solution)/shard_map/ppermute | solution.py:22
  65.2 13.6 %collective-permute-start.14 = (bf16[16,3584]{1,0:T(8,128)(2,1)S(1)}, bf16[16,3584]{1,0:T(8,128)(2,1)S(1)}, u32[]{:S(2)}, u32[]{:S(2)}) collective-permute-start(bf16[16,3584]{1,0:T(8,128)(2,1)S(1)} %get-tuple-element.55), channel_id=1, source_target_pairs={{0,16},{1,17},{2,18},{3,19},{4,20},{5,21},{6,22},{7,23},{8,24},{9,... | collective-permute-start | bytes 344072 | tf_op jit(solution)/shard_map/ppermute | solution.py:22
  69.8 9.0 %collective-permute-start.15 = (bf16[16,3584]{1,0:T(8,128)(2,1)S(1)}, bf16[16,3584]{1,0:T(8,128)(2,1)S(1)}, u32[]{:S(2)}, u32[]{:S(2)}) collective-permute-start(bf16[16,3584]{1,0:T(8,128)(2,1)S(1)} %get-tuple-element.56), channel_id=1, source_target_pairs={{0,24},{1,25},{2,26},{3,27},{4,28},{5,29},{6,30},{7,31},{8,16},{9,... | collective-permute-start | bytes 344072 | tf_op jit(solution)/shard_map/ppermute | solution.py:22
  73.8 6.7 %collective-permute-start.24 = (bf16[16,3584]{1,0:T(8,128)(2,1)S(1)}, bf16[16,3584]{1,0:T(8,128)(2,1)S(1)}, u32[]{:S(2)}, u32[]{:S(2)}) collective-permute-start(bf16[16,3584]{1,0:T(8,128)(2,1)S(1)} %get-tuple-element.71), channel_id=1, source_target_pairs={{0,8},{1,9},{2,10},{3,11},{4,12},{5,13},{6,14},{7,15},{8,0},{9,1},... | collective-permute-start | bytes 344072 | tf_op jit(solution)/shard_map/ppermute | solution.py:22
  74.3 9.4 %collective-permute-start.25 = (bf16[16,3584]{1,0:T(8,128)(2,1)S(1)}, bf16[16,3584]{1,0:T(8,128)(2,1)S(1)}, u32[]{:S(2)}, u32[]{:S(2)}) collective-permute-start(bf16[16,3584]{1,0:T(8,128)(2,1)S(1)} %get-tuple-element.72), channel_id=1, source_target_pairs={{0,16},{1,17},{2,18},{3,19},{4,20},{5,21},{6,22},{7,23},{8,24},{9,... | collective-permute-start | bytes 344072 | tf_op jit(solution)/shard_map/ppermute | solution.py:22
  78.8 6.7 %collective-permute-start.26 = (bf16[16,3584]{1,0:T(8,128)(2,1)S(1)}, bf16[16,3584]{1,0:T(8,128)(2,1)S(1)}, u32[]{:S(2)}, u32[]{:S(2)}) collective-permute-start(bf16[16,3584]{1,0:T(8,128)(2,1)S(1)} %get-tuple-element.73), channel_id=1, source_target_pairs={{0,24},{1,25},{2,26},{3,27},{4,28},{5,29},{6,30},{7,31},{8,16},{9,... | collective-permute-start | bytes 344072 | tf_op jit(solution)/shard_map/ppermute | solution.py:22
